TPU v7x, 128 devices: a whole 4x4x4 slice. The times are simulated.
128 devices in a mesh: row: 16 (over y, x_hi, core), col: 8 (over z, x_lo).
Axes of the slice: x: 4 (x_hi: 2, x_lo: 2; x = x_hi * 2 + x_lo), y: 4, z: 4, core: 2. Of those that a mesh axis runs over, the one named last changes fastest.
Arguments:
- pair_block: bfloat16 [64, 4096, 128], P('row', 'col'), may hold values from -6 to 6
- norm_gain: float32 [128], replicated, may hold values from 0.1 to 1.9
- w_project: bfloat16 [128, 512], replicated, may hold values from -0.5 to 0.5
- w_out: bfloat16 [128, 128], replicated, may hold values from -6 to 6
- head_bias: bfloat16 [4, 4096, 4096], P(None, 'col', 'row'), may hold values from -8 to 250
Outputs:
- ending_update: bfloat16 [4096, 64, 128], P(('col', 'row'))
All inputs are finite; a program needn't handle non-finite values.
Results may differ from a plain program's by a relative error of at most 0.0095.
Values may be sent and summed in bfloat16 or wider, within the bound.
No kernel may reach another device: no remote copies, remote signals or barrier semaphores. Data moves between devices by JAX's collectives and lax.ppermute only.
A program may use at most 192 MiB of HBM per device.

v0:
```python
import jax
import jax.numpy as jnp
from jax import lax
from jax.sharding import PartitionSpec as P


def layer_norm(pair_block, norm_gain):
    values = pair_block.astype(jnp.float32)
    centered = values - jnp.mean(values, axis=-1, keepdims=True)
    variance = jnp.mean(centered * centered, axis=-1, keepdims=True)
    return (centered * lax.rsqrt(variance + 1e-05) * norm_gain).astype(jnp.bfloat16)


def shards(pair_block, norm_gain, w_project, w_out, head_bias):
    row_count, col_count, channels = pair_block.shape
    head_count = head_bias.shape[0]
    inner_width = w_out.shape[0]
    head_size = inner_width // head_count
    normed = layer_norm(pair_block, norm_gain)
    flattened = normed.reshape(row_count * col_count, channels)
    projected = jnp.dot(flattened, w_project, preferred_element_type=jnp.float32)
    query_raw = projected[:, :inner_width]
    gate_raw = projected[:, 3 * inner_width :]
    own_kv = (
        projected[:, inner_width : 3 * inner_width]
        .astype(jnp.bfloat16)
        .reshape(row_count, col_count, 2 * inner_width)
    )
    pairs_kv = lax.all_gather(own_kv, "col", axis=1, tiled=True)
    key_count = pairs_kv.shape[1]
    queries = (
        (query_raw * head_size ** (-0.5))
        .astype(jnp.bfloat16)
        .reshape(row_count, col_count, head_count, head_size)
    )
    gate_value = jax.nn.sigmoid(gate_raw).reshape(row_count, col_count, inner_width)
    all_keys = pairs_kv[..., :inner_width].reshape(row_count, key_count, head_count, head_size)
    all_values = pairs_kv[..., inner_width:].reshape(row_count, key_count, head_count, head_size)
    bias_all = lax.all_gather(head_bias, "row", axis=2, tiled=True)

    def whole_row(row_items):
        query_row, key_row, value_row = row_items
        scores = jnp.einsum(
            "jhd,khd->hjk", query_row, key_row, preferred_element_type=jnp.float32
        ) + bias_all.astype(jnp.float32)
        largest = jnp.max(scores, axis=-1, keepdims=True)
        exponent = jnp.exp(scores - largest)
        running_sum = jnp.sum(exponent, axis=-1)
        result_row = jnp.einsum(
            "hjk,khd->jhd",
            exponent.astype(jnp.bfloat16),
            value_row,
            preferred_element_type=jnp.float32,
        )
        return result_row / jnp.transpose(running_sum)[:, :, None]

    attended = lax.map(whole_row, (queries, all_keys, all_values)).reshape(
        row_count, col_count, inner_width
    )
    gated = (gate_value * attended).astype(jnp.bfloat16)
    update = jnp.einsum("ijf,fc->jic", gated, w_out, preferred_element_type=jnp.float32).astype(
        jnp.bfloat16
    )
    return lax.all_to_all(update, "row", split_axis=0, concat_axis=1, tiled=True)


def solution(mesh):
    in_specs = (P("row", "col", None), P(), P(), P(), P(None, "col", "row"))
    out_specs = P(("col", "row"), None, None)
    return jax.shard_map(shards, mesh=mesh, in_specs=in_specs, out_specs=out_specs, check_vma=False)
```

profile of v0, /device:TPU:1, one launch (start us, length us, event | category | flops | bytes accessed | tf_op | source)
XLA Modules:
  0.0 508.7 jit_solution(15620494186760237358)
XLA Ops:
  6.5 1.3 convert_reduce_fusion
  7.8 1.7 fusion.28
  9.5 1.6 fusion.30
  11.9 1.9 copy-done.2
  15.7 2.8 fusion.31
  19.3 167.4 %all-gather.3.cloned.1.call-done = bf16[4,4096,256]{2,1,0:T(8,128)(2,1)} async-done(((bf16[4,512,256]{2,1,0:T(8,128)(2,1)}), bf16[4,4096,256]{2,1,0:T(8,128)(2,1)}) %all-gather.3.cloned.1.call-update) | async-done | bytes 8388624 | tf_op jit(solution)/shard_map/all_gather | solution.py:29
  186.7 5.7 %fusion.37 = (bf16[4,4096,128]{2,1,0:T(8,128)(2,1)}, bf16[4,4096,128]{2,1,0:T(8,128)(2,1)}) fusion(bf16[4,4096,256]{2,1,0:T(8,128)(2,1)} %all-gather.3.cloned.1.call-done), kind=kLoop, calls=%fused_computation.39 | loop fusion | bytes 16777216 | tf_op jit(solution)/shard_map/slice | solution.py:37
  192.3 6.4 %copy.19 = bf16[4,4096,128]{1,2,0:T(8,128)(2,1)} copy(bf16[4,4096,128]{2,1,0:T(8,128)(2,1)} %get-tuple-element.70) | data formatting | bytes 8388608 | tf_op jit(solution)/shard_map/slice | solution.py:37
  198.7 6.6 %copy.17 = bf16[4,4096,128]{1,2,0:T(8,128)(2,1)} copy(bf16[4,4096,128]{2,1,0:T(8,128)(2,1)} %get-tuple-element.71) | data formatting | bytes 8388608 | tf_op jit(solution)/shard_map/slice | solution.py:38
  205.3 104.1 %all-gather.5.cloned.1.call-done = bf16[4,512,4096]{2,1,0:T(8,128)(2,1)} async-done(((bf16[4,512,256]{2,1,0:T(8,128)(2,1)}), bf16[4,512,4096]{2,1,0:T(8,128)(2,1)}) %all-gather.5.cloned.1.call-update) | async-done | bytes 16777232 | tf_op jit(solution)/shard_map/all_gather | solution.py:39
  309.4 176.3 %while.10 = (s32[]{:T(128)}, f32[4,512,4,32]{1,3,2,0:T(8,128)S(1)}, bf16[4,4096,4,32]{1,3,2,0:T(8,128)(2,1)}, bf16[4,512,4,32]{1,3,2,0:T(8,128)(2,1)S(1)}, bf16[...) while((s32[]{:T(128)}, f32[4,512,4,32]{1,3,2,0:T(8,128)S(1)}, ...), condition=%wide.region_5.6_spmd, body=%wide.region_2.5_spmd.sunk | while | flops 1132523520 | bytes 119973968 | solution.py:57
  309.4 16.9 %fusion.48 = (f32[4,512]{1,0:T(4,128)S(1)}, f32[4,512,4096]{2,1,0:T(8,128)}) fusion(bf16[4,512,4096]{2,1,0:T(8,128)(2,1)} %get-tuple-element.134, bf16[4,4096,4,32]{1,3,2,0:T(8,128)(2,1)} %get-tuple-element.133, s32[]{:T(128)} %get-tuple-element.122, bf16[4,512,4,32]{1,3,2,0:T(8,128)(2,1)S(1)} %get-tuple-element.132), kind=kOutput, calls=%fused_computation.38.clone.1 | convolution fusion | flops 562034688 | bytes 51520512 | tf_op jit(solution)/shard_map/while/body/eval_jaxpr/jhd,khd->hjk/dot_general | solution.py:43
  326.3 13.6 %fusion.49 = f32[4,512]{1,0:T(4,128)S(1)} fusion(f32[4,512,4096]{2,1,0:T(8,128)} %get-tuple-element.113, f32[4,512]{1,0:T(4,128)S(1)} %get-tuple-element.114), kind=kLoop, calls=%fused_computation.2.clone.1 | loop fusion | flops 16775168 | bytes 33570816 | tf_op jit(solution)/shard_map/while/body/eval_jaxpr/reduce_sum | solution.py:48
  339.9 13.6 %fusion.50 = f32[4,512,4,32]{1,3,2,0:T(8,128)S(1)} fusion(f32[4,512,4,32]{1,3,2,0:T(8,128)S(1)} %get-tuple-element.123, s32[]{:T(128)} %get-tuple-element.122, f32[4,512,4096]{2,1,0:T(8,128)} %get-tuple-element.113, f32[4,512]{1,0:T(4,128)S(1)} %get-tuple-element.114, bf16[4,4096,4,32]{1,3,2,0:T(8,128)(2,1)} %get-tuple-element.131, ...), kind=kOutput, calls=%fused_computation.9.clone.1 | convolution fusion | flops 553713664 | bytes 34882560 | tf_op jit(solution)/shard_map/while/body/eval_jaxpr/hjk,khd->jhd/dot_general | solution.py:49
  353.5 16.9 %fusion.48 = (f32[4,512]{1,0:T(4,128)S(1)}, f32[4,512,4096]{2,1,0:T(8,128)}) fusion(bf16[4,512,4096]{2,1,0:T(8,128)(2,1)} %get-tuple-element.134, bf16[4,4096,4,32]{1,3,2,0:T(8,128)(2,1)} %get-tuple-element.133, s32[]{:T(128)} %get-tuple-element.122, bf16[4,512,4,32]{1,3,2,0:T(8,128)(2,1)S(1)} %get-tuple-element.132), kind=kOutput, calls=%fused_computation.38.clone.1 | convolution fusion | flops 562034688 | bytes 51520512 | tf_op jit(solution)/shard_map/while/body/eval_jaxpr/jhd,khd->hjk/dot_general | solution.py:43
  370.4 13.6 %fusion.49 = f32[4,512]{1,0:T(4,128)S(1)} fusion(f32[4,512,4096]{2,1,0:T(8,128)} %get-tuple-element.113, f32[4,512]{1,0:T(4,128)S(1)} %get-tuple-element.114), kind=kLoop, calls=%fused_computation.2.clone.1 | loop fusion | flops 16775168 | bytes 33570816 | tf_op jit(solution)/shard_map/while/body/eval_jaxpr/reduce_sum | solution.py:48
  384.0 13.6 %fusion.50 = f32[4,512,4,32]{1,3,2,0:T(8,128)S(1)} fusion(f32[4,512,4,32]{1,3,2,0:T(8,128)S(1)} %get-tuple-element.123, s32[]{:T(128)} %get-tuple-element.122, f32[4,512,4096]{2,1,0:T(8,128)} %get-tuple-element.113, f32[4,512]{1,0:T(4,128)S(1)} %get-tuple-element.114, bf16[4,4096,4,32]{1,3,2,0:T(8,128)(2,1)} %get-tuple-element.131, ...), kind=kOutput, calls=%fused_computation.9.clone.1 | convolution fusion | flops 553713664 | bytes 34882560 | tf_op jit(solution)/shard_map/while/body/eval_jaxpr/hjk,khd->jhd/dot_general | solution.py:49
  397.6 16.9 %fusion.48 = (f32[4,512]{1,0:T(4,128)S(1)}, f32[4,512,4096]{2,1,0:T(8,128)}) fusion(bf16[4,512,4096]{2,1,0:T(8,128)(2,1)} %get-tuple-element.134, bf16[4,4096,4,32]{1,3,2,0:T(8,128)(2,1)} %get-tuple-element.133, s32[]{:T(128)} %get-tuple-element.122, bf16[4,512,4,32]{1,3,2,0:T(8,128)(2,1)S(1)} %get-tuple-element.132), kind=kOutput, calls=%fused_computation.38.clone.1 | convolution fusion | flops 562034688 | bytes 51520512 | tf_op jit(solution)/shard_map/while/body/eval_jaxpr/jhd,khd->hjk/dot_general | solution.py:43
  414.4 13.6 %fusion.49 = f32[4,512]{1,0:T(4,128)S(1)} fusion(f32[4,512,4096]{2,1,0:T(8,128)} %get-tuple-element.113, f32[4,512]{1,0:T(4,128)S(1)} %get-tuple-element.114), kind=kLoop, calls=%fused_computation.2.clone.1 | loop fusion | flops 16775168 | bytes 33570816 | tf_op jit(solution)/shard_map/while/body/eval_jaxpr/reduce_sum | solution.py:48
  428.0 13.6 %fusion.50 = f32[4,512,4,32]{1,3,2,0:T(8,128)S(1)} fusion(f32[4,512,4,32]{1,3,2,0:T(8,128)S(1)} %get-tuple-element.123, s32[]{:T(128)} %get-tuple-element.122, f32[4,512,4096]{2,1,0:T(8,128)} %get-tuple-element.113, f32[4,512]{1,0:T(4,128)S(1)} %get-tuple-element.114, bf16[4,4096,4,32]{1,3,2,0:T(8,128)(2,1)} %get-tuple-element.131, ...), kind=kOutput, calls=%fused_computation.9.clone.1 | convolution fusion | flops 553713664 | bytes 34882560 | tf_op jit(solution)/shard_map/while/body/eval_jaxpr/hjk,khd->jhd/dot_general | solution.py:49
  441.6 16.9 %fusion.48 = (f32[4,512]{1,0:T(4,128)S(1)}, f32[4,512,4096]{2,1,0:T(8,128)}) fusion(bf16[4,512,4096]{2,1,0:T(8,128)(2,1)} %get-tuple-element.134, bf16[4,4096,4,32]{1,3,2,0:T(8,128)(2,1)} %get-tuple-element.133, s32[]{:T(128)} %get-tuple-element.122, bf16[4,512,4,32]{1,3,2,0:T(8,128)(2,1)S(1)} %get-tuple-element.132), kind=kOutput, calls=%fused_computation.38.clone.1 | convolution fusion | flops 562034688 | bytes 51520512 | tf_op jit(solution)/shard_map/while/body/eval_jaxpr/jhd,khd->hjk/dot_general | solution.py:43
  458.5 13.6 %fusion.49 = f32[4,512]{1,0:T(4,128)S(1)} fusion(f32[4,512,4096]{2,1,0:T(8,128)} %get-tuple-element.113, f32[4,512]{1,0:T(4,128)S(1)} %get-tuple-element.114), kind=kLoop, calls=%fused_computation.2.clone.1 | loop fusion | flops 16775168 | bytes 33570816 | tf_op jit(solution)/shard_map/while/body/eval_jaxpr/reduce_sum | solution.py:48
  472.0 13.6 %fusion.50 = f32[4,512,4,32]{1,3,2,0:T(8,128)S(1)} fusion(f32[4,512,4,32]{1,3,2,0:T(8,128)S(1)} %get-tuple-element.123, s32[]{:T(128)} %get-tuple-element.122, f32[4,512,4096]{2,1,0:T(8,128)} %get-tuple-element.113, f32[4,512]{1,0:T(4,128)S(1)} %get-tuple-element.114, bf16[4,4096,4,32]{1,3,2,0:T(8,128)(2,1)} %get-tuple-element.131, ...), kind=kOutput, calls=%fused_computation.9.clone.1 | convolution fusion | flops 553713664 | bytes 34882560 | tf_op jit(solution)/shard_map/while/body/eval_jaxpr/hjk,khd->jhd/dot_general | solution.py:49
  486.7 14.1 %all_to_all.18 = bf16[512,4,128]{2,1,0:T(4,128)(2,1)S(1)} all-to-all(bf16[512,4,128]{2,1,0:T(4,128)(2,1)S(1)} %copy.22), channel_id=1, replica_groups=mesh['row'=16,'col'=8] {'row'}, dimensions={0} | all-to-all | bytes 1048576 | tf_op jit(solution)/shard_map/all_to_all | solution.py:64
  (25 shorter events, 5.4 us)
Async XLA Ops:
  6.5 4.7 copy-start
  6.5 180.1 %all-gather.3.cloned.1.call-start = ((), (), s32[]{:S(2)}) async-start(), calls=%async_computation.1 | async-start | bytes 9437184 | tf_op jit(solution)/shard_map/all_gather | solution.py:29
  11.9 1.9 copy-start.2
  15.0 294.4 %all-gather.5.cloned.1.call-start = ((), (), s32[]{:S(2)}) async-start(), calls=%async_computation.2 | async-start | bytes 17825792 | tf_op jit(solution)/shard_map/all_gather | solution.py:39
  309.4 176.6 %copy-start.3 = (f32[2048,128]{1,0:T(8,128)S(1)}, f32[2048,128]{1,0:T(8,128)}, u32[]{:S(2)}) copy-start(f32[2048,128]{1,0:T(8,128)} %get-tuple-element.73) | copy-start | bytes 3145732
  309.4 176.6 %copy-start.4 = (bf16[128,128]{1,0:T(8,128)(2,1)S(1)}, bf16[128,128]{1,0:T(8,128)(2,1)}, u32[]{:S(2)}) copy-start(bf16[128,128]{1,0:T(8,128)(2,1)} %param.10) | copy-start | bytes 98308
  485.6 16.2 %copy-start.1 = (bf16[128,512]{1,0:T(8,128)(2,1)S(1)}, bf16[128,512]{1,0:T(8,128)(2,1)}, u32[]{:S(2)}) copy-start(bf16[128,512]{1,0:T(8,128)(2,1)} %param.9) | copy-start | bytes 393220
Sparse Core Ops, SparseCore 0:
  15.1 171.5 all-gather.2
  189.0 120.3 all-gather.4
where the time goes:
time: 510 us; the launch traced here: 509 us
  waiting for transfers between devices  272 us (53%)
  matrix products  123 us (24%)
  other arithmetic  61.7 us (12%)
  local copies, waits for them, and re-layouts  24.2 us (5%)
  blocking collectives  14.1 us (3%)
  between operations  13.5 us (3%)
    all_gather x1, waiting for transfers between devices, shards(): pairs_kv = lax.all_gather(own_kv, 'col', axis=1, tiled=True)  167 us
    all_gather x1, waiting for transfers between devices, shards(): bias_all = lax.all_gather(head_bias, 'row', axis=2, tiled=True)  104 us
    dot_general x4, matrix products, whole_row(): jnp.einsum('jhd,khd->hjk', query_row, key_row, preferred_element_type=jnp...  67.6 us
    dot_general x4, matrix products, whole_row(): jnp.einsum('hjk,khd->jhd', exponent.astype(jnp.bfloat16), value_row, pref...  54.3 us
    reduce_sum x4, other arithmetic, whole_row(): running_sum = jnp.sum(exponent, axis=-1)  54.3 us
    all_to_all x1, blocking collectives, shards(): lax.all_to_all(update, 'row', split_axis=0, concat_axis=1, tiled=True)  14.1 us
    slice x2, local copies, waits for them, and re-layouts, shards(): pairs_kv[..., :inner_width]  12.1 us
  transfers between devices with their start and end apart: 2, of which 2 were waited for; matrix products, arithmetic and copies ran while one was open for 4% of the time, Pallas kernels for 0%

commit v1 on v0

v1 whole, which is shorter than its diff:
```python
import functools

import jax
import jax.numpy as jnp
from jax import lax
from jax.experimental import pallas as pl
from jax.experimental.pallas import tpu as pltpu
from jax.sharding import Mesh, PartitionSpec as P

F32, BF16 = jnp.float32, jnp.bfloat16
HEADS, WIDTH, CHANNELS = 4, 32, 128
COLS, BLOCK, ROWS = 512, 512, 4
KEYS = 4 * BLOCK
PAD = 40
LOG2E = 1.4426950408889634
ROW_AXES = ("y", "xh", "core")
COL_AXES = ("z", "xl")
CONTRACT_FIRST = (((0,), (1,)), ((), ()))


def matmul(a, b, dims=(((1,), (0,)), ((), ()))):
    return lax.dot_general(a, b, dims, preferred_element_type=F32)


def layer_norm(pair_block, norm_gain):
    values = pair_block.astype(F32)
    centered = values - jnp.mean(values, axis=-1, keepdims=True)
    variance = jnp.mean(centered * centered, axis=-1, keepdims=True)
    return (centered * lax.rsqrt(variance + 1e-05) * norm_gain).astype(BF16)


def attend_kernel(xq, xk0, xk1, xk2a, xk2b, xk3, w, *rest):
    biases, (out, lse), (bias_s, k_s, v_s, q_s, sems) = rest[:8], rest[8:10], rest[10:]
    row = pl.program_id(0)
    y, z, core = lax.axis_index("y"), lax.axis_index("z"), lax.axis_index("core")

    def bias_copies():
        copies = []
        for n, ref in enumerate(biases):
            step, other = (0, 1, 3, 2)[n // 2], n % 2
            slot = lax.rem(y + step - z + 4, 4)
            half = core if other == 0 else 1 - core
            dst = bias_s.at[slot, :, pl.ds(pl.multiple_of(half * 256, 256), 256), :]
            copies.append(pltpu.make_async_copy(ref, dst, sems.at[n]))
        return copies

    @pl.when(row == 0)
    def _():
        for copy in bias_copies():
            copy.start()
        q_s[...] = jnp.zeros_like(q_s)
        v_s[:, WIDTH:, :] = jnp.ones((HEADS, PAD - WIDTH, KEYS), BF16)

    x_q = xq[0]
    q_t = matmul(w[:, :128], x_q, CONTRACT_FIRST) * WIDTH ** (-0.5)
    q_t = q_t.astype(BF16)
    gate_t = jax.nn.sigmoid(matmul(w[:, 384:], x_q, CONTRACT_FIRST))
    for h in range(HEADS):
        q_s[h, h * WIDTH : (h + 1) * WIDTH, :] = q_t[h * WIDTH : (h + 1) * WIDTH]
    start = 0
    for x in (xk0, xk1, xk2a, xk2b, xk3):
        x_k = x[0]
        size = x_k.shape[0]
        at = slice(start, start + size)
        k_s[at, :] = matmul(x_k, w[:, 128:256]).astype(BF16)
        v_t = matmul(w[:, 256:384], x_k, CONTRACT_FIRST).astype(BF16)
        for h in range(HEADS):
            v_s[h, :WIDTH, at] = v_t[h * WIDTH : (h + 1) * WIDTH]
        start += size

    @pl.when(row == 0)
    def _():
        for copy in bias_copies():
            copy.wait()

    parts = []
    for h in range(HEADS):
        q = q_s[h]

        def scores(t):
            at = slice(t * BLOCK, (t + 1) * BLOCK)
            return matmul(k_s[at, :], q) + bias_s[t, h].astype(F32)

        s = scores(0)
        largest = total = None
        for t in range(4):
            ahead = scores(t + 1) if t < 3 else None
            top = jnp.max(s, axis=0, keepdims=True)
            fresh = top if t == 0 else jnp.maximum(largest, top)
            p = jnp.exp2((s - fresh) * LOG2E).astype(BF16)
            pv = matmul(v_s[h, :, t * BLOCK : (t + 1) * BLOCK], p)
            total = pv if t == 0 else total * jnp.exp2((largest - fresh) * LOG2E) + pv
            largest, s = fresh, ahead
        mass = total[WIDTH : WIDTH + 1]
        lse[0, h : h + 1, :] = largest + jnp.log(mass)
        parts.append(total[:WIDTH] * (1.0 / mass))
    gated = jnp.concatenate(parts, axis=0) * gate_t
    out[0] = gated.T.astype(BF16)


def attend(x_q, x_ks, w_project, biases):
    def rows(x):
        return pl.BlockSpec((1,) + x.shape[1:], lambda i: (i, 0, 0))

    count = x_q.shape[0]
    scores = count * HEADS * COLS * KEYS
    return pl.pallas_call(
        attend_kernel,
        grid=(count,),
        in_specs=[rows(x_q)]
        + [rows(x) for x in x_ks]
        + [pl.BlockSpec((CHANNELS, 512), lambda i: (0, 0))]
        + [pl.BlockSpec(memory_space=pl.ANY)] * 8,
        out_specs=[
            pl.BlockSpec((1, COLS, CHANNELS), lambda i: (i, 0, 0)),
            pl.BlockSpec((1, HEADS, COLS), lambda i: (i, 0, 0)),
        ],
        out_shape=[
            jax.ShapeDtypeStruct((count, COLS, CHANNELS), BF16),
            jax.ShapeDtypeStruct((count, HEADS, COLS), F32),
        ],
        scratch_shapes=[
            pltpu.VMEM((4, HEADS, BLOCK, COLS), BF16),
            pltpu.VMEM((KEYS, CHANNELS), BF16),
            pltpu.VMEM((HEADS, PAD, KEYS), BF16),
            pltpu.VMEM((HEADS, CHANNELS, COLS), BF16),
            pltpu.SemaphoreType.DMA((8,)),
        ],
        compiler_params=pltpu.CompilerParams(vmem_limit_bytes=56 * 2**20),
        cost_estimate=pl.CostEstimate(
            flops=scores * 512, bytes_accessed=2**24, transcendentals=scores
        ),
        name="attend",
    )(x_q, *x_ks, w_project, *biases)


def ring(step):
    return [(i, (i + step) % 4) for i in range(4)]


def shift(x, axis, step):
    return lax.ppermute(x, axis, ring(step))


def gather_ring(x, axis, cut):
    behind, ahead = shift(x, axis, 1), shift(x, axis, -1)
    half = x.shape[cut] // 2
    far_a = shift(lax.slice_in_dim(behind, 0, half, axis=cut), axis, 1)
    far_b = shift(lax.slice_in_dim(ahead, half, 2 * half, axis=cut), axis, -1)
    return x, ahead, far_a, far_b, behind


def shards(pair_block, norm_gain, w_project, w_out, head_bias):
    xh, xl = lax.axis_index("xh"), lax.axis_index("xl")
    own = layer_norm(pair_block, norm_gain)
    bias_t = jnp.transpose(head_bias, (0, 2, 1))

    x_axis = ("xh", "xl")
    beside = lax.ppermute(own, x_axis, [(0, 1), (3, 2)])
    across = lax.ppermute(own, x_axis, [(1, 2), (2, 1)])
    first_k = jnp.where(xl == xh, own, beside)
    passed = lax.ppermute(across, x_axis, [(1, 0), (2, 3)])
    second_k = jnp.where(xl == xh, passed, across)
    partner = lax.ppermute(own, x_axis, [(3, 1), (0, 2)])
    second_q = jnp.where(xl == xh, passed, partner)

    b0, b1, b2a, b2b, b3 = gather_ring(bias_t, "y", 0)
    b2 = jnp.concatenate([b2a, b2b], axis=0)
    biases = []
    for b in (b0, b1, b3, b2):
        biases += [b, lax.ppermute(b, "core", [(0, 1), (1, 0)])]

    first_ks = gather_ring(first_k, "z", 1)
    second_ks = gather_ring(second_k, "z", 1)

    out1, lse1 = attend(own, first_ks, w_project, biases)
    out2, lse2 = attend(second_q, second_ks, w_project, biases)

    def spread(x, axis):
        return lax.all_to_all(x, ROW_AXES, split_axis=axis, concat_axis=0, tiled=True)

    def flip(x):
        return x.reshape((4, 2, 8) + x.shape[1:])[:, ::-1].reshape(x.shape)

    out1, out2 = spread(out1, 1), flip(spread(out2, 1))
    lse1, lse2 = spread(lse1, 2), flip(spread(lse2, 2))
    lanes = (jnp.arange(CHANNELS)[None, :] // WIDTH == jnp.arange(HEADS)[:, None]).astype(F32)
    share = jax.nn.sigmoid(lse1 - lse2)
    share = jnp.einsum("rhj,hl->rjl", share, lanes, precision=lax.Precision.HIGHEST)
    out2 = out2.astype(F32)
    gated = (out2 + share * (out1.astype(F32) - out2)).astype(BF16)
    return jnp.einsum("ijf,fc->jic", gated, w_out, preferred_element_type=F32).astype(BF16)


def solution(mesh):
    fine = Mesh(mesh.devices.reshape(4, 2, 2, 4, 2), ROW_AXES + COL_AXES)
    in_specs = (P(ROW_AXES, COL_AXES, None), P(), P(), P(), P(None, COL_AXES, ROW_AXES))
    out_specs = P(COL_AXES + ROW_AXES, None, None)
    return jax.shard_map(
        shards, mesh=fine, in_specs=in_specs, out_specs=out_specs, check_vma=False
    )
```

time: 510 us -> 220 us (0.43)
  waiting for transfers between devices: 272 us -> 49.1 us
  matrix products: 123 us -> 1.33 us
  starting transfers between devices: 0.04 us -> 79 us
  Pallas kernels: 0 us -> 62.3 us
  other arithmetic: 61.7 us -> 6.35 us
  blocking collectives: 14.1 us -> 0 us
  between operations: 13.5 us -> 0.47 us
    all_gather x2 -> x0, waiting for transfers between devices: 271 us -> none  [the longest x1 167 us: shards(): pairs_kv = lax.all_gather(own_kv, 'col', axis=1, tiled=True)]
    dot_general x10 -> x2, matrix products: 123 us -> 1.33 us  [the longest x1 1.04 us: shards(): jnp.einsum('rhj,hl->rjl', share, lanes, precision=lax.Precision.HIGHEST)]
    pallas_call x0 -> x2, Pallas kernels: none -> 62.3 us  [attend(): pl.pallas_call(attend_kernel, grid=(count,), in_specs=[rows(x_q)] + [rows...]
    reduce_sum x4 -> x0, other arithmetic: 54.3 us -> none  [whole_row(): running_sum = jnp.sum(exponent, axis=-1)]
    ppermute x0 -> x20, starting transfers between devices: none -> 46.8 us  [the longest x12 18.3 us: shift(): return lax.ppermute(x, axis, ring(step))]
    all_to_all x0 -> x4, starting transfers between devices: none -> 32.2 us  [spread(): lax.all_to_all(x, ROW_AXES, split_axis=axis, concat_axis=0, tiled=True)]
    ppermute x0 -> x20, waiting for transfers between devices: none -> 27.5 us  [the longest x12 25.4 us: shift(): return lax.ppermute(x, axis, ring(step))]
    all_to_all x0 -> x4, waiting for transfers between devices: none -> 21.6 us  [spread(): lax.all_to_all(x, ROW_AXES, split_axis=axis, concat_axis=0, tiled=True)]
  transfers between devices with their start and end apart: 2 -> 24, of which waited for: 2 -> 9; matrix products, arithmetic and copies ran while one was open for 4% -> 9% of each run, Pallas kernels for 0% -> 28%
where the time goes in v1:
time: 220 us; the launch traced here: 219 us
  starting transfers between devices  79 us (36%)
  Pallas kernels  62.3 us (28%)
  waiting for transfers between devices  49.1 us (22%)
  local copies, waits for them, and re-layouts  20.9 us (10%)
  other arithmetic  6.35 us (3%)
    pallas_call x2, Pallas kernels, attend(): pl.pallas_call(attend_kernel, grid=(count,), in_specs=[rows(x_q)] + [rows...  62.3 us
    all_to_all x4, starting transfers between devices, spread(): lax.all_to_all(x, ROW_AXES, split_axis=axis, concat_axis=0, tiled=True)  32.2 us
    ppermute x12, waiting for transfers between devices, shift(): return lax.ppermute(x, axis, ring(step))  25.4 us
    all_to_all x4, waiting for transfers between devices, spread(): lax.all_to_all(x, ROW_AXES, split_axis=axis, concat_axis=0, tiled=True)  21.6 us
    ppermute x12, starting transfers between devices, shift(): return lax.ppermute(x, axis, ring(step))  18.3 us
    ppermute x1, starting transfers between devices, shards(): beside = lax.ppermute(own, x_axis, [(0, 1), (3, 2)])  13.3 us
    unnamed x54, local copies, waits for them, and re-layouts  12.2 us
    ppermute x4, starting transfers between devices, shards(): biases += [b, lax.ppermute(b, 'core', [(0, 1), (1, 0)])]  6.28 us
  transfers between devices with their start and end apart: 24, of which 9 were waited for; matrix products, arithmetic and copies ran while one was open for 9% of the time, Pallas kernels for 28%

profile of v1, /device:TPU:1, one launch (start us, length us, event | category | flops | bytes accessed | tf_op | source)
XLA Modules:
  0.0 219.4 jit_solution(4593794774177034828)
XLA Ops:
  1.6 2.2 %collective-permute-start.10 = (bf16[4,256,512]{2,1,0:T(8,128)(2,1)S(1)}, bf16[4,256,512]{2,1,0:T(8,128)(2,1)S(1)}, u32[]{:S(2)}, u32[]{:S(2)}) collective-permute-start(bf16[4,256,512]{2,1,0:T(8,128)(2,1)S(1)} %bitcast.52), channel_id=1, source_target_pairs={{0,32},{32,64},{64,96},{96,0},{1,33},{33,65},{65,97},{97,1},{2,34}... | collective-permute-start | bytes 3145736 | tf_op jit(solution)/shard_map/ppermute | solution.py:142
  9.7 6.1 %collective-permute-start.2 = (bf16[4,512,128]{2,1,0:T(8,128)(2,1)}, bf16[4,512,128]{2,1,0:T(8,128)(2,1)}, u32[]{:S(2)}, u32[]{:S(2)}) collective-permute-start(bf16[4,512,128]{2,1,0:T(8,128)(2,1)} %fusion.7.xq), channel_id=1, source_target_pairs={{17,1},{0,16},{19,3},{2,18},{21,5},{4,20},{23,7},{6,22},{25,9},{8,... | collective-permute-start | bytes 1572872 | tf_op jit(solution)/shard_map/ppermute | solution.py:164
  18.9 9.1 %collective-permute-done.10.rest_4_ = bf16[4,256,512]{2,1,0:T(8,128)(2,1)S(1)} collective-permute-done((bf16[4,256,512]{2,1,0:T(8,128)(2,1)S(1)}, bf16[4,256,512]{2,1,0:T(8,128)(2,1)S(1)}, u32[]{:S(2)}, u32[]{:S(2)}) %collective-permute-start.10) | collective-permute-done | bytes 1048608 | tf_op jit(solution)/shard_map/ppermute | solution.py:142
  28.9 2.7 %collective-permute-start.13 = (bf16[2,256,512]{2,1,0:T(8,128)(2,1)S(1)}, bf16[2,256,512]{2,1,0:T(8,128)(2,1)S(1)}, u32[]{:S(2)}, u32[]{:S(2)}) collective-permute-start(bf16[2,256,512]{2,1,0:T(8,128)(2,1)S(1)} %slice.27), channel_id=1, source_target_pairs={{0,96},{32,0},{64,32},{96,64},{1,97},{33,1},{65,33},{97,65},{2,98}... | collective-permute-start | bytes 1572872 | tf_op jit(solution)/shard_map/ppermute | solution.py:142
  31.6 13.3 %collective-permute-start.15 = (bf16[4,512,128]{2,1,0:T(8,128)(2,1)}, bf16[4,512,128]{2,1,0:T(8,128)(2,1)S(1)}, u32[]{:S(2)}, u32[]{:S(2)}) collective-permute-start(bf16[4,512,128]{2,1,0:T(8,128)(2,1)} %fusion.7.xq), channel_id=1, source_target_pairs={{0,1},{17,16},{2,3},{19,18},{4,5},{21,20},{6,7},{23,22},{8,9},{25,... | collective-permute-start | bytes 1572872 | tf_op jit(solution)/shard_map/ppermute | solution.py:159
  45.0 2.0 collective-permute-done.1
  47.0 1.9 broadcast_select_fusion.1
  50.5 2.2 %collective-permute-start.3 = (bf16[4,512,128]{2,1,0:T(8,128)(2,1)S(1)}, bf16[4,512,128]{2,1,0:T(8,128)(2,1)S(1)}, u32[]{:S(2)}, u32[]{:S(2)}) collective-permute-start(bf16[4,512,128]{2,1,0:T(8,128)(2,1)S(1)} %get-tuple-element.13.xk0), channel_id=1, source_target_pairs={{0,6},{2,0},{4,2},{6,4},{1,7},{3,1},{5,3},{7,5},{8,14},{10,8},{12,... | collective-permute-start | bytes 1572872 | tf_op jit(solution)/shard_map/ppermute | solution.py:142
  52.8 3.0 %collective-permute-start.11 = (bf16[4,256,512]{2,1,0:T(8,128)(2,1)S(1)}, bf16[4,256,512]{2,1,0:T(8,128)(2,1)S(1)}, u32[]{:S(2)}, u32[]{:S(2)}) collective-permute-start(bf16[4,256,512]{2,1,0:T(8,128)(2,1)S(1)} %copy-done.8), channel_id=1, source_target_pairs={{0,8},{8,0},{1,9},{9,1},{2,10},{10,2},{3,11},{11,3},{4,12},{12,4},... | collective-permute-start | bytes 3145736 | tf_op jit(solution)/shard_map/ppermute | solution.py:171
  58.2 4.0 %collective-permute-done.4.xk3 = bf16[4,512,128]{2,1,0:T(8,128)(2,1)S(1)} collective-permute-done((bf16[4,512,128]{2,1,0:T(8,128)(2,1)S(1)}, bf16[4,512,128]{2,1,0:T(8,128)(2,1)S(1)}, u32[]{:S(2)}, u32[]{:S(2)}) %collective-permute-start.4) | collective-permute-done | bytes 524320 | tf_op jit(solution)/shard_map/ppermute | solution.py:142
  62.3 2.7 %collective-permute-start.16 = (bf16[4,512,128]{2,1,0:T(8,128)(2,1)S(1)}, bf16[4,512,128]{2,1,0:T(8,128)(2,1)S(1)}, u32[]{:S(2)}, u32[]{:S(2)}) collective-permute-start(bf16[4,512,128]{2,1,0:T(8,128)(2,1)S(1)} %broadcast_select_fusion.xk0), channel_id=1, source_target_pairs={{0,6},{2,0},{4,2},{6,4},{1,7},{3,1},{5,3},{7,5},{8,14},{10,8},{12,... | collective-permute-start | bytes 1572872 | tf_op jit(solution)/shard_map/ppermute | solution.py:142
  65.0 8.6 %collective-permute-done.17.xk3 = bf16[4,512,128]{2,1,0:T(8,128)(2,1)S(1)} collective-permute-done((bf16[4,512,128]{2,1,0:T(8,128)(2,1)S(1)}, bf16[4,512,128]{2,1,0:T(8,128)(2,1)S(1)}, u32[]{:S(2)}, u32[]{:S(2)}) %collective-permute-start.17) | collective-permute-done | bytes 524320 | tf_op jit(solution)/shard_map/ppermute | solution.py:142
  73.6 2.7 %collective-permute-start.6 = (bf16[4,256,128]{2,1,0:T(8,128)(2,1)S(1)}, bf16[4,256,128]{2,1,0:T(8,128)(2,1)S(1)}, u32[]{:S(2)}, u32[]{:S(2)}) collective-permute-start(bf16[4,256,128]{2,1,0:T(8,128)(2,1)S(1)} %slice.25), channel_id=1, source_target_pairs={{0,6},{2,0},{4,2},{6,4},{1,7},{3,1},{5,3},{7,5},{8,14},{10,8},{12,... | collective-permute-start | bytes 786440 | tf_op jit(solution)/shard_map/ppermute | solution.py:142
  76.3 3.7 %collective-permute-done.5.xk2a = bf16[4,256,128]{2,1,0:T(8,128)(2,1)S(1)} collective-permute-done((bf16[4,256,128]{2,1,0:T(8,128)(2,1)S(1)}, bf16[4,256,128]{2,1,0:T(8,128)(2,1)S(1)}, u32[]{:S(2)}, u32[]{:S(2)}) %collective-permute-start.5) | collective-permute-done | bytes 262176 | tf_op jit(solution)/shard_map/ppermute | solution.py:142
  80.0 2.7 %collective-permute-start.19 = (bf16[4,256,128]{2,1,0:T(8,128)(2,1)S(1)}, bf16[4,256,128]{2,1,0:T(8,128)(2,1)S(1)}, u32[]{:S(2)}, u32[]{:S(2)}) collective-permute-start(bf16[4,256,128]{2,1,0:T(8,128)(2,1)S(1)} %slice.29), channel_id=1, source_target_pairs={{0,6},{2,0},{4,2},{6,4},{1,7},{3,1},{5,3},{7,5},{8,14},{10,8},{12,... | collective-permute-start | bytes 786440 | tf_op jit(solution)/shard_map/ppermute | solution.py:142
  85.1 31.2 %attend.2 = (bf16[4,512,128]{2,1,0:T(8,128)(2,1)}, f32[4,4,512]{2,1,0:T(4,128)}) custom-call(bf16[4,512,128]{2,1,0:T(8,128)(2,1)} %get-tuple-element.14.xq, bf16[4,512,128]{2,1,0:T(8,128)(2,1)} %copy-done.5, bf16[4,512,128]{2,1,0:T(8,128)(2,1)} %copy-done.13, bf16[4,256,128]{2,1,0:T(8,128)(2,1)} %copy-done.22, bf16[4,256,128]{2,1,0:T(8,128)(2,1)} %copy-done.23, ...), custom_call_target="tpu_custom_call" | custom-call | flops 8589934592 | bytes 16777216 | tf_op jit(solution)/shard_map/attend/pallas_call | solution.py:107
  119.1 16.7 %all-to-all-start.2 = ((f32[16,1,512]{2,1,0:T(1,128)}), f32[16,1,512]{2,1,0:T(1,128)S(1)}, u32[]{:S(2)}, u32[]{:S(2)}) async-start(f32[16,1,512]{2,1,0:T(1,128)} %reshape.78), calls=%async_computation.2 | async-start | bytes 65536 | tf_op jit(solution)/shard_map/all_to_all | solution.py:180
  137.3 31.1 %attend.3 = (bf16[4,512,128]{2,1,0:T(8,128)(2,1)}, f32[4,4,512]{2,1,0:T(4,128)}) custom-call(bf16[4,512,128]{2,1,0:T(8,128)(2,1)} %fusion.7.xq, bf16[4,512,128]{2,1,0:T(8,128)(2,1)} %copy-done.6, bf16[4,512,128]{2,1,0:T(8,128)(2,1)} %copy-done.15, bf16[4,256,128]{2,1,0:T(8,128)(2,1)} %copy-done.20, bf16[4,256,128]{2,1,0:T(8,128)(2,1)} %copy-done.21, ...), custom_call_target="tpu_custom_call" | custom-call | flops 8589934592 | bytes 16777216 | tf_op jit(solution)/shard_map/attend/pallas_call | solution.py:107
  171.4 7.2 %all-to-all-start.1 = ((f32[16,1,512]{2,1,0:T(1,128)}), f32[16,1,512]{2,1,0:T(1,128)S(1)}, u32[]{:S(2)}, u32[]{:S(2)}) async-start(f32[16,1,512]{2,1,0:T(1,128)} %reshape.76), calls=%async_computation.1 | async-start | bytes 65536 | tf_op jit(solution)/shard_map/all_to_all | solution.py:180
  179.8 6.1 %all-to-all-done.1 = f32[16,1,512]{2,1,0:T(1,128)S(1)} async-done(((f32[16,1,512]{2,1,0:T(1,128)}), f32[16,1,512]{2,1,0:T(1,128)S(1)}, u32[]{:S(2)}, u32[]{:S(2)}) %all-to-all-start.1) | async-done | bytes 32800 | tf_op jit(solution)/shard_map/all_to_all | solution.py:180
  185.9 3.8 %all-to-all-start = ((bf16[4,512,128]{2,0,1:T(4,128)(2,1)}), bf16[4,512,128]{2,0,1:T(4,128)(2,1)S(1)}, u32[]{:S(2)}, u32[]{:S(2)}) async-start(bf16[4,512,128]{2,0,1:T(4,128)(2,1)} %copy.26), calls=%async_computation | async-start | bytes 1048576 | tf_op jit(solution)/shard_map/all_to_all | solution.py:180
  190.9 10.2 %all-to-all-done = bf16[4,512,128]{2,0,1:T(4,128)(2,1)S(1)} async-done(((bf16[4,512,128]{2,0,1:T(4,128)(2,1)}), bf16[4,512,128]{2,0,1:T(4,128)(2,1)S(1)}, u32[]{:S(2)}, u32[]{:S(2)}) %all-to-all-start) | async-done | bytes 524320 | tf_op jit(solution)/shard_map/all_to_all | solution.py:180
  201.0 4.5 %all-to-all-start.3 = ((bf16[4,512,128]{2,0,1:T(4,128)(2,1)}), bf16[4,512,128]{2,0,1:T(4,128)(2,1)S(1)}, u32[]{:S(2)}, u32[]{:S(2)}) async-start(bf16[4,512,128]{2,0,1:T(4,128)(2,1)} %copy.34), calls=%async_computation.3 | async-start | bytes 1048576 | tf_op jit(solution)/shard_map/all_to_all | solution.py:180
  211.6 5.3 %all-to-all-done.3 = bf16[4,512,128]{2,0,1:T(4,128)(2,1)S(1)} async-done(((bf16[4,512,128]{2,0,1:T(4,128)(2,1)}), bf16[4,512,128]{2,0,1:T(4,128)(2,1)S(1)}, u32[]{:S(2)}, u32[]{:S(2)}) %all-to-all-start.3) | async-done | bytes 524320 | tf_op jit(solution)/shard_map/all_to_all | solution.py:180
  (113 shorter events, 35.9 us)
Async XLA Ops:
  1.6 26.4 %collective-permute-start.10 = (bf16[4,256,512]{2,1,0:T(8,128)(2,1)S(1)}, bf16[4,256,512]{2,1,0:T(8,128)(2,1)S(1)}, u32[]{:S(2)}, u32[]{:S(2)}) collective-permute-start(bf16[4,256,512]{2,1,0:T(8,128)(2,1)S(1)} %bitcast.52), channel_id=1, source_target_pairs={{0,32},{32,64},{64,96},{96,0},{1,33},{33,65},{65,97},{97,1},{2,34}... | collective-permute-start | bytes 3145736 | tf_op jit(solution)/shard_map/ppermute | solution.py:142
  3.8 25.1 %collective-permute-start.8 = (bf16[4,256,512]{2,1,0:T(8,128)(2,1)S(1)}, bf16[4,256,512]{2,1,0:T(8,128)(2,1)S(1)}, u32[]{:S(2)}, u32[]{:S(2)}) collective-permute-start(bf16[4,256,512]{2,1,0:T(8,128)(2,1)S(1)} %bitcast.53), channel_id=1, source_target_pairs={{0,96},{32,0},{64,32},{96,64},{1,97},{33,1},{65,33},{97,65},{2,98}... | collective-permute-start | bytes 3145736 | tf_op jit(solution)/shard_map/ppermute | solution.py:142
  8.2 7.6 %collective-permute-start = (bf16[4,512,128]{2,1,0:T(8,128)(2,1)}, bf16[4,512,128]{2,1,0:T(8,128)(2,1)}, u32[]{:S(2)}, u32[]{:S(2)}) collective-permute-start(bf16[4,512,128]{2,1,0:T(8,128)(2,1)} %fusion.7.xq), channel_id=1, source_target_pairs={{1,16},{16,1},{3,18},{18,3},{5,20},{20,5},{7,22},{22,7},{9,24},{24... | collective-permute-start | bytes 1572872 | tf_op jit(solution)/shard_map/ppermute | solution.py:160
  9.7 22.0 %collective-permute-start.2 = (bf16[4,512,128]{2,1,0:T(8,128)(2,1)}, bf16[4,512,128]{2,1,0:T(8,128)(2,1)}, u32[]{:S(2)}, u32[]{:S(2)}) collective-permute-start(bf16[4,512,128]{2,1,0:T(8,128)(2,1)} %fusion.7.xq), channel_id=1, source_target_pairs={{17,1},{0,16},{19,3},{2,18},{21,5},{4,20},{23,7},{6,22},{25,9},{8,... | collective-permute-start | bytes 1572872 | tf_op jit(solution)/shard_map/ppermute | solution.py:164
  15.8 31.2 %collective-permute-start.1 = (bf16[4,512,128]{2,1,0:T(8,128)(2,1)}, bf16[4,512,128]{2,1,0:T(8,128)(2,1)}, u32[]{:S(2)}, u32[]{:S(2)}) collective-permute-start(bf16[4,512,128]{2,1,0:T(8,128)(2,1)} %collective-permute-done), channel_id=1, source_target_pairs={{1,0},{16,17},{3,2},{18,19},{5,4},{20,21},{7,6},{22,23},{9,8},{24,... | collective-permute-start | bytes 1572872 | tf_op jit(solution)/shard_map/ppermute | solution.py:162
  17.1 40.3 %collective-permute-start.7 = (bf16[4,256,512]{2,1,0:T(8,128)(2,1)S(1)}, bf16[4,256,512]{2,1,0:T(8,128)(2,1)}, u32[]{:S(2)}, u32[]{:S(2)}) collective-permute-start(bf16[4,256,512]{2,1,0:T(8,128)(2,1)S(1)} %bitcast.54), channel_id=1, source_target_pairs={{0,8},{8,0},{1,9},{9,1},{2,10},{10,2},{3,11},{11,3},{4,12},{12,4},... | collective-permute-start | bytes 3145736 | tf_op jit(solution)/shard_map/ppermute | solution.py:171
  28.8 21.7 %collective-permute-start.12 = (bf16[2,256,512]{2,1,0:T(8,128)(2,1)}, bf16[2,256,512]{2,1,0:T(8,128)(2,1)S(1)}, u32[]{:S(2)}, u32[]{:S(2)}) collective-permute-start(bf16[2,256,512]{2,1,0:T(8,128)(2,1)} %slice.26), channel_id=1, source_target_pairs={{0,32},{32,64},{64,96},{96,0},{1,33},{33,65},{65,97},{97,1},{2,34}... | collective-permute-start | bytes 1572872 | tf_op jit(solution)/shard_map/ppermute | solution.py:142
  28.9 23.9 %collective-permute-start.13 = (bf16[2,256,512]{2,1,0:T(8,128)(2,1)S(1)}, bf16[2,256,512]{2,1,0:T(8,128)(2,1)S(1)}, u32[]{:S(2)}, u32[]{:S(2)}) collective-permute-start(bf16[2,256,512]{2,1,0:T(8,128)(2,1)S(1)} %slice.27), channel_id=1, source_target_pairs={{0,96},{32,0},{64,32},{96,64},{1,97},{33,1},{65,33},{97,65},{2,98}... | collective-permute-start | bytes 1572872 | tf_op jit(solution)/shard_map/ppermute | solution.py:142
  31.6 24.3 %collective-permute-start.15 = (bf16[4,512,128]{2,1,0:T(8,128)(2,1)}, bf16[4,512,128]{2,1,0:T(8,128)(2,1)S(1)}, u32[]{:S(2)}, u32[]{:S(2)}) collective-permute-start(bf16[4,512,128]{2,1,0:T(8,128)(2,1)} %fusion.7.xq), channel_id=1, source_target_pairs={{0,1},{17,16},{2,3},{19,18},{4,5},{21,20},{6,7},{23,22},{8,9},{25,... | collective-permute-start | bytes 1572872 | tf_op jit(solution)/shard_map/ppermute | solution.py:159
  48.9 13.3 %collective-permute-start.4 = (bf16[4,512,128]{2,1,0:T(8,128)(2,1)S(1)}, bf16[4,512,128]{2,1,0:T(8,128)(2,1)S(1)}, u32[]{:S(2)}, u32[]{:S(2)}) collective-permute-start(bf16[4,512,128]{2,1,0:T(8,128)(2,1)S(1)} %get-tuple-element.13.xk0), channel_id=1, source_target_pairs={{0,2},{2,4},{4,6},{6,0},{1,3},{3,5},{5,7},{7,1},{8,10},{10,12},{12... | collective-permute-start | bytes 1572872 | tf_op jit(solution)/shard_map/ppermute | solution.py:142
  50.5 11.7 %collective-permute-start.3 = (bf16[4,512,128]{2,1,0:T(8,128)(2,1)S(1)}, bf16[4,512,128]{2,1,0:T(8,128)(2,1)S(1)}, u32[]{:S(2)}, u32[]{:S(2)}) collective-permute-start(bf16[4,512,128]{2,1,0:T(8,128)(2,1)S(1)} %get-tuple-element.13.xk0), channel_id=1, source_target_pairs={{0,6},{2,0},{4,2},{6,4},{1,7},{3,1},{5,3},{7,5},{8,14},{10,8},{12,... | collective-permute-start | bytes 1572872 | tf_op jit(solution)/shard_map/ppermute | solution.py:142
  52.8 29.9 %collective-permute-start.11 = (bf16[4,256,512]{2,1,0:T(8,128)(2,1)S(1)}, bf16[4,256,512]{2,1,0:T(8,128)(2,1)S(1)}, u32[]{:S(2)}, u32[]{:S(2)}) collective-permute-start(bf16[4,256,512]{2,1,0:T(8,128)(2,1)S(1)} %copy-done.8), channel_id=1, source_target_pairs={{0,8},{8,0},{1,9},{9,1},{2,10},{10,2},{3,11},{11,3},{4,12},{12,4},... | collective-permute-start | bytes 3145736 | tf_op jit(solution)/shard_map/ppermute | solution.py:171
  55.9 26.7 %collective-permute-start.9 = (bf16[4,256,512]{2,1,0:T(8,128)(2,1)S(1)}, bf16[4,256,512]{2,1,0:T(8,128)(2,1)S(1)}, u32[]{:S(2)}, u32[]{:S(2)}) collective-permute-start(bf16[4,256,512]{2,1,0:T(8,128)(2,1)S(1)} %copy-done.10), channel_id=1, source_target_pairs={{0,8},{8,0},{1,9},{9,1},{2,10},{10,2},{3,11},{11,3},{4,12},{12,4},... | collective-permute-start | bytes 3145736 | tf_op jit(solution)/shard_map/ppermute | solution.py:171
  57.4 25.3 %collective-permute-start.14 = (bf16[4,256,512]{2,1,0:T(8,128)(2,1)S(1)}, bf16[4,256,512]{2,1,0:T(8,128)(2,1)S(1)}, u32[]{:S(2)}, u32[]{:S(2)}) collective-permute-start(bf16[4,256,512]{2,1,0:T(8,128)(2,1)S(1)} %constant_dynamic-update-slice_fusion.rest_6_), channel_id=1, source_target_pairs={{0,8},{8,0},{1,9},{9,1},{2,10},{10,2},{3,11},{11,3},{4,12},{12,4},... | collective-permute-start | bytes 3145736 | tf_op jit(solution)/shard_map/ppermute | solution.py:171
  62.2 11.3 %collective-permute-start.17 = (bf16[4,512,128]{2,1,0:T(8,128)(2,1)S(1)}, bf16[4,512,128]{2,1,0:T(8,128)(2,1)S(1)}, u32[]{:S(2)}, u32[]{:S(2)}) collective-permute-start(bf16[4,512,128]{2,1,0:T(8,128)(2,1)S(1)} %broadcast_select_fusion.xk0), channel_id=1, source_target_pairs={{0,2},{2,4},{4,6},{6,0},{1,3},{3,5},{5,7},{7,1},{8,10},{10,12},{12... | collective-permute-start | bytes 1572872 | tf_op jit(solution)/shard_map/ppermute | solution.py:142
  62.3 11.3 %collective-permute-start.16 = (bf16[4,512,128]{2,1,0:T(8,128)(2,1)S(1)}, bf16[4,512,128]{2,1,0:T(8,128)(2,1)S(1)}, u32[]{:S(2)}, u32[]{:S(2)}) collective-permute-start(bf16[4,512,128]{2,1,0:T(8,128)(2,1)S(1)} %broadcast_select_fusion.xk0), channel_id=1, source_target_pairs={{0,6},{2,0},{4,2},{6,4},{1,7},{3,1},{5,3},{7,5},{8,14},{10,8},{12,... | collective-permute-start | bytes 1572872 | tf_op jit(solution)/shard_map/ppermute | solution.py:142
  73.6 6.4 %collective-permute-start.5 = (bf16[4,256,128]{2,1,0:T(8,128)(2,1)S(1)}, bf16[4,256,128]{2,1,0:T(8,128)(2,1)S(1)}, u32[]{:S(2)}, u32[]{:S(2)}) collective-permute-start(bf16[4,256,128]{2,1,0:T(8,128)(2,1)S(1)} %slice.24), channel_id=1, source_target_pairs={{0,2},{2,4},{4,6},{6,0},{1,3},{3,5},{5,7},{7,1},{8,10},{10,12},{12... | collective-permute-start | bytes 786440 | tf_op jit(solution)/shard_map/ppermute | solution.py:142
  73.6 6.4 %collective-permute-start.6 = (bf16[4,256,128]{2,1,0:T(8,128)(2,1)S(1)}, bf16[4,256,128]{2,1,0:T(8,128)(2,1)S(1)}, u32[]{:S(2)}, u32[]{:S(2)}) collective-permute-start(bf16[4,256,128]{2,1,0:T(8,128)(2,1)S(1)} %slice.25), channel_id=1, source_target_pairs={{0,6},{2,0},{4,2},{6,4},{1,7},{3,1},{5,3},{7,5},{8,14},{10,8},{12,... | collective-permute-start | bytes 786440 | tf_op jit(solution)/shard_map/ppermute | solution.py:142
  80.0 55.9 %collective-permute-start.18 = (bf16[4,256,128]{2,1,0:T(8,128)(2,1)S(1)}, bf16[4,256,128]{2,1,0:T(8,128)(2,1)S(1)}, u32[]{:S(2)}, u32[]{:S(2)}) collective-permute-start(bf16[4,256,128]{2,1,0:T(8,128)(2,1)S(1)} %slice.28), channel_id=1, source_target_pairs={{0,2},{2,4},{4,6},{6,0},{1,3},{3,5},{5,7},{7,1},{8,10},{10,12},{12... | collective-permute-start | bytes 786440 | tf_op jit(solution)/shard_map/ppermute | solution.py:142
  80.0 55.9 %collective-permute-start.19 = (bf16[4,256,128]{2,1,0:T(8,128)(2,1)S(1)}, bf16[4,256,128]{2,1,0:T(8,128)(2,1)S(1)}, u32[]{:S(2)}, u32[]{:S(2)}) collective-permute-start(bf16[4,256,128]{2,1,0:T(8,128)(2,1)S(1)} %slice.29), channel_id=1, source_target_pairs={{0,6},{2,0},{4,2},{6,4},{1,7},{3,1},{5,3},{7,5},{8,14},{10,8},{12,... | collective-permute-start | bytes 786440 | tf_op jit(solution)/shard_map/ppermute | solution.py:142
  119.1 52.2 %all-to-all-start.2 = ((f32[16,1,512]{2,1,0:T(1,128)}), f32[16,1,512]{2,1,0:T(1,128)S(1)}, u32[]{:S(2)}, u32[]{:S(2)}) async-start(f32[16,1,512]{2,1,0:T(1,128)} %reshape.78), calls=%async_computation.2 | async-start | bytes 65536 | tf_op jit(solution)/shard_map/all_to_all | solution.py:180
  171.4 14.5 %all-to-all-start.1 = ((f32[16,1,512]{2,1,0:T(1,128)}), f32[16,1,512]{2,1,0:T(1,128)S(1)}, u32[]{:S(2)}, u32[]{:S(2)}) async-start(f32[16,1,512]{2,1,0:T(1,128)} %reshape.76), calls=%async_computation.1 | async-start | bytes 65536 | tf_op jit(solution)/shard_map/all_to_all | solution.py:180
  185.9 15.1 %all-to-all-start = ((bf16[4,512,128]{2,0,1:T(4,128)(2,1)}), bf16[4,512,128]{2,0,1:T(4,128)(2,1)S(1)}, u32[]{:S(2)}, u32[]{:S(2)}) async-start(bf16[4,512,128]{2,0,1:T(4,128)(2,1)} %copy.26), calls=%async_computation | async-start | bytes 1048576 | tf_op jit(solution)/shard_map/all_to_all | solution.py:180
  201.0 15.9 %all-to-all-start.3 = ((bf16[4,512,128]{2,0,1:T(4,128)(2,1)}), bf16[4,512,128]{2,0,1:T(4,128)(2,1)S(1)}, u32[]{:S(2)}, u32[]{:S(2)}) async-start(bf16[4,512,128]{2,0,1:T(4,128)(2,1)} %copy.34), calls=%async_computation.3 | async-start | bytes 1048576 | tf_op jit(solution)/shard_map/all_to_all | solution.py:180
  (24 other events, 379.2 us)

commit v2 on v1

v2 whole, which is shorter than its diff:
```python
import jax
import jax.numpy as jnp
from jax import lax
from jax.experimental import pallas as pl
from jax.experimental.pallas import tpu as pltpu
from jax.sharding import Mesh, PartitionSpec as P

F32, BF16 = jnp.float32, jnp.bfloat16
HEADS, WIDTH, CHANNELS = 4, 32, 128
COLS, BLOCK, ROWS = 512, 512, 4
KEYS = 4 * BLOCK
SHARE = COLS // 16
PAD = 40
STEP = 2
LOG2E = 1.4426950408889634
LOW, HIGH = 1e-26, 1e30
ROW_AXES = ("y", "xh", "core")
COL_AXES = ("z", "xl")
VMEM_LIMIT = 60 * 2**20


def matmul(a, b, first=1, second=0):
    dims = (((first,), (second,)), ((), ()))
    return lax.dot_general(a, b, dims, preferred_element_type=F32)


def prepare_kernel(pair, gain, bias, normed, bias_t):
    values = pair[0].astype(F32)
    centered = values - jnp.mean(values, axis=-1, keepdims=True)
    variance = jnp.mean(centered * centered, axis=-1, keepdims=True)
    normed[0] = (centered * lax.rsqrt(variance + 1e-05) * gain[...]).astype(BF16)
    bias_t[0] = bias[0].astype(F32).T.astype(BF16)


def prepare(pair_block, norm_gain, head_bias):
    def whole(*shape):
        return pl.BlockSpec((1,) + shape, lambda i: (i, 0, 0))

    keys = head_bias.shape[2]
    return pl.pallas_call(
        prepare_kernel,
        grid=(ROWS,),
        in_specs=[
            whole(COLS, CHANNELS),
            pl.BlockSpec((1, CHANNELS), lambda i: (0, 0)),
            whole(COLS, keys),
        ],
        out_specs=[whole(COLS, CHANNELS), whole(keys, COLS)],
        out_shape=[
            jax.ShapeDtypeStruct((ROWS, COLS, CHANNELS), BF16),
            jax.ShapeDtypeStruct((HEADS, keys, COLS), BF16),
        ],
        name="prepare",
    )(pair_block, norm_gain.reshape(1, CHANNELS), head_bias)


def attend_kernel(xq, xk0, xk1, xk2a, xk2b, xk3, w, bias, out, *scratch):
    bias_s, top_s, k_s, v_s, q_s, gate_s, stat_s, sems = scratch
    step = pl.program_id(0)
    z = lax.axis_index("z")

    def bias_copies():
        copies = []
        for t in range(4):
            for c in range(2):
                src = bias.at[lax.rem(z + t, 4) * 2 + c]
                dst = bias_s.at[t, :, pl.ds(c * 256, 256), :]
                copies.append(pltpu.make_async_copy(src, dst, sems.at[t * 2 + c]))
        return copies

    @pl.when(step == 0)
    def _():
        for copy in bias_copies():
            copy.start()
        q_s[...] = jnp.zeros_like(q_s)
        stat_s[...] = jnp.zeros_like(stat_s)
        v_s[:, :, WIDTH:, :] = jnp.ones((STEP, HEADS, PAD - WIDTH, KEYS), BF16)

    def project(r):
        x_q = xq[r]
        q_t = (matmul(w[:, :128], x_q, 0, 1) * WIDTH ** (-0.5)).astype(BF16)
        gate_s[r] = jax.nn.sigmoid(matmul(w[:, 384:], x_q, 0, 1))
        for h in range(HEADS):
            at = slice(h * WIDTH, (h + 1) * WIDTH)
            q_s[r, h, at, :] = q_t[at]
        start = 0
        for x in (xk0, xk1, xk2a, xk2b, xk3):
            size = x.shape[1]
            at = slice(start, start + size)
            k_s[r, at, :] = matmul(x[r], w[:, 128:256]).astype(BF16)
            v_t = matmul(w[:, 256:384], x[r], 0, 1).astype(BF16)
            for h in range(HEADS):
                v_s[r, h, :WIDTH, at] = v_t[h * WIDTH : (h + 1) * WIDTH]
            start += size

    def finish(r, totals, shifts):
        parts, stats = [], []
        for total, shift in zip(totals, shifts):
            mass = total[WIDTH : WIDTH + 1]
            parts.append(total[:WIDTH] * (1.0 / mass))
            stats.append(shift + jnp.log(mass))
        gated = jnp.concatenate(parts, axis=0) * gate_s[r]
        at = step * STEP + r
        out[:, at] = gated.T.astype(BF16).reshape(16, SHARE, CHANNELS)
        stat = jnp.concatenate(stats, axis=0)
        high = stat.astype(BF16).astype(F32)
        middle = (stat - high).astype(BF16).astype(F32)
        low = stat - high - middle
        rows = jnp.concatenate([high, middle, low, jnp.zeros_like(low)], axis=0)
        stat_s[pl.ds(pl.multiple_of(at * 32, 32), 16), :] = rows

    for r in range(STEP):
        project(r)

    @pl.when(step == 0)
    def _():
        for copy in bias_copies():
            copy.wait()
        for h in range(HEADS):
            tops = [jnp.max(bias_s[t, h], axis=0, keepdims=True) for t in range(4)]
            top = jnp.maximum(jnp.maximum(tops[0], tops[1]), jnp.maximum(tops[2], tops[3]))
            top_s[h : h + 1, :] = top.astype(F32)

    fine = []
    for r in range(STEP):
        totals, shifts = [], []
        for h in range(HEADS):
            q, shift = q_s[r, h], top_s[h : h + 1, :]
            total = None
            for t in range(4):
                at = slice(t * BLOCK, (t + 1) * BLOCK)
                s = matmul(k_s[r, at, :], q) + bias_s[t, h].astype(F32)
                p = jnp.exp2((s - shift) * LOG2E).astype(BF16)
                pv = matmul(v_s[r, h, :, at], p)
                total = pv if t == 0 else total + pv
            totals.append(total)
            shifts.append(shift)
        finish(r, totals, shifts)
        mass = jnp.concatenate([total[WIDTH : WIDTH + 1] for total in totals], axis=0)
        inside = jnp.logical_and(mass > LOW, mass < HIGH)
        fine.append(jnp.min(inside.astype(F32)) > 0.5)

    for r in range(STEP):

        @pl.when(jnp.logical_not(fine[r]))
        def _():
            totals, shifts = [], []
            for h in range(HEADS):

                def tile(t, carry):
                    largest, total = carry
                    at = pl.ds(pl.multiple_of(t * BLOCK, BLOCK), BLOCK)
                    s = matmul(k_s[r, at, :], q_s[r, h]) + bias_s[t, h].astype(F32)
                    fresh = jnp.maximum(largest, jnp.max(s, axis=0, keepdims=True))
                    p = jnp.exp2((s - fresh) * LOG2E).astype(BF16)
                    scale = jnp.exp2((largest - fresh) * LOG2E)
                    return fresh, total * scale + matmul(v_s[r, h, :, at], p)

                begin = jnp.full((1, COLS), -jnp.inf, F32), jnp.zeros((PAD, COLS), F32)
                largest, total = lax.fori_loop(0, 4, tile, begin)
                totals.append(total)
                shifts.append(largest)
            finish(r, totals, shifts)

    @pl.when(step == pl.num_programs(0) - 1)
    def _():
        out[:, ROWS] = stat_s[...].T.astype(BF16).reshape(16, SHARE, CHANNELS)


def attend(x_q, x_ks, w_project, bias):
    def rows(x):
        return pl.BlockSpec((STEP,) + x.shape[1:], lambda i: (i, 0, 0))

    scores = ROWS * HEADS * COLS * KEYS
    message = (16, ROWS + 1, SHARE, CHANNELS)
    return pl.pallas_call(
        attend_kernel,
        grid=(ROWS // STEP,),
        in_specs=[rows(x_q)]
        + [rows(x) for x in x_ks]
        + [pl.BlockSpec((CHANNELS, 512), lambda i: (0, 0))]
        + [pl.BlockSpec(memory_space=pl.ANY)],
        out_specs=pl.BlockSpec(message, lambda i: (0, 0, 0, 0)),
        out_shape=jax.ShapeDtypeStruct(message, BF16),
        scratch_shapes=[
            pltpu.VMEM((4, HEADS, BLOCK, COLS), BF16),
            pltpu.VMEM((HEADS, COLS), F32),
            pltpu.VMEM((STEP, KEYS, CHANNELS), BF16),
            pltpu.VMEM((STEP, HEADS, PAD, KEYS), BF16),
            pltpu.VMEM((STEP, HEADS, CHANNELS, COLS), BF16),
            pltpu.VMEM((STEP, CHANNELS, COLS), F32),
            pltpu.VMEM((CHANNELS, COLS), F32),
            pltpu.SemaphoreType.DMA((8,)),
        ],
        compiler_params=pltpu.CompilerParams(vmem_limit_bytes=VMEM_LIMIT),
        cost_estimate=pl.CostEstimate(
            flops=scores * 512, bytes_accessed=2**24, transcendentals=scores
        ),
        name="attend",
    )(x_q, *x_ks, w_project, bias)


def merge_kernel(m1, m2, w, out):
    lane = lax.broadcasted_iota(jnp.int32, (CHANNELS, CHANNELS), 0)
    head = lax.broadcasted_iota(jnp.int32, (CHANNELS, CHANNELS), 1) // WIDTH
    stat1 = m1[:, ROWS].reshape(16 * SHARE, CHANNELS)
    stat2 = jnp.concatenate([m2[s ^ 2, ROWS] for s in range(16)], axis=0)
    for i in range(ROWS):
        part = lane - 32 * i
        inside = (part >= 0) & (part < 12) & (lax.rem(part, 4) == head)
        pick = inside.astype(F32).astype(BF16)
        share = jax.nn.sigmoid(matmul(stat1, pick) - matmul(stat2, pick))
        o1 = m1[:, i].reshape(16 * SHARE, CHANNELS).astype(F32)
        o2 = jnp.concatenate([m2[s ^ 2, i] for s in range(16)], axis=0).astype(F32)
        gated = (o2 + share * (o1 - o2)).astype(BF16)
        out[:, i] = matmul(gated, w[...]).astype(BF16).reshape(16, SHARE, CHANNELS)


def merge(m1, m2, w_out):
    return pl.pallas_call(
        merge_kernel,
        out_shape=jax.ShapeDtypeStruct((16, ROWS, SHARE, CHANNELS), BF16),
        compiler_params=pltpu.CompilerParams(vmem_limit_bytes=VMEM_LIMIT),
        name="merge",
    )(m1, m2, w_out)


def shift(x, axis, step):
    return lax.ppermute(x, axis, [(i, (i + step) % 4) for i in range(4)])


def gather_ring(x, axis, cut):
    behind, ahead = shift(x, axis, 1), shift(x, axis, -1)
    half = x.shape[cut] // 2
    far_a = shift(lax.slice_in_dim(behind, 0, half, axis=cut), axis, 1)
    far_b = shift(lax.slice_in_dim(ahead, half, 2 * half, axis=cut), axis, -1)
    return x, ahead, far_a, far_b, behind


def shards(pair_block, norm_gain, w_project, w_out, head_bias):
    xh, xl = lax.axis_index("xh"), lax.axis_index("xl")
    own, bias_t = prepare(pair_block, norm_gain, head_bias)

    x_axis = ("xh", "xl")
    beside = lax.ppermute(own, x_axis, [(0, 1), (3, 2)])
    across = lax.ppermute(own, x_axis, [(1, 2), (2, 1)])
    first_k = jnp.where(xl == xh, own, beside)
    passed = lax.ppermute(across, x_axis, [(1, 0), (2, 3)])
    second_k = jnp.where(xl == xh, passed, across)
    partner = lax.ppermute(own, x_axis, [(3, 1), (0, 2)])
    second_q = jnp.where(xl == xh, passed, partner)

    bias = lax.all_gather(bias_t, ("y", "core"), axis=0, tiled=False)
    first_ks = gather_ring(first_k, "z", 1)
    second_ks = gather_ring(second_k, "z", 1)

    def spread(x):
        return lax.all_to_all(x, ROW_AXES, split_axis=0, concat_axis=0, tiled=True)

    m1 = spread(attend(own, first_ks, w_project, bias))
    m2 = spread(attend(second_q, second_ks, w_project, bias))
    update = merge(m1, m2, w_out)
    return jnp.transpose(update, (2, 0, 1, 3)).reshape(SHARE, 16 * ROWS, CHANNELS)


def solution(mesh):
    fine = Mesh(mesh.devices.reshape(4, 2, 2, 4, 2), ROW_AXES + COL_AXES)
    in_specs = (P(ROW_AXES, COL_AXES, None), P(), P(), P(), P(None, COL_AXES, ROW_AXES))
    out_specs = P(COL_AXES + ROW_AXES, None, None)
    return jax.shard_map(
        shards, mesh=fine, in_specs=in_specs, out_specs=out_specs, check_vma=False
    )
```

time: 220 us -> 186 us (0.85)
  starting transfers between devices: 79 us -> 53.4 us
  waiting for transfers between devices: 49.1 us -> 26.4 us
  blocking collectives: 0 us -> 20.6 us
  local copies, waits for them, and re-layouts: 20.9 us -> 3.56 us
  between operations: 0.47 us -> 13.6 us
  other arithmetic: 6.35 us -> 1.98 us
  Pallas kernels: 62.3 us -> 65.3 us
    all_to_all x4 -> x1, starting transfers between devices: 32.2 us -> 9.85 us  [spread(): return lax.all_to_all(x, ROW_AXES, split_axis=0, concat_axis=0, tiled=True)]
    all_to_all x4 -> x1, waiting for transfers between devices: 21.6 us -> 0.01 us  [spread(): return lax.all_to_all(x, ROW_AXES, split_axis=0, concat_axis=0, tiled=True)]
    all_to_all x0 -> x1, blocking collectives: none -> 20.6 us  [spread(): return lax.all_to_all(x, ROW_AXES, split_axis=0, concat_axis=0, tiled=True)]
    ppermute x16 -> x8, starting transfers between devices: 24.6 us -> 12.1 us  [shift(): return lax.ppermute(x, axis, [(i, (i + step) % 4) for i in range(4)])]
    unnamed x54 -> x20, local copies, waits for them, and re-layouts: 12.2 us -> 1.45 us
    ppermute x1, starting transfers between devices: 13.3 us -> 22.5 us  [shards(): beside = lax.ppermute(own, x_axis, [(0, 1), (3, 2)])]
    ppermute x16 -> x8, waiting for transfers between devices: 25.4 us -> 17.5 us  [shift(): return lax.ppermute(x, axis, [(i, (i + step) % 4) for i in range(4)])]
    ppermute x1, waiting for transfers between devices: 2.01 us -> 8.88 us  [shards(): passed = lax.ppermute(across, x_axis, [(1, 0), (2, 3)])]
  transfers between devices with their start and end apart: 24 -> 14, of which waited for: 9 -> 4; matrix products, arithmetic and copies ran while one was open for 9% -> 1% of each run, Pallas kernels for 28% -> 31%
where the time goes in v2:
time: 186 us; the launch traced here: 185 us
  Pallas kernels  65.3 us (35%)
  starting transfers between devices  53.4 us (29%)
  waiting for transfers between devices  26.4 us (14%)
  blocking collectives  20.6 us (11%)
  between operations  13.6 us (7%)
  local copies, waits for them, and re-layouts  3.56 us (2%)
  other arithmetic  1.98 us (1%)
    pallas_call x2, Pallas kernels, attend(): pl.pallas_call(attend_kernel, grid=(ROWS // STEP,), in_specs=[rows(x_q)]...  58.1 us
    ppermute x1, starting transfers between devices, shards(): beside = lax.ppermute(own, x_axis, [(0, 1), (3, 2)])  22.5 us
    all_to_all x1, blocking collectives, spread(): return lax.all_to_all(x, ROW_AXES, split_axis=0, concat_axis=0, tiled=True)  20.6 us
    ppermute x8, waiting for transfers between devices, shift(): return lax.ppermute(x, axis, [(i, (i + step) % 4) for i in range(4)])  17.5 us
    ppermute x8, starting transfers between devices, shift(): return lax.ppermute(x, axis, [(i, (i + step) % 4) for i in range(4)])  12.1 us
    all_to_all x1, starting transfers between devices, spread(): return lax.all_to_all(x, ROW_AXES, split_axis=0, concat_axis=0, tiled=True)  9.85 us
    ppermute x1, waiting for transfers between devices, shards(): passed = lax.ppermute(across, x_axis, [(1, 0), (2, 3)])  8.88 us
    ppermute x1, starting transfers between devices, shards(): partner = lax.ppermute(own, x_axis, [(3, 1), (0, 2)])  6.98 us
  transfers between devices with their start and end apart: 14, of which 4 were waited for; matrix products, arithmetic and copies ran while one was open for 1% of the time, Pallas kernels for 31%

profile of v2, /device:TPU:1, one launch (start us, length us, event | category | flops | bytes accessed | tf_op | source)
XLA Modules:
  0.0 185.0 jit_solution(1326316765800758369)
XLA Ops:
  6.5 4.1 %prepare.1 = (bf16[4,512,128]{2,1,0:T(8,128)(2,1)}, bf16[4,256,512]{2,1,0:T(8,128)(2,1)}) custom-call(bf16[4,512,128]{2,1,0:T(8,128)(2,1)} %pair.1, f32[1,128]{1,0:T(1,128)} %bitcast.6, bf16[4,512,256]{2,1,0:T(8,128)(2,1)} %bias.1), custom_call_target="tpu_custom_call" | custom-call | tf_op jit(solution)/shard_map/prepare/pallas_call | solution.py:40
  10.7 0.7 collective-permute-start.5
  11.4 7.0 %collective-permute-start.7 = (bf16[4,512,128]{2,1,0:T(8,128)(2,1)}, bf16[4,512,128]{2,1,0:T(8,128)(2,1)S(1)}, u32[]{:S(2)}, u32[]{:S(2)}) collective-permute-start(bf16[4,512,128]{2,1,0:T(8,128)(2,1)} %get-tuple-element.7.xq), channel_id=1, source_target_pairs={{17,1},{0,16},{19,3},{2,18},{21,5},{4,20},{23,7},{6,22},{25,9},{8,... | collective-permute-start | bytes 1572872 | tf_op jit(solution)/shard_map/ppermute | solution.py:250
  18.4 1.3 collective-permute-start.6
  19.7 22.5 %collective-permute-start = (bf16[4,512,128]{2,1,0:T(8,128)(2,1)}, bf16[4,512,128]{2,1,0:T(8,128)(2,1)S(1)}, u32[]{:S(2)}, u32[]{:S(2)}) collective-permute-start(bf16[4,512,128]{2,1,0:T(8,128)(2,1)} %get-tuple-element.7.xq), channel_id=1, source_target_pairs={{0,1},{17,16},{2,3},{19,18},{4,5},{21,20},{6,7},{23,22},{8,9},{25,... | collective-permute-start | bytes 1572872 | tf_op jit(solution)/shard_map/ppermute | solution.py:245
  42.3 8.9 %collective-permute-done.6 = bf16[4,512,128]{2,1,0:T(8,128)(2,1)S(1)} collective-permute-done((bf16[4,512,128]{2,1,0:T(8,128)(2,1)S(1)}, bf16[4,512,128]{2,1,0:T(8,128)(2,1)S(1)}, u32[]{:S(2)}, u32[]{:S(2)}) %collective-permute-start.6) | collective-permute-done | bytes 524320 | tf_op jit(solution)/shard_map/ppermute | solution.py:248
  51.1 0.9 broadcast_select_fusion
  52.0 1.6 collective-permute-start.9
  53.7 2.1 %collective-permute-start.8 = (bf16[4,512,128]{2,1,0:T(8,128)(2,1)S(1)}, bf16[4,512,128]{2,1,0:T(8,128)(2,1)S(1)}, u32[]{:S(2)}, u32[]{:S(2)}) collective-permute-start(bf16[4,512,128]{2,1,0:T(8,128)(2,1)S(1)} %get-tuple-element.9.xk0), channel_id=1, source_target_pairs={{0,6},{2,0},{4,2},{6,4},{1,7},{3,1},{5,3},{7,5},{8,14},{10,8},{12,... | collective-permute-start | bytes 1572872 | tf_op jit(solution)/shard_map/ppermute | solution.py:229
  55.8 1.1 broadcast_select_fusion.2.xk0
  57.0 2.7 %collective-permute-start.1 = (bf16[4,512,128]{2,1,0:T(8,128)(2,1)S(1)}, bf16[4,512,128]{2,1,0:T(8,128)(2,1)S(1)}, u32[]{:S(2)}, u32[]{:S(2)}) collective-permute-start(bf16[4,512,128]{2,1,0:T(8,128)(2,1)S(1)} %broadcast_select_fusion.2.xk0), channel_id=1, source_target_pairs={{0,6},{2,0},{4,2},{6,4},{1,7},{3,1},{5,3},{7,5},{8,14},{10,8},{12,... | collective-permute-start | bytes 1572872 | tf_op jit(solution)/shard_map/ppermute | solution.py:229
  59.6 6.4 %collective-permute-done.9.xk3 = bf16[4,512,128]{2,1,0:T(8,128)(2,1)S(1)} collective-permute-done((bf16[4,512,128]{2,1,0:T(8,128)(2,1)S(1)}, bf16[4,512,128]{2,1,0:T(8,128)(2,1)S(1)}, u32[]{:S(2)}, u32[]{:S(2)}) %collective-permute-start.9) | collective-permute-done | bytes 524320 | tf_op jit(solution)/shard_map/ppermute | solution.py:229
  66.2 2.7 %collective-permute-start.11 = (bf16[4,256,128]{2,1,0:T(8,128)(2,1)S(1)}, bf16[4,256,128]{2,1,0:T(8,128)(2,1)S(1)}, u32[]{:S(2)}, u32[]{:S(2)}) collective-permute-start(bf16[4,256,128]{2,1,0:T(8,128)(2,1)S(1)} %slice.19), channel_id=1, source_target_pairs={{0,6},{2,0},{4,2},{6,4},{1,7},{3,1},{5,3},{7,5},{8,14},{10,8},{12,... | collective-permute-start | bytes 786440 | tf_op jit(solution)/shard_map/ppermute | solution.py:229
  68.9 8.4 %collective-permute-done.2.xk3 = bf16[4,512,128]{2,1,0:T(8,128)(2,1)S(1)} collective-permute-done((bf16[4,512,128]{2,1,0:T(8,128)(2,1)S(1)}, bf16[4,512,128]{2,1,0:T(8,128)(2,1)S(1)}, u32[]{:S(2)}, u32[]{:S(2)}) %collective-permute-start.2) | collective-permute-done | bytes 524320 | tf_op jit(solution)/shard_map/ppermute | solution.py:229
  77.4 2.7 %collective-permute-start.4 = (bf16[4,256,128]{2,1,0:T(8,128)(2,1)S(1)}, bf16[4,256,128]{2,1,0:T(8,128)(2,1)}, u32[]{:S(2)}, u32[]{:S(2)}) collective-permute-start(bf16[4,256,128]{2,1,0:T(8,128)(2,1)S(1)} %slice.17), channel_id=1, source_target_pairs={{0,6},{2,0},{4,2},{6,4},{1,7},{3,1},{5,3},{7,5},{8,14},{10,8},{12,... | collective-permute-start | bytes 786440 | tf_op jit(solution)/shard_map/ppermute | solution.py:229
  80.1 2.8 %collective-permute-done.10.xk2a = bf16[4,256,128]{2,1,0:T(8,128)(2,1)S(1)} collective-permute-done((bf16[4,256,128]{2,1,0:T(8,128)(2,1)S(1)}, bf16[4,256,128]{2,1,0:T(8,128)(2,1)S(1)}, u32[]{:S(2)}, u32[]{:S(2)}) %collective-permute-start.10) | collective-permute-done | bytes 262176 | tf_op jit(solution)/shard_map/ppermute | solution.py:229
  82.9 0.7 copy-done.8
  83.7 29.2 %attend.3 = bf16[16,5,32,128]{3,2,1,0:T(8,128)(2,1)} custom-call(bf16[4,512,128]{2,1,0:T(8,128)(2,1)} %get-tuple-element.10.xq, bf16[4,512,128]{2,1,0:T(8,128)(2,1)} %copy-done.2, bf16[4,512,128]{2,1,0:T(8,128)(2,1)} %copy-done.6, bf16[4,256,128]{2,1,0:T(8,128)(2,1)} %copy-done.8, bf16[4,256,128]{2,1,0:T(8,128)(2,1)} %copy-done.9, ...), custom_call_target="tpu_custom_call" | custom-call | flops 8589934592 | bytes 16777216 | tf_op jit(solution)/shard_map/attend/pallas_call | solution.py:176
  112.9 9.8 %all-to-all-start.1 = ((bf16[16,5,32,128]{3,2,1,0:T(8,128)(2,1)}), bf16[16,5,32,128]{3,2,1,0:T(8,128)(2,1)S(1)}, u32[]{:S(2)}, u32[]{:S(2)}) async-start(bf16[16,5,32,128]{3,2,1,0:T(8,128)(2,1)} %attend.3), calls=%async_computation.1 | async-start | bytes 1310720 | tf_op jit(solution)/shard_map/all_to_all | solution.py:258
  122.8 0.7 copy-done.7
  123.4 29.0 %attend.2 = bf16[16,5,32,128]{3,2,1,0:T(8,128)(2,1)} custom-call(bf16[4,512,128]{2,1,0:T(8,128)(2,1)} %get-tuple-element.7.xq, bf16[4,512,128]{2,1,0:T(8,128)(2,1)} %copy-done.1, bf16[4,512,128]{2,1,0:T(8,128)(2,1)} %copy-done.4, bf16[4,256,128]{2,1,0:T(8,128)(2,1)} %copy-done.7, bf16[4,256,128]{2,1,0:T(8,128)(2,1)} %collective-permute-done.4.xk2b, ...), custom_call_target="tpu_custom_call" | custom-call | flops 8589934592 | bytes 16777216 | tf_op jit(solution)/shard_map/attend/pallas_call | solution.py:176
  152.4 20.6 %all_to_all.10.m1 = bf16[16,5,32,128]{3,2,1,0:T(8,128)(2,1)} all-to-all(bf16[16,5,32,128]{3,2,1,0:T(8,128)(2,1)} %attend.2), channel_id=1, replica_groups=mesh['y'=4,'xh'=2,'core'=2,'z'=4,'xl'=2] {'y','xh','core'}, dimensions={0} | all-to-all | bytes 1310720 | tf_op jit(solution)/shard_map/all_to_all | solution.py:258
  173.0 3.1 %merge.1 = bf16[16,4,32,128]{3,2,1,0:T(8,128)(2,1)} custom-call(bf16[16,5,32,128]{3,2,1,0:T(8,128)(2,1)} %all_to_all.10.m1, bf16[16,5,32,128]{3,2,1,0:T(8,128)(2,1)} %copy-done, bf16[128,128]{1,0:T(8,128)(2,1)} %w.5), custom_call_target="tpu_custom_call" | custom-call | tf_op jit(solution)/shard_map/merge/pallas_call | solution.py:220
  176.1 2.0 %copy.7 = bf16[32,64,128]{2,1,0:T(8,128)(2,1)} copy(bf16[32,64,128]{2,0,1:T(8,128)(2,1)} %bitcast.5) | data formatting | bytes 1048576 | tf_op jit(solution)/shard_map/reshape | solution.py:263
  (37 shorter events, 0.5 us)
Async XLA Ops:
  6.5 76.4 %all-gather.3.cloned.1.call-start = ((), (), s32[]{:S(2)}) async-start(), calls=%async_computation.2 | async-start | bytes 9437184 | tf_op jit(solution)/shard_map/all_gather | solution.py:253
  10.7 7.7 %collective-permute-start.5 = (bf16[4,512,128]{2,1,0:T(8,128)(2,1)}, bf16[4,512,128]{2,1,0:T(8,128)(2,1)S(1)}, u32[]{:S(2)}, u32[]{:S(2)}) collective-permute-start(bf16[4,512,128]{2,1,0:T(8,128)(2,1)} %get-tuple-element.7.xq), channel_id=1, source_target_pairs={{1,16},{16,1},{3,18},{18,3},{5,20},{20,5},{7,22},{22,7},{9,24},{24... | collective-permute-start | bytes 1572872 | tf_op jit(solution)/shard_map/ppermute | solution.py:246
  11.4 30.8 %collective-permute-start.7 = (bf16[4,512,128]{2,1,0:T(8,128)(2,1)}, bf16[4,512,128]{2,1,0:T(8,128)(2,1)S(1)}, u32[]{:S(2)}, u32[]{:S(2)}) collective-permute-start(bf16[4,512,128]{2,1,0:T(8,128)(2,1)} %get-tuple-element.7.xq), channel_id=1, source_target_pairs={{17,1},{0,16},{19,3},{2,18},{21,5},{4,20},{23,7},{6,22},{25,9},{8,... | collective-permute-start | bytes 1572872 | tf_op jit(solution)/shard_map/ppermute | solution.py:250
  18.4 32.7 %collective-permute-start.6 = (bf16[4,512,128]{2,1,0:T(8,128)(2,1)S(1)}, bf16[4,512,128]{2,1,0:T(8,128)(2,1)S(1)}, u32[]{:S(2)}, u32[]{:S(2)}) collective-permute-start(bf16[4,512,128]{2,1,0:T(8,128)(2,1)S(1)} %collective-permute-done.5), channel_id=1, source_target_pairs={{1,0},{16,17},{3,2},{18,19},{5,4},{20,21},{7,6},{22,23},{9,8},{24,... | collective-permute-start | bytes 1572872 | tf_op jit(solution)/shard_map/ppermute | solution.py:248
  19.7 36.1 %collective-permute-start = (bf16[4,512,128]{2,1,0:T(8,128)(2,1)}, bf16[4,512,128]{2,1,0:T(8,128)(2,1)S(1)}, u32[]{:S(2)}, u32[]{:S(2)}) collective-permute-start(bf16[4,512,128]{2,1,0:T(8,128)(2,1)} %get-tuple-element.7.xq), channel_id=1, source_target_pairs={{0,1},{17,16},{2,3},{19,18},{4,5},{21,20},{6,7},{23,22},{8,9},{25,... | collective-permute-start | bytes 1572872 | tf_op jit(solution)/shard_map/ppermute | solution.py:245
  52.0 30.9 %copy-start.2 = (bf16[4,512,128]{2,1,0:T(8,128)(2,1)}, bf16[4,512,128]{2,1,0:T(8,128)(2,1)S(1)}, u32[]{:S(2)}) copy-start(bf16[4,512,128]{2,1,0:T(8,128)(2,1)S(1)} %get-tuple-element.9.xk0) | copy-start | bytes 1572868
  52.0 14.0 %collective-permute-start.9 = (bf16[4,512,128]{2,1,0:T(8,128)(2,1)S(1)}, bf16[4,512,128]{2,1,0:T(8,128)(2,1)S(1)}, u32[]{:S(2)}, u32[]{:S(2)}) collective-permute-start(bf16[4,512,128]{2,1,0:T(8,128)(2,1)S(1)} %get-tuple-element.9.xk0), channel_id=1, source_target_pairs={{0,2},{2,4},{4,6},{6,0},{1,3},{3,5},{5,7},{7,1},{8,10},{10,12},{12... | collective-permute-start | bytes 1572872 | tf_op jit(solution)/shard_map/ppermute | solution.py:229
  53.7 12.5 %collective-permute-start.8 = (bf16[4,512,128]{2,1,0:T(8,128)(2,1)S(1)}, bf16[4,512,128]{2,1,0:T(8,128)(2,1)S(1)}, u32[]{:S(2)}, u32[]{:S(2)}) collective-permute-start(bf16[4,512,128]{2,1,0:T(8,128)(2,1)S(1)} %get-tuple-element.9.xk0), channel_id=1, source_target_pairs={{0,6},{2,0},{4,2},{6,4},{1,7},{3,1},{5,3},{7,5},{8,14},{10,8},{12,... | collective-permute-start | bytes 1572872 | tf_op jit(solution)/shard_map/ppermute | solution.py:229
  56.9 56.0 %copy-start.1 = (bf16[4,512,128]{2,1,0:T(8,128)(2,1)}, bf16[4,512,128]{2,1,0:T(8,128)(2,1)S(1)}, u32[]{:S(2)}) copy-start(bf16[4,512,128]{2,1,0:T(8,128)(2,1)S(1)} %broadcast_select_fusion.2.xk0) | copy-start | bytes 1572868
  56.9 20.4 %collective-permute-start.2 = (bf16[4,512,128]{2,1,0:T(8,128)(2,1)S(1)}, bf16[4,512,128]{2,1,0:T(8,128)(2,1)S(1)}, u32[]{:S(2)}, u32[]{:S(2)}) collective-permute-start(bf16[4,512,128]{2,1,0:T(8,128)(2,1)S(1)} %broadcast_select_fusion.2.xk0), channel_id=1, source_target_pairs={{0,2},{2,4},{4,6},{6,0},{1,3},{3,5},{5,7},{7,1},{8,10},{10,12},{12... | collective-permute-start | bytes 1572872 | tf_op jit(solution)/shard_map/ppermute | solution.py:229
  57.0 20.4 %collective-permute-start.1 = (bf16[4,512,128]{2,1,0:T(8,128)(2,1)S(1)}, bf16[4,512,128]{2,1,0:T(8,128)(2,1)S(1)}, u32[]{:S(2)}, u32[]{:S(2)}) collective-permute-start(bf16[4,512,128]{2,1,0:T(8,128)(2,1)S(1)} %broadcast_select_fusion.2.xk0), channel_id=1, source_target_pairs={{0,6},{2,0},{4,2},{6,4},{1,7},{3,1},{5,3},{7,5},{8,14},{10,8},{12,... | collective-permute-start | bytes 1572872 | tf_op jit(solution)/shard_map/ppermute | solution.py:229
  66.0 2.9 %copy-start.5 = (bf16[4,512,128]{2,1,0:T(8,128)(2,1)}, bf16[4,512,128]{2,1,0:T(8,128)(2,1)S(1)}, u32[]{:S(2)}) copy-start(bf16[4,512,128]{2,1,0:T(8,128)(2,1)S(1)} %collective-permute-done.9.xk3) | copy-start | bytes 1572868
  66.1 16.8 %collective-permute-start.10 = (bf16[4,256,128]{2,1,0:T(8,128)(2,1)S(1)}, bf16[4,256,128]{2,1,0:T(8,128)(2,1)S(1)}, u32[]{:S(2)}, u32[]{:S(2)}) collective-permute-start(bf16[4,256,128]{2,1,0:T(8,128)(2,1)S(1)} %slice.18), channel_id=1, source_target_pairs={{0,2},{2,4},{4,6},{6,0},{1,3},{3,5},{5,7},{7,1},{8,10},{10,12},{12... | collective-permute-start | bytes 786440 | tf_op jit(solution)/shard_map/ppermute | solution.py:229
  66.2 16.7 %copy-start.6 = (bf16[4,512,128]{2,1,0:T(8,128)(2,1)}, bf16[4,512,128]{2,1,0:T(8,128)(2,1)S(1)}, u32[]{:S(2)}) copy-start(bf16[4,512,128]{2,1,0:T(8,128)(2,1)S(1)} %collective-permute-done.8.xk1) | copy-start | bytes 1572868
  66.2 16.7 %collective-permute-start.11 = (bf16[4,256,128]{2,1,0:T(8,128)(2,1)S(1)}, bf16[4,256,128]{2,1,0:T(8,128)(2,1)S(1)}, u32[]{:S(2)}, u32[]{:S(2)}) collective-permute-start(bf16[4,256,128]{2,1,0:T(8,128)(2,1)S(1)} %slice.19), channel_id=1, source_target_pairs={{0,6},{2,0},{4,2},{6,4},{1,7},{3,1},{5,3},{7,5},{8,14},{10,8},{12,... | collective-permute-start | bytes 786440 | tf_op jit(solution)/shard_map/ppermute | solution.py:229
  77.3 35.6 %copy-start.3 = (bf16[4,512,128]{2,1,0:T(8,128)(2,1)}, bf16[4,512,128]{2,1,0:T(8,128)(2,1)S(1)}, u32[]{:S(2)}) copy-start(bf16[4,512,128]{2,1,0:T(8,128)(2,1)S(1)} %collective-permute-done.2.xk3) | copy-start | bytes 1572868
  77.3 45.4 %collective-permute-start.3 = (bf16[4,256,128]{2,1,0:T(8,128)(2,1)S(1)}, bf16[4,256,128]{2,1,0:T(8,128)(2,1)S(1)}, u32[]{:S(2)}, u32[]{:S(2)}) collective-permute-start(bf16[4,256,128]{2,1,0:T(8,128)(2,1)S(1)} %slice.16), channel_id=1, source_target_pairs={{0,2},{2,4},{4,6},{6,0},{1,3},{3,5},{5,7},{7,1},{8,10},{10,12},{12... | collective-permute-start | bytes 786440 | tf_op jit(solution)/shard_map/ppermute | solution.py:229
  77.4 35.5 %copy-start.4 = (bf16[4,512,128]{2,1,0:T(8,128)(2,1)}, bf16[4,512,128]{2,1,0:T(8,128)(2,1)S(1)}, u32[]{:S(2)}) copy-start(bf16[4,512,128]{2,1,0:T(8,128)(2,1)S(1)} %collective-permute-done.1.xk1) | copy-start | bytes 1572868
  77.4 45.3 %collective-permute-start.4 = (bf16[4,256,128]{2,1,0:T(8,128)(2,1)S(1)}, bf16[4,256,128]{2,1,0:T(8,128)(2,1)}, u32[]{:S(2)}, u32[]{:S(2)}) collective-permute-start(bf16[4,256,128]{2,1,0:T(8,128)(2,1)S(1)} %slice.17), channel_id=1, source_target_pairs={{0,6},{2,0},{4,2},{6,4},{1,7},{3,1},{5,3},{7,5},{8,14},{10,8},{12,... | collective-permute-start | bytes 786440 | tf_op jit(solution)/shard_map/ppermute | solution.py:229
  82.9 0.7 copy-start.8
  82.9 0.8 copy-start.9
  112.9 39.5 %all-to-all-start.1 = ((bf16[16,5,32,128]{3,2,1,0:T(8,128)(2,1)}), bf16[16,5,32,128]{3,2,1,0:T(8,128)(2,1)S(1)}, u32[]{:S(2)}, u32[]{:S(2)}) async-start(bf16[16,5,32,128]{3,2,1,0:T(8,128)(2,1)} %attend.3), calls=%async_computation.1 | async-start | bytes 1310720 | tf_op jit(solution)/shard_map/all_to_all | solution.py:258
  122.7 0.7 copy-start.7
  152.4 20.6 %copy-start = (bf16[16,5,32,128]{3,2,1,0:T(8,128)(2,1)}, bf16[16,5,32,128]{3,2,1,0:T(8,128)(2,1)S(1)}, u32[]{:S(2)}) copy-start(bf16[16,5,32,128]{3,2,1,0:T(8,128)(2,1)S(1)} %all-to-all-done.1.m2) | copy-start | bytes 1966084
Sparse Core Ops, SparseCore 0:
  10.8 53.3 all-gather.2

commit v3 on v2

--- a/solution.py
+++ b/solution.py
@@ -54,18 +54,20 @@
     )(pair_block, norm_gain.reshape(1, CHANNELS), head_bias)
 
 
-def attend_kernel(xq, xk0, xk1, xk2a, xk2b, xk3, w, bias, out, *scratch):
+def attend_kernel(xq, xk0, xk1, xk2, xk3, w, *rest):
+    biases, out, scratch = rest[:8], rest[8], rest[9:]
     bias_s, top_s, k_s, v_s, q_s, gate_s, stat_s, sems = scratch
     step = pl.program_id(0)
-    z = lax.axis_index("z")
+
+    y, z, core = lax.axis_index("y"), lax.axis_index("z"), lax.axis_index("core")
 
     def bias_copies():
         copies = []
-        for t in range(4):
-            for c in range(2):
-                src = bias.at[lax.rem(z + t, 4) * 2 + c]
-                dst = bias_s.at[t, :, pl.ds(c * 256, 256), :]
-                copies.append(pltpu.make_async_copy(src, dst, sems.at[t * 2 + c]))
+        for n, ref in enumerate(biases):
+            slot = lax.rem(y - z + 4 + n // 2, 4)
+            half = core if n % 2 == 0 else 1 - core
+            at = pl.ds(pl.multiple_of(half * 256, 256), 256)
+            copies.append(pltpu.make_async_copy(ref, bias_s.at[slot, :, at, :], sems.at[n]))
         return copies
 
     @pl.when(step == 0)
@@ -84,7 +86,7 @@
             at = slice(h * WIDTH, (h + 1) * WIDTH)
             q_s[r, h, at, :] = q_t[at]
         start = 0
-        for x in (xk0, xk1, xk2a, xk2b, xk3):
+        for x in (xk0, xk1, xk2, xk3):
             size = x.shape[1]
             at = slice(start, start + size)
             k_s[r, at, :] = matmul(x[r], w[:, 128:256]).astype(BF16)
@@ -121,24 +123,31 @@
             top = jnp.maximum(jnp.maximum(tops[0], tops[1]), jnp.maximum(tops[2], tops[3]))
             top_s[h : h + 1, :] = top.astype(F32)
 
-    fine = []
-    for r in range(STEP):
-        totals, shifts = [], []
-        for h in range(HEADS):
-            q, shift = q_s[r, h], top_s[h : h + 1, :]
-            total = None
-            for t in range(4):
-                at = slice(t * BLOCK, (t + 1) * BLOCK)
-                s = matmul(k_s[r, at, :], q) + bias_s[t, h].astype(F32)
-                p = jnp.exp2((s - shift) * LOG2E).astype(BF16)
-                pv = matmul(v_s[r, h, :, at], p)
-                total = pv if t == 0 else total + pv
-            totals.append(total)
-            shifts.append(shift)
-        finish(r, totals, shifts)
+    units = [(r, h, t) for r in range(STEP) for h in range(HEADS) for t in range(4)]
+
+    def scores(r, h, t):
+        at = slice(t * BLOCK, (t + 1) * BLOCK)
+        return matmul(k_s[r, at, :], q_s[r, h]) + bias_s[t, h].astype(F32)
+
+    fine, totals = [], []
+    ahead, total = scores(*units[0]), None
+    for n, (r, h, t) in enumerate(units):
+        s, shift = ahead, top_s[h : h + 1, :]
+        if n + 1 < len(units):
+            ahead = scores(*units[n + 1])
+        p = jnp.exp2((s - shift) * LOG2E).astype(BF16)
+        pv = matmul(v_s[r, h, :, t * BLOCK : (t + 1) * BLOCK], p)
+        total = pv if t == 0 else total + pv
+        if t < 3:
+            continue
+        totals.append(total)
+        if h < HEADS - 1:
+            continue
+        finish(r, totals, [top_s[g : g + 1, :] for g in range(HEADS)])
         mass = jnp.concatenate([total[WIDTH : WIDTH + 1] for total in totals], axis=0)
         inside = jnp.logical_and(mass > LOW, mass < HIGH)
         fine.append(jnp.min(inside.astype(F32)) > 0.5)
+        totals = []
 
     for r in range(STEP):
 
@@ -167,7 +176,7 @@
         out[:, ROWS] = stat_s[...].T.astype(BF16).reshape(16, SHARE, CHANNELS)
 
 
-def attend(x_q, x_ks, w_project, bias):
+def attend(x_q, x_ks, w_project, biases):
     def rows(x):
         return pl.BlockSpec((STEP,) + x.shape[1:], lambda i: (i, 0, 0))
 
@@ -179,7 +188,7 @@
         in_specs=[rows(x_q)]
         + [rows(x) for x in x_ks]
         + [pl.BlockSpec((CHANNELS, 512), lambda i: (0, 0))]
-        + [pl.BlockSpec(memory_space=pl.ANY)],
+        + [pl.BlockSpec(memory_space=pl.ANY)] * 8,
         out_specs=pl.BlockSpec(message, lambda i: (0, 0, 0, 0)),
         out_shape=jax.ShapeDtypeStruct(message, BF16),
         scratch_shapes=[
@@ -197,7 +206,7 @@
             flops=scores * 512, bytes_accessed=2**24, transcendentals=scores
         ),
         name="attend",
-    )(x_q, *x_ks, w_project, bias)
+    )(x_q, *x_ks, w_project, *biases)
 
 
 def merge_kernel(m1, m2, w, out):
@@ -229,12 +238,15 @@
     return lax.ppermute(x, axis, [(i, (i + step) % 4) for i in range(4)])
 
 
-def gather_ring(x, axis, cut):
-    behind, ahead = shift(x, axis, 1), shift(x, axis, -1)
-    half = x.shape[cut] // 2
-    far_a = shift(lax.slice_in_dim(behind, 0, half, axis=cut), axis, 1)
-    far_b = shift(lax.slice_in_dim(ahead, half, 2 * half, axis=cut), axis, -1)
-    return x, ahead, far_a, far_b, behind
+def gather_direct(x, axis):
+    return x, shift(x, axis, -1), shift(x, axis, 2), shift(x, axis, 1)
+
+
+def gather_bias(block):
+    behind, ahead = shift(block, "y", 1), shift(block, "y", -1)
+    far = [shift(behind[:2], "y", 1), shift(ahead[2:], "y", -1)]
+    blocks = [block, ahead, jnp.concatenate(far, axis=0), behind]
+    return [side for b in blocks for side in (b, lax.ppermute(b, "core", [(0, 1), (1, 0)]))]
 
 
 def shards(pair_block, norm_gain, w_project, w_out, head_bias):
@@ -247,18 +259,18 @@
     first_k = jnp.where(xl == xh, own, beside)
     passed = lax.ppermute(across, x_axis, [(1, 0), (2, 3)])
     second_k = jnp.where(xl == xh, passed, across)
-    partner = lax.ppermute(own, x_axis, [(3, 1), (0, 2)])
+    partner = lax.ppermute(beside, x_axis, [(1, 2), (2, 1)])
     second_q = jnp.where(xl == xh, passed, partner)
 
-    bias = lax.all_gather(bias_t, ("y", "core"), axis=0, tiled=False)
-    first_ks = gather_ring(first_k, "z", 1)
-    second_ks = gather_ring(second_k, "z", 1)
+    biases = gather_bias(bias_t)
+    first_ks = gather_direct(first_k, "z")
+    second_ks = gather_direct(second_k, "z")
 
     def spread(x):
         return lax.all_to_all(x, ROW_AXES, split_axis=0, concat_axis=0, tiled=True)
 
-    m1 = spread(attend(own, first_ks, w_project, bias))
-    m2 = spread(attend(second_q, second_ks, w_project, bias))
+    m1 = spread(attend(own, first_ks, w_project, biases))
+    m2 = spread(attend(second_q, second_ks, w_project, biases))
     update = merge(m1, m2, w_out)
     return jnp.transpose(update, (2, 0, 1, 3)).reshape(SHARE, 16 * ROWS, CHANNELS)
 

time: 186 us -> 167 us (0.90)
  starting transfers between devices: 53.4 us -> 39.2 us
  between operations: 13.6 us -> 0.23 us
  waiting for transfers between devices: 26.4 us -> 39.6 us
  Pallas kernels: 65.3 us -> 58.3 us
  local copies, waits for them, and re-layouts: 3.56 us -> 7.21 us
    ppermute x8 -> x10, waiting for transfers between devices: 17.5 us -> 39.5 us  [shift(): return lax.ppermute(x, axis, [(i, (i + step) % 4) for i in range(4)])]
    ppermute x1, starting transfers between devices: 22.5 us -> 3.14 us  [shards(): beside = lax.ppermute(own, x_axis, [(0, 1), (3, 2)])]
    ppermute x1 -> x5, starting transfers between devices: 6.98 us -> 16.1 us  [the longest x4 15.4 us: gather_bias(): lax.ppermute(b, 'core', [(0, 1), (1, 0)])]
    ppermute x1, waiting for transfers between devices: 8.88 us -> 0.01 us  [shards(): passed = lax.ppermute(across, x_axis, [(1, 0), (2, 3)])]
    pallas_call x2, Pallas kernels: 58.1 us -> 51 us  [attend(): pl.pallas_call(attend_kernel, grid=(ROWS // STEP,), in_specs=[rows(x_q)]...]
    all_to_all x1, starting transfers between devices: 9.85 us -> 5.62 us  [spread(): return lax.all_to_all(x, ROW_AXES, split_axis=0, concat_axis=0, tiled=True)]
    unnamed x20 -> x29, local copies, waits for them, and re-layouts: 1.45 us -> 3.61 us
    ppermute x8 -> x10, starting transfers between devices: 12.1 us -> 12.4 us  [shift(): return lax.ppermute(x, axis, [(i, (i + step) % 4) for i in range(4)])]
  transfers between devices with their start and end apart: 14 -> 19, of which waited for: 4 -> 4; matrix products, arithmetic and copies ran while one was open for 1% -> 2% of each run, Pallas kernels for 31% -> 31%
where the time goes in v3:
time: 167 us; the launch traced here: 166 us
  Pallas kernels  58.3 us (35%)
  waiting for transfers between devices  39.6 us (24%)
  starting transfers between devices  39.2 us (23%)
  blocking collectives  20.6 us (12%)
  local copies, waits for them, and re-layouts  7.21 us (4%)
    pallas_call x2, Pallas kernels, attend(): pl.pallas_call(attend_kernel, grid=(ROWS // STEP,), in_specs=[rows(x_q)]...  51 us
    ppermute x10, waiting for transfers between devices, shift(): return lax.ppermute(x, axis, [(i, (i + step) % 4) for i in range(4)])  39.5 us
    all_to_all x1, blocking collectives, spread(): return lax.all_to_all(x, ROW_AXES, split_axis=0, concat_axis=0, tiled=True)  20.6 us
    ppermute x4, starting transfers between devices, gather_bias(): lax.ppermute(b, 'core', [(0, 1), (1, 0)])  15.4 us
    ppermute x10, starting transfers between devices, shift(): return lax.ppermute(x, axis, [(i, (i + step) % 4) for i in range(4)])  12.4 us
    all_to_all x1, starting transfers between devices, spread(): return lax.all_to_all(x, ROW_AXES, split_axis=0, concat_axis=0, tiled=True)  5.62 us
    pallas_call x1, Pallas kernels, prepare(): pl.pallas_call(prepare_kernel, grid=(ROWS,), in_specs=[whole(COLS, CHANNE...  4.1 us
    unnamed x29, local copies, waits for them, and re-layouts  3.61 us
  transfers between devices with their start and end apart: 19, of which 4 were waited for; matrix products, arithmetic and copies ran while one was open for 2% of the time, Pallas kernels for 31%

profile of v3, /device:TPU:1, one launch (start us, length us, event | category | flops | bytes accessed | tf_op | source)
XLA Modules:
  0.0 166.0 jit_solution(13268464154014318740)
XLA Ops:
  0.0 4.1 %prepare.1 = (bf16[4,512,128]{2,1,0:T(8,128)(2,1)}, bf16[4,256,512]{2,1,0:T(8,128)(2,1)}) custom-call(bf16[4,512,128]{2,1,0:T(8,128)(2,1)} %pair.1, f32[1,128]{1,0:T(1,128)} %bitcast.5, bf16[4,512,256]{2,1,0:T(8,128)(2,1)} %bias.1), custom_call_target="tpu_custom_call" | custom-call | tf_op jit(solution)/shard_map/prepare/pallas_call | solution.py:40
  4.1 2.1 %collective-permute-start.7 = (bf16[4,256,512]{2,1,0:T(8,128)(2,1)}, bf16[4,256,512]{2,1,0:T(8,128)(2,1)S(1)}, u32[]{:S(2)}, u32[]{:S(2)}) collective-permute-start(bf16[4,256,512]{2,1,0:T(8,128)(2,1)} %get-tuple-element.8.rest_0_), channel_id=1, source_target_pairs={{0,32},{32,64},{64,96},{96,0},{1,33},{33,65},{65,97},{97,1},{2,34}... | collective-permute-start | bytes 3145736 | tf_op jit(solution)/shard_map/ppermute | solution.py:238
  6.2 1.5 collective-permute-start.5
  7.7 3.1 %collective-permute-start = (bf16[4,512,128]{2,1,0:T(8,128)(2,1)}, bf16[4,512,128]{2,1,0:T(8,128)(2,1)S(1)}, u32[]{:S(2)}, u32[]{:S(2)}) collective-permute-start(bf16[4,512,128]{2,1,0:T(8,128)(2,1)} %get-tuple-element.7.xq), channel_id=1, source_target_pairs={{0,1},{17,16},{2,3},{19,18},{4,5},{21,20},{6,7},{23,22},{8,9},{25,... | collective-permute-start | bytes 1572872 | tf_op jit(solution)/shard_map/ppermute | solution.py:257
  11.5 19.1 %collective-permute-done.7.rest_6_ = bf16[4,256,512]{2,1,0:T(8,128)(2,1)S(1)} collective-permute-done((bf16[4,256,512]{2,1,0:T(8,128)(2,1)}, bf16[4,256,512]{2,1,0:T(8,128)(2,1)S(1)}, u32[]{:S(2)}, u32[]{:S(2)}) %collective-permute-start.7) | collective-permute-done | bytes 1048608 | tf_op jit(solution)/shard_map/ppermute | solution.py:238
  30.8 1.5 slice.9
  32.2 2.3 %collective-permute-start.9 = (bf16[2,256,512]{2,1,0:T(8,128)(2,1)S(1)}, bf16[2,256,512]{2,1,0:T(8,128)(2,1)S(1)}, u32[]{:S(2)}, u32[]{:S(2)}) collective-permute-start(bf16[2,256,512]{2,1,0:T(8,128)(2,1)S(1)} %slice.9), channel_id=1, source_target_pairs={{0,96},{32,0},{64,32},{96,64},{1,97},{33,1},{65,33},{97,65},{2,98}... | collective-permute-start | bytes 1572872 | tf_op jit(solution)/shard_map/ppermute | solution.py:238
  34.6 3.7 %collective-permute-start.1 = (bf16[4,512,128]{2,1,0:T(8,128)(2,1)S(1)}, bf16[4,512,128]{2,1,0:T(8,128)(2,1)S(1)}, u32[]{:S(2)}, u32[]{:S(2)}) collective-permute-start(bf16[4,512,128]{2,1,0:T(8,128)(2,1)S(1)} %broadcast_select_fusion.2.xk0), channel_id=1, source_target_pairs={{0,6},{2,0},{4,2},{6,4},{1,7},{3,1},{5,3},{7,5},{8,14},{10,8},{12,... | collective-permute-start | bytes 1572872 | tf_op jit(solution)/shard_map/ppermute | solution.py:238
  38.4 1.3 collective-permute-start.13
  39.7 4.3 %collective-permute-done.8 = bf16[2,256,512]{2,1,0:T(8,128)(2,1)S(1)} collective-permute-done((bf16[2,256,512]{2,1,0:T(8,128)(2,1)S(1)}, bf16[2,256,512]{2,1,0:T(8,128)(2,1)S(1)}, u32[]{:S(2)}, u32[]{:S(2)}) %collective-permute-start.8) | collective-permute-done | bytes 524320 | tf_op jit(solution)/shard_map/ppermute | solution.py:238
  44.0 2.3 %collective-permute-start.4 = (bf16[4,256,512]{2,1,0:T(8,128)(2,1)S(1)}, bf16[4,256,512]{2,1,0:T(8,128)(2,1)S(1)}, u32[]{:S(2)}, u32[]{:S(2)}) collective-permute-start(bf16[4,256,512]{2,1,0:T(8,128)(2,1)S(1)} %copy-done.6), channel_id=1, source_target_pairs={{0,8},{8,0},{1,9},{9,1},{2,10},{10,2},{3,11},{11,3},{4,12},{12,4},... | collective-permute-start | bytes 3145736 | tf_op jit(solution)/shard_map/ppermute | solution.py:249
  47.1 2.2 %collective-permute-done.1.xk1 = bf16[4,512,128]{2,1,0:T(8,128)(2,1)S(1)} collective-permute-done((bf16[4,512,128]{2,1,0:T(8,128)(2,1)S(1)}, bf16[4,512,128]{2,1,0:T(8,128)(2,1)S(1)}, u32[]{:S(2)}, u32[]{:S(2)}) %collective-permute-start.1) | collective-permute-done | bytes 524320 | tf_op jit(solution)/shard_map/ppermute | solution.py:238
  49.3 12.5 %collective-permute-start.6 = (bf16[4,256,512]{2,1,0:T(8,128)(2,1)}, bf16[4,256,512]{2,1,0:T(8,128)(2,1)S(1)}, u32[]{:S(2)}, u32[]{:S(2)}) collective-permute-start(bf16[4,256,512]{2,1,0:T(8,128)(2,1)} %collective-permute-done.5.rest_2_), channel_id=1, source_target_pairs={{0,8},{8,0},{1,9},{9,1},{2,10},{10,2},{3,11},{11,3},{4,12},{12,4},... | collective-permute-start | bytes 3145736 | tf_op jit(solution)/shard_map/ppermute | solution.py:249
  63.4 0.9 broadcast_select_fusion
  64.2 14.0 %collective-permute-done.3.xk3 = bf16[4,512,128]{2,1,0:T(8,128)(2,1)S(1)} collective-permute-done((bf16[4,512,128]{2,1,0:T(8,128)(2,1)S(1)}, bf16[4,512,128]{2,1,0:T(8,128)(2,1)S(1)}, u32[]{:S(2)}, u32[]{:S(2)}) %collective-permute-start.3) | collective-permute-done | bytes 524320 | tf_op jit(solution)/shard_map/ppermute | solution.py:238
  78.2 0.8 copy-done.13
  79.0 1.3 collective-permute-start.15
  81.7 1.0 copy-done.9
  82.7 25.5 %attend.2 = bf16[16,5,32,128]{3,2,1,0:T(8,128)(2,1)} custom-call(bf16[4,512,128]{2,1,0:T(8,128)(2,1)} %get-tuple-element.7.xq, bf16[4,512,128]{2,1,0:T(8,128)(2,1)} %copy-done.2, bf16[4,512,128]{2,1,0:T(8,128)(2,1)} %copy-done.10, bf16[4,512,128]{2,1,0:T(8,128)(2,1)} %copy-done.11, bf16[4,512,128]{2,1,0:T(8,128)(2,1)} %copy-done.13, bf16[128,512]{1,0:T(8,128)(2,1)} %w.4, ...), custom_call_target="tpu_custom_call" | custom-call | flops 8589934592 | bytes 16777216 | tf_op jit(solution)/shard_map/attend/pallas_call | solution.py:185
  108.3 5.6 %all-to-all-start = ((bf16[16,5,32,128]{3,2,1,0:T(8,128)(2,1)}), bf16[16,5,32,128]{3,2,1,0:T(8,128)(2,1)S(1)}, u32[]{:S(2)}, u32[]{:S(2)}) async-start(bf16[16,5,32,128]{3,2,1,0:T(8,128)(2,1)} %attend.2), calls=%async_computation | async-start | bytes 1310720 | tf_op jit(solution)/shard_map/all_to_all | solution.py:270
  114.7 25.5 %attend.3 = bf16[16,5,32,128]{3,2,1,0:T(8,128)(2,1)} custom-call(bf16[4,512,128]{2,1,0:T(8,128)(2,1)} %get-tuple-element.10.xq, bf16[4,512,128]{2,1,0:T(8,128)(2,1)} %copy-done.3, bf16[4,512,128]{2,1,0:T(8,128)(2,1)} %copy-done.12, bf16[4,512,128]{2,1,0:T(8,128)(2,1)} %collective-permute-done.16.xk2, bf16[4,512,128]{2,1,0:T(8,128)(2,1)} %collective-permute-done.17.xk3, ...), custom_call_target="tpu_custom_call" | custom-call | flops 8589934592 | bytes 16777216 | tf_op jit(solution)/shard_map/attend/pallas_call | solution.py:185
  140.2 20.6 %all_to_all.10.m2 = bf16[16,5,32,128]{3,2,1,0:T(8,128)(2,1)} all-to-all(bf16[16,5,32,128]{3,2,1,0:T(8,128)(2,1)} %attend.3), channel_id=1, replica_groups=mesh['y'=4,'xh'=2,'core'=2,'z'=4,'xl'=2] {'y','xh','core'}, dimensions={0} | all-to-all | bytes 1310720 | tf_op jit(solution)/shard_map/all_to_all | solution.py:270
  160.8 3.1 %merge.1 = bf16[16,4,32,128]{3,2,1,0:T(8,128)(2,1)} custom-call(bf16[16,5,32,128]{3,2,1,0:T(8,128)(2,1)} %copy-done, bf16[16,5,32,128]{3,2,1,0:T(8,128)(2,1)} %all_to_all.10.m2, bf16[128,128]{1,0:T(8,128)(2,1)} %w.5), custom_call_target="tpu_custom_call" | custom-call | tf_op jit(solution)/shard_map/merge/pallas_call | solution.py:229
  164.0 2.0 %copy.6 = bf16[32,64,128]{2,1,0:T(8,128)(2,1)} copy(bf16[32,64,128]{2,0,1:T(8,128)(2,1)} %bitcast.4) | data formatting | bytes 1048576 | tf_op jit(solution)/shard_map/reshape | solution.py:275
  (54 shorter events, 5.4 us)
Async XLA Ops:
  4.1 26.5 %collective-permute-start.7 = (bf16[4,256,512]{2,1,0:T(8,128)(2,1)}, bf16[4,256,512]{2,1,0:T(8,128)(2,1)S(1)}, u32[]{:S(2)}, u32[]{:S(2)}) collective-permute-start(bf16[4,256,512]{2,1,0:T(8,128)(2,1)} %get-tuple-element.8.rest_0_), channel_id=1, source_target_pairs={{0,32},{32,64},{64,96},{96,0},{1,33},{33,65},{65,97},{97,1},{2,34}... | collective-permute-start | bytes 3145736 | tf_op jit(solution)/shard_map/ppermute | solution.py:238
  6.2 24.5 %collective-permute-start.5 = (bf16[4,256,512]{2,1,0:T(8,128)(2,1)}, bf16[4,256,512]{2,1,0:T(8,128)(2,1)}, u32[]{:S(2)}, u32[]{:S(2)}) collective-permute-start(bf16[4,256,512]{2,1,0:T(8,128)(2,1)} %get-tuple-element.8.rest_0_), channel_id=1, source_target_pairs={{0,96},{32,0},{64,32},{96,64},{1,97},{33,1},{65,33},{97,65},{2,98}... | collective-permute-start | bytes 3145736 | tf_op jit(solution)/shard_map/ppermute | solution.py:238
  7.7 26.9 %collective-permute-start = (bf16[4,512,128]{2,1,0:T(8,128)(2,1)}, bf16[4,512,128]{2,1,0:T(8,128)(2,1)S(1)}, u32[]{:S(2)}, u32[]{:S(2)}) collective-permute-start(bf16[4,512,128]{2,1,0:T(8,128)(2,1)} %get-tuple-element.7.xq), channel_id=1, source_target_pairs={{0,1},{17,16},{2,3},{19,18},{4,5},{21,20},{6,7},{23,22},{8,9},{25,... | collective-permute-start | bytes 1572872 | tf_op jit(solution)/shard_map/ppermute | solution.py:257
  10.8 27.5 %collective-permute-start.12 = (bf16[4,512,128]{2,1,0:T(8,128)(2,1)}, bf16[4,512,128]{2,1,0:T(8,128)(2,1)S(1)}, u32[]{:S(2)}, u32[]{:S(2)}) collective-permute-start(bf16[4,512,128]{2,1,0:T(8,128)(2,1)} %get-tuple-element.7.xq), channel_id=1, source_target_pairs={{1,16},{16,1},{3,18},{18,3},{5,20},{20,5},{7,22},{22,7},{9,24},{24... | collective-permute-start | bytes 1572872 | tf_op jit(solution)/shard_map/ppermute | solution.py:258
  30.6 31.2 %copy-start.4 = (bf16[4,256,512]{2,1,0:T(8,128)(2,1)}, bf16[4,256,512]{2,1,0:T(8,128)(2,1)S(1)}, u32[]{:S(2)}) copy-start(bf16[4,256,512]{2,1,0:T(8,128)(2,1)S(1)} %collective-permute-done.7.rest_6_) | copy-start | bytes 3145732
  30.7 13.3 %collective-permute-start.8 = (bf16[2,256,512]{2,1,0:T(8,128)(2,1)S(1)}, bf16[2,256,512]{2,1,0:T(8,128)(2,1)S(1)}, u32[]{:S(2)}, u32[]{:S(2)}) collective-permute-start(bf16[2,256,512]{2,1,0:T(8,128)(2,1)S(1)} %slice.8), channel_id=1, source_target_pairs={{0,32},{32,64},{64,96},{96,0},{1,33},{33,65},{65,97},{97,1},{2,34}... | collective-permute-start | bytes 1572872 | tf_op jit(solution)/shard_map/ppermute | solution.py:238
  32.2 14.1 %collective-permute-start.9 = (bf16[2,256,512]{2,1,0:T(8,128)(2,1)S(1)}, bf16[2,256,512]{2,1,0:T(8,128)(2,1)S(1)}, u32[]{:S(2)}, u32[]{:S(2)}) collective-permute-start(bf16[2,256,512]{2,1,0:T(8,128)(2,1)S(1)} %slice.9), channel_id=1, source_target_pairs={{0,96},{32,0},{64,32},{96,64},{1,97},{33,1},{65,33},{97,65},{2,98}... | collective-permute-start | bytes 1572872 | tf_op jit(solution)/shard_map/ppermute | solution.py:238
  34.6 27.7 %copy-start.2 = (bf16[4,512,128]{2,1,0:T(8,128)(2,1)}, bf16[4,512,128]{2,1,0:T(8,128)(2,1)S(1)}, u32[]{:S(2)}) copy-start(bf16[4,512,128]{2,1,0:T(8,128)(2,1)S(1)} %broadcast_select_fusion.2.xk0) | copy-start | bytes 1572868
  34.6 14.6 %collective-permute-start.1 = (bf16[4,512,128]{2,1,0:T(8,128)(2,1)S(1)}, bf16[4,512,128]{2,1,0:T(8,128)(2,1)S(1)}, u32[]{:S(2)}, u32[]{:S(2)}) collective-permute-start(bf16[4,512,128]{2,1,0:T(8,128)(2,1)S(1)} %broadcast_select_fusion.2.xk0), channel_id=1, source_target_pairs={{0,6},{2,0},{4,2},{6,4},{1,7},{3,1},{5,3},{7,5},{8,14},{10,8},{12,... | collective-permute-start | bytes 1572872 | tf_op jit(solution)/shard_map/ppermute | solution.py:238
  38.4 23.4 %collective-permute-start.2 = (bf16[4,512,128]{2,1,0:T(8,128)(2,1)S(1)}, bf16[4,512,128]{2,1,0:T(8,128)(2,1)S(1)}, u32[]{:S(2)}, u32[]{:S(2)}) collective-permute-start(bf16[4,512,128]{2,1,0:T(8,128)(2,1)S(1)} %broadcast_select_fusion.2.xk0), channel_id=1, source_target_pairs={{0,4},{2,6},{4,0},{6,2},{1,5},{3,7},{5,1},{7,3},{8,12},{10,14},{12... | collective-permute-start | bytes 1572872 | tf_op jit(solution)/shard_map/ppermute | solution.py:238
  38.4 23.5 %collective-permute-start.13 = (bf16[4,512,128]{2,1,0:T(8,128)(2,1)S(1)}, bf16[4,512,128]{2,1,0:T(8,128)(2,1)S(1)}, u32[]{:S(2)}, u32[]{:S(2)}) collective-permute-start(bf16[4,512,128]{2,1,0:T(8,128)(2,1)S(1)} %collective-permute-done.12), channel_id=1, source_target_pairs={{1,0},{16,17},{3,2},{18,19},{5,4},{20,21},{7,6},{22,23},{9,8},{24,... | collective-permute-start | bytes 1572872 | tf_op jit(solution)/shard_map/ppermute | solution.py:260
  44.0 36.3 %collective-permute-start.4 = (bf16[4,256,512]{2,1,0:T(8,128)(2,1)S(1)}, bf16[4,256,512]{2,1,0:T(8,128)(2,1)S(1)}, u32[]{:S(2)}, u32[]{:S(2)}) collective-permute-start(bf16[4,256,512]{2,1,0:T(8,128)(2,1)S(1)} %copy-done.6), channel_id=1, source_target_pairs={{0,8},{8,0},{1,9},{9,1},{2,10},{10,2},{3,11},{11,3},{4,12},{12,4},... | collective-permute-start | bytes 3145736 | tf_op jit(solution)/shard_map/ppermute | solution.py:249
  46.3 16.0 %collective-permute-start.14 = (bf16[4,512,128]{2,1,0:T(8,128)(2,1)S(1)}, bf16[4,512,128]{2,1,0:T(8,128)(2,1)S(1)}, u32[]{:S(2)}, u32[]{:S(2)}) collective-permute-start(bf16[4,512,128]{2,1,0:T(8,128)(2,1)S(1)} %collective-permute-done), channel_id=1, source_target_pairs={{1,16},{16,1},{3,18},{18,3},{5,20},{20,5},{7,22},{22,7},{9,24},{24... | collective-permute-start | bytes 1572872 | tf_op jit(solution)/shard_map/ppermute | solution.py:262
  47.1 17.2 %copy-start.5 = (bf16[4,256,512]{2,1,0:T(8,128)(2,1)}, bf16[4,256,512]{2,1,0:T(8,128)(2,1)S(1)}, u32[]{:S(2)}) copy-start(bf16[4,256,512]{2,1,0:T(8,128)(2,1)S(1)} %constant_dynamic-update-slice_fusion.rest_4_) | copy-start | bytes 3145732
  49.3 31.0 %collective-permute-start.6 = (bf16[4,256,512]{2,1,0:T(8,128)(2,1)}, bf16[4,256,512]{2,1,0:T(8,128)(2,1)S(1)}, u32[]{:S(2)}, u32[]{:S(2)}) collective-permute-start(bf16[4,256,512]{2,1,0:T(8,128)(2,1)} %collective-permute-done.5.rest_2_), channel_id=1, source_target_pairs={{0,8},{8,0},{1,9},{9,1},{2,10},{10,2},{3,11},{11,3},{4,12},{12,4},... | collective-permute-start | bytes 3145736 | tf_op jit(solution)/shard_map/ppermute | solution.py:249
  61.8 19.2 %collective-permute-start.11 = (bf16[4,256,512]{2,1,0:T(8,128)(2,1)S(1)}, bf16[4,256,512]{2,1,0:T(8,128)(2,1)S(1)}, u32[]{:S(2)}, u32[]{:S(2)}) collective-permute-start(bf16[4,256,512]{2,1,0:T(8,128)(2,1)S(1)} %collective-permute-done.7.rest_6_), channel_id=1, source_target_pairs={{0,8},{8,0},{1,9},{9,1},{2,10},{10,2},{3,11},{11,3},{4,12},{12,4},... | collective-permute-start | bytes 3145736 | tf_op jit(solution)/shard_map/ppermute | solution.py:249
  61.9 20.9 %collective-permute-start.10 = (bf16[4,256,512]{2,1,0:T(8,128)(2,1)S(1)}, bf16[4,256,512]{2,1,0:T(8,128)(2,1)}, u32[]{:S(2)}, u32[]{:S(2)}) collective-permute-start(bf16[4,256,512]{2,1,0:T(8,128)(2,1)S(1)} %constant_dynamic-update-slice_fusion.rest_4_), channel_id=1, source_target_pairs={{0,8},{8,0},{1,9},{9,1},{2,10},{10,2},{3,11},{11,3},{4,12},{12,4},... | collective-permute-start | bytes 3145736 | tf_op jit(solution)/shard_map/ppermute | solution.py:249
  62.6 15.6 %collective-permute-start.3 = (bf16[4,512,128]{2,1,0:T(8,128)(2,1)S(1)}, bf16[4,512,128]{2,1,0:T(8,128)(2,1)S(1)}, u32[]{:S(2)}, u32[]{:S(2)}) collective-permute-start(bf16[4,512,128]{2,1,0:T(8,128)(2,1)S(1)} %broadcast_select_fusion.2.xk0), channel_id=1, source_target_pairs={{0,2},{2,4},{4,6},{6,0},{1,3},{3,5},{5,7},{7,1},{8,10},{10,12},{12... | collective-permute-start | bytes 1572872 | tf_op jit(solution)/shard_map/ppermute | solution.py:238
  64.2 44.0 %copy-start.3 = (bf16[4,512,128]{2,1,0:T(8,128)(2,1)}, bf16[4,512,128]{2,1,0:T(8,128)(2,1)S(1)}, u32[]{:S(2)}) copy-start(bf16[4,512,128]{2,1,0:T(8,128)(2,1)S(1)} %get-tuple-element.9.xk0) | copy-start | bytes 1572868
  79.0 34.9 %collective-permute-start.15 = (bf16[4,512,128]{2,1,0:T(8,128)(2,1)S(1)}, bf16[4,512,128]{2,1,0:T(8,128)(2,1)S(1)}, u32[]{:S(2)}, u32[]{:S(2)}) collective-permute-start(bf16[4,512,128]{2,1,0:T(8,128)(2,1)S(1)} %get-tuple-element.9.xk0), channel_id=1, source_target_pairs={{0,6},{2,0},{4,2},{6,4},{1,7},{3,1},{5,3},{7,5},{8,14},{10,8},{12,... | collective-permute-start | bytes 1572872 | tf_op jit(solution)/shard_map/ppermute | solution.py:238
  80.3 33.6 %collective-permute-start.16 = (bf16[4,512,128]{2,1,0:T(8,128)(2,1)S(1)}, bf16[4,512,128]{2,1,0:T(8,128)(2,1)}, u32[]{:S(2)}, u32[]{:S(2)}) collective-permute-start(bf16[4,512,128]{2,1,0:T(8,128)(2,1)S(1)} %get-tuple-element.9.xk0), channel_id=1, source_target_pairs={{0,4},{2,6},{4,0},{6,2},{1,5},{3,7},{5,1},{7,3},{8,12},{10,14},{12... | collective-permute-start | bytes 1572872 | tf_op jit(solution)/shard_map/ppermute | solution.py:238
  80.3 33.6 %collective-permute-start.17 = (bf16[4,512,128]{2,1,0:T(8,128)(2,1)S(1)}, bf16[4,512,128]{2,1,0:T(8,128)(2,1)}, u32[]{:S(2)}, u32[]{:S(2)}) collective-permute-start(bf16[4,512,128]{2,1,0:T(8,128)(2,1)S(1)} %get-tuple-element.9.xk0), channel_id=1, source_target_pairs={{0,2},{2,4},{4,6},{6,0},{1,3},{3,5},{5,7},{7,1},{8,10},{10,12},{12... | collective-permute-start | bytes 1572872 | tf_op jit(solution)/shard_map/ppermute | solution.py:238
  108.3 32.0 %all-to-all-start = ((bf16[16,5,32,128]{3,2,1,0:T(8,128)(2,1)}), bf16[16,5,32,128]{3,2,1,0:T(8,128)(2,1)S(1)}, u32[]{:S(2)}, u32[]{:S(2)}) async-start(bf16[16,5,32,128]{3,2,1,0:T(8,128)(2,1)} %attend.2), calls=%async_computation | async-start | bytes 1310720 | tf_op jit(solution)/shard_map/all_to_all | solution.py:270
  140.2 20.6 %copy-start = (bf16[16,5,32,128]{3,2,1,0:T(8,128)(2,1)}, bf16[16,5,32,128]{3,2,1,0:T(8,128)(2,1)S(1)}, u32[]{:S(2)}) copy-start(bf16[16,5,32,128]{3,2,1,0:T(8,128)(2,1)S(1)} %all-to-all-done.m1) | copy-start | bytes 1966084
  (9 other events, 36.4 us)

commit v4 on v3

--- a/solution.py
+++ b/solution.py
@@ -55,19 +55,18 @@
 
 
 def attend_kernel(xq, xk0, xk1, xk2, xk3, w, *rest):
-    biases, out, scratch = rest[:8], rest[8], rest[9:]
+    biases, out, scratch = rest[:1], rest[1], rest[2:]
     bias_s, top_s, k_s, v_s, q_s, gate_s, stat_s, sems = scratch
     step = pl.program_id(0)
 
-    y, z, core = lax.axis_index("y"), lax.axis_index("z"), lax.axis_index("core")
+    z = lax.axis_index("z")
 
     def bias_copies():
         copies = []
-        for n, ref in enumerate(biases):
-            slot = lax.rem(y - z + 4 + n // 2, 4)
-            half = core if n % 2 == 0 else 1 - core
-            at = pl.ds(pl.multiple_of(half * 256, 256), 256)
-            copies.append(pltpu.make_async_copy(ref, bias_s.at[slot, :, at, :], sems.at[n]))
+        for n in range(8):
+            src = biases[0].at[lax.rem(z + n // 2, 4) * 2 + n % 2]
+            dst = bias_s.at[n // 2, :, pl.ds(n % 2 * 256, 256), :]
+            copies.append(pltpu.make_async_copy(src, dst, sems.at[n]))
         return copies
 
     @pl.when(step == 0)
@@ -188,7 +187,7 @@
         in_specs=[rows(x_q)]
         + [rows(x) for x in x_ks]
         + [pl.BlockSpec((CHANNELS, 512), lambda i: (0, 0))]
-        + [pl.BlockSpec(memory_space=pl.ANY)] * 8,
+        + [pl.BlockSpec(memory_space=pl.ANY)],
         out_specs=pl.BlockSpec(message, lambda i: (0, 0, 0, 0)),
         out_shape=jax.ShapeDtypeStruct(message, BF16),
         scratch_shapes=[
@@ -242,13 +241,6 @@
     return x, shift(x, axis, -1), shift(x, axis, 2), shift(x, axis, 1)
 
 
-def gather_bias(block):
-    behind, ahead = shift(block, "y", 1), shift(block, "y", -1)
-    far = [shift(behind[:2], "y", 1), shift(ahead[2:], "y", -1)]
-    blocks = [block, ahead, jnp.concatenate(far, axis=0), behind]
-    return [side for b in blocks for side in (b, lax.ppermute(b, "core", [(0, 1), (1, 0)]))]
-
-
 def shards(pair_block, norm_gain, w_project, w_out, head_bias):
     xh, xl = lax.axis_index("xh"), lax.axis_index("xl")
     own, bias_t = prepare(pair_block, norm_gain, head_bias)
@@ -262,7 +254,8 @@
     partner = lax.ppermute(beside, x_axis, [(1, 2), (2, 1)])
     second_q = jnp.where(xl == xh, passed, partner)
 
-    biases = gather_bias(bias_t)
+    gathered = lax.all_gather(bias_t, ("y", "core"), axis=0, tiled=False)
+    biases = [gathered]
     first_ks = gather_direct(first_k, "z")
     second_ks = gather_direct(second_k, "z")
 

time: 167 us -> 164 us (0.982)
  between operations: 0.23 us -> 13.5 us
  starting transfers between devices: 39.2 us -> 31.6 us
  waiting for transfers between devices: 39.6 us -> 33.2 us
  local copies, waits for them, and re-layouts: 7.21 us -> 3.97 us
    ppermute x10 -> x6, waiting for transfers between devices: 39.5 us -> 16.6 us  [shift(): return lax.ppermute(x, axis, [(i, (i + step) % 4) for i in range(4)])]
    ppermute x4 -> x0, starting transfers between devices: 15.4 us -> none  [gather_bias(): lax.ppermute(b, 'core', [(0, 1), (1, 0)])]
    ppermute x1, waiting for transfers between devices: 0.01 us -> 9.23 us  [shards(): beside = lax.ppermute(own, x_axis, [(0, 1), (3, 2)])]
    all_to_all x1, starting transfers between devices: 5.62 us -> 14.2 us  [spread(): return lax.all_to_all(x, ROW_AXES, split_axis=0, concat_axis=0, tiled=True)]
    ppermute x1, waiting for transfers between devices: 0.01 us -> 5 us  [shards(): passed = lax.ppermute(across, x_axis, [(1, 0), (2, 3)])]
    ppermute x10 -> x6, starting transfers between devices: 12.4 us -> 8.34 us  [shift(): return lax.ppermute(x, axis, [(i, (i + step) % 4) for i in range(4)])]
    ppermute x1, starting transfers between devices: 3.14 us -> 6.4 us  [shards(): beside = lax.ppermute(own, x_axis, [(0, 1), (3, 2)])]
    all_gather x0 -> x1, waiting for transfers between devices: none -> 2.36 us  [shards(): gathered = lax.all_gather(bias_t, ('y', 'core'), axis=0, tiled=False)]
  transfers between devices with their start and end apart: 19 -> 12, of which waited for: 4 -> 6; matrix products, arithmetic and copies ran while one was open for 2% -> 1% of each run, Pallas kernels for 31% -> 31%
where the time goes in v4:
time: 164 us; the launch traced here: 163 us
  Pallas kernels  58.2 us (35%)
  waiting for transfers between devices  33.2 us (20%)
  starting transfers between devices  31.6 us (19%)
  blocking collectives  20.6 us (13%)
  between operations  13.5 us (8%)
  local copies, waits for them, and re-layouts  3.97 us (2%)
  other arithmetic  2.06 us (1%)
    pallas_call x2, Pallas kernels, attend(): pl.pallas_call(attend_kernel, grid=(ROWS // STEP,), in_specs=[rows(x_q)]...  51 us
    all_to_all x1, blocking collectives, spread(): return lax.all_to_all(x, ROW_AXES, split_axis=0, concat_axis=0, tiled=True)  20.6 us
    ppermute x6, waiting for transfers between devices, shift(): return lax.ppermute(x, axis, [(i, (i + step) % 4) for i in range(4)])  16.6 us
    all_to_all x1, starting transfers between devices, spread(): return lax.all_to_all(x, ROW_AXES, split_axis=0, concat_axis=0, tiled=True)  14.2 us
    ppermute x1, waiting for transfers between devices, shards(): beside = lax.ppermute(own, x_axis, [(0, 1), (3, 2)])  9.23 us
    ppermute x6, starting transfers between devices, shift(): return lax.ppermute(x, axis, [(i, (i + step) % 4) for i in range(4)])  8.34 us
    ppermute x1, starting transfers between devices, shards(): beside = lax.ppermute(own, x_axis, [(0, 1), (3, 2)])  6.4 us
    ppermute x1, waiting for transfers between devices, shards(): passed = lax.ppermute(across, x_axis, [(1, 0), (2, 3)])  5 us
  transfers between devices with their start and end apart: 12, of which 6 were waited for; matrix products, arithmetic and copies ran while one was open for 1% of the time, Pallas kernels for 31%

profile of v4, /device:TPU:1, one launch (start us, length us, event | category | flops | bytes accessed | tf_op | source)
XLA Modules:
  0.0 163.2 jit_solution(9723412074972144899)
XLA Ops:
  6.5 4.1 %prepare.1 = (bf16[4,512,128]{2,1,0:T(8,128)(2,1)}, bf16[4,256,512]{2,1,0:T(8,128)(2,1)}) custom-call(bf16[4,512,128]{2,1,0:T(8,128)(2,1)} %pair.1, f32[1,128]{1,0:T(1,128)} %bitcast.6, bf16[4,512,256]{2,1,0:T(8,128)(2,1)} %bias.1), custom_call_target="tpu_custom_call" | custom-call | tf_op jit(solution)/shard_map/prepare/pallas_call | solution.py:40
  10.7 0.7 collective-permute-start.4
  11.4 6.4 %collective-permute-start = (bf16[4,512,128]{2,1,0:T(8,128)(2,1)}, bf16[4,512,128]{2,1,0:T(8,128)(2,1)S(1)}, u32[]{:S(2)}, u32[]{:S(2)}) collective-permute-start(bf16[4,512,128]{2,1,0:T(8,128)(2,1)} %get-tuple-element.7.xq), channel_id=1, source_target_pairs={{0,1},{17,16},{2,3},{19,18},{4,5},{21,20},{6,7},{23,22},{8,9},{25,... | collective-permute-start | bytes 1572872 | tf_op jit(solution)/shard_map/ppermute | solution.py:249
  17.8 1.3 collective-permute-start.5
  19.1 9.2 %collective-permute-done = bf16[4,512,128]{2,1,0:T(8,128)(2,1)S(1)} collective-permute-done((bf16[4,512,128]{2,1,0:T(8,128)(2,1)}, bf16[4,512,128]{2,1,0:T(8,128)(2,1)S(1)}, u32[]{:S(2)}, u32[]{:S(2)}) %collective-permute-start) | collective-permute-done | bytes 524320 | tf_op jit(solution)/shard_map/ppermute | solution.py:249
  28.3 0.7 collective-permute-start.6
  29.0 1.1 broadcast_select_fusion.2.xk0
  30.1 3.8 %collective-permute-start.1 = (bf16[4,512,128]{2,1,0:T(8,128)(2,1)S(1)}, bf16[4,512,128]{2,1,0:T(8,128)(2,1)S(1)}, u32[]{:S(2)}, u32[]{:S(2)}) collective-permute-start(bf16[4,512,128]{2,1,0:T(8,128)(2,1)S(1)} %broadcast_select_fusion.2.xk0), channel_id=1, source_target_pairs={{0,6},{2,0},{4,2},{6,4},{1,7},{3,1},{5,3},{7,5},{8,14},{10,8},{12,... | collective-permute-start | bytes 1572872 | tf_op jit(solution)/shard_map/ppermute | solution.py:237
  34.0 0.7 collective-permute-start.3
  34.7 5.0 %collective-permute-done.5 = bf16[4,512,128]{2,1,0:T(8,128)(2,1)S(1)} collective-permute-done((bf16[4,512,128]{2,1,0:T(8,128)(2,1)S(1)}, bf16[4,512,128]{2,1,0:T(8,128)(2,1)S(1)}, u32[]{:S(2)}, u32[]{:S(2)}) %collective-permute-start.5) | collective-permute-done | bytes 524320 | tf_op jit(solution)/shard_map/ppermute | solution.py:252
  39.7 1.0 broadcast_select_fusion
  40.6 3.8 %collective-permute-start.7 = (bf16[4,512,128]{2,1,0:T(8,128)(2,1)S(1)}, bf16[4,512,128]{2,1,0:T(8,128)(2,1)S(1)}, u32[]{:S(2)}, u32[]{:S(2)}) collective-permute-start(bf16[4,512,128]{2,1,0:T(8,128)(2,1)S(1)} %get-tuple-element.9.xk0), channel_id=1, source_target_pairs={{0,6},{2,0},{4,2},{6,4},{1,7},{3,1},{5,3},{7,5},{8,14},{10,8},{12,... | collective-permute-start | bytes 1572872 | tf_op jit(solution)/shard_map/ppermute | solution.py:237
  44.4 0.7 collective-permute-done.1.xk1
  45.1 1.7 %collective-permute-done.2.xk2 = bf16[4,512,128]{2,1,0:T(8,128)(2,1)S(1)} collective-permute-done((bf16[4,512,128]{2,1,0:T(8,128)(2,1)S(1)}, bf16[4,512,128]{2,1,0:T(8,128)(2,1)S(1)}, u32[]{:S(2)}, u32[]{:S(2)}) %collective-permute-start.2) | collective-permute-done | bytes 524320 | tf_op jit(solution)/shard_map/ppermute | solution.py:237
  46.8 0.8 copy-done.4
  47.6 14.2 %collective-permute-done.3.xk3 = bf16[4,512,128]{2,1,0:T(8,128)(2,1)} collective-permute-done((bf16[4,512,128]{2,1,0:T(8,128)(2,1)S(1)}, bf16[4,512,128]{2,1,0:T(8,128)(2,1)}, u32[]{:S(2)}, u32[]{:S(2)}) %collective-permute-start.3) | collective-permute-done | bytes 524320 | tf_op jit(solution)/shard_map/ppermute | solution.py:237
  61.8 2.4 %all-gather.3.cloned.1.call-done = bf16[32,256,512]{2,1,0:T(8,128)(2,1)} async-done(((bf16[4,256,512]{2,1,0:T(8,128)(2,1)}), bf16[32,256,512]{2,1,0:T(8,128)(2,1)}) %all-gather.3.cloned.1.call-update) | async-done | bytes 8388624 | tf_op jit(solution)/shard_map/all_gather | solution.py:257
  64.2 25.5 %attend.2 = bf16[16,5,32,128]{3,2,1,0:T(8,128)(2,1)} custom-call(bf16[4,512,128]{2,1,0:T(8,128)(2,1)} %get-tuple-element.7.xq, bf16[4,512,128]{2,1,0:T(8,128)(2,1)} %copy-done.1, bf16[4,512,128]{2,1,0:T(8,128)(2,1)} %copy-done.3, bf16[4,512,128]{2,1,0:T(8,128)(2,1)} %copy-done.4, bf16[4,512,128]{2,1,0:T(8,128)(2,1)} %collective-permute-done.3.xk3, ...), custom_call_target="tpu_custom_call" | custom-call | flops 8589934592 | bytes 16777216 | tf_op jit(solution)/shard_map/attend/pallas_call | solution.py:184
  89.7 14.2 %all-to-all-start = ((bf16[16,5,32,128]{3,2,1,0:T(8,128)(2,1)}), bf16[16,5,32,128]{3,2,1,0:T(8,128)(2,1)S(1)}, u32[]{:S(2)}, u32[]{:S(2)}) async-start(bf16[16,5,32,128]{3,2,1,0:T(8,128)(2,1)} %attend.2), calls=%async_computation | async-start | bytes 1310720 | tf_op jit(solution)/shard_map/all_to_all | solution.py:263
  104.0 0.7 copy-done.5
  105.1 25.5 %attend.3 = bf16[16,5,32,128]{3,2,1,0:T(8,128)(2,1)} custom-call(bf16[4,512,128]{2,1,0:T(8,128)(2,1)} %get-tuple-element.10.xq, bf16[4,512,128]{2,1,0:T(8,128)(2,1)} %copy-done.2, bf16[4,512,128]{2,1,0:T(8,128)(2,1)} %copy-done.5, bf16[4,512,128]{2,1,0:T(8,128)(2,1)} %copy-done.6, bf16[4,512,128]{2,1,0:T(8,128)(2,1)} %copy-done.7, bf16[128,512]{1,0:T(8,128)(2,1)} %w.4, ...), custom_call_target="tpu_custom_call" | custom-call | flops 8589934592 | bytes 16777216 | tf_op jit(solution)/shard_map/attend/pallas_call | solution.py:184
  130.6 20.6 %all_to_all.10.m2 = bf16[16,5,32,128]{3,2,1,0:T(8,128)(2,1)} all-to-all(bf16[16,5,32,128]{3,2,1,0:T(8,128)(2,1)} %attend.3), channel_id=1, replica_groups=mesh['y'=4,'xh'=2,'core'=2,'z'=4,'xl'=2] {'y','xh','core'}, dimensions={0} | all-to-all | bytes 1310720 | tf_op jit(solution)/shard_map/all_to_all | solution.py:263
  151.2 3.1 %merge.1 = bf16[16,4,32,128]{3,2,1,0:T(8,128)(2,1)} custom-call(bf16[16,5,32,128]{3,2,1,0:T(8,128)(2,1)} %copy-done, bf16[16,5,32,128]{3,2,1,0:T(8,128)(2,1)} %all_to_all.10.m2, bf16[128,128]{1,0:T(8,128)(2,1)} %w.5), custom_call_target="tpu_custom_call" | custom-call | tf_op jit(solution)/shard_map/merge/pallas_call | solution.py:228
  154.3 2.0 %copy.7 = bf16[32,64,128]{2,1,0:T(8,128)(2,1)} copy(bf16[32,64,128]{2,0,1:T(8,128)(2,1)} %bitcast.5) | data formatting | bytes 1048576 | tf_op jit(solution)/shard_map/reshape | solution.py:268
  (25 shorter events, 0.5 us)
Async XLA Ops:
  6.5 57.7 %all-gather.3.cloned.1.call-start = ((), (), s32[]{:S(2)}) async-start(), calls=%async_computation.2 | async-start | bytes 9437184 | tf_op jit(solution)/shard_map/all_gather | solution.py:257
  10.7 7.1 %collective-permute-start.4 = (bf16[4,512,128]{2,1,0:T(8,128)(2,1)}, bf16[4,512,128]{2,1,0:T(8,128)(2,1)S(1)}, u32[]{:S(2)}, u32[]{:S(2)}) collective-permute-start(bf16[4,512,128]{2,1,0:T(8,128)(2,1)} %get-tuple-element.7.xq), channel_id=1, source_target_pairs={{1,16},{16,1},{3,18},{18,3},{5,20},{20,5},{7,22},{22,7},{9,24},{24... | collective-permute-start | bytes 1572872 | tf_op jit(solution)/shard_map/ppermute | solution.py:250
  11.4 16.9 %collective-permute-start = (bf16[4,512,128]{2,1,0:T(8,128)(2,1)}, bf16[4,512,128]{2,1,0:T(8,128)(2,1)S(1)}, u32[]{:S(2)}, u32[]{:S(2)}) collective-permute-start(bf16[4,512,128]{2,1,0:T(8,128)(2,1)} %get-tuple-element.7.xq), channel_id=1, source_target_pairs={{0,1},{17,16},{2,3},{19,18},{4,5},{21,20},{6,7},{23,22},{8,9},{25,... | collective-permute-start | bytes 1572872 | tf_op jit(solution)/shard_map/ppermute | solution.py:249
  17.8 21.9 %collective-permute-start.5 = (bf16[4,512,128]{2,1,0:T(8,128)(2,1)S(1)}, bf16[4,512,128]{2,1,0:T(8,128)(2,1)S(1)}, u32[]{:S(2)}, u32[]{:S(2)}) collective-permute-start(bf16[4,512,128]{2,1,0:T(8,128)(2,1)S(1)} %collective-permute-done.4), channel_id=1, source_target_pairs={{1,0},{16,17},{3,2},{18,19},{5,4},{20,21},{7,6},{22,23},{9,8},{24,... | collective-permute-start | bytes 1572872 | tf_op jit(solution)/shard_map/ppermute | solution.py:252
  28.3 11.3 %collective-permute-start.6 = (bf16[4,512,128]{2,1,0:T(8,128)(2,1)S(1)}, bf16[4,512,128]{2,1,0:T(8,128)(2,1)S(1)}, u32[]{:S(2)}, u32[]{:S(2)}) collective-permute-start(bf16[4,512,128]{2,1,0:T(8,128)(2,1)S(1)} %collective-permute-done), channel_id=1, source_target_pairs={{1,16},{16,1},{3,18},{18,3},{5,20},{20,5},{7,22},{22,7},{9,24},{24... | collective-permute-start | bytes 1572872 | tf_op jit(solution)/shard_map/ppermute | solution.py:254
  30.1 34.1 %copy-start.1 = (bf16[4,512,128]{2,1,0:T(8,128)(2,1)}, bf16[4,512,128]{2,1,0:T(8,128)(2,1)S(1)}, u32[]{:S(2)}) copy-start(bf16[4,512,128]{2,1,0:T(8,128)(2,1)S(1)} %broadcast_select_fusion.2.xk0) | copy-start | bytes 1572868
  30.1 14.9 %collective-permute-start.1 = (bf16[4,512,128]{2,1,0:T(8,128)(2,1)S(1)}, bf16[4,512,128]{2,1,0:T(8,128)(2,1)S(1)}, u32[]{:S(2)}, u32[]{:S(2)}) collective-permute-start(bf16[4,512,128]{2,1,0:T(8,128)(2,1)S(1)} %broadcast_select_fusion.2.xk0), channel_id=1, source_target_pairs={{0,6},{2,0},{4,2},{6,4},{1,7},{3,1},{5,3},{7,5},{8,14},{10,8},{12,... | collective-permute-start | bytes 1572872 | tf_op jit(solution)/shard_map/ppermute | solution.py:237
  34.0 12.9 %collective-permute-start.2 = (bf16[4,512,128]{2,1,0:T(8,128)(2,1)S(1)}, bf16[4,512,128]{2,1,0:T(8,128)(2,1)S(1)}, u32[]{:S(2)}, u32[]{:S(2)}) collective-permute-start(bf16[4,512,128]{2,1,0:T(8,128)(2,1)S(1)} %broadcast_select_fusion.2.xk0), channel_id=1, source_target_pairs={{0,4},{2,6},{4,0},{6,2},{1,5},{3,7},{5,1},{7,3},{8,12},{10,14},{12... | collective-permute-start | bytes 1572872 | tf_op jit(solution)/shard_map/ppermute | solution.py:237
  34.0 27.9 %collective-permute-start.3 = (bf16[4,512,128]{2,1,0:T(8,128)(2,1)S(1)}, bf16[4,512,128]{2,1,0:T(8,128)(2,1)}, u32[]{:S(2)}, u32[]{:S(2)}) collective-permute-start(bf16[4,512,128]{2,1,0:T(8,128)(2,1)S(1)} %broadcast_select_fusion.2.xk0), channel_id=1, source_target_pairs={{0,2},{2,4},{4,6},{6,0},{1,3},{3,5},{5,7},{7,1},{8,10},{10,12},{12... | collective-permute-start | bytes 1572872 | tf_op jit(solution)/shard_map/ppermute | solution.py:237
  40.6 49.1 %copy-start.2 = (bf16[4,512,128]{2,1,0:T(8,128)(2,1)}, bf16[4,512,128]{2,1,0:T(8,128)(2,1)S(1)}, u32[]{:S(2)}) copy-start(bf16[4,512,128]{2,1,0:T(8,128)(2,1)S(1)} %get-tuple-element.9.xk0) | copy-start | bytes 1572868
  40.6 63.3 %collective-permute-start.7 = (bf16[4,512,128]{2,1,0:T(8,128)(2,1)S(1)}, bf16[4,512,128]{2,1,0:T(8,128)(2,1)S(1)}, u32[]{:S(2)}, u32[]{:S(2)}) collective-permute-start(bf16[4,512,128]{2,1,0:T(8,128)(2,1)S(1)} %get-tuple-element.9.xk0), channel_id=1, source_target_pairs={{0,6},{2,0},{4,2},{6,4},{1,7},{3,1},{5,3},{7,5},{8,14},{10,8},{12,... | collective-permute-start | bytes 1572872 | tf_op jit(solution)/shard_map/ppermute | solution.py:237
  44.4 59.5 %collective-permute-start.8 = (bf16[4,512,128]{2,1,0:T(8,128)(2,1)S(1)}, bf16[4,512,128]{2,1,0:T(8,128)(2,1)S(1)}, u32[]{:S(2)}, u32[]{:S(2)}) collective-permute-start(bf16[4,512,128]{2,1,0:T(8,128)(2,1)S(1)} %get-tuple-element.9.xk0), channel_id=1, source_target_pairs={{0,4},{2,6},{4,0},{6,2},{1,5},{3,7},{5,1},{7,3},{8,12},{10,14},{12... | collective-permute-start | bytes 1572872 | tf_op jit(solution)/shard_map/ppermute | solution.py:237
  45.0 1.8 %copy-start.3 = (bf16[4,512,128]{2,1,0:T(8,128)(2,1)}, bf16[4,512,128]{2,1,0:T(8,128)(2,1)S(1)}, u32[]{:S(2)}) copy-start(bf16[4,512,128]{2,1,0:T(8,128)(2,1)S(1)} %collective-permute-done.1.xk1) | copy-start | bytes 1572868
  45.0 58.9 %collective-permute-start.9 = (bf16[4,512,128]{2,1,0:T(8,128)(2,1)S(1)}, bf16[4,512,128]{2,1,0:T(8,128)(2,1)S(1)}, u32[]{:S(2)}, u32[]{:S(2)}) collective-permute-start(bf16[4,512,128]{2,1,0:T(8,128)(2,1)S(1)} %get-tuple-element.9.xk0), channel_id=1, source_target_pairs={{0,2},{2,4},{4,6},{6,0},{1,3},{3,5},{5,7},{7,1},{8,10},{10,12},{12... | collective-permute-start | bytes 1572872 | tf_op jit(solution)/shard_map/ppermute | solution.py:237
  46.8 0.8 copy-start.4
  89.7 40.9 %all-to-all-start = ((bf16[16,5,32,128]{3,2,1,0:T(8,128)(2,1)}), bf16[16,5,32,128]{3,2,1,0:T(8,128)(2,1)S(1)}, u32[]{:S(2)}, u32[]{:S(2)}) async-start(bf16[16,5,32,128]{3,2,1,0:T(8,128)(2,1)} %attend.2), calls=%async_computation | async-start | bytes 1310720 | tf_op jit(solution)/shard_map/all_to_all | solution.py:263
  103.9 0.8 copy-start.5
  103.9 0.9 copy-start.6
  103.9 1.1 copy-start.7
  130.6 20.6 %copy-start = (bf16[16,5,32,128]{3,2,1,0:T(8,128)(2,1)}, bf16[16,5,32,128]{3,2,1,0:T(8,128)(2,1)S(1)}, u32[]{:S(2)}) copy-start(bf16[16,5,32,128]{3,2,1,0:T(8,128)(2,1)S(1)} %all-to-all-done.m1) | copy-start | bytes 1966084
Sparse Core Ops, SparseCore 0:
  10.8 53.3 all-gather.2

commit v5 on v3

--- a/solution.py
+++ b/solution.py
@@ -1,3 +1,5 @@
+import functools
+
 import jax
 import jax.numpy as jnp
 from jax import lax
@@ -16,7 +18,7 @@
 LOW, HIGH = 1e-26, 1e30
 ROW_AXES = ("y", "xh", "core")
 COL_AXES = ("z", "xl")
-VMEM_LIMIT = 60 * 2**20
+VMEM_LIMIT = 32 * 2**20
 
 
 def matmul(a, b, first=1, second=0):
@@ -25,11 +27,14 @@
 
 
 def prepare_kernel(pair, gain, bias, normed, bias_t):
+    keys = bias.shape[2]
+    places = [lax.broadcasted_iota(jnp.int32, (keys, keys), axis) for axis in (0, 1)]
+    identity = (places[0] == places[1]).astype(F32).astype(BF16)
     values = pair[0].astype(F32)
     centered = values - jnp.mean(values, axis=-1, keepdims=True)
     variance = jnp.mean(centered * centered, axis=-1, keepdims=True)
     normed[0] = (centered * lax.rsqrt(variance + 1e-05) * gain[...]).astype(BF16)
-    bias_t[0] = bias[0].astype(F32).T.astype(BF16)
+    bias_t[0] = matmul(identity, bias[0], 1, 1).astype(BF16)
 
 
 def prepare(pair_block, norm_gain, head_bias):
@@ -55,7 +60,7 @@
 
 
 def attend_kernel(xq, xk0, xk1, xk2, xk3, w, *rest):
-    biases, out, scratch = rest[:8], rest[8], rest[9:]
+    biases, out, scratch = rest[:10], rest[-9], rest[-8:]
     bias_s, top_s, k_s, v_s, q_s, gate_s, stat_s, sems = scratch
     step = pl.program_id(0)
 
@@ -64,10 +69,12 @@
     def bias_copies():
         copies = []
         for n, ref in enumerate(biases):
-            slot = lax.rem(y - z + 4 + n // 2, 4)
+            place = (0, 1, 3, 2, 2)[n // 2]
+            heads = pl.ds((0, 0, 0, 0, 2)[n // 2], ref.shape[0])
+            slot = lax.rem(y - z + 4 + place, 4)
             half = core if n % 2 == 0 else 1 - core
             at = pl.ds(pl.multiple_of(half * 256, 256), 256)
-            copies.append(pltpu.make_async_copy(ref, bias_s.at[slot, :, at, :], sems.at[n]))
+            copies.append(pltpu.make_async_copy(ref, bias_s.at[slot, heads, at, :], sems.at[n]))
         return copies
 
     @pl.when(step == 0)
@@ -176,21 +183,24 @@
         out[:, ROWS] = stat_s[...].T.astype(BF16).reshape(16, SHARE, CHANNELS)
 
 
-def attend(x_q, x_ks, w_project, biases):
+def attend(x_q, x_ks, w_project, biases, message=()):
+    half = len(message)
+
     def rows(x):
         return pl.BlockSpec((STEP,) + x.shape[1:], lambda i: (i, 0, 0))
 
     scores = ROWS * HEADS * COLS * KEYS
-    message = (16, ROWS + 1, SHARE, CHANNELS)
+    block = (16, ROWS + 1, SHARE, CHANNELS)
     return pl.pallas_call(
         attend_kernel,
         grid=(ROWS // STEP,),
         in_specs=[rows(x_q)]
         + [rows(x) for x in x_ks]
         + [pl.BlockSpec((CHANNELS, 512), lambda i: (0, 0))]
-        + [pl.BlockSpec(memory_space=pl.ANY)] * 8,
-        out_specs=pl.BlockSpec(message, lambda i: (0, 0, 0, 0)),
-        out_shape=jax.ShapeDtypeStruct(message, BF16),
+        + [pl.BlockSpec(memory_space=pl.ANY)] * (len(biases) + len(message)),
+        out_specs=pl.BlockSpec(block, lambda i: (0, half, 0, 0)),
+        out_shape=jax.ShapeDtypeStruct((16, 2 * (ROWS + 1), SHARE, CHANNELS), BF16),
+        input_output_aliases={6 + len(biases): 0} if half else {},
         scratch_shapes=[
             pltpu.VMEM((4, HEADS, BLOCK, COLS), BF16),
             pltpu.VMEM((HEADS, COLS), F32),
@@ -199,80 +209,105 @@
             pltpu.VMEM((STEP, HEADS, CHANNELS, COLS), BF16),
             pltpu.VMEM((STEP, CHANNELS, COLS), F32),
             pltpu.VMEM((CHANNELS, COLS), F32),
-            pltpu.SemaphoreType.DMA((8,)),
+            pltpu.SemaphoreType.DMA((10,)),
         ],
         compiler_params=pltpu.CompilerParams(vmem_limit_bytes=VMEM_LIMIT),
         cost_estimate=pl.CostEstimate(
             flops=scores * 512, bytes_accessed=2**24, transcendentals=scores
         ),
         name="attend",
-    )(x_q, *x_ks, w_project, *biases)
-
-
-def merge_kernel(m1, m2, w, out):
+    )(x_q, *x_ks, w_project, *biases, *message)
+
+
+def merge_kernel(message, w, out):
     lane = lax.broadcasted_iota(jnp.int32, (CHANNELS, CHANNELS), 0)
     head = lax.broadcasted_iota(jnp.int32, (CHANNELS, CHANNELS), 1) // WIDTH
-    stat1 = m1[:, ROWS].reshape(16 * SHARE, CHANNELS)
-    stat2 = jnp.concatenate([m2[s ^ 2, ROWS] for s in range(16)], axis=0)
-    for i in range(ROWS):
-        part = lane - 32 * i
-        inside = (part >= 0) & (part < 12) & (lax.rem(part, 4) == head)
-        pick = inside.astype(F32).astype(BF16)
-        share = jax.nn.sigmoid(matmul(stat1, pick) - matmul(stat2, pick))
-        o1 = m1[:, i].reshape(16 * SHARE, CHANNELS).astype(F32)
-        o2 = jnp.concatenate([m2[s ^ 2, i] for s in range(16)], axis=0).astype(F32)
-        gated = (o2 + share * (o1 - o2)).astype(BF16)
-        out[:, i] = matmul(gated, w[...]).astype(BF16).reshape(16, SHARE, CHANNELS)
-
-
-def merge(m1, m2, w_out):
+    rows = []
+    for s in range(4):
+        other = s ^ 2
+        stat1, stat2 = message[s, ROWS], message[other, 2 * ROWS + 1]
+        for i in range(ROWS):
+            part = lane - 32 * i
+            inside = (part >= 0) & (part < 12) & (lax.rem(part, 4) == head)
+            pick = inside.astype(F32).astype(BF16)
+            share = jax.nn.sigmoid(matmul(stat1, pick) - matmul(stat2, pick))
+            o1 = message[s, i].astype(F32)
+            o2 = message[other, ROWS + 1 + i].astype(F32)
+            rows.append((o2 + share * (o1 - o2)).astype(BF16))
+    update = matmul(jnp.concatenate(rows, axis=0), w[...])
+    update = jnp.swapaxes(update.reshape(4 * ROWS, SHARE, CHANNELS), 0, 1)
+    out[...] = update.astype(BF16)
+
+
+def merge(message, w_out):
     return pl.pallas_call(
         merge_kernel,
-        out_shape=jax.ShapeDtypeStruct((16, ROWS, SHARE, CHANNELS), BF16),
+        grid=(4,),
+        in_specs=[
+            pl.BlockSpec((4,) + message.shape[1:], lambda y: (y, 0, 0, 0)),
+            pl.BlockSpec((CHANNELS, CHANNELS), lambda y: (0, 0)),
+        ],
+        out_specs=pl.BlockSpec((SHARE, 4 * ROWS, CHANNELS), lambda y: (0, y, 0)),
+        out_shape=jax.ShapeDtypeStruct((SHARE, 16 * ROWS, CHANNELS), BF16),
         compiler_params=pltpu.CompilerParams(vmem_limit_bytes=VMEM_LIMIT),
         name="merge",
-    )(m1, m2, w_out)
+    )(message, w_out)
+
+
+def choose(sources, picks, after=()):
+    def kernel(*refs):
+        ins, outs, sems = refs[: len(sources)], refs[len(sources) + len(after) : -1], refs[-1]
+        place = lax.axis_index("xh") * 2 + lax.axis_index("xl")
+        for act in ("start", "wait"):
+            for n, pick in enumerate(picks):
+                for source in sorted(set(pick)):
+                    here = [place == p for p in range(4) if pick[p] == source]
+                    copy = pltpu.make_async_copy(ins[source], outs[n], sems.at[n])
+                    pl.when(functools.reduce(jnp.logical_or, here))(getattr(copy, act))
+
+    anywhere = pl.BlockSpec(memory_space=pl.ANY)
+    shape = jax.ShapeDtypeStruct(sources[0].shape, sources[0].dtype)
+    return pl.pallas_call(
+        kernel,
+        in_specs=[anywhere] * (len(sources) + len(after)),
+        out_specs=[anywhere] * len(picks),
+        out_shape=[shape] * len(picks),
+        scratch_shapes=[pltpu.SemaphoreType.DMA((len(picks),))],
+        name="choose",
+    )(*sources, *after)
 
 
 def shift(x, axis, step):
     return lax.ppermute(x, axis, [(i, (i + step) % 4) for i in range(4)])
 
 
-def gather_direct(x, axis):
-    return x, shift(x, axis, -1), shift(x, axis, 2), shift(x, axis, 1)
+def swap(x):
+    return lax.ppermute(x, "core", [(0, 1), (1, 0)])
 
 
 def gather_bias(block):
     behind, ahead = shift(block, "y", 1), shift(block, "y", -1)
     far = [shift(behind[:2], "y", 1), shift(ahead[2:], "y", -1)]
-    blocks = [block, ahead, jnp.concatenate(far, axis=0), behind]
-    return [side for b in blocks for side in (b, lax.ppermute(b, "core", [(0, 1), (1, 0)]))]
+    return [side for b in (block, ahead, behind, *far) for side in (b, swap(b))]
 
 
 def shards(pair_block, norm_gain, w_project, w_out, head_bias):
-    xh, xl = lax.axis_index("xh"), lax.axis_index("xl")
     own, bias_t = prepare(pair_block, norm_gain, head_bias)
+    biases = gather_bias(bias_t)
 
     x_axis = ("xh", "xl")
-    beside = lax.ppermute(own, x_axis, [(0, 1), (3, 2)])
-    across = lax.ppermute(own, x_axis, [(1, 2), (2, 1)])
-    first_k = jnp.where(xl == xh, own, beside)
-    passed = lax.ppermute(across, x_axis, [(1, 0), (2, 3)])
-    second_k = jnp.where(xl == xh, passed, across)
-    partner = lax.ppermute(beside, x_axis, [(1, 2), (2, 1)])
-    second_q = jnp.where(xl == xh, passed, partner)
-
-    biases = gather_bias(bias_t)
-    first_ks = gather_direct(first_k, "z")
-    second_ks = gather_direct(second_k, "z")
-
-    def spread(x):
-        return lax.all_to_all(x, ROW_AXES, split_axis=0, concat_axis=0, tiled=True)
-
-    m1 = spread(attend(own, first_ks, w_project, biases))
-    m2 = spread(attend(second_q, second_ks, w_project, biases))
-    update = merge(m1, m2, w_out)
-    return jnp.transpose(update, (2, 0, 1, 3)).reshape(SHARE, 16 * ROWS, CHANNELS)
+    behind, ahead = shift(own, x_axis, 1), shift(own, x_axis, -1)
+    (first_k,) = choose([own, behind, ahead], [[0, 1, 2, 0]], [biases[1]])
+    first_near = shift(first_k, "z", -1), shift(first_k, "z", 1)
+    opposite = shift(behind, x_axis, 1)
+    second_k, first_again = choose([opposite, behind, ahead, first_k], [[0, 2, 1, 0], [3] * 4])
+    first_ks = first_k, first_near[0], shift(first_again, "z", 2), first_near[1]
+    second_ks = second_k, shift(second_k, "z", -1), shift(second_k, "z", 2), shift(second_k, "z", 1)
+
+    message = attend(own, first_ks, w_project, biases)
+    message = attend(opposite, second_ks, w_project, biases, (message,))
+    message = lax.all_to_all(message, ROW_AXES, split_axis=0, concat_axis=0, tiled=True)
+    return merge(message, w_out)
 
 
 def solution(mesh):

time: 167 us -> 194 us (1.16)
  Pallas kernels: 58.3 us -> 99.2 us
  starting transfers between devices: 39.2 us -> 23.7 us
  blocking collectives: 20.6 us -> 26.5 us
  local copies, waits for them, and re-layouts: 7.21 us -> 4.97 us
    pallas_call x1 -> x3, Pallas kernels: 3.11 us -> 52.5 us  [the longest x2 49.9 us: choose(): pl.pallas_call(kernel, in_specs=[anywhere] * (len(sources) + len(after)),...]
    ppermute x8 -> x5, starting transfers between devices: 21.2 us -> 6.76 us  [swap(): return lax.ppermute(x, 'core', [(0, 1), (1, 0)])]
    pallas_call x2, Pallas kernels: 51 us -> 42.5 us  [attend(): pl.pallas_call(attend_kernel, grid=(ROWS // STEP,), in_specs=[rows(x_q)]...]
    all_to_all x1, blocking collectives: 20.6 us -> 26.5 us  [shards(): lax.all_to_all(message, ROW_AXES, split_axis=0, concat_axis=0, tiled=True)]
    all_to_all x1 -> x0, starting transfers between devices: 5.62 us -> none  [spread(): return lax.all_to_all(x, ROW_AXES, split_axis=0, concat_axis=0, tiled=True)]
    ppermute x10 -> x13, starting transfers between devices: 12.4 us -> 17 us  [shift(): return lax.ppermute(x, axis, [(i, (i + step) % 4) for i in range(4)])]
    reshape x1 -> x0, local copies, waits for them, and re-layouts: 2.04 us -> none  [shards(): jnp.transpose(update, (2, 0, 1, 3)).reshape(SHARE, 16 * ROWS, CHANNELS)]
    ppermute x10 -> x13, waiting for transfers between devices: 39.5 us -> 39.3 us  [shift(): return lax.ppermute(x, axis, [(i, (i + step) % 4) for i in range(4)])]
  transfers between devices with their start and end apart: 19 -> 18, of which waited for: 4 -> 6; matrix products, arithmetic and copies ran while one was open for 2% -> 1% of each run, Pallas kernels for 31% -> 37%
where the time goes in v5:
time: 194 us
  Pallas kernels  99.2 us (51%)
  waiting for transfers between devices  39.3 us (20%)
  blocking collectives  26.5 us (14%)
  starting transfers between devices  23.7 us (12%)
  local copies, waits for them, and re-layouts  4.97 us (3%)
    pallas_call x2, Pallas kernels, choose(): pl.pallas_call(kernel, in_specs=[anywhere] * (len(sources) + len(after)),...  49.9 us
    pallas_call x2, Pallas kernels, attend(): pl.pallas_call(attend_kernel, grid=(ROWS // STEP,), in_specs=[rows(x_q)]...  42.5 us
    ppermute x13, waiting for transfers between devices, shift(): return lax.ppermute(x, axis, [(i, (i + step) % 4) for i in range(4)])  39.3 us
    all_to_all x1, blocking collectives, shards(): lax.all_to_all(message, ROW_AXES, split_axis=0, concat_axis=0, tiled=True)  26.5 us
    ppermute x13, starting transfers between devices, shift(): return lax.ppermute(x, axis, [(i, (i + step) % 4) for i in range(4)])  17 us
    ppermute x5, starting transfers between devices, swap(): return lax.ppermute(x, 'core', [(0, 1), (1, 0)])  6.76 us
    pallas_call x1, Pallas kernels, prepare(): pl.pallas_call(prepare_kernel, grid=(ROWS,), in_specs=[whole(COLS, CHANNE...  4.11 us
  transfers between devices with their start and end apart: 18, of which 6 were waited for; matrix products, arithmetic and copies ran while one was open for 1% of the time, Pallas kernels for 37%

profile of v5, /device:TPU:1, one launch (start us, length us, event | category | flops | bytes accessed | tf_op | source)
XLA Modules:
  0.0 193.8 jit_solution(9843083481956607674)
XLA Ops:
  0.0 4.1 %prepare.1 = (bf16[4,512,128]{2,1,0:T(8,128)(2,1)}, bf16[4,256,512]{2,1,0:T(8,128)(2,1)}) custom-call(bf16[4,512,128]{2,1,0:T(8,128)(2,1)} %pair.1, f32[1,128]{1,0:T(1,128)} %bitcast.1, bf16[4,512,256]{2,1,0:T(8,128)(2,1)} %bias.1), custom_call_target="tpu_custom_call" | custom-call | tf_op jit(solution)/shard_map/prepare/pallas_call | solution.py:45
  4.1 1.4 collective-permute-start.3
  5.5 1.3 collective-permute-start
  6.8 1.3 collective-permute-start.9
  8.1 1.5 collective-permute-start.2
  9.6 1.4 collective-permute-start.7
  11.0 9.5 %collective-permute-done.refs_1_ = bf16[4,512,128]{2,1,0:T(8,128)(2,1)} collective-permute-done((bf16[4,512,128]{2,1,0:T(8,128)(2,1)}, bf16[4,512,128]{2,1,0:T(8,128)(2,1)}, u32[]{:S(2)}, u32[]{:S(2)}) %collective-permute-start) | collective-permute-done | bytes 524320 | tf_op jit(solution)/shard_map/ppermute | solution.py:281
  23.1 17.0 %choose.2.refs_3_.xk0 = bf16[4,512,128]{2,1,0:T(8,128)(2,1)} custom-call(bf16[4,512,128]{2,1,0:T(8,128)(2,1)} %get-tuple-element.9.refs_0_.xq, bf16[4,512,128]{2,1,0:T(8,128)(2,1)} %collective-permute-done.refs_1_, bf16[4,512,128]{2,1,0:T(8,128)(2,1)} %copy-done.10, bf16[4,256,512]{2,1,0:T(8,128)(2,1)} %copy-done.1), custom_call_target="tpu_custom_call" | custom-call | tf_op jit(solution)/shard_map/choose/pallas_call | solution.py:270
  41.0 32.9 %choose.3 = (bf16[4,512,128]{2,1,0:T(8,128)(2,1)}, bf16[4,512,128]{2,1,0:T(8,128)(2,1)}) custom-call(bf16[4,512,128]{2,1,0:T(8,128)(2,1)} %copy-done.4, bf16[4,512,128]{2,1,0:T(8,128)(2,1)} %collective-permute-done.refs_1_, bf16[4,512,128]{2,1,0:T(8,128)(2,1)} %copy-done.10, bf16[4,512,128]{2,1,0:T(8,128)(2,1)} %choose.2.refs_3_.xk0), custom_call_target="tpu_custom_call" | custom-call | tf_op jit(solution)/shard_map/choose/pallas_call | solution.py:270
  73.9 3.7 %collective-permute-start.16 = (bf16[4,512,128]{2,1,0:T(8,128)(2,1)}, bf16[4,512,128]{2,1,0:T(8,128)(2,1)S(1)}, u32[]{:S(2)}, u32[]{:S(2)}) collective-permute-start(bf16[4,512,128]{2,1,0:T(8,128)(2,1)} %get-tuple-element.12), channel_id=1, source_target_pairs={{0,4},{2,6},{4,0},{6,2},{1,5},{3,7},{5,1},{7,3},{8,12},{10,14},{12... | collective-permute-start | bytes 1572872 | tf_op jit(solution)/shard_map/ppermute | solution.py:281
  78.0 1.4 collective-permute-start.11
  80.5 1.4 collective-permute-start.13
  81.9 2.5 %collective-permute-start.10 = (bf16[4,256,512]{2,1,0:T(8,128)(2,1)S(1)}, bf16[4,256,512]{2,1,0:T(8,128)(2,1)S(1)}, u32[]{:S(2)}, u32[]{:S(2)}) collective-permute-start(bf16[4,256,512]{2,1,0:T(8,128)(2,1)S(1)} %collective-permute-done.9.rest_4_), channel_id=1, source_target_pairs={{0,8},{8,0},{1,9},{9,1},{2,10},{10,2},{3,11},{11,3},{4,12},{12,4},... | collective-permute-start | bytes 3145736 | tf_op jit(solution)/shard_map/ppermute | solution.py:285
  84.4 4.2 %collective-permute-done.16.xk2 = bf16[4,512,128]{2,1,0:T(8,128)(2,1)S(1)} collective-permute-done((bf16[4,512,128]{2,1,0:T(8,128)(2,1)}, bf16[4,512,128]{2,1,0:T(8,128)(2,1)S(1)}, u32[]{:S(2)}, u32[]{:S(2)}) %collective-permute-start.16) | collective-permute-done | bytes 524320 | tf_op jit(solution)/shard_map/ppermute | solution.py:281
  88.6 2.0 %collective-permute-start.8 = (bf16[4,256,512]{2,1,0:T(8,128)(2,1)}, bf16[4,256,512]{2,1,0:T(8,128)(2,1)S(1)}, u32[]{:S(2)}, u32[]{:S(2)}) collective-permute-start(bf16[4,256,512]{2,1,0:T(8,128)(2,1)} %collective-permute-done.7.rest_2_), channel_id=1, source_target_pairs={{0,8},{8,0},{1,9},{9,1},{2,10},{10,2},{3,11},{11,3},{4,12},{12,4},... | collective-permute-start | bytes 3145736 | tf_op jit(solution)/shard_map/ppermute | solution.py:285
  90.6 10.0 %collective-permute-done.15.xk1 = bf16[4,512,128]{2,1,0:T(8,128)(2,1)S(1)} collective-permute-done((bf16[4,512,128]{2,1,0:T(8,128)(2,1)S(1)}, bf16[4,512,128]{2,1,0:T(8,128)(2,1)S(1)}, u32[]{:S(2)}, u32[]{:S(2)}) %collective-permute-start.15) | collective-permute-done | bytes 524320 | tf_op jit(solution)/shard_map/ppermute | solution.py:281
  100.6 1.7 collective-permute-start.17
  103.3 11.5 %collective-permute-done.17.xk3 = bf16[4,512,128]{2,1,0:T(8,128)(2,1)S(1)} collective-permute-done((bf16[4,512,128]{2,1,0:T(8,128)(2,1)S(1)}, bf16[4,512,128]{2,1,0:T(8,128)(2,1)S(1)}, u32[]{:S(2)}, u32[]{:S(2)}) %collective-permute-start.17) | collective-permute-done | bytes 524320 | tf_op jit(solution)/shard_map/ppermute | solution.py:281
  114.7 2.1 %collective-permute-start.4 = (bf16[4,512,128]{2,1,0:T(8,128)(2,1)S(1)}, bf16[4,512,128]{2,1,0:T(8,128)(2,1)S(1)}, u32[]{:S(2)}, u32[]{:S(2)}) collective-permute-start(bf16[4,512,128]{2,1,0:T(8,128)(2,1)S(1)} %copy-done.8), channel_id=1, source_target_pairs={{0,6},{2,0},{4,2},{6,4},{1,7},{3,1},{5,3},{7,5},{8,14},{10,8},{12,... | collective-permute-start | bytes 1572872 | tf_op jit(solution)/shard_map/ppermute | solution.py:281
  118.7 21.3 %attend.2.rest_10_ = bf16[16,10,32,128]{3,2,1,0:T(8,128)(2,1)S(1)} custom-call(bf16[4,512,128]{2,1,0:T(8,128)(2,1)S(1)} %copy-done.3, bf16[4,512,128]{2,1,0:T(8,128)(2,1)S(1)} %copy-done, bf16[4,512,128]{2,1,0:T(8,128)(2,1)S(1)} %collective-permute-done.15.xk1, bf16[4,512,128]{2,1,0:T(8,128)(2,1)S(1)} %collective-permute-done.16.xk2, ...), custom_call_target="tpu_custom_call" | custom-call | flops 8589934592 | bytes 16777216 | tf_op jit(solution)/shard_map/attend/pallas_call | solution.py:194
  140.0 3.4 %collective-permute-done.6.xk3 = bf16[4,512,128]{2,1,0:T(8,128)(2,1)S(1)} collective-permute-done((bf16[4,512,128]{2,1,0:T(8,128)(2,1)S(1)}, bf16[4,512,128]{2,1,0:T(8,128)(2,1)S(1)}, u32[]{:S(2)}, u32[]{:S(2)}) %collective-permute-start.6) | collective-permute-done | bytes 524320 | tf_op jit(solution)/shard_map/ppermute | solution.py:281
  143.4 21.3 %attend.3 = bf16[16,10,32,128]{3,2,1,0:T(8,128)(2,1)S(1)} custom-call(bf16[4,512,128]{2,1,0:T(8,128)(2,1)S(1)} %copy-done.5, bf16[4,512,128]{2,1,0:T(8,128)(2,1)S(1)} %copy-done.8, bf16[4,512,128]{2,1,0:T(8,128)(2,1)S(1)} %collective-permute-done.4.xk1, bf16[4,512,128]{2,1,0:T(8,128)(2,1)S(1)} %collective-permute-done.5.xk2, ...), custom_call_target="tpu_custom_call", output_to_operand_aliasing={{}: (16, {})} | custom-call | flops 8589934592 | bytes 16777216 | tf_op jit(solution)/shard_map/attend/pallas_call | solution.py:194
  164.7 26.5 %all_to_all.5.message = bf16[16,10,32,128]{3,2,1,0:T(8,128)(2,1)S(1)} all-to-all(bf16[16,10,32,128]{3,2,1,0:T(8,128)(2,1)S(1)} %attend.3), channel_id=1, replica_groups=mesh['y'=4,'xh'=2,'core'=2,'z'=4,'xl'=2] {'y','xh','core'}, dimensions={0} | all-to-all | bytes 2621440 | tf_op jit(solution)/shard_map/all_to_all | solution.py:309
  191.2 2.6 %merge.1 = bf16[32,64,128]{2,1,0:T(8,128)(2,1)} custom-call(bf16[16,10,32,128]{3,2,1,0:T(8,128)(2,1)S(1)} %all_to_all.5.message, bf16[128,128]{1,0:T(8,128)(2,1)S(1)} %copy-done.6), custom_call_target="tpu_custom_call" | custom-call | tf_op jit(solution)/shard_map/merge/pallas_call | solution.py:243
  (43 shorter events, 7.7 us)
Async XLA Ops:
  4.1 17.2 %collective-permute-start.3 = (bf16[4,256,512]{2,1,0:T(8,128)(2,1)}, bf16[4,256,512]{2,1,0:T(8,128)(2,1)S(1)}, u32[]{:S(2)}, u32[]{:S(2)}) collective-permute-start(bf16[4,256,512]{2,1,0:T(8,128)(2,1)} %get-tuple-element.10.rest_0_), channel_id=1, source_target_pairs={{0,8},{8,0},{1,9},{9,1},{2,10},{10,2},{3,11},{11,3},{4,12},{12,4},... | collective-permute-start | bytes 3145736 | tf_op jit(solution)/shard_map/ppermute | solution.py:285
  5.5 15.0 %collective-permute-start = (bf16[4,512,128]{2,1,0:T(8,128)(2,1)}, bf16[4,512,128]{2,1,0:T(8,128)(2,1)}, u32[]{:S(2)}, u32[]{:S(2)}) collective-permute-start(bf16[4,512,128]{2,1,0:T(8,128)(2,1)} %get-tuple-element.9.refs_0_.xq), channel_id=1, source_target_pairs={{0,1},{1,16},{16,17},{17,0},{2,3},{3,18},{18,19},{19,2},{4,5},{5,2... | collective-permute-start | bytes 1572872 | tf_op jit(solution)/shard_map/ppermute | solution.py:281
  6.8 71.2 %collective-permute-start.9 = (bf16[4,256,512]{2,1,0:T(8,128)(2,1)}, bf16[4,256,512]{2,1,0:T(8,128)(2,1)S(1)}, u32[]{:S(2)}, u32[]{:S(2)}) collective-permute-start(bf16[4,256,512]{2,1,0:T(8,128)(2,1)} %get-tuple-element.10.rest_0_), channel_id=1, source_target_pairs={{0,32},{32,64},{64,96},{96,0},{1,33},{33,65},{65,97},{97,1},{2,34}... | collective-permute-start | bytes 3145736 | tf_op jit(solution)/shard_map/ppermute | solution.py:281
  8.1 13.2 %collective-permute-start.2 = (bf16[4,512,128]{2,1,0:T(8,128)(2,1)}, bf16[4,512,128]{2,1,0:T(8,128)(2,1)S(1)}, u32[]{:S(2)}, u32[]{:S(2)}) collective-permute-start(bf16[4,512,128]{2,1,0:T(8,128)(2,1)} %get-tuple-element.9.refs_0_.xq), channel_id=1, source_target_pairs={{0,17},{1,0},{16,1},{17,16},{2,19},{3,2},{18,3},{19,18},{4,21},{5,... | collective-permute-start | bytes 1572872 | tf_op jit(solution)/shard_map/ppermute | solution.py:281
  9.6 69.8 %collective-permute-start.7 = (bf16[4,256,512]{2,1,0:T(8,128)(2,1)}, bf16[4,256,512]{2,1,0:T(8,128)(2,1)}, u32[]{:S(2)}, u32[]{:S(2)}) collective-permute-start(bf16[4,256,512]{2,1,0:T(8,128)(2,1)} %get-tuple-element.10.rest_0_), channel_id=1, source_target_pairs={{0,96},{32,0},{64,32},{96,64},{1,97},{33,1},{65,33},{97,65},{2,98}... | collective-permute-start | bytes 3145736 | tf_op jit(solution)/shard_map/ppermute | solution.py:281
  20.6 19.6 %collective-permute-start.1 = (bf16[4,512,128]{2,1,0:T(8,128)(2,1)}, bf16[4,512,128]{2,1,0:T(8,128)(2,1)S(1)}, u32[]{:S(2)}, u32[]{:S(2)}) collective-permute-start(bf16[4,512,128]{2,1,0:T(8,128)(2,1)} %collective-permute-done.refs_1_), channel_id=1, source_target_pairs={{0,1},{1,16},{16,17},{17,0},{2,3},{3,18},{18,19},{19,2},{4,5},{5,2... | collective-permute-start | bytes 1572872 | tf_op jit(solution)/shard_map/ppermute | solution.py:281
  40.1 37.4 %copy-start = (bf16[4,512,128]{2,1,0:T(8,128)(2,1)S(1)}, bf16[4,512,128]{2,1,0:T(8,128)(2,1)}, u32[]{:S(2)}) copy-start(bf16[4,512,128]{2,1,0:T(8,128)(2,1)} %choose.2.refs_3_.xk0) | copy-start | bytes 1572868
  41.0 76.5 %copy-start.9 = (bf16[128,512]{1,0:T(8,128)(2,1)S(1)}, bf16[128,512]{1,0:T(8,128)(2,1)}, u32[]{:S(2)}) copy-start(bf16[128,512]{1,0:T(8,128)(2,1)} %w.4) | copy-start | bytes 393220
  73.8 40.9 %copy-start.8 = (bf16[4,512,128]{2,1,0:T(8,128)(2,1)S(1)}, bf16[4,512,128]{2,1,0:T(8,128)(2,1)}, u32[]{:S(2)}) copy-start(bf16[4,512,128]{2,1,0:T(8,128)(2,1)} %get-tuple-element.11.xk0) | copy-start | bytes 1572868
  73.9 43.6 %copy-start.2 = (bf16[4,256,512]{2,1,0:T(8,128)(2,1)S(1)}, bf16[4,256,512]{2,1,0:T(8,128)(2,1)}, u32[]{:S(2)}) copy-start(bf16[4,256,512]{2,1,0:T(8,128)(2,1)} %copy-done.1) | copy-start | bytes 3145732
  73.9 43.6 %copy-start.3 = (bf16[4,512,128]{2,1,0:T(8,128)(2,1)S(1)}, bf16[4,512,128]{2,1,0:T(8,128)(2,1)}, u32[]{:S(2)}) copy-start(bf16[4,512,128]{2,1,0:T(8,128)(2,1)} %get-tuple-element.9.refs_0_.xq) | copy-start | bytes 1572868
  73.9 14.8 %collective-permute-start.16 = (bf16[4,512,128]{2,1,0:T(8,128)(2,1)}, bf16[4,512,128]{2,1,0:T(8,128)(2,1)S(1)}, u32[]{:S(2)}, u32[]{:S(2)}) collective-permute-start(bf16[4,512,128]{2,1,0:T(8,128)(2,1)} %get-tuple-element.12), channel_id=1, source_target_pairs={{0,4},{2,6},{4,0},{6,2},{1,5},{3,7},{5,1},{7,3},{8,12},{10,14},{12... | collective-permute-start | bytes 1572872 | tf_op jit(solution)/shard_map/ppermute | solution.py:281
  77.6 23.1 %collective-permute-start.15 = (bf16[4,512,128]{2,1,0:T(8,128)(2,1)S(1)}, bf16[4,512,128]{2,1,0:T(8,128)(2,1)S(1)}, u32[]{:S(2)}, u32[]{:S(2)}) collective-permute-start(bf16[4,512,128]{2,1,0:T(8,128)(2,1)S(1)} %copy-done), channel_id=1, source_target_pairs={{0,6},{2,0},{4,2},{6,4},{1,7},{3,1},{5,3},{7,5},{8,14},{10,8},{12,... | collective-permute-start | bytes 1572872 | tf_op jit(solution)/shard_map/ppermute | solution.py:281
  78.0 24.4 %collective-permute-start.11 = (bf16[2,256,512]{2,1,0:T(8,128)(2,1)S(1)}, bf16[2,256,512]{2,1,0:T(8,128)(2,1)S(1)}, u32[]{:S(2)}, u32[]{:S(2)}) collective-permute-start(bf16[2,256,512]{2,1,0:T(8,128)(2,1)S(1)} %slice.8), channel_id=1, source_target_pairs={{0,32},{32,64},{64,96},{96,0},{1,33},{33,65},{65,97},{97,1},{2,34}... | collective-permute-start | bytes 1572872 | tf_op jit(solution)/shard_map/ppermute | solution.py:281
  80.5 22.7 %collective-permute-start.13 = (bf16[2,256,512]{2,1,0:T(8,128)(2,1)S(1)}, bf16[2,256,512]{2,1,0:T(8,128)(2,1)S(1)}, u32[]{:S(2)}, u32[]{:S(2)}) collective-permute-start(bf16[2,256,512]{2,1,0:T(8,128)(2,1)S(1)} %slice.9), channel_id=1, source_target_pairs={{0,96},{32,0},{64,32},{96,64},{1,97},{33,1},{65,33},{97,65},{2,98}... | collective-permute-start | bytes 1572872 | tf_op jit(solution)/shard_map/ppermute | solution.py:281
  81.9 35.5 %collective-permute-start.10 = (bf16[4,256,512]{2,1,0:T(8,128)(2,1)S(1)}, bf16[4,256,512]{2,1,0:T(8,128)(2,1)S(1)}, u32[]{:S(2)}, u32[]{:S(2)}) collective-permute-start(bf16[4,256,512]{2,1,0:T(8,128)(2,1)S(1)} %collective-permute-done.9.rest_4_), channel_id=1, source_target_pairs={{0,8},{8,0},{1,9},{9,1},{2,10},{10,2},{3,11},{11,3},{4,12},{12,4},... | collective-permute-start | bytes 3145736 | tf_op jit(solution)/shard_map/ppermute | solution.py:285
  88.6 28.8 %collective-permute-start.8 = (bf16[4,256,512]{2,1,0:T(8,128)(2,1)}, bf16[4,256,512]{2,1,0:T(8,128)(2,1)S(1)}, u32[]{:S(2)}, u32[]{:S(2)}) collective-permute-start(bf16[4,256,512]{2,1,0:T(8,128)(2,1)} %collective-permute-done.7.rest_2_), channel_id=1, source_target_pairs={{0,8},{8,0},{1,9},{9,1},{2,10},{10,2},{3,11},{11,3},{4,12},{12,4},... | collective-permute-start | bytes 3145736 | tf_op jit(solution)/shard_map/ppermute | solution.py:285
  100.6 14.1 %collective-permute-start.17 = (bf16[4,512,128]{2,1,0:T(8,128)(2,1)S(1)}, bf16[4,512,128]{2,1,0:T(8,128)(2,1)S(1)}, u32[]{:S(2)}, u32[]{:S(2)}) collective-permute-start(bf16[4,512,128]{2,1,0:T(8,128)(2,1)S(1)} %copy-done), channel_id=1, source_target_pairs={{0,2},{2,4},{4,6},{6,0},{1,3},{3,5},{5,7},{7,1},{8,10},{10,12},{12... | collective-permute-start | bytes 1572872 | tf_op jit(solution)/shard_map/ppermute | solution.py:281
  102.4 14.4 %collective-permute-start.12 = (bf16[2,256,512]{2,1,0:T(8,128)(2,1)S(1)}, bf16[2,256,512]{2,1,0:T(8,128)(2,1)S(1)}, u32[]{:S(2)}, u32[]{:S(2)}) collective-permute-start(bf16[2,256,512]{2,1,0:T(8,128)(2,1)S(1)} %collective-permute-done.11.rest_6_), channel_id=1, source_target_pairs={{0,8},{8,0},{1,9},{9,1},{2,10},{10,2},{3,11},{11,3},{4,12},{12,4},... | collective-permute-start | bytes 1572872 | tf_op jit(solution)/shard_map/ppermute | solution.py:285
  103.2 14.0 %collective-permute-start.14 = (bf16[2,256,512]{2,1,0:T(8,128)(2,1)S(1)}, bf16[2,256,512]{2,1,0:T(8,128)(2,1)S(1)}, u32[]{:S(2)}, u32[]{:S(2)}) collective-permute-start(bf16[2,256,512]{2,1,0:T(8,128)(2,1)S(1)} %collective-permute-done.13.rest_8_), channel_id=1, source_target_pairs={{0,8},{8,0},{1,9},{9,1},{2,10},{10,2},{3,11},{11,3},{4,12},{12,4},... | collective-permute-start | bytes 1572872 | tf_op jit(solution)/shard_map/ppermute | solution.py:285
  114.7 28.7 %copy-start.5 = (bf16[4,512,128]{2,1,0:T(8,128)(2,1)S(1)}, bf16[4,512,128]{2,1,0:T(8,128)(2,1)}, u32[]{:S(2)}) copy-start(bf16[4,512,128]{2,1,0:T(8,128)(2,1)} %copy-done.4) | copy-start | bytes 1572868
  114.7 25.3 %collective-permute-start.4 = (bf16[4,512,128]{2,1,0:T(8,128)(2,1)S(1)}, bf16[4,512,128]{2,1,0:T(8,128)(2,1)S(1)}, u32[]{:S(2)}, u32[]{:S(2)}) collective-permute-start(bf16[4,512,128]{2,1,0:T(8,128)(2,1)S(1)} %copy-done.8), channel_id=1, source_target_pairs={{0,6},{2,0},{4,2},{6,4},{1,7},{3,1},{5,3},{7,5},{8,14},{10,8},{12,... | collective-permute-start | bytes 1572872 | tf_op jit(solution)/shard_map/ppermute | solution.py:281
  116.8 23.2 %collective-permute-start.5 = (bf16[4,512,128]{2,1,0:T(8,128)(2,1)S(1)}, bf16[4,512,128]{2,1,0:T(8,128)(2,1)S(1)}, u32[]{:S(2)}, u32[]{:S(2)}) collective-permute-start(bf16[4,512,128]{2,1,0:T(8,128)(2,1)S(1)} %copy-done.8), channel_id=1, source_target_pairs={{0,4},{2,6},{4,0},{6,2},{1,5},{3,7},{5,1},{7,3},{8,12},{10,14},{12... | collective-permute-start | bytes 1572872 | tf_op jit(solution)/shard_map/ppermute | solution.py:281
  117.2 26.2 %collective-permute-start.6 = (bf16[4,512,128]{2,1,0:T(8,128)(2,1)S(1)}, bf16[4,512,128]{2,1,0:T(8,128)(2,1)S(1)}, u32[]{:S(2)}, u32[]{:S(2)}) collective-permute-start(bf16[4,512,128]{2,1,0:T(8,128)(2,1)S(1)} %copy-done.8), channel_id=1, source_target_pairs={{0,2},{2,4},{4,6},{6,0},{1,3},{3,5},{5,7},{7,1},{8,10},{10,12},{12... | collective-permute-start | bytes 1572872 | tf_op jit(solution)/shard_map/ppermute | solution.py:281
  (5 other events, 30.4 us)

commit v6 on v5

--- a/solution.py
+++ b/solution.py
@@ -1,5 +1,3 @@
-import functools
-
 import jax
 import jax.numpy as jnp
 from jax import lax
@@ -254,27 +252,10 @@
     )(message, w_out)
 
 
-def choose(sources, picks, after=()):
-    def kernel(*refs):
-        ins, outs, sems = refs[: len(sources)], refs[len(sources) + len(after) : -1], refs[-1]
-        place = lax.axis_index("xh") * 2 + lax.axis_index("xl")
-        for act in ("start", "wait"):
-            for n, pick in enumerate(picks):
-                for source in sorted(set(pick)):
-                    here = [place == p for p in range(4) if pick[p] == source]
-                    copy = pltpu.make_async_copy(ins[source], outs[n], sems.at[n])
-                    pl.when(functools.reduce(jnp.logical_or, here))(getattr(copy, act))
-
-    anywhere = pl.BlockSpec(memory_space=pl.ANY)
-    shape = jax.ShapeDtypeStruct(sources[0].shape, sources[0].dtype)
-    return pl.pallas_call(
-        kernel,
-        in_specs=[anywhere] * (len(sources) + len(after)),
-        out_specs=[anywhere] * len(picks),
-        out_shape=[shape] * len(picks),
-        scratch_shapes=[pltpu.SemaphoreType.DMA((len(picks),))],
-        name="choose",
-    )(*sources, *after)
+def tied(x, *before):
+    for array in before:
+        x = x + 0 * array[(0,) * array.ndim]
+    return x
 
 
 def shift(x, axis, step):
@@ -283,6 +264,10 @@
 
 def swap(x):
     return lax.ppermute(x, "core", [(0, 1), (1, 0)])
+
+
+def gather_direct(x, axis):
+    return x, shift(x, axis, -1), shift(x, axis, 2), shift(x, axis, 1)
 
 
 def gather_bias(block):
@@ -295,14 +280,13 @@
     own, bias_t = prepare(pair_block, norm_gain, head_bias)
     biases = gather_bias(bias_t)
 
-    x_axis = ("xh", "xl")
-    behind, ahead = shift(own, x_axis, 1), shift(own, x_axis, -1)
-    (first_k,) = choose([own, behind, ahead], [[0, 1, 2, 0]], [biases[1]])
-    first_near = shift(first_k, "z", -1), shift(first_k, "z", 1)
-    opposite = shift(behind, x_axis, 1)
-    second_k, first_again = choose([opposite, behind, ahead, first_k], [[0, 2, 1, 0], [3] * 4])
-    first_ks = first_k, first_near[0], shift(first_again, "z", 2), first_near[1]
-    second_ks = second_k, shift(second_k, "z", -1), shift(second_k, "z", 2), shift(second_k, "z", 1)
+    xh, xl = lax.axis_index("xh"), lax.axis_index("xl")
+    behind, ahead = shift(own, ("xh", "xl"), 1), shift(own, ("xh", "xl"), -1)
+    opposite = shift(behind, ("xh", "xl"), 1)
+    near = jnp.where(xh == 0, behind, ahead)
+    first_ks = gather_direct(tied(jnp.where(xl == xh, own, near), biases[1]), "z")
+    near = jnp.where(xh == 0, ahead, behind)
+    second_ks = gather_direct(tied(jnp.where(xl == xh, opposite, near), *first_ks[1:]), "z")
 
     message = attend(own, first_ks, w_project, biases)
     message = attend(opposite, second_ks, w_project, biases, (message,))

time: 194 us -> 144 us (0.74)
  Pallas kernels: 99.2 us -> 49.6 us
  starting transfers between devices: 23.7 us -> 20.2 us
  local copies, waits for them, and re-layouts: 4.97 us -> 2.29 us
  between operations: 0.16 us -> 2.76 us
  other arithmetic: 0 us -> 2.41 us
    pallas_call x2 -> x0, Pallas kernels: 49.9 us -> none  [choose(): pl.pallas_call(kernel, in_specs=[anywhere] * (len(sources) + len(after)),...]
    unnamed x22 -> x8, local copies, waits for them, and re-layouts: 3.86 us -> 0.02 us
    add x0 -> x2, other arithmetic: none -> 2.41 us  [tied(): x = x + 0 * array[(0,) * array.ndim]]
    ppermute x5, starting transfers between devices: 6.76 us -> 4.5 us  [swap(): return lax.ppermute(x, 'core', [(0, 1), (1, 0)])]
    slice x0 -> x4, local copies, waits for them, and re-layouts: none -> 2.2 us  [tied(): x = x + 0 * array[(0,) * array.ndim]]
  transfers between devices with their start and end apart: 18 -> 18, of which waited for: 6 -> 6; matrix products, arithmetic and copies ran while one was open for 1% -> 3% of each run, Pallas kernels for 37% -> 15%
where the time goes in v6:
time: 144 us
  Pallas kernels  49.6 us (34%)
  waiting for transfers between devices  41.1 us (29%)
  blocking collectives  25.4 us (18%)
  starting transfers between devices  20.2 us (14%)
  between operations  2.76 us (2%)
  other arithmetic  2.41 us (2%)
  local copies, waits for them, and re-layouts  2.29 us (2%)
    pallas_call x2, Pallas kernels, attend(): pl.pallas_call(attend_kernel, grid=(ROWS // STEP,), in_specs=[rows(x_q)]...  42.9 us
    ppermute x13, waiting for transfers between devices, shift(): return lax.ppermute(x, axis, [(i, (i + step) % 4) for i in range(4)])  41.1 us
    all_to_all x1, blocking collectives, shards(): lax.all_to_all(message, ROW_AXES, split_axis=0, concat_axis=0, tiled=True)  25.4 us
    ppermute x13, starting transfers between devices, shift(): return lax.ppermute(x, axis, [(i, (i + step) % 4) for i in range(4)])  15.7 us
    ppermute x5, starting transfers between devices, swap(): return lax.ppermute(x, 'core', [(0, 1), (1, 0)])  4.5 us
    pallas_call x1, Pallas kernels, prepare(): pl.pallas_call(prepare_kernel, grid=(ROWS,), in_specs=[whole(COLS, CHANNE...  4.09 us
  transfers between devices with their start and end apart: 18, of which 6 were waited for; matrix products, arithmetic and copies ran while one was open for 3% of the time, Pallas kernels for 15%

profile of v6, /device:TPU:1, one launch (start us, length us, event | category | flops | bytes accessed | tf_op | source)
XLA Modules:
  0.0 143.7 jit_solution(10902004034450234897)
XLA Ops:
  0.0 4.1 %prepare.1 = (bf16[4,512,128]{2,1,0:T(8,128)(2,1)}, bf16[4,256,512]{2,1,0:T(8,128)(2,1)}) custom-call(bf16[4,512,128]{2,1,0:T(8,128)(2,1)} %pair.1, f32[1,128]{1,0:T(1,128)} %bitcast.5, bf16[4,512,256]{2,1,0:T(8,128)(2,1)} %bias.1), custom_call_target="tpu_custom_call" | custom-call | tf_op jit(solution)/shard_map/prepare/pallas_call | solution.py:43
  4.1 1.4 collective-permute-start.3
  5.5 1.3 collective-permute-start
  6.8 1.4 collective-permute-start.2
  8.2 1.4 collective-permute-start.12
  9.6 1.4 %collective-permute-start.10 = (bf16[4,256,512]{2,1,0:T(8,128)(2,1)}, bf16[4,256,512]{2,1,0:T(8,128)(2,1)S(1)}, u32[]{:S(2)}, u32[]{:S(2)}) collective-permute-start(bf16[4,256,512]{2,1,0:T(8,128)(2,1)} %get-tuple-element.8.rest_0_), channel_id=1, source_target_pairs={{0,96},{32,0},{64,32},{96,64},{1,97},{33,1},{65,33},{97,65},{2,98}... | collective-permute-start | bytes 3145736 | tf_op jit(solution)/shard_map/ppermute | solution.py:262
  12.2 8.4 %collective-permute-done = bf16[4,512,128]{2,1,0:T(8,128)(2,1)} collective-permute-done((bf16[4,512,128]{2,1,0:T(8,128)(2,1)}, bf16[4,512,128]{2,1,0:T(8,128)(2,1)}, u32[]{:S(2)}, u32[]{:S(2)}) %collective-permute-start) | collective-permute-done | bytes 524320 | tf_op jit(solution)/shard_map/ppermute | solution.py:262
  20.5 1.3 select_add_fusion.xk0
  21.8 3.9 %collective-permute-start.4 = (bf16[4,512,128]{2,1,0:T(8,128)(2,1)S(1)}, bf16[4,512,128]{2,1,0:T(8,128)(2,1)S(1)}, u32[]{:S(2)}, u32[]{:S(2)}) collective-permute-start(bf16[4,512,128]{2,1,0:T(8,128)(2,1)S(1)} %select_add_fusion.xk0), channel_id=1, source_target_pairs={{0,6},{2,0},{4,2},{6,4},{1,7},{3,1},{5,3},{7,5},{8,14},{10,8},{12,... | collective-permute-start | bytes 1572872 | tf_op jit(solution)/shard_map/ppermute | solution.py:262
  26.4 7.6 %collective-permute-done.12.rest_4_ = bf16[4,256,512]{2,1,0:T(8,128)(2,1)S(1)} collective-permute-done((bf16[4,256,512]{2,1,0:T(8,128)(2,1)}, bf16[4,256,512]{2,1,0:T(8,128)(2,1)S(1)}, u32[]{:S(2)}, u32[]{:S(2)}) %collective-permute-start.12) | collective-permute-done | bytes 1048608 | tf_op jit(solution)/shard_map/ppermute | solution.py:262
  34.2 2.7 %collective-permute-start.16 = (bf16[2,256,512]{2,1,0:T(8,128)(2,1)S(1)}, bf16[2,256,512]{2,1,0:T(8,128)(2,1)S(1)}, u32[]{:S(2)}, u32[]{:S(2)}) collective-permute-start(bf16[2,256,512]{2,1,0:T(8,128)(2,1)S(1)} %slice.29), channel_id=1, source_target_pairs={{0,96},{32,0},{64,32},{96,64},{1,97},{33,1},{65,33},{97,65},{2,98}... | collective-permute-start | bytes 1572872 | tf_op jit(solution)/shard_map/ppermute | solution.py:262
  37.0 10.3 %collective-permute-done.4.xk1 = bf16[4,512,128]{2,1,0:T(8,128)(2,1)S(1)} collective-permute-done((bf16[4,512,128]{2,1,0:T(8,128)(2,1)S(1)}, bf16[4,512,128]{2,1,0:T(8,128)(2,1)S(1)}, u32[]{:S(2)}, u32[]{:S(2)}) %collective-permute-start.4) | collective-permute-done | bytes 524320 | tf_op jit(solution)/shard_map/ppermute | solution.py:262
  47.2 1.9 %collective-permute-start.11 = (bf16[4,256,512]{2,1,0:T(8,128)(2,1)S(1)}, bf16[4,256,512]{2,1,0:T(8,128)(2,1)S(1)}, u32[]{:S(2)}, u32[]{:S(2)}) collective-permute-start(bf16[4,256,512]{2,1,0:T(8,128)(2,1)S(1)} %collective-permute-done.10.rest_2_), channel_id=1, source_target_pairs={{0,8},{8,0},{1,9},{9,1},{2,10},{10,2},{3,11},{11,3},{4,12},{12,4},... | collective-permute-start | bytes 3145736 | tf_op jit(solution)/shard_map/ppermute | solution.py:266
  49.1 2.6 %collective-permute-done.6.xk3 = bf16[4,512,128]{2,1,0:T(8,128)(2,1)S(1)} collective-permute-done((bf16[4,512,128]{2,1,0:T(8,128)(2,1)S(1)}, bf16[4,512,128]{2,1,0:T(8,128)(2,1)S(1)}, u32[]{:S(2)}, u32[]{:S(2)}) %collective-permute-start.6) | collective-permute-done | bytes 524320 | tf_op jit(solution)/shard_map/ppermute | solution.py:262
  51.7 0.7 collective-permute-start.1
  52.4 1.1 collective-permute-start.15
  57.3 8.4 %collective-permute-done.1.xq = bf16[4,512,128]{2,1,0:T(8,128)(2,1)S(1)} collective-permute-done((bf16[4,512,128]{2,1,0:T(8,128)(2,1)}, bf16[4,512,128]{2,1,0:T(8,128)(2,1)S(1)}, u32[]{:S(2)}, u32[]{:S(2)}) %collective-permute-start.1) | collective-permute-done | bytes 524320 | tf_op jit(solution)/shard_map/ppermute | solution.py:262
  65.7 1.1 add_add_fusion.xk0
  66.8 1.3 collective-permute-start.7
  68.9 21.6 %attend.2.rest_10_ = bf16[16,10,32,128]{3,2,1,0:T(8,128)(2,1)S(1)} custom-call(bf16[4,512,128]{2,1,0:T(8,128)(2,1)S(1)} %copy-done, bf16[4,512,128]{2,1,0:T(8,128)(2,1)S(1)} %select_add_fusion.xk0, bf16[4,512,128]{2,1,0:T(8,128)(2,1)S(1)} %collective-permute-done.4.xk1, bf16[4,512,128]{2,1,0:T(8,128)(2,1)S(1)} %collective-permute-done.5.xk2, ...), custom_call_target="tpu_custom_call" | custom-call | flops 8589934592 | bytes 16777216 | tf_op jit(solution)/shard_map/attend/pallas_call | solution.py:192
  90.5 3.8 %collective-permute-done.9.xk3 = bf16[4,512,128]{2,1,0:T(8,128)(2,1)S(1)} collective-permute-done((bf16[4,512,128]{2,1,0:T(8,128)(2,1)S(1)}, bf16[4,512,128]{2,1,0:T(8,128)(2,1)S(1)}, u32[]{:S(2)}, u32[]{:S(2)}) %collective-permute-start.9) | collective-permute-done | bytes 524320 | tf_op jit(solution)/shard_map/ppermute | solution.py:262
  94.3 21.3 %attend.3 = bf16[16,10,32,128]{3,2,1,0:T(8,128)(2,1)S(1)} custom-call(bf16[4,512,128]{2,1,0:T(8,128)(2,1)S(1)} %collective-permute-done.1.xq, bf16[4,512,128]{2,1,0:T(8,128)(2,1)S(1)} %add_add_fusion.xk0, bf16[4,512,128]{2,1,0:T(8,128)(2,1)S(1)} %collective-permute-done.7.xk1, ...), custom_call_target="tpu_custom_call", output_to_operand_aliasing={{}: (16, {})} | custom-call | flops 8589934592 | bytes 16777216 | tf_op jit(solution)/shard_map/attend/pallas_call | solution.py:192
  115.6 25.4 %all_to_all.5.message = bf16[16,10,32,128]{3,2,1,0:T(8,128)(2,1)S(1)} all-to-all(bf16[16,10,32,128]{3,2,1,0:T(8,128)(2,1)S(1)} %attend.3), channel_id=1, replica_groups=mesh['y'=4,'xh'=2,'core'=2,'z'=4,'xl'=2] {'y','xh','core'}, dimensions={0} | all-to-all | bytes 2621440 | tf_op jit(solution)/shard_map/all_to_all | solution.py:293
  141.1 2.6 %merge.1 = bf16[32,64,128]{2,1,0:T(8,128)(2,1)} custom-call(bf16[16,10,32,128]{3,2,1,0:T(8,128)(2,1)S(1)} %all_to_all.5.message, bf16[128,128]{1,0:T(8,128)(2,1)S(1)} %copy-done.1), custom_call_target="tpu_custom_call" | custom-call | tf_op jit(solution)/shard_map/merge/pallas_call | solution.py:241
  (33 shorter events, 3.9 us)
Async XLA Ops:
  4.1 6.9 %collective-permute-start.3 = (bf16[4,256,512]{2,1,0:T(8,128)(2,1)}, bf16[4,256,512]{2,1,0:T(8,128)(2,1)S(1)}, u32[]{:S(2)}, u32[]{:S(2)}) collective-permute-start(bf16[4,256,512]{2,1,0:T(8,128)(2,1)} %get-tuple-element.8.rest_0_), channel_id=1, source_target_pairs={{0,8},{8,0},{1,9},{9,1},{2,10},{10,2},{3,11},{11,3},{4,12},{12,4},... | collective-permute-start | bytes 3145736 | tf_op jit(solution)/shard_map/ppermute | solution.py:266
  5.5 15.0 %collective-permute-start = (bf16[4,512,128]{2,1,0:T(8,128)(2,1)}, bf16[4,512,128]{2,1,0:T(8,128)(2,1)}, u32[]{:S(2)}, u32[]{:S(2)}) collective-permute-start(bf16[4,512,128]{2,1,0:T(8,128)(2,1)} %get-tuple-element.7.xq), channel_id=1, source_target_pairs={{0,1},{1,16},{16,17},{17,0},{2,3},{3,18},{18,19},{19,2},{4,5},{5,2... | collective-permute-start | bytes 1572872 | tf_op jit(solution)/shard_map/ppermute | solution.py:262
  6.8 13.7 %collective-permute-start.2 = (bf16[4,512,128]{2,1,0:T(8,128)(2,1)}, bf16[4,512,128]{2,1,0:T(8,128)(2,1)}, u32[]{:S(2)}, u32[]{:S(2)}) collective-permute-start(bf16[4,512,128]{2,1,0:T(8,128)(2,1)} %get-tuple-element.7.xq), channel_id=1, source_target_pairs={{0,17},{1,0},{16,1},{17,16},{2,19},{3,2},{18,3},{19,18},{4,21},{5,... | collective-permute-start | bytes 1572872 | tf_op jit(solution)/shard_map/ppermute | solution.py:262
  8.2 25.8 %collective-permute-start.12 = (bf16[4,256,512]{2,1,0:T(8,128)(2,1)}, bf16[4,256,512]{2,1,0:T(8,128)(2,1)S(1)}, u32[]{:S(2)}, u32[]{:S(2)}) collective-permute-start(bf16[4,256,512]{2,1,0:T(8,128)(2,1)} %get-tuple-element.8.rest_0_), channel_id=1, source_target_pairs={{0,32},{32,64},{64,96},{96,0},{1,33},{33,65},{65,97},{97,1},{2,34}... | collective-permute-start | bytes 3145736 | tf_op jit(solution)/shard_map/ppermute | solution.py:262
  9.6 24.6 %collective-permute-start.10 = (bf16[4,256,512]{2,1,0:T(8,128)(2,1)}, bf16[4,256,512]{2,1,0:T(8,128)(2,1)S(1)}, u32[]{:S(2)}, u32[]{:S(2)}) collective-permute-start(bf16[4,256,512]{2,1,0:T(8,128)(2,1)} %get-tuple-element.8.rest_0_), channel_id=1, source_target_pairs={{0,96},{32,0},{64,32},{96,64},{1,97},{33,1},{65,33},{97,65},{2,98}... | collective-permute-start | bytes 3145736 | tf_op jit(solution)/shard_map/ppermute | solution.py:262
  21.8 25.4 %collective-permute-start.4 = (bf16[4,512,128]{2,1,0:T(8,128)(2,1)S(1)}, bf16[4,512,128]{2,1,0:T(8,128)(2,1)S(1)}, u32[]{:S(2)}, u32[]{:S(2)}) collective-permute-start(bf16[4,512,128]{2,1,0:T(8,128)(2,1)S(1)} %select_add_fusion.xk0), channel_id=1, source_target_pairs={{0,6},{2,0},{4,2},{6,4},{1,7},{3,1},{5,3},{7,5},{8,14},{10,8},{12,... | collective-permute-start | bytes 1572872 | tf_op jit(solution)/shard_map/ppermute | solution.py:262
  25.7 23.4 %collective-permute-start.5 = (bf16[4,512,128]{2,1,0:T(8,128)(2,1)S(1)}, bf16[4,512,128]{2,1,0:T(8,128)(2,1)S(1)}, u32[]{:S(2)}, u32[]{:S(2)}) collective-permute-start(bf16[4,512,128]{2,1,0:T(8,128)(2,1)S(1)} %select_add_fusion.xk0), channel_id=1, source_target_pairs={{0,4},{2,6},{4,0},{6,2},{1,5},{3,7},{5,1},{7,3},{8,12},{10,14},{12... | collective-permute-start | bytes 1572872 | tf_op jit(solution)/shard_map/ppermute | solution.py:262
  25.7 25.9 %collective-permute-start.6 = (bf16[4,512,128]{2,1,0:T(8,128)(2,1)S(1)}, bf16[4,512,128]{2,1,0:T(8,128)(2,1)S(1)}, u32[]{:S(2)}, u32[]{:S(2)}) collective-permute-start(bf16[4,512,128]{2,1,0:T(8,128)(2,1)S(1)} %select_add_fusion.xk0), channel_id=1, source_target_pairs={{0,2},{2,4},{4,6},{6,0},{1,3},{3,5},{5,7},{7,1},{8,10},{10,12},{12... | collective-permute-start | bytes 1572872 | tf_op jit(solution)/shard_map/ppermute | solution.py:262
  34.1 18.4 %collective-permute-start.14 = (bf16[2,256,512]{2,1,0:T(8,128)(2,1)S(1)}, bf16[2,256,512]{2,1,0:T(8,128)(2,1)S(1)}, u32[]{:S(2)}, u32[]{:S(2)}) collective-permute-start(bf16[2,256,512]{2,1,0:T(8,128)(2,1)S(1)} %slice.28), channel_id=1, source_target_pairs={{0,32},{32,64},{64,96},{96,0},{1,33},{33,65},{65,97},{97,1},{2,34}... | collective-permute-start | bytes 1572872 | tf_op jit(solution)/shard_map/ppermute | solution.py:262
  34.2 34.7 %copy-start = (bf16[4,512,128]{2,1,0:T(8,128)(2,1)S(1)}, bf16[4,512,128]{2,1,0:T(8,128)(2,1)}, u32[]{:S(2)}) copy-start(bf16[4,512,128]{2,1,0:T(8,128)(2,1)} %get-tuple-element.7.xq) | copy-start | bytes 1572868
  34.2 34.7 %copy-start.2 = (bf16[4,256,512]{2,1,0:T(8,128)(2,1)S(1)}, bf16[4,256,512]{2,1,0:T(8,128)(2,1)}, u32[]{:S(2)}) copy-start(bf16[4,256,512]{2,1,0:T(8,128)(2,1)} %get-tuple-element.8.rest_0_) | copy-start | bytes 3145732
  34.2 34.7 %copy-start.3 = (bf16[128,512]{1,0:T(8,128)(2,1)S(1)}, bf16[128,512]{1,0:T(8,128)(2,1)}, u32[]{:S(2)}) copy-start(bf16[128,512]{1,0:T(8,128)(2,1)} %w.4) | copy-start | bytes 393220
  34.2 19.3 %collective-permute-start.16 = (bf16[2,256,512]{2,1,0:T(8,128)(2,1)S(1)}, bf16[2,256,512]{2,1,0:T(8,128)(2,1)S(1)}, u32[]{:S(2)}, u32[]{:S(2)}) collective-permute-start(bf16[2,256,512]{2,1,0:T(8,128)(2,1)S(1)} %slice.29), channel_id=1, source_target_pairs={{0,96},{32,0},{64,32},{96,64},{1,97},{33,1},{65,33},{97,65},{2,98}... | collective-permute-start | bytes 1572872 | tf_op jit(solution)/shard_map/ppermute | solution.py:262
  47.2 21.6 %collective-permute-start.11 = (bf16[4,256,512]{2,1,0:T(8,128)(2,1)S(1)}, bf16[4,256,512]{2,1,0:T(8,128)(2,1)S(1)}, u32[]{:S(2)}, u32[]{:S(2)}) collective-permute-start(bf16[4,256,512]{2,1,0:T(8,128)(2,1)S(1)} %collective-permute-done.10.rest_2_), channel_id=1, source_target_pairs={{0,8},{8,0},{1,9},{9,1},{2,10},{10,2},{3,11},{11,3},{4,12},{12,4},... | collective-permute-start | bytes 3145736 | tf_op jit(solution)/shard_map/ppermute | solution.py:266
  49.1 19.8 %collective-permute-start.13 = (bf16[4,256,512]{2,1,0:T(8,128)(2,1)S(1)}, bf16[4,256,512]{2,1,0:T(8,128)(2,1)S(1)}, u32[]{:S(2)}, u32[]{:S(2)}) collective-permute-start(bf16[4,256,512]{2,1,0:T(8,128)(2,1)S(1)} %collective-permute-done.12.rest_4_), channel_id=1, source_target_pairs={{0,8},{8,0},{1,9},{9,1},{2,10},{10,2},{3,11},{11,3},{4,12},{12,4},... | collective-permute-start | bytes 3145736 | tf_op jit(solution)/shard_map/ppermute | solution.py:266
  51.7 14.0 %collective-permute-start.1 = (bf16[4,512,128]{2,1,0:T(8,128)(2,1)}, bf16[4,512,128]{2,1,0:T(8,128)(2,1)S(1)}, u32[]{:S(2)}, u32[]{:S(2)}) collective-permute-start(bf16[4,512,128]{2,1,0:T(8,128)(2,1)} %collective-permute-done), channel_id=1, source_target_pairs={{0,1},{1,16},{16,17},{17,0},{2,3},{3,18},{18,19},{19,2},{4,5},{5,2... | collective-permute-start | bytes 1572872 | tf_op jit(solution)/shard_map/ppermute | solution.py:262
  52.4 15.8 %collective-permute-start.15 = (bf16[2,256,512]{2,1,0:T(8,128)(2,1)S(1)}, bf16[2,256,512]{2,1,0:T(8,128)(2,1)S(1)}, u32[]{:S(2)}, u32[]{:S(2)}) collective-permute-start(bf16[2,256,512]{2,1,0:T(8,128)(2,1)S(1)} %collective-permute-done.14.rest_6_), channel_id=1, source_target_pairs={{0,8},{8,0},{1,9},{9,1},{2,10},{10,2},{3,11},{11,3},{4,12},{12,4},... | collective-permute-start | bytes 1572872 | tf_op jit(solution)/shard_map/ppermute | solution.py:266
  53.5 14.6 %collective-permute-start.17 = (bf16[2,256,512]{2,1,0:T(8,128)(2,1)S(1)}, bf16[2,256,512]{2,1,0:T(8,128)(2,1)S(1)}, u32[]{:S(2)}, u32[]{:S(2)}) collective-permute-start(bf16[2,256,512]{2,1,0:T(8,128)(2,1)S(1)} %collective-permute-done.16.rest_8_), channel_id=1, source_target_pairs={{0,8},{8,0},{1,9},{9,1},{2,10},{10,2},{3,11},{11,3},{4,12},{12,4},... | collective-permute-start | bytes 1572872 | tf_op jit(solution)/shard_map/ppermute | solution.py:266
  66.8 23.6 %collective-permute-start.7 = (bf16[4,512,128]{2,1,0:T(8,128)(2,1)S(1)}, bf16[4,512,128]{2,1,0:T(8,128)(2,1)S(1)}, u32[]{:S(2)}, u32[]{:S(2)}) collective-permute-start(bf16[4,512,128]{2,1,0:T(8,128)(2,1)S(1)} %add_add_fusion.xk0), channel_id=1, source_target_pairs={{0,6},{2,0},{4,2},{6,4},{1,7},{3,1},{5,3},{7,5},{8,14},{10,8},{12,... | collective-permute-start | bytes 1572872 | tf_op jit(solution)/shard_map/ppermute | solution.py:262
  68.2 22.3 %collective-permute-start.8 = (bf16[4,512,128]{2,1,0:T(8,128)(2,1)S(1)}, bf16[4,512,128]{2,1,0:T(8,128)(2,1)S(1)}, u32[]{:S(2)}, u32[]{:S(2)}) collective-permute-start(bf16[4,512,128]{2,1,0:T(8,128)(2,1)S(1)} %add_add_fusion.xk0), channel_id=1, source_target_pairs={{0,4},{2,6},{4,0},{6,2},{1,5},{3,7},{5,1},{7,3},{8,12},{10,14},{12... | collective-permute-start | bytes 1572872 | tf_op jit(solution)/shard_map/ppermute | solution.py:262
  68.2 26.1 %collective-permute-start.9 = (bf16[4,512,128]{2,1,0:T(8,128)(2,1)S(1)}, bf16[4,512,128]{2,1,0:T(8,128)(2,1)S(1)}, u32[]{:S(2)}, u32[]{:S(2)}) collective-permute-start(bf16[4,512,128]{2,1,0:T(8,128)(2,1)S(1)} %add_add_fusion.xk0), channel_id=1, source_target_pairs={{0,2},{2,4},{4,6},{6,0},{1,3},{3,5},{5,7},{7,1},{8,10},{10,12},{12... | collective-permute-start | bytes 1572872 | tf_op jit(solution)/shard_map/ppermute | solution.py:262
  115.6 25.4 %copy-start.1 = (bf16[128,128]{1,0:T(8,128)(2,1)S(1)}, bf16[128,128]{1,0:T(8,128)(2,1)}, u32[]{:S(2)}) copy-start(bf16[128,128]{1,0:T(8,128)(2,1)} %w.5) | copy-start | bytes 98308

commit v7 on v6

--- a/solution.py
+++ b/solution.py
@@ -11,6 +11,7 @@
 KEYS = 4 * BLOCK
 SHARE = COLS // 16
 PAD = 40
+PARTIAL = CHANNELS + 4 * HEADS
 STEP = 2
 LOG2E = 1.4426950408889634
 LOW, HIGH = 1e-26, 1e30
@@ -58,10 +59,8 @@
 
 
 def attend_kernel(xq, xk0, xk1, xk2, xk3, w, *rest):
-    biases, out, scratch = rest[:10], rest[-9], rest[-8:]
-    bias_s, top_s, k_s, v_s, q_s, gate_s, stat_s, sems = scratch
+    biases, out, (bias_s, top_s, k_s, v_s, q_s, sems) = rest[:10], rest[10], rest[11:]
     step = pl.program_id(0)
-
     y, z, core = lax.axis_index("y"), lax.axis_index("z"), lax.axis_index("core")
 
     def bias_copies():
@@ -80,13 +79,11 @@
         for copy in bias_copies():
             copy.start()
         q_s[...] = jnp.zeros_like(q_s)
-        stat_s[...] = jnp.zeros_like(stat_s)
         v_s[:, :, WIDTH:, :] = jnp.ones((STEP, HEADS, PAD - WIDTH, KEYS), BF16)
 
     def project(r):
         x_q = xq[r]
         q_t = (matmul(w[:, :128], x_q, 0, 1) * WIDTH ** (-0.5)).astype(BF16)
-        gate_s[r] = jax.nn.sigmoid(matmul(w[:, 384:], x_q, 0, 1))
         for h in range(HEADS):
             at = slice(h * WIDTH, (h + 1) * WIDTH)
             q_s[r, h, at, :] = q_t[at]
@@ -106,15 +103,12 @@
             mass = total[WIDTH : WIDTH + 1]
             parts.append(total[:WIDTH] * (1.0 / mass))
             stats.append(shift + jnp.log(mass))
-        gated = jnp.concatenate(parts, axis=0) * gate_s[r]
-        at = step * STEP + r
-        out[:, at] = gated.T.astype(BF16).reshape(16, SHARE, CHANNELS)
         stat = jnp.concatenate(stats, axis=0)
         high = stat.astype(BF16).astype(F32)
         middle = (stat - high).astype(BF16).astype(F32)
         low = stat - high - middle
-        rows = jnp.concatenate([high, middle, low, jnp.zeros_like(low)], axis=0)
-        stat_s[pl.ds(pl.multiple_of(at * 32, 32), 16), :] = rows
+        rows = parts + [high, middle, low, jnp.zeros_like(low)]
+        out[r] = jnp.concatenate(rows, axis=0).astype(out.dtype)
 
     for r in range(STEP):
         project(r)
@@ -176,37 +170,27 @@
                 shifts.append(largest)
             finish(r, totals, shifts)
 
-    @pl.when(step == pl.num_programs(0) - 1)
-    def _():
-        out[:, ROWS] = stat_s[...].T.astype(BF16).reshape(16, SHARE, CHANNELS)
-
-
-def attend(x_q, x_ks, w_project, biases, message=()):
-    half = len(message)
-
+
+def attend(x_q, x_ks, w_project, biases, dtype):
     def rows(x):
         return pl.BlockSpec((STEP,) + x.shape[1:], lambda i: (i, 0, 0))
 
     scores = ROWS * HEADS * COLS * KEYS
-    block = (16, ROWS + 1, SHARE, CHANNELS)
     return pl.pallas_call(
         attend_kernel,
         grid=(ROWS // STEP,),
         in_specs=[rows(x_q)]
         + [rows(x) for x in x_ks]
         + [pl.BlockSpec((CHANNELS, 512), lambda i: (0, 0))]
-        + [pl.BlockSpec(memory_space=pl.ANY)] * (len(biases) + len(message)),
-        out_specs=pl.BlockSpec(block, lambda i: (0, half, 0, 0)),
-        out_shape=jax.ShapeDtypeStruct((16, 2 * (ROWS + 1), SHARE, CHANNELS), BF16),
-        input_output_aliases={6 + len(biases): 0} if half else {},
+        + [pl.BlockSpec(memory_space=pl.ANY)] * len(biases),
+        out_specs=pl.BlockSpec((STEP, PARTIAL, COLS), lambda i: (i, 0, 0)),
+        out_shape=jax.ShapeDtypeStruct((ROWS, PARTIAL, COLS), dtype),
         scratch_shapes=[
             pltpu.VMEM((4, HEADS, BLOCK, COLS), BF16),
             pltpu.VMEM((HEADS, COLS), F32),
             pltpu.VMEM((STEP, KEYS, CHANNELS), BF16),
             pltpu.VMEM((STEP, HEADS, PAD, KEYS), BF16),
             pltpu.VMEM((STEP, HEADS, CHANNELS, COLS), BF16),
-            pltpu.VMEM((STEP, CHANNELS, COLS), F32),
-            pltpu.VMEM((CHANNELS, COLS), F32),
             pltpu.SemaphoreType.DMA((10,)),
         ],
         compiler_params=pltpu.CompilerParams(vmem_limit_bytes=VMEM_LIMIT),
@@ -214,42 +198,57 @@
             flops=scores * 512, bytes_accessed=2**24, transcendentals=scores
         ),
         name="attend",
-    )(x_q, *x_ks, w_project, *biases, *message)
-
-
-def merge_kernel(message, w, out):
-    lane = lax.broadcasted_iota(jnp.int32, (CHANNELS, CHANNELS), 0)
-    head = lax.broadcasted_iota(jnp.int32, (CHANNELS, CHANNELS), 1) // WIDTH
-    rows = []
-    for s in range(4):
-        other = s ^ 2
-        stat1, stat2 = message[s, ROWS], message[other, 2 * ROWS + 1]
-        for i in range(ROWS):
-            part = lane - 32 * i
-            inside = (part >= 0) & (part < 12) & (lax.rem(part, 4) == head)
-            pick = inside.astype(F32).astype(BF16)
-            share = jax.nn.sigmoid(matmul(stat1, pick) - matmul(stat2, pick))
-            o1 = message[s, i].astype(F32)
-            o2 = message[other, ROWS + 1 + i].astype(F32)
-            rows.append((o2 + share * (o1 - o2)).astype(BF16))
-    update = matmul(jnp.concatenate(rows, axis=0), w[...])
-    update = jnp.swapaxes(update.reshape(4 * ROWS, SHARE, CHANNELS), 0, 1)
-    out[...] = update.astype(BF16)
-
-
-def merge(message, w_out):
+    )(x_q, *x_ks, w_project, *biases)
+
+
+def update_kernel(x, w, w_out, mine, theirs, out):
+    def parts(partial):
+        p = partial[0].astype(F32)
+        stat = p[CHANNELS : CHANNELS + 4] + p[CHANNELS + 4 : CHANNELS + 8]
+        return p[:CHANNELS], stat + p[CHANNELS + 8 : CHANNELS + 12]
+
+    (o1, stat1), (o2, stat2) = parts(mine), parts(theirs)
+    share = jax.nn.sigmoid(stat1 - stat2)
+    lines = [jnp.broadcast_to(share[h : h + 1], (WIDTH, COLS)) for h in range(HEADS)]
+    attended = o2 + jnp.concatenate(lines, axis=0) * (o1 - o2)
+    gate = jax.nn.sigmoid(matmul(w[:, 384:], x[0], 0, 1))
+    gated = (gate * attended).astype(BF16)
+    update = matmul(gated, w_out[...], 0, 0).astype(BF16)
+    out[:, 0] = update.reshape(16, SHARE, CHANNELS)
+
+
+def update_rows(x, w_project, w_out, mine, theirs):
+    def row(a):
+        return pl.BlockSpec((1,) + a.shape[1:], lambda i: (i, 0, 0))
+
+    def whole(a):
+        return pl.BlockSpec(a.shape, lambda i: (0, 0))
+
     return pl.pallas_call(
-        merge_kernel,
+        update_kernel,
+        grid=(ROWS,),
+        in_specs=[row(x), whole(w_project), whole(w_out), row(mine), row(theirs)],
+        out_specs=pl.BlockSpec((16, 1, SHARE, CHANNELS), lambda i: (0, i, 0, 0)),
+        out_shape=jax.ShapeDtypeStruct((16, ROWS, SHARE, CHANNELS), BF16),
+        compiler_params=pltpu.CompilerParams(vmem_limit_bytes=VMEM_LIMIT),
+        name="update",
+    )(x, w_project, w_out, mine, theirs)
+
+
+def reorder_kernel(update, out):
+    rows = update[...].astype(F32).reshape(4 * ROWS, SHARE, CHANNELS)
+    out[...] = jnp.swapaxes(rows, 0, 1).astype(BF16)
+
+
+def reorder(update):
+    return pl.pallas_call(
+        reorder_kernel,
         grid=(4,),
-        in_specs=[
-            pl.BlockSpec((4,) + message.shape[1:], lambda y: (y, 0, 0, 0)),
-            pl.BlockSpec((CHANNELS, CHANNELS), lambda y: (0, 0)),
-        ],
+        in_specs=[pl.BlockSpec((4,) + update.shape[1:], lambda y: (y, 0, 0, 0))],
         out_specs=pl.BlockSpec((SHARE, 4 * ROWS, CHANNELS), lambda y: (0, y, 0)),
         out_shape=jax.ShapeDtypeStruct((SHARE, 16 * ROWS, CHANNELS), BF16),
-        compiler_params=pltpu.CompilerParams(vmem_limit_bytes=VMEM_LIMIT),
-        name="merge",
-    )(message, w_out)
+        name="reorder",
+    )(update)
 
 
 def tied(x, *before):
@@ -281,17 +280,19 @@
     biases = gather_bias(bias_t)
 
     xh, xl = lax.axis_index("xh"), lax.axis_index("xl")
-    behind, ahead = shift(own, ("xh", "xl"), 1), shift(own, ("xh", "xl"), -1)
-    opposite = shift(behind, ("xh", "xl"), 1)
-    near = jnp.where(xh == 0, behind, ahead)
-    first_ks = gather_direct(tied(jnp.where(xl == xh, own, near), biases[1]), "z")
-    near = jnp.where(xh == 0, ahead, behind)
-    second_ks = gather_direct(tied(jnp.where(xl == xh, opposite, near), *first_ks[1:]), "z")
-
-    message = attend(own, first_ks, w_project, biases)
-    message = attend(opposite, second_ks, w_project, biases, (message,))
-    message = lax.all_to_all(message, ROW_AXES, split_axis=0, concat_axis=0, tiled=True)
-    return merge(message, w_out)
+    opposite = lax.ppermute(own, "xh", [(0, 1), (1, 0)])
+    across = lax.ppermute(own, ("xh", "xl"), [(1, 2), (2, 1)])
+    beside = lax.ppermute(own, ("xh", "xl"), [(0, 1), (3, 2)])
+    their_k = tied(jnp.where(xl == xh, opposite, across), biases[1])
+    their_ks = gather_direct(their_k, "z")
+    own_k = tied(jnp.where(xl == xh, own, beside), *their_ks[1:])
+    own_ks = gather_direct(own_k, "z")
+
+    theirs = attend(opposite, their_ks, w_project, biases, BF16)
+    theirs = lax.ppermute(theirs, "xh", [(0, 1), (1, 0)])
+    mine = attend(own, own_ks, w_project, biases, F32)
+    update = update_rows(own, w_project, w_out, mine, theirs)
+    return reorder(lax.all_to_all(update, ROW_AXES, split_axis=0, concat_axis=0, tiled=True))
 
 
 def solution(mesh):

time: 144 us -> 146 us (1.014)
  starting transfers between devices: 20.2 us -> 42.1 us
  waiting for transfers between devices: 41.1 us -> 24.7 us
  blocking collectives: 25.4 us -> 21.2 us
  other arithmetic: 2.41 us -> 0.15 us
  Pallas kernels: 49.6 us -> 51.2 us
    ppermute x13 -> x10, waiting for transfers between devices: 41.1 us -> 24.7 us  [shift(): return lax.ppermute(x, axis, [(i, (i + step) % 4) for i in range(4)])]
    ppermute x0 -> x4, starting transfers between devices: none -> 10.5 us  [the longest x1 4.42 us: shards(): beside = lax.ppermute(own, ('xh', 'xl'), [(0, 1), (3, 2)])]
    ppermute x13 -> x10, starting transfers between devices: 15.7 us -> 22.3 us  [shift(): return lax.ppermute(x, axis, [(i, (i + step) % 4) for i in range(4)])]
    ppermute x5, starting transfers between devices: 4.5 us -> 9.28 us  [swap(): return lax.ppermute(x, 'core', [(0, 1), (1, 0)])]
    all_to_all x1, blocking collectives: 25.4 us -> 21.2 us  [shards(): lax.all_to_all(update, ROW_AXES, split_axis=0, concat_axis=0, tiled=True)]
    pallas_call x1 -> x2, Pallas kernels: 2.63 us -> 5.09 us  [the longest x1 3.25 us: reorder(): pl.pallas_call(reorder_kernel, grid=(4,), in_specs=[pl.BlockSpec((4,) + u...]
    add x2, other arithmetic: 2.41 us -> 0.15 us  [tied(): x = x + 0 * array[(0,) * array.ndim]]
  transfers between devices with their start and end apart: 18 -> 19, of which waited for: 6 -> 3; matrix products, arithmetic and copies ran while one was open for 3% -> 2% of each run, Pallas kernels for 15% -> 29%
where the time goes in v7:
time: 146 us; the launch traced here: 145 us
  Pallas kernels  51.2 us (35%)
  starting transfers between devices  42.1 us (29%)
  waiting for transfers between devices  24.7 us (17%)
  blocking collectives  21.2 us (15%)
  local copies, waits for them, and re-layouts  2.99 us (2%)
  between operations  2.82 us (2%)
    pallas_call x2, Pallas kernels, attend(): pl.pallas_call(attend_kernel, grid=(ROWS // STEP,), in_specs=[rows(x_q)]...  42.1 us
    ppermute x10, waiting for transfers between devices, shift(): return lax.ppermute(x, axis, [(i, (i + step) % 4) for i in range(4)])  24.7 us
    ppermute x10, starting transfers between devices, shift(): return lax.ppermute(x, axis, [(i, (i + step) % 4) for i in range(4)])  22.3 us
    all_to_all x1, blocking collectives, shards(): lax.all_to_all(update, ROW_AXES, split_axis=0, concat_axis=0, tiled=True)  21.2 us
    ppermute x5, starting transfers between devices, swap(): return lax.ppermute(x, 'core', [(0, 1), (1, 0)])  9.28 us
    ppermute x1, starting transfers between devices, shards(): beside = lax.ppermute(own, ('xh', 'xl'), [(0, 1), (3, 2)])  4.42 us
    pallas_call x1, Pallas kernels, prepare(): pl.pallas_call(prepare_kernel, grid=(ROWS,), in_specs=[whole(COLS, CHANNE...  4.08 us
    ppermute x1, starting transfers between devices, shards(): opposite = lax.ppermute(own, 'xh', [(0, 1), (1, 0)])  3.62 us
  transfers between devices with their start and end apart: 19, of which 3 were waited for; matrix products, arithmetic and copies ran while one was open for 2% of the time, Pallas kernels for 29%

profile of v7, /device:TPU:1, one launch (start us, length us, event | category | flops | bytes accessed | tf_op | source)
XLA Modules:
  0.0 145.2 jit_solution(17773807698806787005)
XLA Ops:
  0.0 4.1 %prepare.1 = (bf16[4,512,128]{2,1,0:T(8,128)(2,1)}, bf16[4,256,512]{2,1,0:T(8,128)(2,1)}) custom-call(bf16[4,512,128]{2,1,0:T(8,128)(2,1)} %pair.1, f32[1,128]{1,0:T(1,128)} %bitcast.5, bf16[4,512,256]{2,1,0:T(8,128)(2,1)} %bias.1), custom_call_target="tpu_custom_call" | custom-call | tf_op jit(solution)/shard_map/prepare/pallas_call | solution.py:44
  4.1 2.1 %collective-permute-start.12 = (bf16[4,256,512]{2,1,0:T(8,128)(2,1)}, bf16[4,256,512]{2,1,0:T(8,128)(2,1)S(1)}, u32[]{:S(2)}, u32[]{:S(2)}) collective-permute-start(bf16[4,256,512]{2,1,0:T(8,128)(2,1)} %get-tuple-element.8.rest_0_), channel_id=1, source_target_pairs={{0,32},{32,64},{64,96},{96,0},{1,33},{33,65},{65,97},{97,1},{2,34}... | collective-permute-start | bytes 3145736 | tf_op jit(solution)/shard_map/ppermute | solution.py:261
  6.2 1.5 %collective-permute-start.10 = (bf16[4,256,512]{2,1,0:T(8,128)(2,1)}, bf16[4,256,512]{2,1,0:T(8,128)(2,1)S(1)}, u32[]{:S(2)}, u32[]{:S(2)}) collective-permute-start(bf16[4,256,512]{2,1,0:T(8,128)(2,1)} %get-tuple-element.8.rest_0_), channel_id=1, source_target_pairs={{0,96},{32,0},{64,32},{96,64},{1,97},{33,1},{65,33},{97,65},{2,98}... | collective-permute-start | bytes 3145736 | tf_op jit(solution)/shard_map/ppermute | solution.py:261
  8.7 1.4 collective-permute-start.2
  10.2 3.6 %collective-permute-start.1 = (bf16[4,512,128]{2,1,0:T(8,128)(2,1)}, bf16[4,512,128]{2,1,0:T(8,128)(2,1)S(1)}, u32[]{:S(2)}, u32[]{:S(2)}) collective-permute-start(bf16[4,512,128]{2,1,0:T(8,128)(2,1)} %get-tuple-element.7.xq.x), channel_id=1, source_target_pairs={{0,16},{16,0},{1,17},{17,1},{2,18},{18,2},{3,19},{19,3},{4,20},{20... | collective-permute-start | bytes 1572872 | tf_op jit(solution)/shard_map/ppermute | solution.py:283
  13.8 16.8 %collective-permute-done.12.rest_4_ = bf16[4,256,512]{2,1,0:T(8,128)(2,1)S(1)} collective-permute-done((bf16[4,256,512]{2,1,0:T(8,128)(2,1)}, bf16[4,256,512]{2,1,0:T(8,128)(2,1)S(1)}, u32[]{:S(2)}, u32[]{:S(2)}) %collective-permute-start.12) | collective-permute-done | bytes 1048608 | tf_op jit(solution)/shard_map/ppermute | solution.py:261
  30.8 2.7 %collective-permute-start.16 = (bf16[2,256,512]{2,1,0:T(8,128)(2,1)S(1)}, bf16[2,256,512]{2,1,0:T(8,128)(2,1)S(1)}, u32[]{:S(2)}, u32[]{:S(2)}) collective-permute-start(bf16[2,256,512]{2,1,0:T(8,128)(2,1)S(1)} %slice.29), channel_id=1, source_target_pairs={{0,96},{32,0},{64,32},{96,64},{1,97},{33,1},{65,33},{97,65},{2,98}... | collective-permute-start | bytes 1572872 | tf_op jit(solution)/shard_map/ppermute | solution.py:261
  33.5 1.2 slice.24
  35.5 1.6 %collective-permute-start.6 = (bf16[4,512,128]{2,1,0:T(8,128)(2,1)S(1)}, bf16[4,512,128]{2,1,0:T(8,128)(2,1)S(1)}, u32[]{:S(2)}, u32[]{:S(2)}) collective-permute-start(bf16[4,512,128]{2,1,0:T(8,128)(2,1)S(1)} %select_add_fusion.xk0), channel_id=1, source_target_pairs={{0,2},{2,4},{4,6},{6,0},{1,3},{3,5},{5,7},{7,1},{8,10},{10,12},{12... | collective-permute-start | bytes 1572872 | tf_op jit(solution)/shard_map/ppermute | solution.py:261
  37.1 3.3 %collective-permute-start.5 = (bf16[4,512,128]{2,1,0:T(8,128)(2,1)S(1)}, bf16[4,512,128]{2,1,0:T(8,128)(2,1)S(1)}, u32[]{:S(2)}, u32[]{:S(2)}) collective-permute-start(bf16[4,512,128]{2,1,0:T(8,128)(2,1)S(1)} %select_add_fusion.xk0), channel_id=1, source_target_pairs={{0,4},{2,6},{4,0},{6,2},{1,5},{3,7},{5,1},{7,3},{8,12},{10,14},{12... | collective-permute-start | bytes 1572872 | tf_op jit(solution)/shard_map/ppermute | solution.py:261
  40.4 2.6 %collective-permute-start.13 = (bf16[4,256,512]{2,1,0:T(8,128)(2,1)S(1)}, bf16[4,256,512]{2,1,0:T(8,128)(2,1)S(1)}, u32[]{:S(2)}, u32[]{:S(2)}) collective-permute-start(bf16[4,256,512]{2,1,0:T(8,128)(2,1)S(1)} %collective-permute-done.12.rest_4_), channel_id=1, source_target_pairs={{0,8},{8,0},{1,9},{9,1},{2,10},{10,2},{3,11},{11,3},{4,12},{12,4},... | collective-permute-start | bytes 3145736 | tf_op jit(solution)/shard_map/ppermute | solution.py:265
  43.9 3.6 %collective-permute-start.4 = (bf16[4,512,128]{2,1,0:T(8,128)(2,1)S(1)}, bf16[4,512,128]{2,1,0:T(8,128)(2,1)S(1)}, u32[]{:S(2)}, u32[]{:S(2)}) collective-permute-start(bf16[4,512,128]{2,1,0:T(8,128)(2,1)S(1)} %select_add_fusion.xk0), channel_id=1, source_target_pairs={{0,6},{2,0},{4,2},{6,4},{1,7},{3,1},{5,3},{7,5},{8,14},{10,8},{12,... | collective-permute-start | bytes 1572872 | tf_op jit(solution)/shard_map/ppermute | solution.py:261
  47.5 2.7 %collective-permute-start.11 = (bf16[4,256,512]{2,1,0:T(8,128)(2,1)S(1)}, bf16[4,256,512]{2,1,0:T(8,128)(2,1)S(1)}, u32[]{:S(2)}, u32[]{:S(2)}) collective-permute-start(bf16[4,256,512]{2,1,0:T(8,128)(2,1)S(1)} %collective-permute-done.10.rest_2_), channel_id=1, source_target_pairs={{0,8},{8,0},{1,9},{9,1},{2,10},{10,2},{3,11},{11,3},{4,12},{12,4},... | collective-permute-start | bytes 3145736 | tf_op jit(solution)/shard_map/ppermute | solution.py:265
  50.2 4.4 %collective-permute-start = (bf16[4,512,128]{2,1,0:T(8,128)(2,1)S(1)}, bf16[4,512,128]{2,1,0:T(8,128)(2,1)S(1)}, u32[]{:S(2)}, u32[]{:S(2)}) collective-permute-start(bf16[4,512,128]{2,1,0:T(8,128)(2,1)S(1)} %copy-done), channel_id=1, source_target_pairs={{0,1},{17,16},{2,3},{19,18},{4,5},{21,20},{6,7},{23,22},{8,9},{25,... | collective-permute-start | bytes 1572872 | tf_op jit(solution)/shard_map/ppermute | solution.py:285
  54.6 6.9 %collective-permute-done.5.xk2 = bf16[4,512,128]{2,1,0:T(8,128)(2,1)S(1)} collective-permute-done((bf16[4,512,128]{2,1,0:T(8,128)(2,1)S(1)}, bf16[4,512,128]{2,1,0:T(8,128)(2,1)S(1)}, u32[]{:S(2)}, u32[]{:S(2)}) %collective-permute-start.5) | collective-permute-done | bytes 524320 | tf_op jit(solution)/shard_map/ppermute | solution.py:261
  61.5 3.0 %collective-permute-start.15 = (bf16[2,256,512]{2,1,0:T(8,128)(2,1)S(1)}, bf16[2,256,512]{2,1,0:T(8,128)(2,1)S(1)}, u32[]{:S(2)}, u32[]{:S(2)}) collective-permute-start(bf16[2,256,512]{2,1,0:T(8,128)(2,1)S(1)} %collective-permute-done.14.rest_6_), channel_id=1, source_target_pairs={{0,8},{8,0},{1,9},{9,1},{2,10},{10,2},{3,11},{11,3},{4,12},{12,4},... | collective-permute-start | bytes 1572872 | tf_op jit(solution)/shard_map/ppermute | solution.py:265
  68.3 2.9 %collective-permute-start.9 = (bf16[4,512,128]{2,1,0:T(8,128)(2,1)S(1)}, bf16[4,512,128]{2,1,0:T(8,128)(2,1)S(1)}, u32[]{:S(2)}, u32[]{:S(2)}) collective-permute-start(bf16[4,512,128]{2,1,0:T(8,128)(2,1)S(1)} %add_add_fusion.xk0), channel_id=1, source_target_pairs={{0,2},{2,4},{4,6},{6,0},{1,3},{3,5},{5,7},{7,1},{8,10},{10,12},{12... | collective-permute-start | bytes 1572872 | tf_op jit(solution)/shard_map/ppermute | solution.py:261
  71.2 2.6 %collective-permute-start.8 = (bf16[4,512,128]{2,1,0:T(8,128)(2,1)S(1)}, bf16[4,512,128]{2,1,0:T(8,128)(2,1)S(1)}, u32[]{:S(2)}, u32[]{:S(2)}) collective-permute-start(bf16[4,512,128]{2,1,0:T(8,128)(2,1)S(1)} %add_add_fusion.xk0), channel_id=1, source_target_pairs={{0,4},{2,6},{4,0},{6,2},{1,5},{3,7},{5,1},{7,3},{8,12},{10,14},{12... | collective-permute-start | bytes 1572872 | tf_op jit(solution)/shard_map/ppermute | solution.py:261
  73.7 2.0 %collective-permute-start.7 = (bf16[4,512,128]{2,1,0:T(8,128)(2,1)S(1)}, bf16[4,512,128]{2,1,0:T(8,128)(2,1)S(1)}, u32[]{:S(2)}, u32[]{:S(2)}) collective-permute-start(bf16[4,512,128]{2,1,0:T(8,128)(2,1)S(1)} %add_add_fusion.xk0), channel_id=1, source_target_pairs={{0,6},{2,0},{4,2},{6,4},{1,7},{3,1},{5,3},{7,5},{8,14},{10,8},{12,... | collective-permute-start | bytes 1572872 | tf_op jit(solution)/shard_map/ppermute | solution.py:261
  75.7 21.3 %attend.3 = bf16[4,144,512]{2,1,0:T(8,128)(2,1)S(1)} custom-call(bf16[4,512,128]{2,1,0:T(8,128)(2,1)S(1)} %collective-permute-done.1.xq, bf16[4,512,128]{2,1,0:T(8,128)(2,1)S(1)} %select_add_fusion.xk0, bf16[4,512,128]{2,1,0:T(8,128)(2,1)S(1)} %collective-permute-done.4.xk1, bf16[4,512,128]{2,1,0:T(8,128)(2,1)S(1)} %collective-permute-done.5.xk2, ...), custom_call_target="tpu_custom_call" | custom-call | flops 8589934592 | bytes 16777216 | tf_op jit(solution)/shard_map/attend/pallas_call | solution.py:179
  98.2 20.7 %attend.2.mine = f32[4,144,512]{2,1,0:T(8,128)S(1)} custom-call(bf16[4,512,128]{2,1,0:T(8,128)(2,1)S(1)} %copy-done, bf16[4,512,128]{2,1,0:T(8,128)(2,1)S(1)} %add_add_fusion.xk0, bf16[4,512,128]{2,1,0:T(8,128)(2,1)S(1)} %collective-permute-done.7.xk1, bf16[4,512,128]{2,1,0:T(8,128)(2,1)S(1)} %collective-permute-done.8.xk2, ...), custom_call_target="tpu_custom_call" | custom-call | flops 8589934592 | bytes 16777216 | tf_op jit(solution)/shard_map/attend/pallas_call | solution.py:179
  118.9 1.8 %update.1 = bf16[16,4,32,128]{3,2,1,0:T(8,128)(2,1)S(1)} custom-call(bf16[4,512,128]{2,1,0:T(8,128)(2,1)S(1)} %copy-done, bf16[128,512]{1,0:T(8,128)(2,1)S(1)} %copy-done.1, bf16[128,128]{1,0:T(8,128)(2,1)S(1)} %copy-done.2, f32[4,144,512]{2,1,0:T(8,128)S(1)} %attend.2.mine, bf16[4,144,512]{2,1,0:T(8,128)(2,1)S(1)} %collective-permute-done.18.theirs), custom_call_target="tpu_custom_call" | custom-call | tf_op jit(solution)/shard_map/update/pallas_call | solution.py:227
  120.8 21.2 %all_to_all.5.update = bf16[16,4,32,128]{3,2,1,0:T(8,128)(2,1)} all-to-all(bf16[16,4,32,128]{3,2,1,0:T(8,128)(2,1)S(1)} %update.1), channel_id=1, replica_groups=mesh['y'=4,'xh'=2,'core'=2,'z'=4,'xl'=2] {'y','xh','core'}, dimensions={0} | all-to-all | bytes 1048576 | tf_op jit(solution)/shard_map/all_to_all | solution.py:295
  141.9 3.3 %reorder.1 = bf16[32,64,128]{2,1,0:T(8,128)(2,1)} custom-call(bf16[16,4,32,128]{3,2,1,0:T(8,128)(2,1)} %all_to_all.5.update), custom_call_target="tpu_custom_call" | custom-call | tf_op jit(solution)/shard_map/reorder/pallas_call | solution.py:244
  (36 shorter events, 5.1 us)
Async XLA Ops:
  4.1 26.5 %collective-permute-start.12 = (bf16[4,256,512]{2,1,0:T(8,128)(2,1)}, bf16[4,256,512]{2,1,0:T(8,128)(2,1)S(1)}, u32[]{:S(2)}, u32[]{:S(2)}) collective-permute-start(bf16[4,256,512]{2,1,0:T(8,128)(2,1)} %get-tuple-element.8.rest_0_), channel_id=1, source_target_pairs={{0,32},{32,64},{64,96},{96,0},{1,33},{33,65},{65,97},{97,1},{2,34}... | collective-permute-start | bytes 3145736 | tf_op jit(solution)/shard_map/ppermute | solution.py:261
  6.2 24.5 %collective-permute-start.10 = (bf16[4,256,512]{2,1,0:T(8,128)(2,1)}, bf16[4,256,512]{2,1,0:T(8,128)(2,1)S(1)}, u32[]{:S(2)}, u32[]{:S(2)}) collective-permute-start(bf16[4,256,512]{2,1,0:T(8,128)(2,1)} %get-tuple-element.8.rest_0_), channel_id=1, source_target_pairs={{0,96},{32,0},{64,32},{96,64},{1,97},{33,1},{65,33},{97,65},{2,98}... | collective-permute-start | bytes 3145736 | tf_op jit(solution)/shard_map/ppermute | solution.py:261
  7.7 25.8 %collective-permute-start.3 = (bf16[4,256,512]{2,1,0:T(8,128)(2,1)}, bf16[4,256,512]{2,1,0:T(8,128)(2,1)}, u32[]{:S(2)}, u32[]{:S(2)}) collective-permute-start(bf16[4,256,512]{2,1,0:T(8,128)(2,1)} %get-tuple-element.8.rest_0_), channel_id=1, source_target_pairs={{0,8},{8,0},{1,9},{9,1},{2,10},{10,2},{3,11},{11,3},{4,12},{12,4},... | collective-permute-start | bytes 3145736 | tf_op jit(solution)/shard_map/ppermute | solution.py:265
  8.7 26.6 %collective-permute-start.2 = (bf16[4,512,128]{2,1,0:T(8,128)(2,1)}, bf16[4,512,128]{2,1,0:T(8,128)(2,1)}, u32[]{:S(2)}, u32[]{:S(2)}) collective-permute-start(bf16[4,512,128]{2,1,0:T(8,128)(2,1)} %get-tuple-element.7.xq.x), channel_id=1, source_target_pairs={{1,16},{16,1},{3,18},{18,3},{5,20},{20,5},{7,22},{22,7},{9,24},{24... | collective-permute-start | bytes 1572872 | tf_op jit(solution)/shard_map/ppermute | solution.py:284
  10.2 25.2 %collective-permute-start.1 = (bf16[4,512,128]{2,1,0:T(8,128)(2,1)}, bf16[4,512,128]{2,1,0:T(8,128)(2,1)S(1)}, u32[]{:S(2)}, u32[]{:S(2)}) collective-permute-start(bf16[4,512,128]{2,1,0:T(8,128)(2,1)} %get-tuple-element.7.xq.x), channel_id=1, source_target_pairs={{0,16},{16,0},{1,17},{17,1},{2,18},{18,2},{3,19},{19,3},{4,20},{20... | collective-permute-start | bytes 1572872 | tf_op jit(solution)/shard_map/ppermute | solution.py:283
  30.6 19.6 %copy-start = (bf16[4,512,128]{2,1,0:T(8,128)(2,1)S(1)}, bf16[4,512,128]{2,1,0:T(8,128)(2,1)}, u32[]{:S(2)}) copy-start(bf16[4,512,128]{2,1,0:T(8,128)(2,1)} %get-tuple-element.7.xq.x) | copy-start | bytes 1572868
  30.6 13.3 %collective-permute-start.14 = (bf16[2,256,512]{2,1,0:T(8,128)(2,1)S(1)}, bf16[2,256,512]{2,1,0:T(8,128)(2,1)S(1)}, u32[]{:S(2)}, u32[]{:S(2)}) collective-permute-start(bf16[2,256,512]{2,1,0:T(8,128)(2,1)S(1)} %slice.28), channel_id=1, source_target_pairs={{0,32},{32,64},{64,96},{96,0},{1,33},{33,65},{65,97},{97,1},{2,34}... | collective-permute-start | bytes 1572872 | tf_op jit(solution)/shard_map/ppermute | solution.py:261
  30.8 16.8 %collective-permute-start.16 = (bf16[2,256,512]{2,1,0:T(8,128)(2,1)S(1)}, bf16[2,256,512]{2,1,0:T(8,128)(2,1)S(1)}, u32[]{:S(2)}, u32[]{:S(2)}) collective-permute-start(bf16[2,256,512]{2,1,0:T(8,128)(2,1)S(1)} %slice.29), channel_id=1, source_target_pairs={{0,96},{32,0},{64,32},{96,64},{1,97},{33,1},{65,33},{97,65},{2,98}... | collective-permute-start | bytes 1572872 | tf_op jit(solution)/shard_map/ppermute | solution.py:261
  35.5 40.3 %copy-start.1 = (bf16[128,512]{1,0:T(8,128)(2,1)S(1)}, bf16[128,512]{1,0:T(8,128)(2,1)}, u32[]{:S(2)}) copy-start(bf16[128,512]{1,0:T(8,128)(2,1)} %w.5) | copy-start | bytes 393220
  35.5 40.3 %copy-start.3 = (bf16[4,256,512]{2,1,0:T(8,128)(2,1)S(1)}, bf16[4,256,512]{2,1,0:T(8,128)(2,1)}, u32[]{:S(2)}) copy-start(bf16[4,256,512]{2,1,0:T(8,128)(2,1)} %get-tuple-element.8.rest_0_) | copy-start | bytes 3145732
  35.5 14.7 %collective-permute-start.6 = (bf16[4,512,128]{2,1,0:T(8,128)(2,1)S(1)}, bf16[4,512,128]{2,1,0:T(8,128)(2,1)S(1)}, u32[]{:S(2)}, u32[]{:S(2)}) collective-permute-start(bf16[4,512,128]{2,1,0:T(8,128)(2,1)S(1)} %select_add_fusion.xk0), channel_id=1, source_target_pairs={{0,2},{2,4},{4,6},{6,0},{1,3},{3,5},{5,7},{7,1},{8,10},{10,12},{12... | collective-permute-start | bytes 1572872 | tf_op jit(solution)/shard_map/ppermute | solution.py:261
  37.1 24.5 %collective-permute-start.5 = (bf16[4,512,128]{2,1,0:T(8,128)(2,1)S(1)}, bf16[4,512,128]{2,1,0:T(8,128)(2,1)S(1)}, u32[]{:S(2)}, u32[]{:S(2)}) collective-permute-start(bf16[4,512,128]{2,1,0:T(8,128)(2,1)S(1)} %select_add_fusion.xk0), channel_id=1, source_target_pairs={{0,4},{2,6},{4,0},{6,2},{1,5},{3,7},{5,1},{7,3},{8,12},{10,14},{12... | collective-permute-start | bytes 1572872 | tf_op jit(solution)/shard_map/ppermute | solution.py:261
  40.4 33.4 %collective-permute-start.13 = (bf16[4,256,512]{2,1,0:T(8,128)(2,1)S(1)}, bf16[4,256,512]{2,1,0:T(8,128)(2,1)S(1)}, u32[]{:S(2)}, u32[]{:S(2)}) collective-permute-start(bf16[4,256,512]{2,1,0:T(8,128)(2,1)S(1)} %collective-permute-done.12.rest_4_), channel_id=1, source_target_pairs={{0,8},{8,0},{1,9},{9,1},{2,10},{10,2},{3,11},{11,3},{4,12},{12,4},... | collective-permute-start | bytes 3145736 | tf_op jit(solution)/shard_map/ppermute | solution.py:265
  43.9 20.6 %collective-permute-start.4 = (bf16[4,512,128]{2,1,0:T(8,128)(2,1)S(1)}, bf16[4,512,128]{2,1,0:T(8,128)(2,1)S(1)}, u32[]{:S(2)}, u32[]{:S(2)}) collective-permute-start(bf16[4,512,128]{2,1,0:T(8,128)(2,1)S(1)} %select_add_fusion.xk0), channel_id=1, source_target_pairs={{0,6},{2,0},{4,2},{6,4},{1,7},{3,1},{5,3},{7,5},{8,14},{10,8},{12,... | collective-permute-start | bytes 1572872 | tf_op jit(solution)/shard_map/ppermute | solution.py:261
  47.5 28.2 %collective-permute-start.11 = (bf16[4,256,512]{2,1,0:T(8,128)(2,1)S(1)}, bf16[4,256,512]{2,1,0:T(8,128)(2,1)S(1)}, u32[]{:S(2)}, u32[]{:S(2)}) collective-permute-start(bf16[4,256,512]{2,1,0:T(8,128)(2,1)S(1)} %collective-permute-done.10.rest_2_), channel_id=1, source_target_pairs={{0,8},{8,0},{1,9},{9,1},{2,10},{10,2},{3,11},{11,3},{4,12},{12,4},... | collective-permute-start | bytes 3145736 | tf_op jit(solution)/shard_map/ppermute | solution.py:265
  50.2 18.0 %collective-permute-start = (bf16[4,512,128]{2,1,0:T(8,128)(2,1)S(1)}, bf16[4,512,128]{2,1,0:T(8,128)(2,1)S(1)}, u32[]{:S(2)}, u32[]{:S(2)}) collective-permute-start(bf16[4,512,128]{2,1,0:T(8,128)(2,1)S(1)} %copy-done), channel_id=1, source_target_pairs={{0,1},{17,16},{2,3},{19,18},{4,5},{21,20},{6,7},{23,22},{8,9},{25,... | collective-permute-start | bytes 1572872 | tf_op jit(solution)/shard_map/ppermute | solution.py:285
  61.5 9.6 %collective-permute-start.15 = (bf16[2,256,512]{2,1,0:T(8,128)(2,1)S(1)}, bf16[2,256,512]{2,1,0:T(8,128)(2,1)S(1)}, u32[]{:S(2)}, u32[]{:S(2)}) collective-permute-start(bf16[2,256,512]{2,1,0:T(8,128)(2,1)S(1)} %collective-permute-done.14.rest_6_), channel_id=1, source_target_pairs={{0,8},{8,0},{1,9},{9,1},{2,10},{10,2},{3,11},{11,3},{4,12},{12,4},... | collective-permute-start | bytes 1572872 | tf_op jit(solution)/shard_map/ppermute | solution.py:265
  64.5 11.2 %collective-permute-start.17 = (bf16[2,256,512]{2,1,0:T(8,128)(2,1)S(1)}, bf16[2,256,512]{2,1,0:T(8,128)(2,1)S(1)}, u32[]{:S(2)}, u32[]{:S(2)}) collective-permute-start(bf16[2,256,512]{2,1,0:T(8,128)(2,1)S(1)} %collective-permute-done.16.rest_8_), channel_id=1, source_target_pairs={{0,8},{8,0},{1,9},{9,1},{2,10},{10,2},{3,11},{11,3},{4,12},{12,4},... | collective-permute-start | bytes 1572872 | tf_op jit(solution)/shard_map/ppermute | solution.py:265
  68.3 29.9 %collective-permute-start.9 = (bf16[4,512,128]{2,1,0:T(8,128)(2,1)S(1)}, bf16[4,512,128]{2,1,0:T(8,128)(2,1)S(1)}, u32[]{:S(2)}, u32[]{:S(2)}) collective-permute-start(bf16[4,512,128]{2,1,0:T(8,128)(2,1)S(1)} %add_add_fusion.xk0), channel_id=1, source_target_pairs={{0,2},{2,4},{4,6},{6,0},{1,3},{3,5},{5,7},{7,1},{8,10},{10,12},{12... | collective-permute-start | bytes 1572872 | tf_op jit(solution)/shard_map/ppermute | solution.py:261
  71.2 27.0 %collective-permute-start.8 = (bf16[4,512,128]{2,1,0:T(8,128)(2,1)S(1)}, bf16[4,512,128]{2,1,0:T(8,128)(2,1)S(1)}, u32[]{:S(2)}, u32[]{:S(2)}) collective-permute-start(bf16[4,512,128]{2,1,0:T(8,128)(2,1)S(1)} %add_add_fusion.xk0), channel_id=1, source_target_pairs={{0,4},{2,6},{4,0},{6,2},{1,5},{3,7},{5,1},{7,3},{8,12},{10,14},{12... | collective-permute-start | bytes 1572872 | tf_op jit(solution)/shard_map/ppermute | solution.py:261
  73.7 24.4 %collective-permute-start.7 = (bf16[4,512,128]{2,1,0:T(8,128)(2,1)S(1)}, bf16[4,512,128]{2,1,0:T(8,128)(2,1)S(1)}, u32[]{:S(2)}, u32[]{:S(2)}) collective-permute-start(bf16[4,512,128]{2,1,0:T(8,128)(2,1)S(1)} %add_add_fusion.xk0), channel_id=1, source_target_pairs={{0,6},{2,0},{4,2},{6,4},{1,7},{3,1},{5,3},{7,5},{8,14},{10,8},{12,... | collective-permute-start | bytes 1572872 | tf_op jit(solution)/shard_map/ppermute | solution.py:261
  97.1 21.8 %copy-start.2 = (bf16[128,128]{1,0:T(8,128)(2,1)S(1)}, bf16[128,128]{1,0:T(8,128)(2,1)}, u32[]{:S(2)}) copy-start(bf16[128,128]{1,0:T(8,128)(2,1)} %w_out.1) | copy-start | bytes 98308
  97.1 21.8 %collective-permute-start.18 = (bf16[4,144,512]{2,1,0:T(8,128)(2,1)S(1)}, bf16[4,144,512]{2,1,0:T(8,128)(2,1)S(1)}, u32[]{:S(2)}, u32[]{:S(2)}) collective-permute-start(bf16[4,144,512]{2,1,0:T(8,128)(2,1)S(1)} %attend.3), channel_id=1, source_target_pairs={{0,16},{16,0},{1,17},{17,1},{2,18},{18,2},{3,19},{19,3},{4,20},{20... | collective-permute-start | bytes 1769480 | tf_op jit(solution)/shard_map/ppermute | solution.py:292

commit v8 on v7

--- a/solution.py
+++ b/solution.py
@@ -1,3 +1,5 @@
+import functools
+
 import jax
 import jax.numpy as jnp
 from jax import lax
@@ -29,21 +31,22 @@
     keys = bias.shape[2]
     places = [lax.broadcasted_iota(jnp.int32, (keys, keys), axis) for axis in (0, 1)]
     identity = (places[0] == places[1]).astype(F32).astype(BF16)
-    values = pair[0].astype(F32)
+    values = pair[...].astype(F32)
     centered = values - jnp.mean(values, axis=-1, keepdims=True)
     variance = jnp.mean(centered * centered, axis=-1, keepdims=True)
-    normed[0] = (centered * lax.rsqrt(variance + 1e-05) * gain[...]).astype(BF16)
-    bias_t[0] = matmul(identity, bias[0], 1, 1).astype(BF16)
+    normed[...] = (centered * lax.rsqrt(variance + 1e-05) * gain[...]).astype(BF16)
+    for h in range(bias.shape[0]):
+        bias_t[h] = matmul(identity, bias[h], 1, 1).astype(BF16)
 
 
 def prepare(pair_block, norm_gain, head_bias):
     def whole(*shape):
-        return pl.BlockSpec((1,) + shape, lambda i: (i, 0, 0))
+        return pl.BlockSpec((2,) + shape, lambda i: (i, 0, 0))
 
     keys = head_bias.shape[2]
     return pl.pallas_call(
         prepare_kernel,
-        grid=(ROWS,),
+        grid=(ROWS // 2,),
         in_specs=[
             whole(COLS, CHANNELS),
             pl.BlockSpec((1, CHANNELS), lambda i: (0, 0)),
@@ -58,7 +61,8 @@
     )(pair_block, norm_gain.reshape(1, CHANNELS), head_bias)
 
 
-def attend_kernel(xq, xk0, xk1, xk2, xk3, w, *rest):
+def attend_kernel(blocks, xq, *rest):
+    xks, w, rest = rest[:blocks], rest[blocks], rest[blocks + 1 :]
     biases, out, (bias_s, top_s, k_s, v_s, q_s, sems) = rest[:10], rest[10], rest[11:]
     step = pl.program_id(0)
     y, z, core = lax.axis_index("y"), lax.axis_index("z"), lax.axis_index("core")
@@ -88,7 +92,7 @@
             at = slice(h * WIDTH, (h + 1) * WIDTH)
             q_s[r, h, at, :] = q_t[at]
         start = 0
-        for x in (xk0, xk1, xk2, xk3):
+        for x in xks:
             size = x.shape[1]
             at = slice(start, start + size)
             k_s[r, at, :] = matmul(x[r], w[:, 128:256]).astype(BF16)
@@ -177,7 +181,7 @@
 
     scores = ROWS * HEADS * COLS * KEYS
     return pl.pallas_call(
-        attend_kernel,
+        functools.partial(attend_kernel, len(x_ks)),
         grid=(ROWS // STEP,),
         in_specs=[rows(x_q)]
         + [rows(x) for x in x_ks]
@@ -235,22 +239,6 @@
     )(x, w_project, w_out, mine, theirs)
 
 
-def reorder_kernel(update, out):
-    rows = update[...].astype(F32).reshape(4 * ROWS, SHARE, CHANNELS)
-    out[...] = jnp.swapaxes(rows, 0, 1).astype(BF16)
-
-
-def reorder(update):
-    return pl.pallas_call(
-        reorder_kernel,
-        grid=(4,),
-        in_specs=[pl.BlockSpec((4,) + update.shape[1:], lambda y: (y, 0, 0, 0))],
-        out_specs=pl.BlockSpec((SHARE, 4 * ROWS, CHANNELS), lambda y: (0, y, 0)),
-        out_shape=jax.ShapeDtypeStruct((SHARE, 16 * ROWS, CHANNELS), BF16),
-        name="reorder",
-    )(update)
-
-
 def tied(x, *before):
     for array in before:
         x = x + 0 * array[(0,) * array.ndim]
@@ -266,33 +254,42 @@
 
 
 def gather_direct(x, axis):
-    return x, shift(x, axis, -1), shift(x, axis, 2), shift(x, axis, 1)
-
-
-def gather_bias(block):
-    behind, ahead = shift(block, "y", 1), shift(block, "y", -1)
-    far = [shift(behind[:2], "y", 1), shift(ahead[2:], "y", -1)]
-    return [side for b in (block, ahead, behind, *far) for side in (b, swap(b))]
+    far = shift(x, axis, 2)
+    return x, shift(x, axis, -1), far, shift(x, axis, 1)
+
+
+def gather_ring(x, axis):
+    behind, ahead = shift(x, axis, 1), shift(x, axis, -1)
+    parts = tied(behind[:, :256], ahead), tied(ahead[:, 256:], behind)
+    far = shift(parts[0], axis, 1), shift(parts[1], axis, -1)
+    return x, ahead, *far, behind
 
 
 def shards(pair_block, norm_gain, w_project, w_out, head_bias):
     own, bias_t = prepare(pair_block, norm_gain, head_bias)
-    biases = gather_bias(bias_t)
+    bias_own = bias_t, swap(bias_t)
+    behind, ahead = shift(bias_t, "y", 1), shift(bias_t, "y", -1)
 
     xh, xl = lax.axis_index("xh"), lax.axis_index("xl")
     opposite = lax.ppermute(own, "xh", [(0, 1), (1, 0)])
     across = lax.ppermute(own, ("xh", "xl"), [(1, 2), (2, 1)])
     beside = lax.ppermute(own, ("xh", "xl"), [(0, 1), (3, 2)])
-    their_k = tied(jnp.where(xl == xh, opposite, across), biases[1])
-    their_ks = gather_direct(their_k, "z")
-    own_k = tied(jnp.where(xl == xh, own, beside), *their_ks[1:])
+    their_k = tied(jnp.where(xl == xh, opposite, across), bias_own[1])
+    their_ks = gather_ring(their_k, "z")
+    own_k = tied(jnp.where(xl == xh, own, beside), their_ks[1], their_ks[4])
     own_ks = gather_direct(own_k, "z")
+
+    far = shift(behind[:2], "y", 1), shift(ahead[2:], "y", -1)
+    biases = [*bias_own]
+    for block in (ahead, behind, *far):
+        biases += [block, swap(block)]
 
     theirs = attend(opposite, their_ks, w_project, biases, BF16)
     theirs = lax.ppermute(theirs, "xh", [(0, 1), (1, 0)])
     mine = attend(own, own_ks, w_project, biases, F32)
     update = update_rows(own, w_project, w_out, mine, theirs)
-    return reorder(lax.all_to_all(update, ROW_AXES, split_axis=0, concat_axis=0, tiled=True))
+    update = lax.all_to_all(update, ROW_AXES, split_axis=0, concat_axis=0, tiled=True)
+    return jnp.transpose(update, (2, 0, 1, 3)).reshape(SHARE, 16 * ROWS, CHANNELS)
 
 
 def solution(mesh):

time: 146 us -> 143 us (0.979)
  starting transfers between devices: 42.1 us -> 47.1 us
  Pallas kernels: 51.2 us -> 46.7 us
  blocking collectives: 21.2 us -> 18.9 us
    ppermute x10 -> x11, waiting for transfers between devices: 24.7 us -> 12.6 us  [shift(): return lax.ppermute(x, axis, [(i, (i + step) % 4) for i in range(4)])]
    ppermute x1, starting transfers between devices: 4.42 us -> 13.9 us  [shards(): beside = lax.ppermute(own, ('xh', 'xl'), [(0, 1), (3, 2)])]
    ppermute x10 -> x11, starting transfers between devices: 22.3 us -> 13.4 us  [shift(): return lax.ppermute(x, axis, [(i, (i + step) % 4) for i in range(4)])]
    ppermute x1, waiting for transfers between devices: 0.01 us -> 7.54 us  [shards(): opposite = lax.ppermute(own, 'xh', [(0, 1), (1, 0)])]
    ppermute x1, starting transfers between devices: 1.03 us -> 8.11 us  [shards(): theirs = lax.ppermute(theirs, 'xh', [(0, 1), (1, 0)])]
    pallas_call x4 -> x3, Pallas kernels: 49.4 us -> 44.9 us  [the longest x2 42.1 us: attend(): pl.pallas_call(functools.partial(attend_kernel, len(x_ks)), grid=(ROWS //...]
    ppermute x1, waiting for transfers between devices: 0.01 us -> 3.67 us  [shards(): beside = lax.ppermute(own, ('xh', 'xl'), [(0, 1), (3, 2)])]
    ppermute x5, starting transfers between devices: 9.28 us -> 6.68 us  [swap(): return lax.ppermute(x, 'core', [(0, 1), (1, 0)])]
  transfers between devices with their start and end apart: 19 -> 20, of which waited for: 3 -> 5; matrix products, arithmetic and copies ran while one was open for 2% -> 2% of each run, Pallas kernels for 29% -> 30%
where the time goes in v8:
time: 143 us; the launch traced here: 142 us
  starting transfers between devices  47.1 us (33%)
  Pallas kernels  46.7 us (33%)
  waiting for transfers between devices  23.8 us (17%)
  blocking collectives  18.9 us (13%)
  local copies, waits for them, and re-layouts  3.38 us (2%)
  between operations  2.19 us (2%)
    pallas_call x2, Pallas kernels, attend(): pl.pallas_call(functools.partial(attend_kernel, len(x_ks)), grid=(ROWS //...  42.1 us
    all_to_all x1, blocking collectives, shards(): lax.all_to_all(update, ROW_AXES, split_axis=0, concat_axis=0, tiled=True)  18.9 us
    ppermute x1, starting transfers between devices, shards(): beside = lax.ppermute(own, ('xh', 'xl'), [(0, 1), (3, 2)])  13.9 us
    ppermute x11, starting transfers between devices, shift(): return lax.ppermute(x, axis, [(i, (i + step) % 4) for i in range(4)])  13.4 us
    ppermute x11, waiting for transfers between devices, shift(): return lax.ppermute(x, axis, [(i, (i + step) % 4) for i in range(4)])  12.6 us
    ppermute x1, starting transfers between devices, shards(): theirs = lax.ppermute(theirs, 'xh', [(0, 1), (1, 0)])  8.11 us
    ppermute x1, waiting for transfers between devices, shards(): opposite = lax.ppermute(own, 'xh', [(0, 1), (1, 0)])  7.54 us
    ppermute x5, starting transfers between devices, swap(): return lax.ppermute(x, 'core', [(0, 1), (1, 0)])  6.68 us
  transfers between devices with their start and end apart: 20, of which 5 were waited for; matrix products, arithmetic and copies ran while one was open for 2% of the time, Pallas kernels for 30%

profile of v8, /device:TPU:1, one launch (start us, length us, event | category | flops | bytes accessed | tf_op | source)
XLA Modules:
  0.0 142.3 jit_solution(10374861635915068369)
XLA Ops:
  0.0 2.8 %prepare.1 = (bf16[4,512,128]{2,1,0:T(8,128)(2,1)}, bf16[4,256,512]{2,1,0:T(8,128)(2,1)}) custom-call(bf16[4,512,128]{2,1,0:T(8,128)(2,1)} %pair.1, f32[1,128]{1,0:T(1,128)} %bitcast.8, bf16[4,512,256]{2,1,0:T(8,128)(2,1)} %bias.1), custom_call_target="tpu_custom_call" | custom-call | tf_op jit(solution)/shard_map/prepare/pallas_call | solution.py:47
  2.8 1.4 collective-permute-start.3
  4.2 1.5 %collective-permute-start.2 = (bf16[4,512,128]{2,1,0:T(8,128)(2,1)}, bf16[4,512,128]{2,1,0:T(8,128)(2,1)}, u32[]{:S(2)}, u32[]{:S(2)}) collective-permute-start(bf16[4,512,128]{2,1,0:T(8,128)(2,1)} %get-tuple-element.7.xq.x), channel_id=1, source_target_pairs={{1,16},{16,1},{3,18},{18,3},{5,20},{20,5},{7,22},{22,7},{9,24},{24... | collective-permute-start | bytes 1572872 | tf_op jit(solution)/shard_map/ppermute | solution.py:275
  5.7 3.6 %collective-permute-start.1 = (bf16[4,512,128]{2,1,0:T(8,128)(2,1)}, bf16[4,512,128]{2,1,0:T(8,128)(2,1)S(1)}, u32[]{:S(2)}, u32[]{:S(2)}) collective-permute-start(bf16[4,512,128]{2,1,0:T(8,128)(2,1)} %get-tuple-element.7.xq.x), channel_id=1, source_target_pairs={{0,16},{16,0},{1,17},{17,1},{2,18},{18,2},{3,19},{19,3},{4,20},{20... | collective-permute-start | bytes 1572872 | tf_op jit(solution)/shard_map/ppermute | solution.py:274
  9.3 1.3 collective-permute-start.11
  10.6 1.4 %collective-permute-start.9 = (bf16[4,256,512]{2,1,0:T(8,128)(2,1)}, bf16[4,256,512]{2,1,0:T(8,128)(2,1)S(1)}, u32[]{:S(2)}, u32[]{:S(2)}) collective-permute-start(bf16[4,256,512]{2,1,0:T(8,128)(2,1)} %get-tuple-element.8.rest_5_.rest_6_), channel_id=1, source_target_pairs={{0,96},{32,0},{64,32},{96,64},{1,97},{33,1},{65,33},{97,65},{2,98}... | collective-permute-start | bytes 3145736 | tf_op jit(solution)/shard_map/ppermute | solution.py:249
  13.9 7.5 %collective-permute-done.1.xq = bf16[4,512,128]{2,1,0:T(8,128)(2,1)S(1)} collective-permute-done((bf16[4,512,128]{2,1,0:T(8,128)(2,1)}, bf16[4,512,128]{2,1,0:T(8,128)(2,1)S(1)}, u32[]{:S(2)}, u32[]{:S(2)}) %collective-permute-start.1) | collective-permute-done | bytes 524320 | tf_op jit(solution)/shard_map/ppermute | solution.py:274
  21.5 1.7 %collective-permute-start.5 = (bf16[4,512,128]{2,1,0:T(8,128)(2,1)S(1)}, bf16[4,512,128]{2,1,0:T(8,128)(2,1)S(1)}, u32[]{:S(2)}, u32[]{:S(2)}) collective-permute-start(bf16[4,512,128]{2,1,0:T(8,128)(2,1)S(1)} %select_add_fusion.rest_0_), channel_id=1, source_target_pairs={{0,2},{2,4},{4,6},{6,0},{1,3},{3,5},{5,7},{7,1},{8,10},{10,12},{12... | collective-permute-start | bytes 1572872 | tf_op jit(solution)/shard_map/ppermute | solution.py:249
  23.2 2.2 %collective-permute-start.4 = (bf16[4,512,128]{2,1,0:T(8,128)(2,1)S(1)}, bf16[4,512,128]{2,1,0:T(8,128)(2,1)S(1)}, u32[]{:S(2)}, u32[]{:S(2)}) collective-permute-start(bf16[4,512,128]{2,1,0:T(8,128)(2,1)S(1)} %select_add_fusion.rest_0_), channel_id=1, source_target_pairs={{0,6},{2,0},{4,2},{6,4},{1,7},{3,1},{5,3},{7,5},{8,14},{10,8},{12,... | collective-permute-start | bytes 1572872 | tf_op jit(solution)/shard_map/ppermute | solution.py:249
  25.4 13.9 %collective-permute-start = (bf16[4,512,128]{2,1,0:T(8,128)(2,1)S(1)}, bf16[4,512,128]{2,1,0:T(8,128)(2,1)S(1)}, u32[]{:S(2)}, u32[]{:S(2)}) collective-permute-start(bf16[4,512,128]{2,1,0:T(8,128)(2,1)S(1)} %copy-done), channel_id=1, source_target_pairs={{0,1},{17,16},{2,3},{19,18},{4,5},{21,20},{6,7},{23,22},{8,9},{25,... | collective-permute-start | bytes 1572872 | tf_op jit(solution)/shard_map/ppermute | solution.py:276
  39.3 1.4 collective-permute-start.13
  40.7 1.8 %collective-permute-start.12 = (bf16[4,256,512]{2,1,0:T(8,128)(2,1)S(1)}, bf16[4,256,512]{2,1,0:T(8,128)(2,1)S(1)}, u32[]{:S(2)}, u32[]{:S(2)}) collective-permute-start(bf16[4,256,512]{2,1,0:T(8,128)(2,1)S(1)} %collective-permute-done.11.rest_9_.rest_10_), channel_id=1, source_target_pairs={{0,8},{8,0},{1,9},{9,1},{2,10},{10,2},{3,11},{11,3},{4,12},{12,4},... | collective-permute-start | bytes 3145736 | tf_op jit(solution)/shard_map/ppermute | solution.py:253
  42.5 1.5 %collective-permute-start.15 = (bf16[2,256,512]{2,1,0:T(8,128)(2,1)S(1)}, bf16[2,256,512]{2,1,0:T(8,128)(2,1)S(1)}, u32[]{:S(2)}, u32[]{:S(2)}) collective-permute-start(bf16[2,256,512]{2,1,0:T(8,128)(2,1)S(1)} %slice.34), channel_id=1, source_target_pairs={{0,96},{32,0},{64,32},{96,64},{1,97},{33,1},{65,33},{97,65},{2,98}... | collective-permute-start | bytes 1572872 | tf_op jit(solution)/shard_map/ppermute | solution.py:249
  45.5 3.7 %collective-permute-done = bf16[4,512,128]{2,1,0:T(8,128)(2,1)S(1)} collective-permute-done((bf16[4,512,128]{2,1,0:T(8,128)(2,1)S(1)}, bf16[4,512,128]{2,1,0:T(8,128)(2,1)S(1)}, u32[]{:S(2)}, u32[]{:S(2)}) %collective-permute-start) | collective-permute-done | bytes 524320 | tf_op jit(solution)/shard_map/ppermute | solution.py:276
  50.3 2.3 %collective-permute-done.13.rest_11_.rest_12_ = bf16[2,256,512]{2,1,0:T(8,128)(2,1)S(1)} collective-permute-done((bf16[2,256,512]{2,1,0:T(8,128)(2,1)S(1)}, bf16[2,256,512]{2,1,0:T(8,128)(2,1)S(1)}, u32[]{:S(2)}, u32[]{:S(2)}) %collective-permute-start.13) | collective-permute-done | bytes 524320 | tf_op jit(solution)/shard_map/ppermute | solution.py:249
  52.6 2.4 %collective-permute-start.14 = (bf16[2,256,512]{2,1,0:T(8,128)(2,1)S(1)}, bf16[2,256,512]{2,1,0:T(8,128)(2,1)S(1)}, u32[]{:S(2)}, u32[]{:S(2)}) collective-permute-start(bf16[2,256,512]{2,1,0:T(8,128)(2,1)S(1)} %collective-permute-done.13.rest_11_.rest_12_), channel_id=1, source_target_pairs={{0,8},{8,0},{1,9},{9,1},{2,10},{10,2},{3,11},{11,3},{4,12},{12,4},... | collective-permute-start | bytes 1572872 | tf_op jit(solution)/shard_map/ppermute | solution.py:253
  58.4 9.1 %collective-permute-done.17.rest_2_ = bf16[4,256,128]{2,1,0:T(8,128)(2,1)S(1)} collective-permute-done((bf16[4,256,128]{2,1,0:T(8,128)(2,1)S(1)}, bf16[4,256,128]{2,1,0:T(8,128)(2,1)S(1)}, u32[]{:S(2)}, u32[]{:S(2)}) %collective-permute-start.17) | collective-permute-done | bytes 262176 | tf_op jit(solution)/shard_map/ppermute | solution.py:249
  67.5 1.3 collective-permute-start.7
  68.8 1.4 %collective-permute-start.6 = (bf16[4,512,128]{2,1,0:T(8,128)(2,1)S(1)}, bf16[4,512,128]{2,1,0:T(8,128)(2,1)S(1)}, u32[]{:S(2)}, u32[]{:S(2)}) collective-permute-start(bf16[4,512,128]{2,1,0:T(8,128)(2,1)S(1)} %add_add_fusion.rest_0_), channel_id=1, source_target_pairs={{0,6},{2,0},{4,2},{6,4},{1,7},{3,1},{5,3},{7,5},{8,14},{10,8},{12,... | collective-permute-start | bytes 1572872 | tf_op jit(solution)/shard_map/ppermute | solution.py:249
  70.3 21.3 %attend.3 = bf16[4,144,512]{2,1,0:T(8,128)(2,1)S(1)} custom-call(bf16[4,512,128]{2,1,0:T(8,128)(2,1)S(1)} %collective-permute-done.1.xq, bf16[4,512,128]{2,1,0:T(8,128)(2,1)S(1)} %select_add_fusion.rest_0_, bf16[4,512,128]{2,1,0:T(8,128)(2,1)S(1)} %collective-permute-done.4.rest_1_, bf16[4,256,128]{2,1,0:T(8,128)(2,1)S(1)} %collective-permute-done.17.rest_2_, ...), custom_call_target="tpu_custom_call" | custom-call | flops 8589934592 | bytes 16777216 | tf_op jit(solution)/shard_map/attend/pallas_call | solution.py:183
  91.7 8.1 %collective-permute-start.19 = (bf16[4,144,512]{2,1,0:T(8,128)(2,1)S(1)}, bf16[4,144,512]{2,1,0:T(8,128)(2,1)S(1)}, u32[]{:S(2)}, u32[]{:S(2)}) collective-permute-start(bf16[4,144,512]{2,1,0:T(8,128)(2,1)S(1)} %attend.3), channel_id=1, source_target_pairs={{0,16},{16,0},{1,17},{17,1},{2,18},{18,2},{3,19},{19,3},{4,20},{20... | collective-permute-start | bytes 1769480 | tf_op jit(solution)/shard_map/ppermute | solution.py:288
  99.8 20.7 %attend.2.mine = f32[4,144,512]{2,1,0:T(8,128)S(1)} custom-call(bf16[4,512,128]{2,1,0:T(8,128)(2,1)S(1)} %copy-done, bf16[4,512,128]{2,1,0:T(8,128)(2,1)S(1)} %add_add_fusion.rest_0_, bf16[4,512,128]{2,1,0:T(8,128)(2,1)S(1)} %collective-permute-done.6.rest_1_, bf16[4,512,128]{2,1,0:T(8,128)(2,1)S(1)} %collective-permute-done.7.rest_2_, ...), custom_call_target="tpu_custom_call" | custom-call | flops 8589934592 | bytes 16777216 | tf_op jit(solution)/shard_map/attend/pallas_call | solution.py:183
  120.5 1.8 %update.1 = bf16[16,4,32,128]{3,2,1,0:T(8,128)(2,1)S(1)} custom-call(bf16[4,512,128]{2,1,0:T(8,128)(2,1)S(1)} %copy-done, bf16[128,512]{1,0:T(8,128)(2,1)S(1)} %copy-done.1, bf16[128,128]{1,0:T(8,128)(2,1)S(1)} %copy-done.2, f32[4,144,512]{2,1,0:T(8,128)S(1)} %attend.2.mine, bf16[4,144,512]{2,1,0:T(8,128)(2,1)S(1)} %collective-permute-done.19.theirs), custom_call_target="tpu_custom_call" | custom-call | tf_op jit(solution)/shard_map/update/pallas_call | solution.py:231
  122.4 18.9 %all_to_all.5 = bf16[16,4,32,128]{3,2,1,0:T(8,128)(2,1)S(1)} all-to-all(bf16[16,4,32,128]{3,2,1,0:T(8,128)(2,1)S(1)} %update.1), channel_id=1, replica_groups=mesh['y'=4,'xh'=2,'core'=2,'z'=4,'xl'=2] {'y','xh','core'}, dimensions={0} | all-to-all | bytes 1048576 | tf_op jit(solution)/shard_map/all_to_all | solution.py:291
  (39 shorter events, 7.0 us)
Async XLA Ops:
  2.8 22.6 %copy-start = (bf16[4,512,128]{2,1,0:T(8,128)(2,1)S(1)}, bf16[4,512,128]{2,1,0:T(8,128)(2,1)}, u32[]{:S(2)}) copy-start(bf16[4,512,128]{2,1,0:T(8,128)(2,1)} %get-tuple-element.7.xq.x) | copy-start | bytes 1572868
  2.8 9.2 %collective-permute-start.3 = (bf16[4,256,512]{2,1,0:T(8,128)(2,1)}, bf16[4,256,512]{2,1,0:T(8,128)(2,1)}, u32[]{:S(2)}, u32[]{:S(2)}) collective-permute-start(bf16[4,256,512]{2,1,0:T(8,128)(2,1)} %get-tuple-element.8.rest_5_.rest_6_), channel_id=1, source_target_pairs={{0,8},{8,0},{1,9},{9,1},{2,10},{10,2},{3,11},{11,3},{4,12},{12,4},... | collective-permute-start | bytes 3145736 | tf_op jit(solution)/shard_map/ppermute | solution.py:253
  4.2 9.6 %collective-permute-start.2 = (bf16[4,512,128]{2,1,0:T(8,128)(2,1)}, bf16[4,512,128]{2,1,0:T(8,128)(2,1)}, u32[]{:S(2)}, u32[]{:S(2)}) collective-permute-start(bf16[4,512,128]{2,1,0:T(8,128)(2,1)} %get-tuple-element.7.xq.x), channel_id=1, source_target_pairs={{1,16},{16,1},{3,18},{18,3},{5,20},{20,5},{7,22},{22,7},{9,24},{24... | collective-permute-start | bytes 1572872 | tf_op jit(solution)/shard_map/ppermute | solution.py:275
  5.7 15.7 %collective-permute-start.1 = (bf16[4,512,128]{2,1,0:T(8,128)(2,1)}, bf16[4,512,128]{2,1,0:T(8,128)(2,1)S(1)}, u32[]{:S(2)}, u32[]{:S(2)}) collective-permute-start(bf16[4,512,128]{2,1,0:T(8,128)(2,1)} %get-tuple-element.7.xq.x), channel_id=1, source_target_pairs={{0,16},{16,0},{1,17},{17,1},{2,18},{18,2},{3,19},{19,3},{4,20},{20... | collective-permute-start | bytes 1572872 | tf_op jit(solution)/shard_map/ppermute | solution.py:274
  9.3 30.0 %collective-permute-start.11 = (bf16[4,256,512]{2,1,0:T(8,128)(2,1)}, bf16[4,256,512]{2,1,0:T(8,128)(2,1)S(1)}, u32[]{:S(2)}, u32[]{:S(2)}) collective-permute-start(bf16[4,256,512]{2,1,0:T(8,128)(2,1)} %get-tuple-element.8.rest_5_.rest_6_), channel_id=1, source_target_pairs={{0,32},{32,64},{64,96},{96,0},{1,33},{33,65},{65,97},{97,1},{2,34}... | collective-permute-start | bytes 3145736 | tf_op jit(solution)/shard_map/ppermute | solution.py:249
  10.6 30.1 %collective-permute-start.9 = (bf16[4,256,512]{2,1,0:T(8,128)(2,1)}, bf16[4,256,512]{2,1,0:T(8,128)(2,1)S(1)}, u32[]{:S(2)}, u32[]{:S(2)}) collective-permute-start(bf16[4,256,512]{2,1,0:T(8,128)(2,1)} %get-tuple-element.8.rest_5_.rest_6_), channel_id=1, source_target_pairs={{0,96},{32,0},{64,32},{96,64},{1,97},{33,1},{65,33},{97,65},{2,98}... | collective-permute-start | bytes 3145736 | tf_op jit(solution)/shard_map/ppermute | solution.py:249
  21.5 21.1 %collective-permute-start.5 = (bf16[4,512,128]{2,1,0:T(8,128)(2,1)S(1)}, bf16[4,512,128]{2,1,0:T(8,128)(2,1)S(1)}, u32[]{:S(2)}, u32[]{:S(2)}) collective-permute-start(bf16[4,512,128]{2,1,0:T(8,128)(2,1)S(1)} %select_add_fusion.rest_0_), channel_id=1, source_target_pairs={{0,2},{2,4},{4,6},{6,0},{1,3},{3,5},{5,7},{7,1},{8,10},{10,12},{12... | collective-permute-start | bytes 1572872 | tf_op jit(solution)/shard_map/ppermute | solution.py:249
  23.2 20.8 %collective-permute-start.4 = (bf16[4,512,128]{2,1,0:T(8,128)(2,1)S(1)}, bf16[4,512,128]{2,1,0:T(8,128)(2,1)S(1)}, u32[]{:S(2)}, u32[]{:S(2)}) collective-permute-start(bf16[4,512,128]{2,1,0:T(8,128)(2,1)S(1)} %select_add_fusion.rest_0_), channel_id=1, source_target_pairs={{0,6},{2,0},{4,2},{6,4},{1,7},{3,1},{5,3},{7,5},{8,14},{10,8},{12,... | collective-permute-start | bytes 1572872 | tf_op jit(solution)/shard_map/ppermute | solution.py:249
  25.4 23.8 %collective-permute-start = (bf16[4,512,128]{2,1,0:T(8,128)(2,1)S(1)}, bf16[4,512,128]{2,1,0:T(8,128)(2,1)S(1)}, u32[]{:S(2)}, u32[]{:S(2)}) collective-permute-start(bf16[4,512,128]{2,1,0:T(8,128)(2,1)S(1)} %copy-done), channel_id=1, source_target_pairs={{0,1},{17,16},{2,3},{19,18},{4,5},{21,20},{6,7},{23,22},{8,9},{25,... | collective-permute-start | bytes 1572872 | tf_op jit(solution)/shard_map/ppermute | solution.py:276
  39.3 13.3 %collective-permute-start.13 = (bf16[2,256,512]{2,1,0:T(8,128)(2,1)S(1)}, bf16[2,256,512]{2,1,0:T(8,128)(2,1)S(1)}, u32[]{:S(2)}, u32[]{:S(2)}) collective-permute-start(bf16[2,256,512]{2,1,0:T(8,128)(2,1)S(1)} %slice.33), channel_id=1, source_target_pairs={{0,32},{32,64},{64,96},{96,0},{1,33},{33,65},{65,97},{97,1},{2,34}... | collective-permute-start | bytes 1572872 | tf_op jit(solution)/shard_map/ppermute | solution.py:249
  40.7 28.1 %collective-permute-start.12 = (bf16[4,256,512]{2,1,0:T(8,128)(2,1)S(1)}, bf16[4,256,512]{2,1,0:T(8,128)(2,1)S(1)}, u32[]{:S(2)}, u32[]{:S(2)}) collective-permute-start(bf16[4,256,512]{2,1,0:T(8,128)(2,1)S(1)} %collective-permute-done.11.rest_9_.rest_10_), channel_id=1, source_target_pairs={{0,8},{8,0},{1,9},{9,1},{2,10},{10,2},{3,11},{11,3},{4,12},{12,4},... | collective-permute-start | bytes 3145736 | tf_op jit(solution)/shard_map/ppermute | solution.py:253
  42.5 13.6 %collective-permute-start.15 = (bf16[2,256,512]{2,1,0:T(8,128)(2,1)S(1)}, bf16[2,256,512]{2,1,0:T(8,128)(2,1)S(1)}, u32[]{:S(2)}, u32[]{:S(2)}) collective-permute-start(bf16[2,256,512]{2,1,0:T(8,128)(2,1)S(1)} %slice.34), channel_id=1, source_target_pairs={{0,96},{32,0},{64,32},{96,64},{1,97},{33,1},{65,33},{97,65},{2,98}... | collective-permute-start | bytes 1572872 | tf_op jit(solution)/shard_map/ppermute | solution.py:249
  44.0 26.3 %collective-permute-start.10 = (bf16[4,256,512]{2,1,0:T(8,128)(2,1)S(1)}, bf16[4,256,512]{2,1,0:T(8,128)(2,1)S(1)}, u32[]{:S(2)}, u32[]{:S(2)}) collective-permute-start(bf16[4,256,512]{2,1,0:T(8,128)(2,1)S(1)} %collective-permute-done.9.rest_7_.rest_8_), channel_id=1, source_target_pairs={{0,8},{8,0},{1,9},{9,1},{2,10},{10,2},{3,11},{11,3},{4,12},{12,4},... | collective-permute-start | bytes 3145736 | tf_op jit(solution)/shard_map/ppermute | solution.py:253
  45.5 24.8 %copy-start.1 = (bf16[128,512]{1,0:T(8,128)(2,1)S(1)}, bf16[128,512]{1,0:T(8,128)(2,1)}, u32[]{:S(2)}) copy-start(bf16[128,512]{1,0:T(8,128)(2,1)} %w.1) | copy-start | bytes 393220
  45.5 24.8 %copy-start.3 = (bf16[4,256,512]{2,1,0:T(8,128)(2,1)S(1)}, bf16[4,256,512]{2,1,0:T(8,128)(2,1)}, u32[]{:S(2)}) copy-start(bf16[4,256,512]{2,1,0:T(8,128)(2,1)} %get-tuple-element.8.rest_5_.rest_6_) | copy-start | bytes 3145732
  49.2 9.1 %collective-permute-start.18 = (bf16[4,256,128]{2,1,0:T(8,128)(2,1)S(1)}, bf16[4,256,128]{2,1,0:T(8,128)(2,1)S(1)}, u32[]{:S(2)}, u32[]{:S(2)}) collective-permute-start(bf16[4,256,128]{2,1,0:T(8,128)(2,1)S(1)} %slice_add_fusion), channel_id=1, source_target_pairs={{0,6},{2,0},{4,2},{6,4},{1,7},{3,1},{5,3},{7,5},{8,14},{10,8},{12,... | collective-permute-start | bytes 786440 | tf_op jit(solution)/shard_map/ppermute | solution.py:249
  52.6 14.9 %collective-permute-start.14 = (bf16[2,256,512]{2,1,0:T(8,128)(2,1)S(1)}, bf16[2,256,512]{2,1,0:T(8,128)(2,1)S(1)}, u32[]{:S(2)}, u32[]{:S(2)}) collective-permute-start(bf16[2,256,512]{2,1,0:T(8,128)(2,1)S(1)} %collective-permute-done.13.rest_11_.rest_12_), channel_id=1, source_target_pairs={{0,8},{8,0},{1,9},{9,1},{2,10},{10,2},{3,11},{11,3},{4,12},{12,4},... | collective-permute-start | bytes 1572872 | tf_op jit(solution)/shard_map/ppermute | solution.py:253
  56.2 14.1 %collective-permute-start.16 = (bf16[2,256,512]{2,1,0:T(8,128)(2,1)S(1)}, bf16[2,256,512]{2,1,0:T(8,128)(2,1)S(1)}, u32[]{:S(2)}, u32[]{:S(2)}) collective-permute-start(bf16[2,256,512]{2,1,0:T(8,128)(2,1)S(1)} %collective-permute-done.15.rest_13_.rest_14_), channel_id=1, source_target_pairs={{0,8},{8,0},{1,9},{9,1},{2,10},{10,2},{3,11},{11,3},{4,12},{12,4},... | collective-permute-start | bytes 1572872 | tf_op jit(solution)/shard_map/ppermute | solution.py:253
  58.3 9.2 %collective-permute-start.17 = (bf16[4,256,128]{2,1,0:T(8,128)(2,1)S(1)}, bf16[4,256,128]{2,1,0:T(8,128)(2,1)S(1)}, u32[]{:S(2)}, u32[]{:S(2)}) collective-permute-start(bf16[4,256,128]{2,1,0:T(8,128)(2,1)S(1)} %slice_add_fusion.1), channel_id=1, source_target_pairs={{0,2},{2,4},{4,6},{6,0},{1,3},{3,5},{5,7},{7,1},{8,10},{10,12},{12... | collective-permute-start | bytes 786440 | tf_op jit(solution)/shard_map/ppermute | solution.py:249
  67.5 32.3 %collective-permute-start.8 = (bf16[4,512,128]{2,1,0:T(8,128)(2,1)S(1)}, bf16[4,512,128]{2,1,0:T(8,128)(2,1)S(1)}, u32[]{:S(2)}, u32[]{:S(2)}) collective-permute-start(bf16[4,512,128]{2,1,0:T(8,128)(2,1)S(1)} %add_add_fusion.rest_0_), channel_id=1, source_target_pairs={{0,2},{2,4},{4,6},{6,0},{1,3},{3,5},{5,7},{7,1},{8,10},{10,12},{12... | collective-permute-start | bytes 1572872 | tf_op jit(solution)/shard_map/ppermute | solution.py:249
  67.5 32.3 %collective-permute-start.7 = (bf16[4,512,128]{2,1,0:T(8,128)(2,1)S(1)}, bf16[4,512,128]{2,1,0:T(8,128)(2,1)S(1)}, u32[]{:S(2)}, u32[]{:S(2)}) collective-permute-start(bf16[4,512,128]{2,1,0:T(8,128)(2,1)S(1)} %add_add_fusion.rest_0_), channel_id=1, source_target_pairs={{0,4},{2,6},{4,0},{6,2},{1,5},{3,7},{5,1},{7,3},{8,12},{10,14},{12... | collective-permute-start | bytes 1572872 | tf_op jit(solution)/shard_map/ppermute | solution.py:249
  68.8 30.9 %collective-permute-start.6 = (bf16[4,512,128]{2,1,0:T(8,128)(2,1)S(1)}, bf16[4,512,128]{2,1,0:T(8,128)(2,1)S(1)}, u32[]{:S(2)}, u32[]{:S(2)}) collective-permute-start(bf16[4,512,128]{2,1,0:T(8,128)(2,1)S(1)} %add_add_fusion.rest_0_), channel_id=1, source_target_pairs={{0,6},{2,0},{4,2},{6,4},{1,7},{3,1},{5,3},{7,5},{8,14},{10,8},{12,... | collective-permute-start | bytes 1572872 | tf_op jit(solution)/shard_map/ppermute | solution.py:249
  91.6 28.9 %copy-start.2 = (bf16[128,128]{1,0:T(8,128)(2,1)S(1)}, bf16[128,128]{1,0:T(8,128)(2,1)}, u32[]{:S(2)}) copy-start(bf16[128,128]{1,0:T(8,128)(2,1)} %w_out.1) | copy-start | bytes 98308
  91.7 28.9 %collective-permute-start.19 = (bf16[4,144,512]{2,1,0:T(8,128)(2,1)S(1)}, bf16[4,144,512]{2,1,0:T(8,128)(2,1)S(1)}, u32[]{:S(2)}, u32[]{:S(2)}) collective-permute-start(bf16[4,144,512]{2,1,0:T(8,128)(2,1)S(1)} %attend.3), channel_id=1, source_target_pairs={{0,16},{16,0},{1,17},{17,1},{2,18},{18,2},{3,19},{19,3},{4,20},{20... | collective-permute-start | bytes 1769480 | tf_op jit(solution)/shard_map/ppermute | solution.py:288

commit v9 on v8

--- a/solution.py
+++ b/solution.py
@@ -63,19 +63,16 @@
 
 def attend_kernel(blocks, xq, *rest):
     xks, w, rest = rest[:blocks], rest[blocks], rest[blocks + 1 :]
-    biases, out, (bias_s, top_s, k_s, v_s, q_s, sems) = rest[:10], rest[10], rest[11:]
+    biases, out, (bias_s, top_s, k_s, v_s, q_s, sems) = rest[:1], rest[1], rest[2:]
     step = pl.program_id(0)
-    y, z, core = lax.axis_index("y"), lax.axis_index("z"), lax.axis_index("core")
+    z = lax.axis_index("z")
 
     def bias_copies():
         copies = []
-        for n, ref in enumerate(biases):
-            place = (0, 1, 3, 2, 2)[n // 2]
-            heads = pl.ds((0, 0, 0, 0, 2)[n // 2], ref.shape[0])
-            slot = lax.rem(y - z + 4 + place, 4)
-            half = core if n % 2 == 0 else 1 - core
-            at = pl.ds(pl.multiple_of(half * 256, 256), 256)
-            copies.append(pltpu.make_async_copy(ref, bias_s.at[slot, heads, at, :], sems.at[n]))
+        for n in range(8):
+            src = biases[0].at[lax.rem(z + n // 2, 4) * 2 + n % 2]
+            dst = bias_s.at[n // 2, :, pl.ds(n % 2 * 256, 256), :]
+            copies.append(pltpu.make_async_copy(src, dst, sems.at[n]))
         return copies
 
     @pl.when(step == 0)
@@ -195,7 +192,7 @@
             pltpu.VMEM((STEP, KEYS, CHANNELS), BF16),
             pltpu.VMEM((STEP, HEADS, PAD, KEYS), BF16),
             pltpu.VMEM((STEP, HEADS, CHANNELS, COLS), BF16),
-            pltpu.SemaphoreType.DMA((10,)),
+            pltpu.SemaphoreType.DMA((8,)),
         ],
         compiler_params=pltpu.CompilerParams(vmem_limit_bytes=VMEM_LIMIT),
         cost_estimate=pl.CostEstimate(
@@ -249,42 +246,29 @@
     return lax.ppermute(x, axis, [(i, (i + step) % 4) for i in range(4)])
 
 
-def swap(x):
-    return lax.ppermute(x, "core", [(0, 1), (1, 0)])
-
-
 def gather_direct(x, axis):
     far = shift(x, axis, 2)
     return x, shift(x, axis, -1), far, shift(x, axis, 1)
 
 
-def gather_ring(x, axis):
-    behind, ahead = shift(x, axis, 1), shift(x, axis, -1)
-    parts = tied(behind[:, :256], ahead), tied(ahead[:, 256:], behind)
-    far = shift(parts[0], axis, 1), shift(parts[1], axis, -1)
-    return x, ahead, *far, behind
-
-
 def shards(pair_block, norm_gain, w_project, w_out, head_bias):
     own, bias_t = prepare(pair_block, norm_gain, head_bias)
-    bias_own = bias_t, swap(bias_t)
-    behind, ahead = shift(bias_t, "y", 1), shift(bias_t, "y", -1)
+    biases = [lax.all_gather(bias_t, ("y", "core"), axis=0, tiled=False)]
 
     xh, xl = lax.axis_index("xh"), lax.axis_index("xl")
-    opposite = lax.ppermute(own, "xh", [(0, 1), (1, 0)])
-    across = lax.ppermute(own, ("xh", "xl"), [(1, 2), (2, 1)])
-    beside = lax.ppermute(own, ("xh", "xl"), [(0, 1), (3, 2)])
-    their_k = tied(jnp.where(xl == xh, opposite, across), bias_own[1])
-    their_ks = gather_ring(their_k, "z")
-    own_k = tied(jnp.where(xl == xh, own, beside), their_ks[1], their_ks[4])
-    own_ks = gather_direct(own_k, "z")
-
-    far = shift(behind[:2], "y", 1), shift(ahead[2:], "y", -1)
-    biases = [*bias_own]
-    for block in (ahead, behind, *far):
-        biases += [block, swap(block)]
-
-    theirs = attend(opposite, their_ks, w_project, biases, BF16)
+
+    def send(x, *pairs):
+        return lax.ppermute(x, ("xh", "xl"), pairs)
+
+    far, across = send(own, (2, 0), (1, 3)), send(own, (1, 2), (2, 1))
+    their_k = jnp.where(xl == xh, far, across)
+    their_ks = gather_direct(their_k, "z")
+    again = tied(own, their_k)
+    their_q = jnp.where(xl == xh, far, send(again, (3, 1), (0, 2)))
+    own_k = jnp.where(xl == xh, own, send(again, (0, 1), (3, 2)))
+    own_ks = gather_direct(tied(own_k, *their_ks[1:]), "z")
+
+    theirs = attend(their_q, their_ks, w_project, biases, BF16)
     theirs = lax.ppermute(theirs, "xh", [(0, 1), (1, 0)])
     mine = attend(own, own_ks, w_project, biases, F32)
     update = update_rows(own, w_project, w_out, mine, theirs)

time: 143 us -> 142 us (level)
  starting transfers between devices: 47.1 us -> 16.1 us
  between operations: 2.19 us -> 16 us
  waiting for transfers between devices: 23.8 us -> 31.5 us
  local copies, waits for them, and re-layouts: 3.38 us -> 7.18 us
  other arithmetic: 0.17 us -> 3.36 us
    ppermute x8 -> x4, starting transfers between devices: 25.6 us -> 5.14 us  [send(): return lax.ppermute(x, ('xh', 'xl'), pairs)]
    ppermute x1, starting transfers between devices: 8.11 us -> 1.17 us  [shards(): theirs = lax.ppermute(theirs, 'xh', [(0, 1), (1, 0)])]
    ppermute x8 -> x4, waiting for transfers between devices: 11.2 us -> 16.6 us  [send(): return lax.ppermute(x, ('xh', 'xl'), pairs)]
    unnamed x8 -> x12, local copies, waits for them, and re-layouts: 0.02 us -> 4.13 us
    ppermute x11 -> x6, starting transfers between devices: 13.4 us -> 9.81 us  [shift(): return lax.ppermute(x, axis, [(i, (i + step) % 4) for i in range(4)])]
    ppermute x11 -> x6, waiting for transfers between devices: 12.6 us -> 14.9 us  [shift(): return lax.ppermute(x, axis, [(i, (i + step) % 4) for i in range(4)])]
    add x4 -> x2, other arithmetic: 0.17 us -> 2.21 us  [tied(): x = x + 0 * array[(0,) * array.ndim]]
  transfers between devices with their start and end apart: 20 -> 12, of which waited for: 5 -> 3; matrix products, arithmetic and copies ran while one was open for 2% -> 4% of each run, Pallas kernels for 30% -> 30%
where the time goes in v9:
time: 142 us
  Pallas kernels  47.6 us (34%)
  waiting for transfers between devices  31.5 us (22%)
  blocking collectives  20 us (14%)
  starting transfers between devices  16.1 us (11%)
  between operations  16 us (11%)
  local copies, waits for them, and re-layouts  7.18 us (5%)
  other arithmetic  3.36 us (2%)
    pallas_call x2, Pallas kernels, attend(): pl.pallas_call(functools.partial(attend_kernel, len(x_ks)), grid=(ROWS //...  43 us
    all_to_all x1, blocking collectives, shards(): lax.all_to_all(update, ROW_AXES, split_axis=0, concat_axis=0, tiled=True)  20 us
    ppermute x4, waiting for transfers between devices, send(): return lax.ppermute(x, ('xh', 'xl'), pairs)  16.6 us
    ppermute x6, waiting for transfers between devices, shift(): return lax.ppermute(x, axis, [(i, (i + step) % 4) for i in range(4)])  14.9 us
    ppermute x6, starting transfers between devices, shift(): return lax.ppermute(x, axis, [(i, (i + step) % 4) for i in range(4)])  9.81 us
    ppermute x4, starting transfers between devices, send(): return lax.ppermute(x, ('xh', 'xl'), pairs)  5.14 us
    unnamed x12, local copies, waits for them, and re-layouts  4.13 us
  transfers between devices with their start and end apart: 12, of which 3 were waited for; matrix products, arithmetic and copies ran while one was open for 4% of the time, Pallas kernels for 30%

profile of v9, /device:TPU:1, one launch (start us, length us, event | category | flops | bytes accessed | tf_op | source)
XLA Modules:
  0.0 141.8 jit_solution(10112950055162373705)
XLA Ops:
  6.5 2.8 %prepare.1 = (bf16[4,512,128]{2,1,0:T(8,128)(2,1)}, bf16[4,256,512]{2,1,0:T(8,128)(2,1)}) custom-call(bf16[4,512,128]{2,1,0:T(8,128)(2,1)} %pair.1, f32[1,128]{1,0:T(1,128)} %bitcast.12, bf16[4,512,256]{2,1,0:T(8,128)(2,1)} %bias.1), custom_call_target="tpu_custom_call" | custom-call | tf_op jit(solution)/shard_map/prepare/pallas_call | solution.py:47
  9.4 0.7 collective-permute-start.1
  10.1 1.3 collective-permute-start
  11.4 16.5 %collective-permute-done = bf16[4,512,128]{2,1,0:T(8,128)(2,1)S(1)} collective-permute-done((bf16[4,512,128]{2,1,0:T(8,128)(2,1)}, bf16[4,512,128]{2,1,0:T(8,128)(2,1)S(1)}, u32[]{:S(2)}, u32[]{:S(2)}) %collective-permute-start) | collective-permute-done | bytes 524320 | tf_op jit(solution)/shard_map/ppermute | solution.py:261
  28.0 0.7 copy-done.5
  29.3 1.6 %collective-permute-start.5 = (bf16[4,512,128]{2,1,0:T(8,128)(2,1)S(1)}, bf16[4,512,128]{2,1,0:T(8,128)(2,1)S(1)}, u32[]{:S(2)}, u32[]{:S(2)}) collective-permute-start(bf16[4,512,128]{2,1,0:T(8,128)(2,1)S(1)} %broadcast_select_fusion.1.rest_0_), channel_id=1, source_target_pairs={{0,2},{2,4},{4,6},{6,0},{1,3},{3,5},{5,7},{7,1},{8,10},{10,12},{12... | collective-permute-start | bytes 1572872 | tf_op jit(solution)/shard_map/ppermute | solution.py:246
  30.9 3.3 %collective-permute-start.4 = (bf16[4,512,128]{2,1,0:T(8,128)(2,1)S(1)}, bf16[4,512,128]{2,1,0:T(8,128)(2,1)S(1)}, u32[]{:S(2)}, u32[]{:S(2)}) collective-permute-start(bf16[4,512,128]{2,1,0:T(8,128)(2,1)S(1)} %broadcast_select_fusion.1.rest_0_), channel_id=1, source_target_pairs={{0,4},{2,6},{4,0},{6,2},{1,5},{3,7},{5,1},{7,3},{8,12},{10,14},{12... | collective-permute-start | bytes 1572872 | tf_op jit(solution)/shard_map/ppermute | solution.py:246
  34.2 0.7 collective-permute-start.3
  35.6 1.1 broadcast_add_fusion
  36.6 1.3 collective-permute-start.2
  38.0 1.8 %collective-permute-start.9 = (bf16[4,512,128]{2,1,0:T(8,128)(2,1)S(1)}, bf16[4,512,128]{2,1,0:T(8,128)(2,1)S(1)}, u32[]{:S(2)}, u32[]{:S(2)}) collective-permute-start(bf16[4,512,128]{2,1,0:T(8,128)(2,1)S(1)} %broadcast_add_fusion), channel_id=1, source_target_pairs={{17,1},{0,16},{19,3},{2,18},{21,5},{4,20},{23,7},{6,22},{25,9},{8,... | collective-permute-start | bytes 1572872 | tf_op jit(solution)/shard_map/ppermute | solution.py:261
  39.8 4.0 %collective-permute-done.5.rest_3_ = bf16[4,512,128]{2,1,0:T(8,128)(2,1)S(1)} collective-permute-done((bf16[4,512,128]{2,1,0:T(8,128)(2,1)S(1)}, bf16[4,512,128]{2,1,0:T(8,128)(2,1)S(1)}, u32[]{:S(2)}, u32[]{:S(2)}) %collective-permute-start.5) | collective-permute-done | bytes 524320 | tf_op jit(solution)/shard_map/ppermute | solution.py:246
  45.0 10.9 %collective-permute-done.4.rest_2_ = bf16[4,512,128]{2,1,0:T(8,128)(2,1)S(1)} collective-permute-done((bf16[4,512,128]{2,1,0:T(8,128)(2,1)S(1)}, bf16[4,512,128]{2,1,0:T(8,128)(2,1)S(1)}, u32[]{:S(2)}, u32[]{:S(2)}) %collective-permute-start.4) | collective-permute-done | bytes 524320 | tf_op jit(solution)/shard_map/ppermute | solution.py:246
  58.1 1.1 add_add_fusion.rest_0_
  59.2 1.5 %collective-permute-start.8 = (bf16[4,512,128]{2,1,0:T(8,128)(2,1)S(1)}, bf16[4,512,128]{2,1,0:T(8,128)(2,1)}, u32[]{:S(2)}, u32[]{:S(2)}) collective-permute-start(bf16[4,512,128]{2,1,0:T(8,128)(2,1)S(1)} %add_add_fusion.rest_0_), channel_id=1, source_target_pairs={{0,2},{2,4},{4,6},{6,0},{1,3},{3,5},{5,7},{7,1},{8,10},{10,12},{12... | collective-permute-start | bytes 1572872 | tf_op jit(solution)/shard_map/ppermute | solution.py:246
  60.8 2.6 %collective-permute-start.7 = (bf16[4,512,128]{2,1,0:T(8,128)(2,1)S(1)}, bf16[4,512,128]{2,1,0:T(8,128)(2,1)}, u32[]{:S(2)}, u32[]{:S(2)}) collective-permute-start(bf16[4,512,128]{2,1,0:T(8,128)(2,1)S(1)} %add_add_fusion.rest_0_), channel_id=1, source_target_pairs={{0,4},{2,6},{4,0},{6,2},{1,5},{3,7},{5,1},{7,3},{8,12},{10,14},{12... | collective-permute-start | bytes 1572872 | tf_op jit(solution)/shard_map/ppermute | solution.py:246
  63.4 1.1 broadcast_select_fusion.xq
  64.5 3.4 %copy-done.3 = bf16[32,256,512]{2,1,0:T(8,128)(2,1)S(1)} copy-done((bf16[32,256,512]{2,1,0:T(8,128)(2,1)S(1)}, bf16[32,256,512]{2,1,0:T(8,128)(2,1)}, u32[]{:S(2)}) %copy-start.3) | copy-done | bytes 8388632
  67.9 20.9 %attend.3 = bf16[4,144,512]{2,1,0:T(8,128)(2,1)S(1)} custom-call(bf16[4,512,128]{2,1,0:T(8,128)(2,1)S(1)} %broadcast_select_fusion.xq, bf16[4,512,128]{2,1,0:T(8,128)(2,1)S(1)} %broadcast_select_fusion.1.rest_0_, bf16[4,512,128]{2,1,0:T(8,128)(2,1)S(1)} %collective-permute-done.3.rest_1_, bf16[4,512,128]{2,1,0:T(8,128)(2,1)S(1)} %collective-permute-done.4.rest_2_, ...), custom_call_target="tpu_custom_call" | custom-call | flops 8589934592 | bytes 16777216 | tf_op jit(solution)/shard_map/attend/pallas_call | solution.py:180
  88.9 1.2 collective-permute-start.10
  90.1 22.0 %attend.2.mine = f32[4,144,512]{2,1,0:T(8,128)S(1)} custom-call(bf16[4,512,128]{2,1,0:T(8,128)(2,1)S(1)} %copy-done, bf16[4,512,128]{2,1,0:T(8,128)(2,1)S(1)} %add_add_fusion.rest_0_, bf16[4,512,128]{2,1,0:T(8,128)(2,1)} %collective-permute-done.6.rest_1_, bf16[4,512,128]{2,1,0:T(8,128)(2,1)} %collective-permute-done.7.rest_2_, ...), custom_call_target="tpu_custom_call" | custom-call | flops 8589934592 | bytes 16777216 | tf_op jit(solution)/shard_map/attend/pallas_call | solution.py:180
  112.1 1.8 %update.1 = bf16[16,4,32,128]{3,2,1,0:T(8,128)(2,1)S(1)} custom-call(bf16[4,512,128]{2,1,0:T(8,128)(2,1)S(1)} %copy-done, bf16[128,512]{1,0:T(8,128)(2,1)S(1)} %copy-done.1, bf16[128,128]{1,0:T(8,128)(2,1)S(1)} %copy-done.2, f32[4,144,512]{2,1,0:T(8,128)S(1)} %attend.2.mine, bf16[4,144,512]{2,1,0:T(8,128)(2,1)S(1)} %collective-permute-done.10.theirs), custom_call_target="tpu_custom_call" | custom-call | tf_op jit(solution)/shard_map/update/pallas_call | solution.py:228
  114.0 20.0 %all_to_all.5 = bf16[16,4,32,128]{3,2,1,0:T(8,128)(2,1)S(1)} all-to-all(bf16[16,4,32,128]{3,2,1,0:T(8,128)(2,1)S(1)} %update.1), channel_id=1, replica_groups=mesh['y'=4,'xh'=2,'core'=2,'z'=4,'xl'=2] {'y','xh','core'}, dimensions={0} | all-to-all | bytes 1048576 | tf_op jit(solution)/shard_map/all_to_all | solution.py:275
  134.0 1.0 copy.7
  (27 shorter events, 2.2 us)
Async XLA Ops:
  6.5 58.0 %copy-start.1 = (bf16[128,512]{1,0:T(8,128)(2,1)S(1)}, bf16[128,512]{1,0:T(8,128)(2,1)}, u32[]{:S(2)}) copy-start(bf16[128,512]{1,0:T(8,128)(2,1)} %w.1) | copy-start | bytes 393220
  6.5 58.0 %all-gather.3.cloned.1.call-start = ((), (), s32[]{:S(2)}) async-start(), calls=%async_computation.1 | async-start | bytes 9437184 | tf_op jit(solution)/shard_map/all_gather | solution.py:256
  9.4 2.0 %collective-permute-start.1 = (bf16[4,512,128]{2,1,0:T(8,128)(2,1)}, bf16[4,512,128]{2,1,0:T(8,128)(2,1)S(1)}, u32[]{:S(2)}, u32[]{:S(2)}) collective-permute-start(bf16[4,512,128]{2,1,0:T(8,128)(2,1)} %get-tuple-element.7.xq.x), channel_id=1, source_target_pairs={{1,16},{16,1},{3,18},{18,3},{5,20},{20,5},{7,22},{22,7},{9,24},{24... | collective-permute-start | bytes 1572872 | tf_op jit(solution)/shard_map/ppermute | solution.py:261
  10.1 17.9 %collective-permute-start = (bf16[4,512,128]{2,1,0:T(8,128)(2,1)}, bf16[4,512,128]{2,1,0:T(8,128)(2,1)S(1)}, u32[]{:S(2)}, u32[]{:S(2)}) collective-permute-start(bf16[4,512,128]{2,1,0:T(8,128)(2,1)} %get-tuple-element.7.xq.x), channel_id=1, source_target_pairs={{16,0},{1,17},{18,2},{3,19},{20,4},{5,21},{22,6},{7,23},{24,8},{9,... | collective-permute-start | bytes 1572872 | tf_op jit(solution)/shard_map/ppermute | solution.py:261
  28.0 0.8 copy-start.5
  29.3 14.5 %collective-permute-start.5 = (bf16[4,512,128]{2,1,0:T(8,128)(2,1)S(1)}, bf16[4,512,128]{2,1,0:T(8,128)(2,1)S(1)}, u32[]{:S(2)}, u32[]{:S(2)}) collective-permute-start(bf16[4,512,128]{2,1,0:T(8,128)(2,1)S(1)} %broadcast_select_fusion.1.rest_0_), channel_id=1, source_target_pairs={{0,2},{2,4},{4,6},{6,0},{1,3},{3,5},{5,7},{7,1},{8,10},{10,12},{12... | collective-permute-start | bytes 1572872 | tf_op jit(solution)/shard_map/ppermute | solution.py:246
  30.9 24.9 %collective-permute-start.4 = (bf16[4,512,128]{2,1,0:T(8,128)(2,1)S(1)}, bf16[4,512,128]{2,1,0:T(8,128)(2,1)S(1)}, u32[]{:S(2)}, u32[]{:S(2)}) collective-permute-start(bf16[4,512,128]{2,1,0:T(8,128)(2,1)S(1)} %broadcast_select_fusion.1.rest_0_), channel_id=1, source_target_pairs={{0,4},{2,6},{4,0},{6,2},{1,5},{3,7},{5,1},{7,3},{8,12},{10,14},{12... | collective-permute-start | bytes 1572872 | tf_op jit(solution)/shard_map/ppermute | solution.py:246
  34.2 22.7 %collective-permute-start.3 = (bf16[4,512,128]{2,1,0:T(8,128)(2,1)S(1)}, bf16[4,512,128]{2,1,0:T(8,128)(2,1)S(1)}, u32[]{:S(2)}, u32[]{:S(2)}) collective-permute-start(bf16[4,512,128]{2,1,0:T(8,128)(2,1)S(1)} %broadcast_select_fusion.1.rest_0_), channel_id=1, source_target_pairs={{0,6},{2,0},{4,2},{6,4},{1,7},{3,1},{5,3},{7,5},{8,14},{10,8},{12,... | collective-permute-start | bytes 1572872 | tf_op jit(solution)/shard_map/ppermute | solution.py:246
  36.6 21.4 %collective-permute-start.2 = (bf16[4,512,128]{2,1,0:T(8,128)(2,1)S(1)}, bf16[4,512,128]{2,1,0:T(8,128)(2,1)S(1)}, u32[]{:S(2)}, u32[]{:S(2)}) collective-permute-start(bf16[4,512,128]{2,1,0:T(8,128)(2,1)S(1)} %broadcast_add_fusion), channel_id=1, source_target_pairs={{0,1},{17,16},{2,3},{19,18},{4,5},{21,20},{6,7},{23,22},{8,9},{25,... | collective-permute-start | bytes 1572872 | tf_op jit(solution)/shard_map/ppermute | solution.py:261
  38.0 25.4 %collective-permute-start.9 = (bf16[4,512,128]{2,1,0:T(8,128)(2,1)S(1)}, bf16[4,512,128]{2,1,0:T(8,128)(2,1)S(1)}, u32[]{:S(2)}, u32[]{:S(2)}) collective-permute-start(bf16[4,512,128]{2,1,0:T(8,128)(2,1)S(1)} %broadcast_add_fusion), channel_id=1, source_target_pairs={{17,1},{0,16},{19,3},{2,18},{21,5},{4,20},{23,7},{6,22},{25,9},{8,... | collective-permute-start | bytes 1572872 | tf_op jit(solution)/shard_map/ppermute | solution.py:261
  59.2 30.8 %collective-permute-start.8 = (bf16[4,512,128]{2,1,0:T(8,128)(2,1)S(1)}, bf16[4,512,128]{2,1,0:T(8,128)(2,1)}, u32[]{:S(2)}, u32[]{:S(2)}) collective-permute-start(bf16[4,512,128]{2,1,0:T(8,128)(2,1)S(1)} %add_add_fusion.rest_0_), channel_id=1, source_target_pairs={{0,2},{2,4},{4,6},{6,0},{1,3},{3,5},{5,7},{7,1},{8,10},{10,12},{12... | collective-permute-start | bytes 1572872 | tf_op jit(solution)/shard_map/ppermute | solution.py:246
  60.8 29.3 %collective-permute-start.7 = (bf16[4,512,128]{2,1,0:T(8,128)(2,1)S(1)}, bf16[4,512,128]{2,1,0:T(8,128)(2,1)}, u32[]{:S(2)}, u32[]{:S(2)}) collective-permute-start(bf16[4,512,128]{2,1,0:T(8,128)(2,1)S(1)} %add_add_fusion.rest_0_), channel_id=1, source_target_pairs={{0,4},{2,6},{4,0},{6,2},{1,5},{3,7},{5,1},{7,3},{8,12},{10,14},{12... | collective-permute-start | bytes 1572872 | tf_op jit(solution)/shard_map/ppermute | solution.py:246
  63.4 26.7 %collective-permute-start.6 = (bf16[4,512,128]{2,1,0:T(8,128)(2,1)S(1)}, bf16[4,512,128]{2,1,0:T(8,128)(2,1)}, u32[]{:S(2)}, u32[]{:S(2)}) collective-permute-start(bf16[4,512,128]{2,1,0:T(8,128)(2,1)S(1)} %add_add_fusion.rest_0_), channel_id=1, source_target_pairs={{0,6},{2,0},{4,2},{6,4},{1,7},{3,1},{5,3},{7,5},{8,14},{10,8},{12,... | collective-permute-start | bytes 1572872 | tf_op jit(solution)/shard_map/ppermute | solution.py:246
  64.5 3.4 %copy-start.3 = (bf16[32,256,512]{2,1,0:T(8,128)(2,1)S(1)}, bf16[32,256,512]{2,1,0:T(8,128)(2,1)}, u32[]{:S(2)}) copy-start(bf16[32,256,512]{2,1,0:T(8,128)(2,1)} %all-gather.3.cloned.1.call-done) | copy-start | bytes 25165828
  67.9 22.1 %copy-start = (bf16[4,512,128]{2,1,0:T(8,128)(2,1)S(1)}, bf16[4,512,128]{2,1,0:T(8,128)(2,1)}, u32[]{:S(2)}) copy-start(bf16[4,512,128]{2,1,0:T(8,128)(2,1)} %get-tuple-element.7.xq.x) | copy-start | bytes 1572868
  67.9 22.1 %copy-start.4 = (bf16[32,256,512]{2,1,0:T(8,128)(2,1)S(1)}, bf16[32,256,512]{2,1,0:T(8,128)(2,1)}, u32[]{:S(2)}) copy-start(bf16[32,256,512]{2,1,0:T(8,128)(2,1)} %all-gather.3.cloned.1.call-done) | copy-start | bytes 25165828
  88.8 23.3 %copy-start.2 = (bf16[128,128]{1,0:T(8,128)(2,1)S(1)}, bf16[128,128]{1,0:T(8,128)(2,1)}, u32[]{:S(2)}) copy-start(bf16[128,128]{1,0:T(8,128)(2,1)} %w_out.1) | copy-start | bytes 98308
  88.9 23.3 %collective-permute-start.10 = (bf16[4,144,512]{2,1,0:T(8,128)(2,1)S(1)}, bf16[4,144,512]{2,1,0:T(8,128)(2,1)S(1)}, u32[]{:S(2)}, u32[]{:S(2)}) collective-permute-start(bf16[4,144,512]{2,1,0:T(8,128)(2,1)S(1)} %attend.3), channel_id=1, source_target_pairs={{0,16},{16,0},{1,17},{17,1},{2,18},{18,2},{3,19},{19,3},{4,20},{20... | collective-permute-start | bytes 1769480 | tf_op jit(solution)/shard_map/ppermute | solution.py:272
Sparse Core Ops, SparseCore 0:
  9.5 53.3 all-gather.2

commit v10 on v8

--- a/solution.py
+++ b/solution.py
@@ -258,33 +258,30 @@
     return x, shift(x, axis, -1), far, shift(x, axis, 1)
 
 
-def gather_ring(x, axis):
-    behind, ahead = shift(x, axis, 1), shift(x, axis, -1)
-    parts = tied(behind[:, :256], ahead), tied(ahead[:, 256:], behind)
-    far = shift(parts[0], axis, 1), shift(parts[1], axis, -1)
-    return x, ahead, *far, behind
-
-
 def shards(pair_block, norm_gain, w_project, w_out, head_bias):
     own, bias_t = prepare(pair_block, norm_gain, head_bias)
     bias_own = bias_t, swap(bias_t)
     behind, ahead = shift(bias_t, "y", 1), shift(bias_t, "y", -1)
 
     xh, xl = lax.axis_index("xh"), lax.axis_index("xl")
-    opposite = lax.ppermute(own, "xh", [(0, 1), (1, 0)])
-    across = lax.ppermute(own, ("xh", "xl"), [(1, 2), (2, 1)])
-    beside = lax.ppermute(own, ("xh", "xl"), [(0, 1), (3, 2)])
-    their_k = tied(jnp.where(xl == xh, opposite, across), bias_own[1])
-    their_ks = gather_ring(their_k, "z")
-    own_k = tied(jnp.where(xl == xh, own, beside), their_ks[1], their_ks[4])
-    own_ks = gather_direct(own_k, "z")
-
-    far = shift(behind[:2], "y", 1), shift(ahead[2:], "y", -1)
+
+    def send(x, *pairs):
+        return lax.ppermute(x, ("xh", "xl"), pairs)
+
+    far, across = send(own, (2, 0), (1, 3)), send(own, (1, 2), (2, 1))
+    their_k = tied(jnp.where(xl == xh, far, across), bias_own[1])
+    their_ks = gather_direct(their_k, "z")
+    again = tied(own, their_k)
+    their_q = jnp.where(xl == xh, far, send(again, (3, 1), (0, 2)))
+    own_k = jnp.where(xl == xh, own, send(again, (0, 1), (3, 2)))
+    own_ks = gather_direct(tied(own_k, *their_ks[1:]), "z")
+
+    far = shift(tied(behind[:2], their_k), "y", 1), shift(tied(ahead[2:], their_k), "y", -1)
     biases = [*bias_own]
     for block in (ahead, behind, *far):
         biases += [block, swap(block)]
 
-    theirs = attend(opposite, their_ks, w_project, biases, BF16)
+    theirs = attend(their_q, their_ks, w_project, biases, BF16)
     theirs = lax.ppermute(theirs, "xh", [(0, 1), (1, 0)])
     mine = attend(own, own_ks, w_project, biases, F32)
     update = update_rows(own, w_project, w_out, mine, theirs)

time: 143 us -> 146 us (1.021)
  waiting for transfers between devices: 23.8 us -> 37.9 us
  starting transfers between devices: 47.1 us -> 33.2 us
  other arithmetic: 0.17 us -> 2.45 us
    ppermute x3 -> x4, starting transfers between devices: 19 us -> 10.3 us  [send(): return lax.ppermute(x, ('xh', 'xl'), pairs)]
    ppermute x3 -> x4, waiting for transfers between devices: 11.2 us -> 19.8 us  [send(): return lax.ppermute(x, ('xh', 'xl'), pairs)]
    ppermute x11 -> x10, waiting for transfers between devices: 12.6 us -> 18.1 us  [shift(): return lax.ppermute(x, axis, [(i, (i + step) % 4) for i in range(4)])]
    ppermute x1, starting transfers between devices: 8.11 us -> 2.73 us  [shards(): theirs = lax.ppermute(theirs, 'xh', [(0, 1), (1, 0)])]
    ppermute x11 -> x10, starting transfers between devices: 13.4 us -> 14.1 us  [shift(): return lax.ppermute(x, axis, [(i, (i + step) % 4) for i in range(4)])]
  transfers between devices with their start and end apart: 20 -> 20, of which waited for: 5 -> 5; matrix products, arithmetic and copies ran while one was open for 2% -> 4% of each run, Pallas kernels for 30% -> 29%
where the time goes in v10:
time: 146 us
  Pallas kernels  46.9 us (32%)
  waiting for transfers between devices  37.9 us (26%)
  starting transfers between devices  33.2 us (23%)
  blocking collectives  18 us (12%)
  local copies, waits for them, and re-layouts  3.82 us (3%)
  between operations  3.46 us (2%)
  other arithmetic  2.45 us (2%)
    pallas_call x2, Pallas kernels, attend(): pl.pallas_call(functools.partial(attend_kernel, len(x_ks)), grid=(ROWS //...  42.3 us
    ppermute x4, waiting for transfers between devices, send(): return lax.ppermute(x, ('xh', 'xl'), pairs)  19.8 us
    ppermute x10, waiting for transfers between devices, shift(): return lax.ppermute(x, axis, [(i, (i + step) % 4) for i in range(4)])  18.1 us
    all_to_all x1, blocking collectives, shards(): lax.all_to_all(update, ROW_AXES, split_axis=0, concat_axis=0, tiled=True)  18 us
    ppermute x10, starting transfers between devices, shift(): return lax.ppermute(x, axis, [(i, (i + step) % 4) for i in range(4)])  14.1 us
    ppermute x4, starting transfers between devices, send(): return lax.ppermute(x, ('xh', 'xl'), pairs)  10.3 us
    ppermute x5, starting transfers between devices, swap(): return lax.ppermute(x, 'core', [(0, 1), (1, 0)])  6 us
  transfers between devices with their start and end apart: 20, of which 5 were waited for; matrix products, arithmetic and copies ran while one was open for 4% of the time, Pallas kernels for 29%

profile of v10, /device:TPU:1, one launch (start us, length us, event | category | flops | bytes accessed | tf_op | source)
XLA Modules:
  0.0 145.6 jit_solution(8514118441393602214)
XLA Ops:
  0.0 2.8 %prepare.1 = (bf16[4,512,128]{2,1,0:T(8,128)(2,1)}, bf16[4,256,512]{2,1,0:T(8,128)(2,1)}) custom-call(bf16[4,512,128]{2,1,0:T(8,128)(2,1)} %pair.1, f32[1,128]{1,0:T(1,128)} %bitcast.10, bf16[4,512,256]{2,1,0:T(8,128)(2,1)} %bias.1), custom_call_target="tpu_custom_call" | custom-call | tf_op jit(solution)/shard_map/prepare/pallas_call | solution.py:47
  2.8 1.4 collective-permute-start.2
  4.2 1.4 collective-permute-start.12
  5.6 1.5 %collective-permute-start.1 = (bf16[4,512,128]{2,1,0:T(8,128)(2,1)}, bf16[4,512,128]{2,1,0:T(8,128)(2,1)}, u32[]{:S(2)}, u32[]{:S(2)}) collective-permute-start(bf16[4,512,128]{2,1,0:T(8,128)(2,1)} %get-tuple-element.7.xq.x), channel_id=1, source_target_pairs={{1,16},{16,1},{3,18},{18,3},{5,20},{20,5},{7,22},{22,7},{9,24},{24... | collective-permute-start | bytes 1572872 | tf_op jit(solution)/shard_map/ppermute | solution.py:269
  7.0 1.3 collective-permute-start
  8.3 1.5 %collective-permute-start.10 = (bf16[4,256,512]{2,1,0:T(8,128)(2,1)}, bf16[4,256,512]{2,1,0:T(8,128)(2,1)S(1)}, u32[]{:S(2)}, u32[]{:S(2)}) collective-permute-start(bf16[4,256,512]{2,1,0:T(8,128)(2,1)} %get-tuple-element.8.rest_5_), channel_id=1, source_target_pairs={{0,96},{32,0},{64,32},{96,64},{1,97},{33,1},{65,33},{97,65},{2,98}... | collective-permute-start | bytes 3145736 | tf_op jit(solution)/shard_map/ppermute | solution.py:249
  11.2 12.7 %collective-permute-done = bf16[4,512,128]{2,1,0:T(8,128)(2,1)} collective-permute-done((bf16[4,512,128]{2,1,0:T(8,128)(2,1)}, bf16[4,512,128]{2,1,0:T(8,128)(2,1)}, u32[]{:S(2)}, u32[]{:S(2)}) %collective-permute-start) | collective-permute-done | bytes 524320 | tf_op jit(solution)/shard_map/ppermute | solution.py:269
  26.3 4.4 %collective-permute-done.12.rest_9_ = bf16[4,256,512]{2,1,0:T(8,128)(2,1)S(1)} collective-permute-done((bf16[4,256,512]{2,1,0:T(8,128)(2,1)}, bf16[4,256,512]{2,1,0:T(8,128)(2,1)S(1)}, u32[]{:S(2)}, u32[]{:S(2)}) %collective-permute-start.12) | collective-permute-done | bytes 1048608 | tf_op jit(solution)/shard_map/ppermute | solution.py:249
  30.8 1.6 %collective-permute-start.6 = (bf16[4,512,128]{2,1,0:T(8,128)(2,1)S(1)}, bf16[4,512,128]{2,1,0:T(8,128)(2,1)S(1)}, u32[]{:S(2)}, u32[]{:S(2)}) collective-permute-start(bf16[4,512,128]{2,1,0:T(8,128)(2,1)S(1)} %select_add_fusion.rest_0_), channel_id=1, source_target_pairs={{0,2},{2,4},{4,6},{6,0},{1,3},{3,5},{5,7},{7,1},{8,10},{10,12},{12... | collective-permute-start | bytes 1572872 | tf_op jit(solution)/shard_map/ppermute | solution.py:249
  32.4 3.3 %collective-permute-start.5 = (bf16[4,512,128]{2,1,0:T(8,128)(2,1)S(1)}, bf16[4,512,128]{2,1,0:T(8,128)(2,1)S(1)}, u32[]{:S(2)}, u32[]{:S(2)}) collective-permute-start(bf16[4,512,128]{2,1,0:T(8,128)(2,1)S(1)} %select_add_fusion.rest_0_), channel_id=1, source_target_pairs={{0,4},{2,6},{4,0},{6,2},{1,5},{3,7},{5,1},{7,3},{8,12},{10,14},{12... | collective-permute-start | bytes 1572872 | tf_op jit(solution)/shard_map/ppermute | solution.py:249
  36.5 2.7 %collective-permute-start.16 = (bf16[2,256,512]{2,1,0:T(8,128)(2,1)S(1)}, bf16[2,256,512]{2,1,0:T(8,128)(2,1)S(1)}, u32[]{:S(2)}, u32[]{:S(2)}) collective-permute-start(bf16[2,256,512]{2,1,0:T(8,128)(2,1)S(1)} %slice_add_fusion), channel_id=1, source_target_pairs={{0,96},{32,0},{64,32},{96,64},{1,97},{33,1},{65,33},{97,65},{2,98}... | collective-permute-start | bytes 1572872 | tf_op jit(solution)/shard_map/ppermute | solution.py:249
  39.2 5.5 %collective-permute-done.14.rest_11_ = bf16[2,256,512]{2,1,0:T(8,128)(2,1)S(1)} collective-permute-done((bf16[2,256,512]{2,1,0:T(8,128)(2,1)S(1)}, bf16[2,256,512]{2,1,0:T(8,128)(2,1)S(1)}, u32[]{:S(2)}, u32[]{:S(2)}) %collective-permute-start.14) | collective-permute-done | bytes 524320 | tf_op jit(solution)/shard_map/ppermute | solution.py:249
  44.7 2.9 %collective-permute-start.3 = (bf16[4,512,128]{2,1,0:T(8,128)(2,1)S(1)}, bf16[4,512,128]{2,1,0:T(8,128)(2,1)S(1)}, u32[]{:S(2)}, u32[]{:S(2)}) collective-permute-start(bf16[4,512,128]{2,1,0:T(8,128)(2,1)S(1)} %broadcast_add_fusion), channel_id=1, source_target_pairs={{0,1},{17,16},{2,3},{19,18},{4,5},{21,20},{6,7},{23,22},{8,9},{25,... | collective-permute-start | bytes 1572872 | tf_op jit(solution)/shard_map/ppermute | solution.py:269
  47.7 2.0 %collective-permute-start.13 = (bf16[4,256,512]{2,1,0:T(8,128)(2,1)S(1)}, bf16[4,256,512]{2,1,0:T(8,128)(2,1)S(1)}, u32[]{:S(2)}, u32[]{:S(2)}) collective-permute-start(bf16[4,256,512]{2,1,0:T(8,128)(2,1)S(1)} %collective-permute-done.12.rest_9_), channel_id=1, source_target_pairs={{0,8},{8,0},{1,9},{9,1},{2,10},{10,2},{3,11},{11,3},{4,12},{12,4},... | collective-permute-start | bytes 3145736 | tf_op jit(solution)/shard_map/ppermute | solution.py:253
  49.7 8.1 %collective-permute-done.5.rest_2_ = bf16[4,512,128]{2,1,0:T(8,128)(2,1)S(1)} collective-permute-done((bf16[4,512,128]{2,1,0:T(8,128)(2,1)S(1)}, bf16[4,512,128]{2,1,0:T(8,128)(2,1)S(1)}, u32[]{:S(2)}, u32[]{:S(2)}) %collective-permute-start.5) | collective-permute-done | bytes 524320 | tf_op jit(solution)/shard_map/ppermute | solution.py:249
  57.8 1.9 %collective-permute-start.11 = (bf16[4,256,512]{2,1,0:T(8,128)(2,1)S(1)}, bf16[4,256,512]{2,1,0:T(8,128)(2,1)S(1)}, u32[]{:S(2)}, u32[]{:S(2)}) collective-permute-start(bf16[4,256,512]{2,1,0:T(8,128)(2,1)S(1)} %collective-permute-done.10.rest_7_), channel_id=1, source_target_pairs={{0,8},{8,0},{1,9},{9,1},{2,10},{10,2},{3,11},{11,3},{4,12},{12,4},... | collective-permute-start | bytes 3145736 | tf_op jit(solution)/shard_map/ppermute | solution.py:253
  59.8 4.7 %collective-permute-start.18 = (bf16[4,512,128]{2,1,0:T(8,128)(2,1)S(1)}, bf16[4,512,128]{2,1,0:T(8,128)(2,1)S(1)}, u32[]{:S(2)}, u32[]{:S(2)}) collective-permute-start(bf16[4,512,128]{2,1,0:T(8,128)(2,1)S(1)} %broadcast_add_fusion), channel_id=1, source_target_pairs={{17,1},{0,16},{19,3},{2,18},{21,5},{4,20},{23,7},{6,22},{25,9},{8,... | collective-permute-start | bytes 1572872 | tf_op jit(solution)/shard_map/ppermute | solution.py:269
  68.7 7.0 %collective-permute-done.18 = bf16[4,512,128]{2,1,0:T(8,128)(2,1)S(1)} collective-permute-done((bf16[4,512,128]{2,1,0:T(8,128)(2,1)S(1)}, bf16[4,512,128]{2,1,0:T(8,128)(2,1)S(1)}, u32[]{:S(2)}, u32[]{:S(2)}) %collective-permute-start.18) | collective-permute-done | bytes 524320 | tf_op jit(solution)/shard_map/ppermute | solution.py:269
  76.9 2.1 %collective-permute-start.8 = (bf16[4,512,128]{2,1,0:T(8,128)(2,1)S(1)}, bf16[4,512,128]{2,1,0:T(8,128)(2,1)S(1)}, u32[]{:S(2)}, u32[]{:S(2)}) collective-permute-start(bf16[4,512,128]{2,1,0:T(8,128)(2,1)S(1)} %add_add_fusion.rest_0_), channel_id=1, source_target_pairs={{0,4},{2,6},{4,0},{6,2},{1,5},{3,7},{5,1},{7,3},{8,12},{10,14},{12... | collective-permute-start | bytes 1572872 | tf_op jit(solution)/shard_map/ppermute | solution.py:249
  79.8 21.4 %attend.3 = bf16[4,144,512]{2,1,0:T(8,128)(2,1)S(1)} custom-call(bf16[4,512,128]{2,1,0:T(8,128)(2,1)S(1)} %broadcast_select_fusion.xq, bf16[4,512,128]{2,1,0:T(8,128)(2,1)S(1)} %select_add_fusion.rest_0_, bf16[4,512,128]{2,1,0:T(8,128)(2,1)S(1)} %collective-permute-done.4.rest_1_, bf16[4,512,128]{2,1,0:T(8,128)(2,1)S(1)} %collective-permute-done.5.rest_2_, ...), custom_call_target="tpu_custom_call" | custom-call | flops 8589934592 | bytes 16777216 | tf_op jit(solution)/shard_map/attend/pallas_call | solution.py:183
  101.2 2.7 %collective-permute-start.19 = (bf16[4,144,512]{2,1,0:T(8,128)(2,1)S(1)}, bf16[4,144,512]{2,1,0:T(8,128)(2,1)S(1)}, u32[]{:S(2)}, u32[]{:S(2)}) collective-permute-start(bf16[4,144,512]{2,1,0:T(8,128)(2,1)S(1)} %attend.3), channel_id=1, source_target_pairs={{0,16},{16,0},{1,17},{17,1},{2,18},{18,2},{3,19},{19,3},{4,20},{20... | collective-permute-start | bytes 1769480 | tf_op jit(solution)/shard_map/ppermute | solution.py:285
  104.0 20.8 %attend.2.mine = f32[4,144,512]{2,1,0:T(8,128)S(1)} custom-call(bf16[4,512,128]{2,1,0:T(8,128)(2,1)S(1)} %copy-done, bf16[4,512,128]{2,1,0:T(8,128)(2,1)S(1)} %add_add_fusion.rest_0_, bf16[4,512,128]{2,1,0:T(8,128)(2,1)S(1)} %collective-permute-done.7.rest_1_, bf16[4,512,128]{2,1,0:T(8,128)(2,1)S(1)} %collective-permute-done.8.rest_2_, ...), custom_call_target="tpu_custom_call" | custom-call | flops 8589934592 | bytes 16777216 | tf_op jit(solution)/shard_map/attend/pallas_call | solution.py:183
  124.8 1.8 %update.1 = bf16[16,4,32,128]{3,2,1,0:T(8,128)(2,1)S(1)} custom-call(bf16[4,512,128]{2,1,0:T(8,128)(2,1)S(1)} %copy-done, bf16[128,512]{1,0:T(8,128)(2,1)S(1)} %copy-done.1, bf16[128,128]{1,0:T(8,128)(2,1)S(1)} %copy-done.2, f32[4,144,512]{2,1,0:T(8,128)S(1)} %attend.2.mine, bf16[4,144,512]{2,1,0:T(8,128)(2,1)S(1)} %collective-permute-done.19.theirs), custom_call_target="tpu_custom_call" | custom-call | tf_op jit(solution)/shard_map/update/pallas_call | solution.py:231
  126.7 18.0 %all_to_all.5 = bf16[16,4,32,128]{3,2,1,0:T(8,128)(2,1)S(1)} all-to-all(bf16[16,4,32,128]{3,2,1,0:T(8,128)(2,1)S(1)} %update.1), channel_id=1, replica_groups=mesh['y'=4,'xh'=2,'core'=2,'z'=4,'xl'=2] {'y','xh','core'}, dimensions={0} | all-to-all | bytes 1048576 | tf_op jit(solution)/shard_map/all_to_all | solution.py:288
  (41 shorter events, 8.5 us)
Async XLA Ops:
  2.8 7.1 %collective-permute-start.2 = (bf16[4,256,512]{2,1,0:T(8,128)(2,1)}, bf16[4,256,512]{2,1,0:T(8,128)(2,1)S(1)}, u32[]{:S(2)}, u32[]{:S(2)}) collective-permute-start(bf16[4,256,512]{2,1,0:T(8,128)(2,1)} %get-tuple-element.8.rest_5_), channel_id=1, source_target_pairs={{0,8},{8,0},{1,9},{9,1},{2,10},{10,2},{3,11},{11,3},{4,12},{12,4},... | collective-permute-start | bytes 3145736 | tf_op jit(solution)/shard_map/ppermute | solution.py:253
  4.2 26.4 %collective-permute-start.12 = (bf16[4,256,512]{2,1,0:T(8,128)(2,1)}, bf16[4,256,512]{2,1,0:T(8,128)(2,1)S(1)}, u32[]{:S(2)}, u32[]{:S(2)}) collective-permute-start(bf16[4,256,512]{2,1,0:T(8,128)(2,1)} %get-tuple-element.8.rest_5_), channel_id=1, source_target_pairs={{0,32},{32,64},{64,96},{96,0},{1,33},{33,65},{65,97},{97,1},{2,34}... | collective-permute-start | bytes 3145736 | tf_op jit(solution)/shard_map/ppermute | solution.py:249
  5.6 5.6 %collective-permute-start.1 = (bf16[4,512,128]{2,1,0:T(8,128)(2,1)}, bf16[4,512,128]{2,1,0:T(8,128)(2,1)}, u32[]{:S(2)}, u32[]{:S(2)}) collective-permute-start(bf16[4,512,128]{2,1,0:T(8,128)(2,1)} %get-tuple-element.7.xq.x), channel_id=1, source_target_pairs={{1,16},{16,1},{3,18},{18,3},{5,20},{20,5},{7,22},{22,7},{9,24},{24... | collective-permute-start | bytes 1572872 | tf_op jit(solution)/shard_map/ppermute | solution.py:269
  7.0 16.9 %collective-permute-start = (bf16[4,512,128]{2,1,0:T(8,128)(2,1)}, bf16[4,512,128]{2,1,0:T(8,128)(2,1)}, u32[]{:S(2)}, u32[]{:S(2)}) collective-permute-start(bf16[4,512,128]{2,1,0:T(8,128)(2,1)} %get-tuple-element.7.xq.x), channel_id=1, source_target_pairs={{16,0},{1,17},{18,2},{3,19},{20,4},{5,21},{22,6},{7,23},{24,8},{9,... | collective-permute-start | bytes 1572872 | tf_op jit(solution)/shard_map/ppermute | solution.py:269
  8.3 28.1 %collective-permute-start.10 = (bf16[4,256,512]{2,1,0:T(8,128)(2,1)}, bf16[4,256,512]{2,1,0:T(8,128)(2,1)S(1)}, u32[]{:S(2)}, u32[]{:S(2)}) collective-permute-start(bf16[4,256,512]{2,1,0:T(8,128)(2,1)} %get-tuple-element.8.rest_5_), channel_id=1, source_target_pairs={{0,96},{32,0},{64,32},{96,64},{1,97},{33,1},{65,33},{97,65},{2,98}... | collective-permute-start | bytes 3145736 | tf_op jit(solution)/shard_map/ppermute | solution.py:249
  23.9 12.5 %copy-start = (bf16[4,512,128]{2,1,0:T(8,128)(2,1)S(1)}, bf16[4,512,128]{2,1,0:T(8,128)(2,1)}, u32[]{:S(2)}) copy-start(bf16[4,512,128]{2,1,0:T(8,128)(2,1)} %get-tuple-element.7.xq.x) | copy-start | bytes 1572868
  30.7 14.0 %collective-permute-start.14 = (bf16[2,256,512]{2,1,0:T(8,128)(2,1)S(1)}, bf16[2,256,512]{2,1,0:T(8,128)(2,1)S(1)}, u32[]{:S(2)}, u32[]{:S(2)}) collective-permute-start(bf16[2,256,512]{2,1,0:T(8,128)(2,1)S(1)} %slice_add_fusion.1), channel_id=1, source_target_pairs={{0,32},{32,64},{64,96},{96,0},{1,33},{33,65},{65,97},{97,1},{2,34}... | collective-permute-start | bytes 1572872 | tf_op jit(solution)/shard_map/ppermute | solution.py:249
  30.8 16.9 %collective-permute-start.6 = (bf16[4,512,128]{2,1,0:T(8,128)(2,1)S(1)}, bf16[4,512,128]{2,1,0:T(8,128)(2,1)S(1)}, u32[]{:S(2)}, u32[]{:S(2)}) collective-permute-start(bf16[4,512,128]{2,1,0:T(8,128)(2,1)S(1)} %select_add_fusion.rest_0_), channel_id=1, source_target_pairs={{0,2},{2,4},{4,6},{6,0},{1,3},{3,5},{5,7},{7,1},{8,10},{10,12},{12... | collective-permute-start | bytes 1572872 | tf_op jit(solution)/shard_map/ppermute | solution.py:249
  32.4 25.5 %collective-permute-start.5 = (bf16[4,512,128]{2,1,0:T(8,128)(2,1)S(1)}, bf16[4,512,128]{2,1,0:T(8,128)(2,1)S(1)}, u32[]{:S(2)}, u32[]{:S(2)}) collective-permute-start(bf16[4,512,128]{2,1,0:T(8,128)(2,1)S(1)} %select_add_fusion.rest_0_), channel_id=1, source_target_pairs={{0,4},{2,6},{4,0},{6,2},{1,5},{3,7},{5,1},{7,3},{8,12},{10,14},{12... | collective-permute-start | bytes 1572872 | tf_op jit(solution)/shard_map/ppermute | solution.py:249
  35.7 24.1 %collective-permute-start.4 = (bf16[4,512,128]{2,1,0:T(8,128)(2,1)S(1)}, bf16[4,512,128]{2,1,0:T(8,128)(2,1)S(1)}, u32[]{:S(2)}, u32[]{:S(2)}) collective-permute-start(bf16[4,512,128]{2,1,0:T(8,128)(2,1)S(1)} %select_add_fusion.rest_0_), channel_id=1, source_target_pairs={{0,6},{2,0},{4,2},{6,4},{1,7},{3,1},{5,3},{7,5},{8,14},{10,8},{12,... | collective-permute-start | bytes 1572872 | tf_op jit(solution)/shard_map/ppermute | solution.py:249
  36.5 31.5 %collective-permute-start.16 = (bf16[2,256,512]{2,1,0:T(8,128)(2,1)S(1)}, bf16[2,256,512]{2,1,0:T(8,128)(2,1)S(1)}, u32[]{:S(2)}, u32[]{:S(2)}) collective-permute-start(bf16[2,256,512]{2,1,0:T(8,128)(2,1)S(1)} %slice_add_fusion), channel_id=1, source_target_pairs={{0,96},{32,0},{64,32},{96,64},{1,97},{33,1},{65,33},{97,65},{2,98}... | collective-permute-start | bytes 1572872 | tf_op jit(solution)/shard_map/ppermute | solution.py:249
  44.7 23.7 %collective-permute-start.3 = (bf16[4,512,128]{2,1,0:T(8,128)(2,1)S(1)}, bf16[4,512,128]{2,1,0:T(8,128)(2,1)S(1)}, u32[]{:S(2)}, u32[]{:S(2)}) collective-permute-start(bf16[4,512,128]{2,1,0:T(8,128)(2,1)S(1)} %broadcast_add_fusion), channel_id=1, source_target_pairs={{0,1},{17,16},{2,3},{19,18},{4,5},{21,20},{6,7},{23,22},{8,9},{25,... | collective-permute-start | bytes 1572872 | tf_op jit(solution)/shard_map/ppermute | solution.py:269
  47.7 29.2 %collective-permute-start.13 = (bf16[4,256,512]{2,1,0:T(8,128)(2,1)S(1)}, bf16[4,256,512]{2,1,0:T(8,128)(2,1)S(1)}, u32[]{:S(2)}, u32[]{:S(2)}) collective-permute-start(bf16[4,256,512]{2,1,0:T(8,128)(2,1)S(1)} %collective-permute-done.12.rest_9_), channel_id=1, source_target_pairs={{0,8},{8,0},{1,9},{9,1},{2,10},{10,2},{3,11},{11,3},{4,12},{12,4},... | collective-permute-start | bytes 3145736 | tf_op jit(solution)/shard_map/ppermute | solution.py:253
  57.8 21.2 %collective-permute-start.11 = (bf16[4,256,512]{2,1,0:T(8,128)(2,1)S(1)}, bf16[4,256,512]{2,1,0:T(8,128)(2,1)S(1)}, u32[]{:S(2)}, u32[]{:S(2)}) collective-permute-start(bf16[4,256,512]{2,1,0:T(8,128)(2,1)S(1)} %collective-permute-done.10.rest_7_), channel_id=1, source_target_pairs={{0,8},{8,0},{1,9},{9,1},{2,10},{10,2},{3,11},{11,3},{4,12},{12,4},... | collective-permute-start | bytes 3145736 | tf_op jit(solution)/shard_map/ppermute | solution.py:253
  59.8 16.0 %collective-permute-start.18 = (bf16[4,512,128]{2,1,0:T(8,128)(2,1)S(1)}, bf16[4,512,128]{2,1,0:T(8,128)(2,1)S(1)}, u32[]{:S(2)}, u32[]{:S(2)}) collective-permute-start(bf16[4,512,128]{2,1,0:T(8,128)(2,1)S(1)} %broadcast_add_fusion), channel_id=1, source_target_pairs={{17,1},{0,16},{19,3},{2,18},{21,5},{4,20},{23,7},{6,22},{25,9},{8,... | collective-permute-start | bytes 1572872 | tf_op jit(solution)/shard_map/ppermute | solution.py:269
  68.1 11.7 %collective-permute-start.15 = (bf16[2,256,512]{2,1,0:T(8,128)(2,1)S(1)}, bf16[2,256,512]{2,1,0:T(8,128)(2,1)S(1)}, u32[]{:S(2)}, u32[]{:S(2)}) collective-permute-start(bf16[2,256,512]{2,1,0:T(8,128)(2,1)S(1)} %collective-permute-done.14.rest_11_), channel_id=1, source_target_pairs={{0,8},{8,0},{1,9},{9,1},{2,10},{10,2},{3,11},{11,3},{4,12},{12,4},... | collective-permute-start | bytes 1572872 | tf_op jit(solution)/shard_map/ppermute | solution.py:253
  68.4 11.3 %collective-permute-start.17 = (bf16[2,256,512]{2,1,0:T(8,128)(2,1)S(1)}, bf16[2,256,512]{2,1,0:T(8,128)(2,1)S(1)}, u32[]{:S(2)}, u32[]{:S(2)}) collective-permute-start(bf16[2,256,512]{2,1,0:T(8,128)(2,1)S(1)} %collective-permute-done.16.rest_13_), channel_id=1, source_target_pairs={{0,8},{8,0},{1,9},{9,1},{2,10},{10,2},{3,11},{11,3},{4,12},{12,4},... | collective-permute-start | bytes 1572872 | tf_op jit(solution)/shard_map/ppermute | solution.py:253
  68.7 11.0 %copy-start.1 = (bf16[128,512]{1,0:T(8,128)(2,1)S(1)}, bf16[128,512]{1,0:T(8,128)(2,1)}, u32[]{:S(2)}) copy-start(bf16[128,512]{1,0:T(8,128)(2,1)} %w.1) | copy-start | bytes 393220
  68.7 11.0 %copy-start.3 = (bf16[4,256,512]{2,1,0:T(8,128)(2,1)S(1)}, bf16[4,256,512]{2,1,0:T(8,128)(2,1)}, u32[]{:S(2)}) copy-start(bf16[4,256,512]{2,1,0:T(8,128)(2,1)} %get-tuple-element.8.rest_5_) | copy-start | bytes 3145732
  75.8 28.2 %collective-permute-start.9 = (bf16[4,512,128]{2,1,0:T(8,128)(2,1)S(1)}, bf16[4,512,128]{2,1,0:T(8,128)(2,1)S(1)}, u32[]{:S(2)}, u32[]{:S(2)}) collective-permute-start(bf16[4,512,128]{2,1,0:T(8,128)(2,1)S(1)} %add_add_fusion.rest_0_), channel_id=1, source_target_pairs={{0,2},{2,4},{4,6},{6,0},{1,3},{3,5},{5,7},{7,1},{8,10},{10,12},{12... | collective-permute-start | bytes 1572872 | tf_op jit(solution)/shard_map/ppermute | solution.py:249
  76.9 27.1 %collective-permute-start.8 = (bf16[4,512,128]{2,1,0:T(8,128)(2,1)S(1)}, bf16[4,512,128]{2,1,0:T(8,128)(2,1)S(1)}, u32[]{:S(2)}, u32[]{:S(2)}) collective-permute-start(bf16[4,512,128]{2,1,0:T(8,128)(2,1)S(1)} %add_add_fusion.rest_0_), channel_id=1, source_target_pairs={{0,4},{2,6},{4,0},{6,2},{1,5},{3,7},{5,1},{7,3},{8,12},{10,14},{12... | collective-permute-start | bytes 1572872 | tf_op jit(solution)/shard_map/ppermute | solution.py:249
  79.0 25.0 %collective-permute-start.7 = (bf16[4,512,128]{2,1,0:T(8,128)(2,1)S(1)}, bf16[4,512,128]{2,1,0:T(8,128)(2,1)S(1)}, u32[]{:S(2)}, u32[]{:S(2)}) collective-permute-start(bf16[4,512,128]{2,1,0:T(8,128)(2,1)S(1)} %add_add_fusion.rest_0_), channel_id=1, source_target_pairs={{0,6},{2,0},{4,2},{6,4},{1,7},{3,1},{5,3},{7,5},{8,14},{10,8},{12,... | collective-permute-start | bytes 1572872 | tf_op jit(solution)/shard_map/ppermute | solution.py:249
  101.2 23.6 %copy-start.2 = (bf16[128,128]{1,0:T(8,128)(2,1)S(1)}, bf16[128,128]{1,0:T(8,128)(2,1)}, u32[]{:S(2)}) copy-start(bf16[128,128]{1,0:T(8,128)(2,1)} %w_out.1) | copy-start | bytes 98308
  101.2 23.6 %collective-permute-start.19 = (bf16[4,144,512]{2,1,0:T(8,128)(2,1)S(1)}, bf16[4,144,512]{2,1,0:T(8,128)(2,1)S(1)}, u32[]{:S(2)}, u32[]{:S(2)}) collective-permute-start(bf16[4,144,512]{2,1,0:T(8,128)(2,1)S(1)} %attend.3), channel_id=1, source_target_pairs={{0,16},{16,0},{1,17},{17,1},{2,18},{18,2},{3,19},{19,3},{4,20},{20... | collective-permute-start | bytes 1769480 | tf_op jit(solution)/shard_map/ppermute | solution.py:285

commit v11 on v6

--- a/solution.py
+++ b/solution.py
@@ -1,3 +1,5 @@
+import functools
+
 import jax
 import jax.numpy as jnp
 from jax import lax
@@ -28,21 +30,22 @@
     keys = bias.shape[2]
     places = [lax.broadcasted_iota(jnp.int32, (keys, keys), axis) for axis in (0, 1)]
     identity = (places[0] == places[1]).astype(F32).astype(BF16)
-    values = pair[0].astype(F32)
+    values = pair[...].astype(F32)
     centered = values - jnp.mean(values, axis=-1, keepdims=True)
     variance = jnp.mean(centered * centered, axis=-1, keepdims=True)
-    normed[0] = (centered * lax.rsqrt(variance + 1e-05) * gain[...]).astype(BF16)
-    bias_t[0] = matmul(identity, bias[0], 1, 1).astype(BF16)
+    normed[...] = (centered * lax.rsqrt(variance + 1e-05) * gain[...]).astype(BF16)
+    for h in range(bias.shape[0]):
+        bias_t[h] = matmul(identity, bias[h], 1, 1).astype(BF16)
 
 
 def prepare(pair_block, norm_gain, head_bias):
     def whole(*shape):
-        return pl.BlockSpec((1,) + shape, lambda i: (i, 0, 0))
+        return pl.BlockSpec((2,) + shape, lambda i: (i, 0, 0))
 
     keys = head_bias.shape[2]
     return pl.pallas_call(
         prepare_kernel,
-        grid=(ROWS,),
+        grid=(ROWS // 2,),
         in_specs=[
             whole(COLS, CHANNELS),
             pl.BlockSpec((1, CHANNELS), lambda i: (0, 0)),
@@ -57,7 +60,8 @@
     )(pair_block, norm_gain.reshape(1, CHANNELS), head_bias)
 
 
-def attend_kernel(xq, xk0, xk1, xk2, xk3, w, *rest):
+def attend_kernel(blocks, xq, *rest):
+    xks, w, rest = rest[:blocks], rest[blocks], rest[blocks + 1 :]
     biases, out, scratch = rest[:10], rest[-9], rest[-8:]
     bias_s, top_s, k_s, v_s, q_s, gate_s, stat_s, sems = scratch
     step = pl.program_id(0)
@@ -91,7 +95,7 @@
             at = slice(h * WIDTH, (h + 1) * WIDTH)
             q_s[r, h, at, :] = q_t[at]
         start = 0
-        for x in (xk0, xk1, xk2, xk3):
+        for x in xks:
             size = x.shape[1]
             at = slice(start, start + size)
             k_s[r, at, :] = matmul(x[r], w[:, 128:256]).astype(BF16)
@@ -190,7 +194,7 @@
     scores = ROWS * HEADS * COLS * KEYS
     block = (16, ROWS + 1, SHARE, CHANNELS)
     return pl.pallas_call(
-        attend_kernel,
+        functools.partial(attend_kernel, len(x_ks)),
         grid=(ROWS // STEP,),
         in_specs=[rows(x_q)]
         + [rows(x) for x in x_ks]
@@ -198,7 +202,7 @@
         + [pl.BlockSpec(memory_space=pl.ANY)] * (len(biases) + len(message)),
         out_specs=pl.BlockSpec(block, lambda i: (0, half, 0, 0)),
         out_shape=jax.ShapeDtypeStruct((16, 2 * (ROWS + 1), SHARE, CHANNELS), BF16),
-        input_output_aliases={6 + len(biases): 0} if half else {},
+        input_output_aliases={2 + len(x_ks) + len(biases): 0} if half else {},
         scratch_shapes=[
             pltpu.VMEM((4, HEADS, BLOCK, COLS), BF16),
             pltpu.VMEM((HEADS, COLS), F32),
@@ -270,6 +274,13 @@
     return x, shift(x, axis, -1), shift(x, axis, 2), shift(x, axis, 1)
 
 
+def gather_ring(x, axis):
+    behind, ahead = shift(x, axis, 1), shift(x, axis, -1)
+    parts = tied(behind[:, :256], ahead), tied(ahead[:, 256:], behind)
+    far = shift(parts[0], axis, 1), shift(parts[1], axis, -1)
+    return x, ahead, *far, behind
+
+
 def gather_bias(block):
     behind, ahead = shift(block, "y", 1), shift(block, "y", -1)
     far = [shift(behind[:2], "y", 1), shift(ahead[2:], "y", -1)]
@@ -284,9 +295,9 @@
     behind, ahead = shift(own, ("xh", "xl"), 1), shift(own, ("xh", "xl"), -1)
     opposite = shift(behind, ("xh", "xl"), 1)
     near = jnp.where(xh == 0, behind, ahead)
-    first_ks = gather_direct(tied(jnp.where(xl == xh, own, near), biases[1]), "z")
+    first_ks = gather_ring(tied(jnp.where(xl == xh, own, near), biases[1]), "z")
     near = jnp.where(xh == 0, ahead, behind)
-    second_ks = gather_direct(tied(jnp.where(xl == xh, opposite, near), *first_ks[1:]), "z")
+    second_ks = gather_direct(tied(jnp.where(xl == xh, opposite, near), first_ks[1], first_ks[4]), "z")
 
     message = attend(own, first_ks, w_project, biases)
     message = attend(opposite, second_ks, w_project, biases, (message,))

time: 144 us -> 139 us (0.965)
  waiting for transfers between devices: 41.1 us -> 31.8 us
  starting transfers between devices: 20.2 us -> 26 us
    ppermute x13 -> x14, waiting for transfers between devices: 41.1 us -> 31.7 us  [shift(): return lax.ppermute(x, axis, [(i, (i + step) % 4) for i in range(4)])]
    ppermute x5, starting transfers between devices: 4.5 us -> 9.66 us  [swap(): return lax.ppermute(x, 'core', [(0, 1), (1, 0)])]
    ppermute x13 -> x14, starting transfers between devices: 15.7 us -> 16.4 us  [shift(): return lax.ppermute(x, axis, [(i, (i + step) % 4) for i in range(4)])]
  transfers between devices with their start and end apart: 18 -> 19, of which waited for: 6 -> 9; matrix products, arithmetic and copies ran while one was open for 3% -> 3% of each run, Pallas kernels for 15% -> 15%
where the time goes in v11:
time: 139 us
  Pallas kernels  48.3 us (35%)
  waiting for transfers between devices  31.8 us (23%)
  blocking collectives  26.6 us (19%)
  starting transfers between devices  26 us (19%)
  other arithmetic  2.54 us (2%)
  between operations  2.14 us (2%)
  local copies, waits for them, and re-layouts  1.81 us (1%)
    pallas_call x2, Pallas kernels, attend(): pl.pallas_call(functools.partial(attend_kernel, len(x_ks)), grid=(ROWS //...  42.8 us
    ppermute x14, waiting for transfers between devices, shift(): return lax.ppermute(x, axis, [(i, (i + step) % 4) for i in range(4)])  31.7 us
    all_to_all x1, blocking collectives, shards(): lax.all_to_all(message, ROW_AXES, split_axis=0, concat_axis=0, tiled=True)  26.6 us
    ppermute x14, starting transfers between devices, shift(): return lax.ppermute(x, axis, [(i, (i + step) % 4) for i in range(4)])  16.4 us
    ppermute x5, starting transfers between devices, swap(): return lax.ppermute(x, 'core', [(0, 1), (1, 0)])  9.66 us
    pallas_call x1, Pallas kernels, prepare(): pl.pallas_call(prepare_kernel, grid=(ROWS // 2,), in_specs=[whole(COLS, C...  2.79 us
  transfers between devices with their start and end apart: 19, of which 9 were waited for; matrix products, arithmetic and copies ran while one was open for 3% of the time, Pallas kernels for 15%

profile of v11, /device:TPU:1, one launch (start us, length us, event | category | flops | bytes accessed | tf_op | source)
XLA Modules:
  0.0 139.2 jit_solution(11048136001629931212)
XLA Ops:
  0.0 2.8 %prepare.1 = (bf16[4,512,128]{2,1,0:T(8,128)(2,1)}, bf16[4,256,512]{2,1,0:T(8,128)(2,1)}) custom-call(bf16[4,512,128]{2,1,0:T(8,128)(2,1)} %pair.1, f32[1,128]{1,0:T(1,128)} %bitcast.4, bf16[4,512,256]{2,1,0:T(8,128)(2,1)} %bias.1), custom_call_target="tpu_custom_call" | custom-call | tf_op jit(solution)/shard_map/prepare/pallas_call | solution.py:46
  2.8 1.4 %collective-permute-start.3 = (bf16[4,256,512]{2,1,0:T(8,128)(2,1)}, bf16[4,256,512]{2,1,0:T(8,128)(2,1)S(1)}, u32[]{:S(2)}, u32[]{:S(2)}) collective-permute-start(bf16[4,256,512]{2,1,0:T(8,128)(2,1)} %get-tuple-element.8.rest_6_.rest_5_), channel_id=1, source_target_pairs={{0,8},{8,0},{1,9},{9,1},{2,10},{10,2},{3,11},{11,3},{4,12},{12,4},... | collective-permute-start | bytes 3145736 | tf_op jit(solution)/shard_map/ppermute | solution.py:270
  4.2 2.6 %collective-permute-start.2 = (bf16[4,512,128]{2,1,0:T(8,128)(2,1)}, bf16[4,512,128]{2,1,0:T(8,128)(2,1)}, u32[]{:S(2)}, u32[]{:S(2)}) collective-permute-start(bf16[4,512,128]{2,1,0:T(8,128)(2,1)} %get-tuple-element.7.xq), channel_id=1, source_target_pairs={{0,17},{1,0},{16,1},{17,16},{2,19},{3,2},{18,3},{19,18},{4,21},{5,... | collective-permute-start | bytes 1572872 | tf_op jit(solution)/shard_map/ppermute | solution.py:266
  6.8 1.3 collective-permute-start.11
  8.1 1.4 %collective-permute-start.9 = (bf16[4,256,512]{2,1,0:T(8,128)(2,1)}, bf16[4,256,512]{2,1,0:T(8,128)(2,1)S(1)}, u32[]{:S(2)}, u32[]{:S(2)}) collective-permute-start(bf16[4,256,512]{2,1,0:T(8,128)(2,1)} %get-tuple-element.8.rest_6_.rest_5_), channel_id=1, source_target_pairs={{0,96},{32,0},{64,32},{96,64},{1,97},{33,1},{65,33},{97,65},{2,98}... | collective-permute-start | bytes 3145736 | tf_op jit(solution)/shard_map/ppermute | solution.py:266
  10.7 7.6 %collective-permute-done.2 = bf16[4,512,128]{2,1,0:T(8,128)(2,1)} collective-permute-done((bf16[4,512,128]{2,1,0:T(8,128)(2,1)}, bf16[4,512,128]{2,1,0:T(8,128)(2,1)}, u32[]{:S(2)}, u32[]{:S(2)}) %collective-permute-start.2) | collective-permute-done | bytes 524320 | tf_op jit(solution)/shard_map/ppermute | solution.py:266
  18.4 3.1 %collective-permute-done = bf16[4,512,128]{2,1,0:T(8,128)(2,1)} collective-permute-done((bf16[4,512,128]{2,1,0:T(8,128)(2,1)}, bf16[4,512,128]{2,1,0:T(8,128)(2,1)}, u32[]{:S(2)}, u32[]{:S(2)}) %collective-permute-start) | collective-permute-done | bytes 524320 | tf_op jit(solution)/shard_map/ppermute | solution.py:266
  22.7 1.7 %collective-permute-start.5 = (bf16[4,512,128]{2,1,0:T(8,128)(2,1)S(1)}, bf16[4,512,128]{2,1,0:T(8,128)(2,1)S(1)}, u32[]{:S(2)}, u32[]{:S(2)}) collective-permute-start(bf16[4,512,128]{2,1,0:T(8,128)(2,1)S(1)} %select_add_fusion.rest_0_), channel_id=1, source_target_pairs={{0,2},{2,4},{4,6},{6,0},{1,3},{3,5},{5,7},{7,1},{8,10},{10,12},{12... | collective-permute-start | bytes 1572872 | tf_op jit(solution)/shard_map/ppermute | solution.py:266
  24.4 2.2 %collective-permute-start.4 = (bf16[4,512,128]{2,1,0:T(8,128)(2,1)S(1)}, bf16[4,512,128]{2,1,0:T(8,128)(2,1)S(1)}, u32[]{:S(2)}, u32[]{:S(2)}) collective-permute-start(bf16[4,512,128]{2,1,0:T(8,128)(2,1)S(1)} %select_add_fusion.rest_0_), channel_id=1, source_target_pairs={{0,6},{2,0},{4,2},{6,4},{1,7},{3,1},{5,3},{7,5},{8,14},{10,8},{12,... | collective-permute-start | bytes 1572872 | tf_op jit(solution)/shard_map/ppermute | solution.py:266
  26.6 6.1 %collective-permute-done.11.rest_10_.rest_9_ = bf16[4,256,512]{2,1,0:T(8,128)(2,1)S(1)} collective-permute-done((bf16[4,256,512]{2,1,0:T(8,128)(2,1)}, bf16[4,256,512]{2,1,0:T(8,128)(2,1)S(1)}, u32[]{:S(2)}, u32[]{:S(2)}) %collective-permute-start.11) | collective-permute-done | bytes 1048608 | tf_op jit(solution)/shard_map/ppermute | solution.py:266
  32.9 1.4 collective-permute-start.12
  34.3 3.3 %collective-permute-done.5.rest_4_ = bf16[4,512,128]{2,1,0:T(8,128)(2,1)S(1)} collective-permute-done((bf16[4,512,128]{2,1,0:T(8,128)(2,1)S(1)}, bf16[4,512,128]{2,1,0:T(8,128)(2,1)S(1)}, u32[]{:S(2)}, u32[]{:S(2)}) %collective-permute-start.5) | collective-permute-done | bytes 524320 | tf_op jit(solution)/shard_map/ppermute | solution.py:266
  37.6 2.7 %collective-permute-start.15 = (bf16[2,256,512]{2,1,0:T(8,128)(2,1)S(1)}, bf16[2,256,512]{2,1,0:T(8,128)(2,1)S(1)}, u32[]{:S(2)}, u32[]{:S(2)}) collective-permute-start(bf16[2,256,512]{2,1,0:T(8,128)(2,1)S(1)} %slice.34), channel_id=1, source_target_pairs={{0,96},{32,0},{64,32},{96,64},{1,97},{33,1},{65,33},{97,65},{2,98}... | collective-permute-start | bytes 1572872 | tf_op jit(solution)/shard_map/ppermute | solution.py:266
  40.4 2.1 %collective-permute-start.10 = (bf16[4,256,512]{2,1,0:T(8,128)(2,1)S(1)}, bf16[4,256,512]{2,1,0:T(8,128)(2,1)S(1)}, u32[]{:S(2)}, u32[]{:S(2)}) collective-permute-start(bf16[4,256,512]{2,1,0:T(8,128)(2,1)S(1)} %collective-permute-done.9.rest_8_.rest_7_), channel_id=1, source_target_pairs={{0,8},{8,0},{1,9},{9,1},{2,10},{10,2},{3,11},{11,3},{4,12},{12,4},... | collective-permute-start | bytes 3145736 | tf_op jit(solution)/shard_map/ppermute | solution.py:270
  43.7 1.5 %collective-permute-start.18 = (bf16[4,256,128]{2,1,0:T(8,128)(2,1)S(1)}, bf16[4,256,128]{2,1,0:T(8,128)(2,1)S(1)}, u32[]{:S(2)}, u32[]{:S(2)}) collective-permute-start(bf16[4,256,128]{2,1,0:T(8,128)(2,1)S(1)} %slice_add_fusion), channel_id=1, source_target_pairs={{0,6},{2,0},{4,2},{6,4},{1,7},{3,1},{5,3},{7,5},{8,14},{10,8},{12,... | collective-permute-start | bytes 786440 | tf_op jit(solution)/shard_map/ppermute | solution.py:266
  46.4 2.0 %collective-permute-start.14 = (bf16[2,256,512]{2,1,0:T(8,128)(2,1)S(1)}, bf16[2,256,512]{2,1,0:T(8,128)(2,1)S(1)}, u32[]{:S(2)}, u32[]{:S(2)}) collective-permute-start(bf16[2,256,512]{2,1,0:T(8,128)(2,1)S(1)} %collective-permute-done.13.rest_12_.rest_11_), channel_id=1, source_target_pairs={{0,8},{8,0},{1,9},{9,1},{2,10},{10,2},{3,11},{11,3},{4,12},{12,4},... | collective-permute-start | bytes 1572872 | tf_op jit(solution)/shard_map/ppermute | solution.py:270
  48.4 1.4 collective-permute-done.15.rest_14_.rest_13_
  49.8 2.7 %collective-permute-start.16 = (bf16[2,256,512]{2,1,0:T(8,128)(2,1)S(1)}, bf16[2,256,512]{2,1,0:T(8,128)(2,1)S(1)}, u32[]{:S(2)}, u32[]{:S(2)}) collective-permute-start(bf16[2,256,512]{2,1,0:T(8,128)(2,1)S(1)} %collective-permute-done.15.rest_14_.rest_13_), channel_id=1, source_target_pairs={{0,8},{8,0},{1,9},{9,1},{2,10},{10,2},{3,11},{11,3},{4,12},{12,4},... | collective-permute-start | bytes 1572872 | tf_op jit(solution)/shard_map/ppermute | solution.py:270
  55.2 7.9 %collective-permute-done.17.rest_2_ = bf16[4,256,128]{2,1,0:T(8,128)(2,1)S(1)} collective-permute-done((bf16[4,256,128]{2,1,0:T(8,128)(2,1)S(1)}, bf16[4,256,128]{2,1,0:T(8,128)(2,1)S(1)}, u32[]{:S(2)}, u32[]{:S(2)}) %collective-permute-start.17) | collective-permute-done | bytes 262176 | tf_op jit(solution)/shard_map/ppermute | solution.py:266
  64.2 1.7 %collective-permute-start.6 = (bf16[4,512,128]{2,1,0:T(8,128)(2,1)S(1)}, bf16[4,512,128]{2,1,0:T(8,128)(2,1)S(1)}, u32[]{:S(2)}, u32[]{:S(2)}) collective-permute-start(bf16[4,512,128]{2,1,0:T(8,128)(2,1)S(1)} %add_add_fusion.rest_0_), channel_id=1, source_target_pairs={{0,6},{2,0},{4,2},{6,4},{1,7},{3,1},{5,3},{7,5},{8,14},{10,8},{12,... | collective-permute-start | bytes 1572872 | tf_op jit(solution)/shard_map/ppermute | solution.py:266
  65.9 21.5 %attend.2.rest_15_ = bf16[16,10,32,128]{3,2,1,0:T(8,128)(2,1)S(1)} custom-call(bf16[4,512,128]{2,1,0:T(8,128)(2,1)S(1)} %copy-done, bf16[4,512,128]{2,1,0:T(8,128)(2,1)S(1)} %select_add_fusion.rest_0_, bf16[4,512,128]{2,1,0:T(8,128)(2,1)S(1)} %collective-permute-done.4.rest_1_, bf16[4,256,128]{2,1,0:T(8,128)(2,1)S(1)} %collective-permute-done.17.rest_2_, ...), custom_call_target="tpu_custom_call" | custom-call | flops 8589934592 | bytes 16777216 | tf_op jit(solution)/shard_map/attend/pallas_call | solution.py:196
  88.6 21.3 %attend.3 = bf16[16,10,32,128]{3,2,1,0:T(8,128)(2,1)S(1)} custom-call(bf16[4,512,128]{2,1,0:T(8,128)(2,1)S(1)} %collective-permute-done.1.xq, bf16[4,512,128]{2,1,0:T(8,128)(2,1)S(1)} %add_add_fusion.rest_0_, bf16[4,512,128]{2,1,0:T(8,128)(2,1)S(1)} %collective-permute-done.6.rest_1_, ...), custom_call_target="tpu_custom_call", output_to_operand_aliasing={{}: (16, {})} | custom-call | flops 8589934592 | bytes 16777216 | tf_op jit(solution)/shard_map/attend/pallas_call | solution.py:196
  109.9 26.6 %all_to_all.5.message = bf16[16,10,32,128]{3,2,1,0:T(8,128)(2,1)S(1)} all-to-all(bf16[16,10,32,128]{3,2,1,0:T(8,128)(2,1)S(1)} %attend.3), channel_id=1, replica_groups=mesh['y'=4,'xh'=2,'core'=2,'z'=4,'xl'=2] {'y','xh','core'}, dimensions={0} | all-to-all | bytes 2621440 | tf_op jit(solution)/shard_map/all_to_all | solution.py:304
  136.5 2.6 %merge.1 = bf16[32,64,128]{2,1,0:T(8,128)(2,1)} custom-call(bf16[16,10,32,128]{3,2,1,0:T(8,128)(2,1)S(1)} %all_to_all.5.message, bf16[128,128]{1,0:T(8,128)(2,1)S(1)} %copy-done.1), custom_call_target="tpu_custom_call" | custom-call | tf_op jit(solution)/shard_map/merge/pallas_call | solution.py:245
  (36 shorter events, 7.9 us)
Async XLA Ops:
  2.8 6.7 %collective-permute-start.3 = (bf16[4,256,512]{2,1,0:T(8,128)(2,1)}, bf16[4,256,512]{2,1,0:T(8,128)(2,1)S(1)}, u32[]{:S(2)}, u32[]{:S(2)}) collective-permute-start(bf16[4,256,512]{2,1,0:T(8,128)(2,1)} %get-tuple-element.8.rest_6_.rest_5_), channel_id=1, source_target_pairs={{0,8},{8,0},{1,9},{9,1},{2,10},{10,2},{3,11},{11,3},{4,12},{12,4},... | collective-permute-start | bytes 3145736 | tf_op jit(solution)/shard_map/ppermute | solution.py:270
  4.2 14.2 %collective-permute-start.2 = (bf16[4,512,128]{2,1,0:T(8,128)(2,1)}, bf16[4,512,128]{2,1,0:T(8,128)(2,1)}, u32[]{:S(2)}, u32[]{:S(2)}) collective-permute-start(bf16[4,512,128]{2,1,0:T(8,128)(2,1)} %get-tuple-element.7.xq), channel_id=1, source_target_pairs={{0,17},{1,0},{16,1},{17,16},{2,19},{3,2},{18,3},{19,18},{4,21},{5,... | collective-permute-start | bytes 1572872 | tf_op jit(solution)/shard_map/ppermute | solution.py:266
  6.8 14.7 %collective-permute-start = (bf16[4,512,128]{2,1,0:T(8,128)(2,1)}, bf16[4,512,128]{2,1,0:T(8,128)(2,1)}, u32[]{:S(2)}, u32[]{:S(2)}) collective-permute-start(bf16[4,512,128]{2,1,0:T(8,128)(2,1)} %get-tuple-element.7.xq), channel_id=1, source_target_pairs={{0,1},{1,16},{16,17},{17,0},{2,3},{3,18},{18,19},{19,2},{4,5},{5,2... | collective-permute-start | bytes 1572872 | tf_op jit(solution)/shard_map/ppermute | solution.py:266
  6.8 26.0 %collective-permute-start.11 = (bf16[4,256,512]{2,1,0:T(8,128)(2,1)}, bf16[4,256,512]{2,1,0:T(8,128)(2,1)S(1)}, u32[]{:S(2)}, u32[]{:S(2)}) collective-permute-start(bf16[4,256,512]{2,1,0:T(8,128)(2,1)} %get-tuple-element.8.rest_6_.rest_5_), channel_id=1, source_target_pairs={{0,32},{32,64},{64,96},{96,0},{1,33},{33,65},{65,97},{97,1},{2,34}... | collective-permute-start | bytes 3145736 | tf_op jit(solution)/shard_map/ppermute | solution.py:266
  8.1 24.8 %collective-permute-start.9 = (bf16[4,256,512]{2,1,0:T(8,128)(2,1)}, bf16[4,256,512]{2,1,0:T(8,128)(2,1)S(1)}, u32[]{:S(2)}, u32[]{:S(2)}) collective-permute-start(bf16[4,256,512]{2,1,0:T(8,128)(2,1)} %get-tuple-element.8.rest_6_.rest_5_), channel_id=1, source_target_pairs={{0,96},{32,0},{64,32},{96,64},{1,97},{33,1},{65,33},{97,65},{2,98}... | collective-permute-start | bytes 3145736 | tf_op jit(solution)/shard_map/ppermute | solution.py:266
  22.7 14.9 %collective-permute-start.5 = (bf16[4,512,128]{2,1,0:T(8,128)(2,1)S(1)}, bf16[4,512,128]{2,1,0:T(8,128)(2,1)S(1)}, u32[]{:S(2)}, u32[]{:S(2)}) collective-permute-start(bf16[4,512,128]{2,1,0:T(8,128)(2,1)S(1)} %select_add_fusion.rest_0_), channel_id=1, source_target_pairs={{0,2},{2,4},{4,6},{6,0},{1,3},{3,5},{5,7},{7,1},{8,10},{10,12},{12... | collective-permute-start | bytes 1572872 | tf_op jit(solution)/shard_map/ppermute | solution.py:266
  24.4 15.9 %collective-permute-start.4 = (bf16[4,512,128]{2,1,0:T(8,128)(2,1)S(1)}, bf16[4,512,128]{2,1,0:T(8,128)(2,1)S(1)}, u32[]{:S(2)}, u32[]{:S(2)}) collective-permute-start(bf16[4,512,128]{2,1,0:T(8,128)(2,1)S(1)} %select_add_fusion.rest_0_), channel_id=1, source_target_pairs={{0,6},{2,0},{4,2},{6,4},{1,7},{3,1},{5,3},{7,5},{8,14},{10,8},{12,... | collective-permute-start | bytes 1572872 | tf_op jit(solution)/shard_map/ppermute | solution.py:266
  26.6 17.1 %collective-permute-start.1 = (bf16[4,512,128]{2,1,0:T(8,128)(2,1)}, bf16[4,512,128]{2,1,0:T(8,128)(2,1)S(1)}, u32[]{:S(2)}, u32[]{:S(2)}) collective-permute-start(bf16[4,512,128]{2,1,0:T(8,128)(2,1)} %collective-permute-done), channel_id=1, source_target_pairs={{0,1},{1,16},{16,17},{17,0},{2,3},{3,18},{18,19},{19,2},{4,5},{5,2... | collective-permute-start | bytes 1572872 | tf_op jit(solution)/shard_map/ppermute | solution.py:266
  32.8 13.6 %collective-permute-start.13 = (bf16[2,256,512]{2,1,0:T(8,128)(2,1)S(1)}, bf16[2,256,512]{2,1,0:T(8,128)(2,1)S(1)}, u32[]{:S(2)}, u32[]{:S(2)}) collective-permute-start(bf16[2,256,512]{2,1,0:T(8,128)(2,1)S(1)} %slice.33), channel_id=1, source_target_pairs={{0,32},{32,64},{64,96},{96,0},{1,33},{33,65},{65,97},{97,1},{2,34}... | collective-permute-start | bytes 1572872 | tf_op jit(solution)/shard_map/ppermute | solution.py:266
  32.9 31.3 %collective-permute-start.12 = (bf16[4,256,512]{2,1,0:T(8,128)(2,1)S(1)}, bf16[4,256,512]{2,1,0:T(8,128)(2,1)S(1)}, u32[]{:S(2)}, u32[]{:S(2)}) collective-permute-start(bf16[4,256,512]{2,1,0:T(8,128)(2,1)S(1)} %collective-permute-done.11.rest_10_.rest_9_), channel_id=1, source_target_pairs={{0,8},{8,0},{1,9},{9,1},{2,10},{10,2},{3,11},{11,3},{4,12},{12,4},... | collective-permute-start | bytes 3145736 | tf_op jit(solution)/shard_map/ppermute | solution.py:270
  37.6 12.1 %collective-permute-start.15 = (bf16[2,256,512]{2,1,0:T(8,128)(2,1)S(1)}, bf16[2,256,512]{2,1,0:T(8,128)(2,1)S(1)}, u32[]{:S(2)}, u32[]{:S(2)}) collective-permute-start(bf16[2,256,512]{2,1,0:T(8,128)(2,1)S(1)} %slice.34), channel_id=1, source_target_pairs={{0,96},{32,0},{64,32},{96,64},{1,97},{33,1},{65,33},{97,65},{2,98}... | collective-permute-start | bytes 1572872 | tf_op jit(solution)/shard_map/ppermute | solution.py:266
  40.4 25.5 %collective-permute-start.10 = (bf16[4,256,512]{2,1,0:T(8,128)(2,1)S(1)}, bf16[4,256,512]{2,1,0:T(8,128)(2,1)S(1)}, u32[]{:S(2)}, u32[]{:S(2)}) collective-permute-start(bf16[4,256,512]{2,1,0:T(8,128)(2,1)S(1)} %collective-permute-done.9.rest_8_.rest_7_), channel_id=1, source_target_pairs={{0,8},{8,0},{1,9},{9,1},{2,10},{10,2},{3,11},{11,3},{4,12},{12,4},... | collective-permute-start | bytes 3145736 | tf_op jit(solution)/shard_map/ppermute | solution.py:270
  43.7 10.2 %collective-permute-start.18 = (bf16[4,256,128]{2,1,0:T(8,128)(2,1)S(1)}, bf16[4,256,128]{2,1,0:T(8,128)(2,1)S(1)}, u32[]{:S(2)}, u32[]{:S(2)}) collective-permute-start(bf16[4,256,128]{2,1,0:T(8,128)(2,1)S(1)} %slice_add_fusion), channel_id=1, source_target_pairs={{0,6},{2,0},{4,2},{6,4},{1,7},{3,1},{5,3},{7,5},{8,14},{10,8},{12,... | collective-permute-start | bytes 786440 | tf_op jit(solution)/shard_map/ppermute | solution.py:266
  46.4 16.7 %collective-permute-start.14 = (bf16[2,256,512]{2,1,0:T(8,128)(2,1)S(1)}, bf16[2,256,512]{2,1,0:T(8,128)(2,1)S(1)}, u32[]{:S(2)}, u32[]{:S(2)}) collective-permute-start(bf16[2,256,512]{2,1,0:T(8,128)(2,1)S(1)} %collective-permute-done.13.rest_12_.rest_11_), channel_id=1, source_target_pairs={{0,8},{8,0},{1,9},{9,1},{2,10},{10,2},{3,11},{11,3},{4,12},{12,4},... | collective-permute-start | bytes 1572872 | tf_op jit(solution)/shard_map/ppermute | solution.py:270
  49.8 16.1 %collective-permute-start.16 = (bf16[2,256,512]{2,1,0:T(8,128)(2,1)S(1)}, bf16[2,256,512]{2,1,0:T(8,128)(2,1)S(1)}, u32[]{:S(2)}, u32[]{:S(2)}) collective-permute-start(bf16[2,256,512]{2,1,0:T(8,128)(2,1)S(1)} %collective-permute-done.15.rest_14_.rest_13_), channel_id=1, source_target_pairs={{0,8},{8,0},{1,9},{9,1},{2,10},{10,2},{3,11},{11,3},{4,12},{12,4},... | collective-permute-start | bytes 1572872 | tf_op jit(solution)/shard_map/ppermute | solution.py:270
  53.8 12.1 %copy-start = (bf16[4,512,128]{2,1,0:T(8,128)(2,1)S(1)}, bf16[4,512,128]{2,1,0:T(8,128)(2,1)}, u32[]{:S(2)}) copy-start(bf16[4,512,128]{2,1,0:T(8,128)(2,1)} %get-tuple-element.7.xq) | copy-start | bytes 1572868
  53.8 12.1 %copy-start.2 = (bf16[4,256,512]{2,1,0:T(8,128)(2,1)S(1)}, bf16[4,256,512]{2,1,0:T(8,128)(2,1)}, u32[]{:S(2)}) copy-start(bf16[4,256,512]{2,1,0:T(8,128)(2,1)} %get-tuple-element.8.rest_6_.rest_5_) | copy-start | bytes 3145732
  53.8 12.1 %copy-start.3 = (bf16[128,512]{1,0:T(8,128)(2,1)S(1)}, bf16[128,512]{1,0:T(8,128)(2,1)}, u32[]{:S(2)}) copy-start(bf16[128,512]{1,0:T(8,128)(2,1)} %rest_4_.1) | copy-start | bytes 393220
  53.9 9.2 %collective-permute-start.17 = (bf16[4,256,128]{2,1,0:T(8,128)(2,1)S(1)}, bf16[4,256,128]{2,1,0:T(8,128)(2,1)S(1)}, u32[]{:S(2)}, u32[]{:S(2)}) collective-permute-start(bf16[4,256,128]{2,1,0:T(8,128)(2,1)S(1)} %slice_add_fusion.1), channel_id=1, source_target_pairs={{0,2},{2,4},{4,6},{6,0},{1,3},{3,5},{5,7},{7,1},{8,10},{10,12},{12... | collective-permute-start | bytes 786440 | tf_op jit(solution)/shard_map/ppermute | solution.py:266
  63.1 25.1 %collective-permute-start.8 = (bf16[4,512,128]{2,1,0:T(8,128)(2,1)S(1)}, bf16[4,512,128]{2,1,0:T(8,128)(2,1)S(1)}, u32[]{:S(2)}, u32[]{:S(2)}) collective-permute-start(bf16[4,512,128]{2,1,0:T(8,128)(2,1)S(1)} %add_add_fusion.rest_0_), channel_id=1, source_target_pairs={{0,2},{2,4},{4,6},{6,0},{1,3},{3,5},{5,7},{7,1},{8,10},{10,12},{12... | collective-permute-start | bytes 1572872 | tf_op jit(solution)/shard_map/ppermute | solution.py:266
  63.1 25.1 %collective-permute-start.7 = (bf16[4,512,128]{2,1,0:T(8,128)(2,1)S(1)}, bf16[4,512,128]{2,1,0:T(8,128)(2,1)S(1)}, u32[]{:S(2)}, u32[]{:S(2)}) collective-permute-start(bf16[4,512,128]{2,1,0:T(8,128)(2,1)S(1)} %add_add_fusion.rest_0_), channel_id=1, source_target_pairs={{0,4},{2,6},{4,0},{6,2},{1,5},{3,7},{5,1},{7,3},{8,12},{10,14},{12... | collective-permute-start | bytes 1572872 | tf_op jit(solution)/shard_map/ppermute | solution.py:266
  64.2 24.4 %collective-permute-start.6 = (bf16[4,512,128]{2,1,0:T(8,128)(2,1)S(1)}, bf16[4,512,128]{2,1,0:T(8,128)(2,1)S(1)}, u32[]{:S(2)}, u32[]{:S(2)}) collective-permute-start(bf16[4,512,128]{2,1,0:T(8,128)(2,1)S(1)} %add_add_fusion.rest_0_), channel_id=1, source_target_pairs={{0,6},{2,0},{4,2},{6,4},{1,7},{3,1},{5,3},{7,5},{8,14},{10,8},{12,... | collective-permute-start | bytes 1572872 | tf_op jit(solution)/shard_map/ppermute | solution.py:266
  109.9 26.6 %copy-start.1 = (bf16[128,128]{1,0:T(8,128)(2,1)S(1)}, bf16[128,128]{1,0:T(8,128)(2,1)}, u32[]{:S(2)}) copy-start(bf16[128,128]{1,0:T(8,128)(2,1)} %w.1) | copy-start | bytes 98308

commit v12 on v11

--- a/solution.py
+++ b/solution.py
@@ -18,7 +18,7 @@
 LOW, HIGH = 1e-26, 1e30
 ROW_AXES = ("y", "xh", "core")
 COL_AXES = ("z", "xl")
-VMEM_LIMIT = 32 * 2**20
+VMEM_LIMIT = 40 * 2**20
 
 
 def matmul(a, b, first=1, second=0):
@@ -62,8 +62,8 @@
 
 def attend_kernel(blocks, xq, *rest):
     xks, w, rest = rest[:blocks], rest[blocks], rest[blocks + 1 :]
-    biases, out, scratch = rest[:10], rest[-9], rest[-8:]
-    bias_s, top_s, k_s, v_s, q_s, gate_s, stat_s, sems = scratch
+    biases, out, scratch = rest[:10], rest[-10], rest[-9:]
+    bias_s, scaled_s, top_s, k_s, v_s, q_s, gate_s, stat_s, sems = scratch
     step = pl.program_id(0)
 
     y, z, core = lax.axis_index("y"), lax.axis_index("z"), lax.axis_index("core")
@@ -130,21 +130,24 @@
         for h in range(HEADS):
             tops = [jnp.max(bias_s[t, h], axis=0, keepdims=True) for t in range(4)]
             top = jnp.maximum(jnp.maximum(tops[0], tops[1]), jnp.maximum(tops[2], tops[3]))
-            top_s[h : h + 1, :] = top.astype(F32)
+            top = top.astype(F32)
+            top_s[h : h + 1, :] = top
+            for t in range(4):
+                scaled_s[t, h] = (bias_s[t, h].astype(F32) - top) * LOG2E
 
     units = [(r, h, t) for r in range(STEP) for h in range(HEADS) for t in range(4)]
 
     def scores(r, h, t):
         at = slice(t * BLOCK, (t + 1) * BLOCK)
-        return matmul(k_s[r, at, :], q_s[r, h]) + bias_s[t, h].astype(F32)
+        return matmul(k_s[r, at, :], q_s[r, h])
 
     fine, totals = [], []
     ahead, total = scores(*units[0]), None
     for n, (r, h, t) in enumerate(units):
-        s, shift = ahead, top_s[h : h + 1, :]
+        s = ahead
         if n + 1 < len(units):
             ahead = scores(*units[n + 1])
-        p = jnp.exp2((s - shift) * LOG2E).astype(BF16)
+        p = jnp.exp2(s * LOG2E + scaled_s[t, h]).astype(BF16)
         pv = matmul(v_s[r, h, :, t * BLOCK : (t + 1) * BLOCK], p)
         total = pv if t == 0 else total + pv
         if t < 3:
@@ -205,6 +208,7 @@
         input_output_aliases={2 + len(x_ks) + len(biases): 0} if half else {},
         scratch_shapes=[
             pltpu.VMEM((4, HEADS, BLOCK, COLS), BF16),
+            pltpu.VMEM((4, HEADS, BLOCK, COLS), F32),
             pltpu.VMEM((HEADS, COLS), F32),
             pltpu.VMEM((STEP, KEYS, CHANNELS), BF16),
             pltpu.VMEM((STEP, HEADS, PAD, KEYS), BF16),

time: 139 us -> 138 us (level)
  Pallas kernels: 48.3 us -> 46.2 us
    pallas_call x2, Pallas kernels: 42.8 us -> 40.8 us  [attend(): pl.pallas_call(functools.partial(attend_kernel, len(x_ks)), grid=(ROWS //...]
where the time goes in v12:
time: 138 us
  Pallas kernels  46.2 us (33%)
  waiting for transfers between devices  32.7 us (24%)
  blocking collectives  26.6 us (19%)
  starting transfers between devices  26 us (19%)
  other arithmetic  2.54 us (2%)
  between operations  2.14 us (2%)
  local copies, waits for them, and re-layouts  1.81 us (1%)
    pallas_call x2, Pallas kernels, attend(): pl.pallas_call(functools.partial(attend_kernel, len(x_ks)), grid=(ROWS //...  40.8 us
    ppermute x14, waiting for transfers between devices, shift(): return lax.ppermute(x, axis, [(i, (i + step) % 4) for i in range(4)])  32.7 us
    all_to_all x1, blocking collectives, shards(): lax.all_to_all(message, ROW_AXES, split_axis=0, concat_axis=0, tiled=True)  26.6 us
    ppermute x14, starting transfers between devices, shift(): return lax.ppermute(x, axis, [(i, (i + step) % 4) for i in range(4)])  16.4 us
    ppermute x5, starting transfers between devices, swap(): return lax.ppermute(x, 'core', [(0, 1), (1, 0)])  9.66 us
    pallas_call x1, Pallas kernels, prepare(): pl.pallas_call(prepare_kernel, grid=(ROWS // 2,), in_specs=[whole(COLS, C...  2.79 us
  transfers between devices with their start and end apart: 19, of which 9 were waited for; matrix products, arithmetic and copies ran while one was open for 3% of the time, Pallas kernels for 15%

profile of v12, /device:TPU:1, one launch (start us, length us, event | category | flops | bytes accessed | tf_op | source)
XLA Modules:
  0.0 138.1 jit_solution(15889295950010248883)
XLA Ops:
  0.0 2.8 %prepare.1 = (bf16[4,512,128]{2,1,0:T(8,128)(2,1)}, bf16[4,256,512]{2,1,0:T(8,128)(2,1)}) custom-call(bf16[4,512,128]{2,1,0:T(8,128)(2,1)} %pair.1, f32[1,128]{1,0:T(1,128)} %bitcast.4, bf16[4,512,256]{2,1,0:T(8,128)(2,1)} %bias.1), custom_call_target="tpu_custom_call" | custom-call | tf_op jit(solution)/shard_map/prepare/pallas_call | solution.py:46
  2.8 1.4 %collective-permute-start.3 = (bf16[4,256,512]{2,1,0:T(8,128)(2,1)}, bf16[4,256,512]{2,1,0:T(8,128)(2,1)S(1)}, u32[]{:S(2)}, u32[]{:S(2)}) collective-permute-start(bf16[4,256,512]{2,1,0:T(8,128)(2,1)} %get-tuple-element.8.rest_6_.rest_5_), channel_id=1, source_target_pairs={{0,8},{8,0},{1,9},{9,1},{2,10},{10,2},{3,11},{11,3},{4,12},{12,4},... | collective-permute-start | bytes 3145736 | tf_op jit(solution)/shard_map/ppermute | solution.py:274
  4.2 2.6 %collective-permute-start.2 = (bf16[4,512,128]{2,1,0:T(8,128)(2,1)}, bf16[4,512,128]{2,1,0:T(8,128)(2,1)}, u32[]{:S(2)}, u32[]{:S(2)}) collective-permute-start(bf16[4,512,128]{2,1,0:T(8,128)(2,1)} %get-tuple-element.7.xq), channel_id=1, source_target_pairs={{0,17},{1,0},{16,1},{17,16},{2,19},{3,2},{18,3},{19,18},{4,21},{5,... | collective-permute-start | bytes 1572872 | tf_op jit(solution)/shard_map/ppermute | solution.py:270
  8.1 1.4 %collective-permute-start.9 = (bf16[4,256,512]{2,1,0:T(8,128)(2,1)}, bf16[4,256,512]{2,1,0:T(8,128)(2,1)S(1)}, u32[]{:S(2)}, u32[]{:S(2)}) collective-permute-start(bf16[4,256,512]{2,1,0:T(8,128)(2,1)} %get-tuple-element.8.rest_6_.rest_5_), channel_id=1, source_target_pairs={{0,96},{32,0},{64,32},{96,64},{1,97},{33,1},{65,33},{97,65},{2,98}... | collective-permute-start | bytes 3145736 | tf_op jit(solution)/shard_map/ppermute | solution.py:270
  10.7 7.6 %collective-permute-done.2 = bf16[4,512,128]{2,1,0:T(8,128)(2,1)} collective-permute-done((bf16[4,512,128]{2,1,0:T(8,128)(2,1)}, bf16[4,512,128]{2,1,0:T(8,128)(2,1)}, u32[]{:S(2)}, u32[]{:S(2)}) %collective-permute-start.2) | collective-permute-done | bytes 524320 | tf_op jit(solution)/shard_map/ppermute | solution.py:270
  18.4 3.1 %collective-permute-done = bf16[4,512,128]{2,1,0:T(8,128)(2,1)} collective-permute-done((bf16[4,512,128]{2,1,0:T(8,128)(2,1)}, bf16[4,512,128]{2,1,0:T(8,128)(2,1)}, u32[]{:S(2)}, u32[]{:S(2)}) %collective-permute-start) | collective-permute-done | bytes 524320 | tf_op jit(solution)/shard_map/ppermute | solution.py:270
  22.7 1.7 %collective-permute-start.5 = (bf16[4,512,128]{2,1,0:T(8,128)(2,1)S(1)}, bf16[4,512,128]{2,1,0:T(8,128)(2,1)S(1)}, u32[]{:S(2)}, u32[]{:S(2)}) collective-permute-start(bf16[4,512,128]{2,1,0:T(8,128)(2,1)S(1)} %select_add_fusion.rest_0_), channel_id=1, source_target_pairs={{0,2},{2,4},{4,6},{6,0},{1,3},{3,5},{5,7},{7,1},{8,10},{10,12},{12... | collective-permute-start | bytes 1572872 | tf_op jit(solution)/shard_map/ppermute | solution.py:270
  24.4 2.2 %collective-permute-start.4 = (bf16[4,512,128]{2,1,0:T(8,128)(2,1)S(1)}, bf16[4,512,128]{2,1,0:T(8,128)(2,1)S(1)}, u32[]{:S(2)}, u32[]{:S(2)}) collective-permute-start(bf16[4,512,128]{2,1,0:T(8,128)(2,1)S(1)} %select_add_fusion.rest_0_), channel_id=1, source_target_pairs={{0,6},{2,0},{4,2},{6,4},{1,7},{3,1},{5,3},{7,5},{8,14},{10,8},{12,... | collective-permute-start | bytes 1572872 | tf_op jit(solution)/shard_map/ppermute | solution.py:270
  26.6 6.1 %collective-permute-done.11.rest_10_.rest_9_ = bf16[4,256,512]{2,1,0:T(8,128)(2,1)S(1)} collective-permute-done((bf16[4,256,512]{2,1,0:T(8,128)(2,1)}, bf16[4,256,512]{2,1,0:T(8,128)(2,1)S(1)}, u32[]{:S(2)}, u32[]{:S(2)}) %collective-permute-start.11) | collective-permute-done | bytes 1048608 | tf_op jit(solution)/shard_map/ppermute | solution.py:270
  32.9 1.4 %collective-permute-start.12 = (bf16[4,256,512]{2,1,0:T(8,128)(2,1)S(1)}, bf16[4,256,512]{2,1,0:T(8,128)(2,1)S(1)}, u32[]{:S(2)}, u32[]{:S(2)}) collective-permute-start(bf16[4,256,512]{2,1,0:T(8,128)(2,1)S(1)} %collective-permute-done.11.rest_10_.rest_9_), channel_id=1, source_target_pairs={{0,8},{8,0},{1,9},{9,1},{2,10},{10,2},{3,11},{11,3},{4,12},{12,4},... | collective-permute-start | bytes 3145736 | tf_op jit(solution)/shard_map/ppermute | solution.py:274
  34.3 3.3 %collective-permute-done.5.rest_4_ = bf16[4,512,128]{2,1,0:T(8,128)(2,1)S(1)} collective-permute-done((bf16[4,512,128]{2,1,0:T(8,128)(2,1)S(1)}, bf16[4,512,128]{2,1,0:T(8,128)(2,1)S(1)}, u32[]{:S(2)}, u32[]{:S(2)}) %collective-permute-start.5) | collective-permute-done | bytes 524320 | tf_op jit(solution)/shard_map/ppermute | solution.py:270
  37.6 2.7 %collective-permute-start.15 = (bf16[2,256,512]{2,1,0:T(8,128)(2,1)S(1)}, bf16[2,256,512]{2,1,0:T(8,128)(2,1)S(1)}, u32[]{:S(2)}, u32[]{:S(2)}) collective-permute-start(bf16[2,256,512]{2,1,0:T(8,128)(2,1)S(1)} %slice.34), channel_id=1, source_target_pairs={{0,96},{32,0},{64,32},{96,64},{1,97},{33,1},{65,33},{97,65},{2,98}... | collective-permute-start | bytes 1572872 | tf_op jit(solution)/shard_map/ppermute | solution.py:270
  40.4 2.1 %collective-permute-start.10 = (bf16[4,256,512]{2,1,0:T(8,128)(2,1)S(1)}, bf16[4,256,512]{2,1,0:T(8,128)(2,1)S(1)}, u32[]{:S(2)}, u32[]{:S(2)}) collective-permute-start(bf16[4,256,512]{2,1,0:T(8,128)(2,1)S(1)} %collective-permute-done.9.rest_8_.rest_7_), channel_id=1, source_target_pairs={{0,8},{8,0},{1,9},{9,1},{2,10},{10,2},{3,11},{11,3},{4,12},{12,4},... | collective-permute-start | bytes 3145736 | tf_op jit(solution)/shard_map/ppermute | solution.py:274
  43.7 1.5 %collective-permute-start.18 = (bf16[4,256,128]{2,1,0:T(8,128)(2,1)S(1)}, bf16[4,256,128]{2,1,0:T(8,128)(2,1)S(1)}, u32[]{:S(2)}, u32[]{:S(2)}) collective-permute-start(bf16[4,256,128]{2,1,0:T(8,128)(2,1)S(1)} %slice_add_fusion), channel_id=1, source_target_pairs={{0,6},{2,0},{4,2},{6,4},{1,7},{3,1},{5,3},{7,5},{8,14},{10,8},{12,... | collective-permute-start | bytes 786440 | tf_op jit(solution)/shard_map/ppermute | solution.py:270
  46.4 2.0 %collective-permute-start.14 = (bf16[2,256,512]{2,1,0:T(8,128)(2,1)S(1)}, bf16[2,256,512]{2,1,0:T(8,128)(2,1)S(1)}, u32[]{:S(2)}, u32[]{:S(2)}) collective-permute-start(bf16[2,256,512]{2,1,0:T(8,128)(2,1)S(1)} %collective-permute-done.13.rest_12_.rest_11_), channel_id=1, source_target_pairs={{0,8},{8,0},{1,9},{9,1},{2,10},{10,2},{3,11},{11,3},{4,12},{12,4},... | collective-permute-start | bytes 1572872 | tf_op jit(solution)/shard_map/ppermute | solution.py:274
  48.4 1.4 collective-permute-done.15.rest_14_.rest_13_
  49.8 2.7 %collective-permute-start.16 = (bf16[2,256,512]{2,1,0:T(8,128)(2,1)S(1)}, bf16[2,256,512]{2,1,0:T(8,128)(2,1)S(1)}, u32[]{:S(2)}, u32[]{:S(2)}) collective-permute-start(bf16[2,256,512]{2,1,0:T(8,128)(2,1)S(1)} %collective-permute-done.15.rest_14_.rest_13_), channel_id=1, source_target_pairs={{0,8},{8,0},{1,9},{9,1},{2,10},{10,2},{3,11},{11,3},{4,12},{12,4},... | collective-permute-start | bytes 1572872 | tf_op jit(solution)/shard_map/ppermute | solution.py:274
  55.2 7.9 %collective-permute-done.17.rest_2_ = bf16[4,256,128]{2,1,0:T(8,128)(2,1)S(1)} collective-permute-done((bf16[4,256,128]{2,1,0:T(8,128)(2,1)S(1)}, bf16[4,256,128]{2,1,0:T(8,128)(2,1)S(1)}, u32[]{:S(2)}, u32[]{:S(2)}) %collective-permute-start.17) | collective-permute-done | bytes 262176 | tf_op jit(solution)/shard_map/ppermute | solution.py:270
  64.2 1.7 %collective-permute-start.6 = (bf16[4,512,128]{2,1,0:T(8,128)(2,1)S(1)}, bf16[4,512,128]{2,1,0:T(8,128)(2,1)S(1)}, u32[]{:S(2)}, u32[]{:S(2)}) collective-permute-start(bf16[4,512,128]{2,1,0:T(8,128)(2,1)S(1)} %add_add_fusion.rest_0_), channel_id=1, source_target_pairs={{0,6},{2,0},{4,2},{6,4},{1,7},{3,1},{5,3},{7,5},{8,14},{10,8},{12,... | collective-permute-start | bytes 1572872 | tf_op jit(solution)/shard_map/ppermute | solution.py:270
  65.9 20.5 %attend.2.rest_15_ = bf16[16,10,32,128]{3,2,1,0:T(8,128)(2,1)S(1)} custom-call(bf16[4,512,128]{2,1,0:T(8,128)(2,1)S(1)} %copy-done, bf16[4,512,128]{2,1,0:T(8,128)(2,1)S(1)} %select_add_fusion.rest_0_, bf16[4,512,128]{2,1,0:T(8,128)(2,1)S(1)} %collective-permute-done.4.rest_1_, bf16[4,256,128]{2,1,0:T(8,128)(2,1)S(1)} %collective-permute-done.17.rest_2_, ...), custom_call_target="tpu_custom_call" | custom-call | flops 8589934592 | bytes 16777216 | tf_op jit(solution)/shard_map/attend/pallas_call | solution.py:199
  86.4 1.8 %collective-permute-done.8.rest_3_ = bf16[4,512,128]{2,1,0:T(8,128)(2,1)S(1)} collective-permute-done((bf16[4,512,128]{2,1,0:T(8,128)(2,1)S(1)}, bf16[4,512,128]{2,1,0:T(8,128)(2,1)S(1)}, u32[]{:S(2)}, u32[]{:S(2)}) %collective-permute-start.8) | collective-permute-done | bytes 524320 | tf_op jit(solution)/shard_map/ppermute | solution.py:270
  88.6 20.3 %attend.3 = bf16[16,10,32,128]{3,2,1,0:T(8,128)(2,1)S(1)} custom-call(bf16[4,512,128]{2,1,0:T(8,128)(2,1)S(1)} %collective-permute-done.1.xq, bf16[4,512,128]{2,1,0:T(8,128)(2,1)S(1)} %add_add_fusion.rest_0_, bf16[4,512,128]{2,1,0:T(8,128)(2,1)S(1)} %collective-permute-done.6.rest_1_, ...), custom_call_target="tpu_custom_call", output_to_operand_aliasing={{}: (16, {})} | custom-call | flops 8589934592 | bytes 16777216 | tf_op jit(solution)/shard_map/attend/pallas_call | solution.py:199
  108.9 26.6 %all_to_all.5.message = bf16[16,10,32,128]{3,2,1,0:T(8,128)(2,1)S(1)} all-to-all(bf16[16,10,32,128]{3,2,1,0:T(8,128)(2,1)S(1)} %attend.3), channel_id=1, replica_groups=mesh['y'=4,'xh'=2,'core'=2,'z'=4,'xl'=2] {'y','xh','core'}, dimensions={0} | all-to-all | bytes 2621440 | tf_op jit(solution)/shard_map/all_to_all | solution.py:308
  135.5 2.6 %merge.1 = bf16[32,64,128]{2,1,0:T(8,128)(2,1)} custom-call(bf16[16,10,32,128]{3,2,1,0:T(8,128)(2,1)S(1)} %all_to_all.5.message, bf16[128,128]{1,0:T(8,128)(2,1)S(1)} %copy-done.1), custom_call_target="tpu_custom_call" | custom-call | tf_op jit(solution)/shard_map/merge/pallas_call | solution.py:249
  (36 shorter events, 8.4 us)
Async XLA Ops:
  2.8 6.7 %collective-permute-start.3 = (bf16[4,256,512]{2,1,0:T(8,128)(2,1)}, bf16[4,256,512]{2,1,0:T(8,128)(2,1)S(1)}, u32[]{:S(2)}, u32[]{:S(2)}) collective-permute-start(bf16[4,256,512]{2,1,0:T(8,128)(2,1)} %get-tuple-element.8.rest_6_.rest_5_), channel_id=1, source_target_pairs={{0,8},{8,0},{1,9},{9,1},{2,10},{10,2},{3,11},{11,3},{4,12},{12,4},... | collective-permute-start | bytes 3145736 | tf_op jit(solution)/shard_map/ppermute | solution.py:274
  4.2 14.2 %collective-permute-start.2 = (bf16[4,512,128]{2,1,0:T(8,128)(2,1)}, bf16[4,512,128]{2,1,0:T(8,128)(2,1)}, u32[]{:S(2)}, u32[]{:S(2)}) collective-permute-start(bf16[4,512,128]{2,1,0:T(8,128)(2,1)} %get-tuple-element.7.xq), channel_id=1, source_target_pairs={{0,17},{1,0},{16,1},{17,16},{2,19},{3,2},{18,3},{19,18},{4,21},{5,... | collective-permute-start | bytes 1572872 | tf_op jit(solution)/shard_map/ppermute | solution.py:270
  6.8 14.7 %collective-permute-start = (bf16[4,512,128]{2,1,0:T(8,128)(2,1)}, bf16[4,512,128]{2,1,0:T(8,128)(2,1)}, u32[]{:S(2)}, u32[]{:S(2)}) collective-permute-start(bf16[4,512,128]{2,1,0:T(8,128)(2,1)} %get-tuple-element.7.xq), channel_id=1, source_target_pairs={{0,1},{1,16},{16,17},{17,0},{2,3},{3,18},{18,19},{19,2},{4,5},{5,2... | collective-permute-start | bytes 1572872 | tf_op jit(solution)/shard_map/ppermute | solution.py:270
  6.8 26.0 %collective-permute-start.11 = (bf16[4,256,512]{2,1,0:T(8,128)(2,1)}, bf16[4,256,512]{2,1,0:T(8,128)(2,1)S(1)}, u32[]{:S(2)}, u32[]{:S(2)}) collective-permute-start(bf16[4,256,512]{2,1,0:T(8,128)(2,1)} %get-tuple-element.8.rest_6_.rest_5_), channel_id=1, source_target_pairs={{0,32},{32,64},{64,96},{96,0},{1,33},{33,65},{65,97},{97,1},{2,34}... | collective-permute-start | bytes 3145736 | tf_op jit(solution)/shard_map/ppermute | solution.py:270
  8.1 24.8 %collective-permute-start.9 = (bf16[4,256,512]{2,1,0:T(8,128)(2,1)}, bf16[4,256,512]{2,1,0:T(8,128)(2,1)S(1)}, u32[]{:S(2)}, u32[]{:S(2)}) collective-permute-start(bf16[4,256,512]{2,1,0:T(8,128)(2,1)} %get-tuple-element.8.rest_6_.rest_5_), channel_id=1, source_target_pairs={{0,96},{32,0},{64,32},{96,64},{1,97},{33,1},{65,33},{97,65},{2,98}... | collective-permute-start | bytes 3145736 | tf_op jit(solution)/shard_map/ppermute | solution.py:270
  22.7 14.9 %collective-permute-start.5 = (bf16[4,512,128]{2,1,0:T(8,128)(2,1)S(1)}, bf16[4,512,128]{2,1,0:T(8,128)(2,1)S(1)}, u32[]{:S(2)}, u32[]{:S(2)}) collective-permute-start(bf16[4,512,128]{2,1,0:T(8,128)(2,1)S(1)} %select_add_fusion.rest_0_), channel_id=1, source_target_pairs={{0,2},{2,4},{4,6},{6,0},{1,3},{3,5},{5,7},{7,1},{8,10},{10,12},{12... | collective-permute-start | bytes 1572872 | tf_op jit(solution)/shard_map/ppermute | solution.py:270
  24.4 15.9 %collective-permute-start.4 = (bf16[4,512,128]{2,1,0:T(8,128)(2,1)S(1)}, bf16[4,512,128]{2,1,0:T(8,128)(2,1)S(1)}, u32[]{:S(2)}, u32[]{:S(2)}) collective-permute-start(bf16[4,512,128]{2,1,0:T(8,128)(2,1)S(1)} %select_add_fusion.rest_0_), channel_id=1, source_target_pairs={{0,6},{2,0},{4,2},{6,4},{1,7},{3,1},{5,3},{7,5},{8,14},{10,8},{12,... | collective-permute-start | bytes 1572872 | tf_op jit(solution)/shard_map/ppermute | solution.py:270
  26.6 17.1 %collective-permute-start.1 = (bf16[4,512,128]{2,1,0:T(8,128)(2,1)}, bf16[4,512,128]{2,1,0:T(8,128)(2,1)S(1)}, u32[]{:S(2)}, u32[]{:S(2)}) collective-permute-start(bf16[4,512,128]{2,1,0:T(8,128)(2,1)} %collective-permute-done), channel_id=1, source_target_pairs={{0,1},{1,16},{16,17},{17,0},{2,3},{3,18},{18,19},{19,2},{4,5},{5,2... | collective-permute-start | bytes 1572872 | tf_op jit(solution)/shard_map/ppermute | solution.py:270
  32.8 13.6 %collective-permute-start.13 = (bf16[2,256,512]{2,1,0:T(8,128)(2,1)S(1)}, bf16[2,256,512]{2,1,0:T(8,128)(2,1)S(1)}, u32[]{:S(2)}, u32[]{:S(2)}) collective-permute-start(bf16[2,256,512]{2,1,0:T(8,128)(2,1)S(1)} %slice.33), channel_id=1, source_target_pairs={{0,32},{32,64},{64,96},{96,0},{1,33},{33,65},{65,97},{97,1},{2,34}... | collective-permute-start | bytes 1572872 | tf_op jit(solution)/shard_map/ppermute | solution.py:270
  32.9 31.3 %collective-permute-start.12 = (bf16[4,256,512]{2,1,0:T(8,128)(2,1)S(1)}, bf16[4,256,512]{2,1,0:T(8,128)(2,1)S(1)}, u32[]{:S(2)}, u32[]{:S(2)}) collective-permute-start(bf16[4,256,512]{2,1,0:T(8,128)(2,1)S(1)} %collective-permute-done.11.rest_10_.rest_9_), channel_id=1, source_target_pairs={{0,8},{8,0},{1,9},{9,1},{2,10},{10,2},{3,11},{11,3},{4,12},{12,4},... | collective-permute-start | bytes 3145736 | tf_op jit(solution)/shard_map/ppermute | solution.py:274
  37.6 12.1 %collective-permute-start.15 = (bf16[2,256,512]{2,1,0:T(8,128)(2,1)S(1)}, bf16[2,256,512]{2,1,0:T(8,128)(2,1)S(1)}, u32[]{:S(2)}, u32[]{:S(2)}) collective-permute-start(bf16[2,256,512]{2,1,0:T(8,128)(2,1)S(1)} %slice.34), channel_id=1, source_target_pairs={{0,96},{32,0},{64,32},{96,64},{1,97},{33,1},{65,33},{97,65},{2,98}... | collective-permute-start | bytes 1572872 | tf_op jit(solution)/shard_map/ppermute | solution.py:270
  40.4 25.5 %collective-permute-start.10 = (bf16[4,256,512]{2,1,0:T(8,128)(2,1)S(1)}, bf16[4,256,512]{2,1,0:T(8,128)(2,1)S(1)}, u32[]{:S(2)}, u32[]{:S(2)}) collective-permute-start(bf16[4,256,512]{2,1,0:T(8,128)(2,1)S(1)} %collective-permute-done.9.rest_8_.rest_7_), channel_id=1, source_target_pairs={{0,8},{8,0},{1,9},{9,1},{2,10},{10,2},{3,11},{11,3},{4,12},{12,4},... | collective-permute-start | bytes 3145736 | tf_op jit(solution)/shard_map/ppermute | solution.py:274
  43.7 10.2 %collective-permute-start.18 = (bf16[4,256,128]{2,1,0:T(8,128)(2,1)S(1)}, bf16[4,256,128]{2,1,0:T(8,128)(2,1)S(1)}, u32[]{:S(2)}, u32[]{:S(2)}) collective-permute-start(bf16[4,256,128]{2,1,0:T(8,128)(2,1)S(1)} %slice_add_fusion), channel_id=1, source_target_pairs={{0,6},{2,0},{4,2},{6,4},{1,7},{3,1},{5,3},{7,5},{8,14},{10,8},{12,... | collective-permute-start | bytes 786440 | tf_op jit(solution)/shard_map/ppermute | solution.py:270
  46.4 16.7 %collective-permute-start.14 = (bf16[2,256,512]{2,1,0:T(8,128)(2,1)S(1)}, bf16[2,256,512]{2,1,0:T(8,128)(2,1)S(1)}, u32[]{:S(2)}, u32[]{:S(2)}) collective-permute-start(bf16[2,256,512]{2,1,0:T(8,128)(2,1)S(1)} %collective-permute-done.13.rest_12_.rest_11_), channel_id=1, source_target_pairs={{0,8},{8,0},{1,9},{9,1},{2,10},{10,2},{3,11},{11,3},{4,12},{12,4},... | collective-permute-start | bytes 1572872 | tf_op jit(solution)/shard_map/ppermute | solution.py:274
  49.8 16.1 %collective-permute-start.16 = (bf16[2,256,512]{2,1,0:T(8,128)(2,1)S(1)}, bf16[2,256,512]{2,1,0:T(8,128)(2,1)S(1)}, u32[]{:S(2)}, u32[]{:S(2)}) collective-permute-start(bf16[2,256,512]{2,1,0:T(8,128)(2,1)S(1)} %collective-permute-done.15.rest_14_.rest_13_), channel_id=1, source_target_pairs={{0,8},{8,0},{1,9},{9,1},{2,10},{10,2},{3,11},{11,3},{4,12},{12,4},... | collective-permute-start | bytes 1572872 | tf_op jit(solution)/shard_map/ppermute | solution.py:274
  53.8 12.1 %copy-start = (bf16[4,512,128]{2,1,0:T(8,128)(2,1)S(1)}, bf16[4,512,128]{2,1,0:T(8,128)(2,1)}, u32[]{:S(2)}) copy-start(bf16[4,512,128]{2,1,0:T(8,128)(2,1)} %get-tuple-element.7.xq) | copy-start | bytes 1572868
  53.8 12.1 %copy-start.2 = (bf16[4,256,512]{2,1,0:T(8,128)(2,1)S(1)}, bf16[4,256,512]{2,1,0:T(8,128)(2,1)}, u32[]{:S(2)}) copy-start(bf16[4,256,512]{2,1,0:T(8,128)(2,1)} %get-tuple-element.8.rest_6_.rest_5_) | copy-start | bytes 3145732
  53.8 12.1 %copy-start.3 = (bf16[128,512]{1,0:T(8,128)(2,1)S(1)}, bf16[128,512]{1,0:T(8,128)(2,1)}, u32[]{:S(2)}) copy-start(bf16[128,512]{1,0:T(8,128)(2,1)} %rest_4_.1) | copy-start | bytes 393220
  53.9 9.2 %collective-permute-start.17 = (bf16[4,256,128]{2,1,0:T(8,128)(2,1)S(1)}, bf16[4,256,128]{2,1,0:T(8,128)(2,1)S(1)}, u32[]{:S(2)}, u32[]{:S(2)}) collective-permute-start(bf16[4,256,128]{2,1,0:T(8,128)(2,1)S(1)} %slice_add_fusion.1), channel_id=1, source_target_pairs={{0,2},{2,4},{4,6},{6,0},{1,3},{3,5},{5,7},{7,1},{8,10},{10,12},{12... | collective-permute-start | bytes 786440 | tf_op jit(solution)/shard_map/ppermute | solution.py:270
  63.1 25.1 %collective-permute-start.8 = (bf16[4,512,128]{2,1,0:T(8,128)(2,1)S(1)}, bf16[4,512,128]{2,1,0:T(8,128)(2,1)S(1)}, u32[]{:S(2)}, u32[]{:S(2)}) collective-permute-start(bf16[4,512,128]{2,1,0:T(8,128)(2,1)S(1)} %add_add_fusion.rest_0_), channel_id=1, source_target_pairs={{0,2},{2,4},{4,6},{6,0},{1,3},{3,5},{5,7},{7,1},{8,10},{10,12},{12... | collective-permute-start | bytes 1572872 | tf_op jit(solution)/shard_map/ppermute | solution.py:270
  63.1 25.1 %collective-permute-start.7 = (bf16[4,512,128]{2,1,0:T(8,128)(2,1)S(1)}, bf16[4,512,128]{2,1,0:T(8,128)(2,1)S(1)}, u32[]{:S(2)}, u32[]{:S(2)}) collective-permute-start(bf16[4,512,128]{2,1,0:T(8,128)(2,1)S(1)} %add_add_fusion.rest_0_), channel_id=1, source_target_pairs={{0,4},{2,6},{4,0},{6,2},{1,5},{3,7},{5,1},{7,3},{8,12},{10,14},{12... | collective-permute-start | bytes 1572872 | tf_op jit(solution)/shard_map/ppermute | solution.py:270
  64.2 24.4 %collective-permute-start.6 = (bf16[4,512,128]{2,1,0:T(8,128)(2,1)S(1)}, bf16[4,512,128]{2,1,0:T(8,128)(2,1)S(1)}, u32[]{:S(2)}, u32[]{:S(2)}) collective-permute-start(bf16[4,512,128]{2,1,0:T(8,128)(2,1)S(1)} %add_add_fusion.rest_0_), channel_id=1, source_target_pairs={{0,6},{2,0},{4,2},{6,4},{1,7},{3,1},{5,3},{7,5},{8,14},{10,8},{12,... | collective-permute-start | bytes 1572872 | tf_op jit(solution)/shard_map/ppermute | solution.py:270
  108.8 26.6 %copy-start.1 = (bf16[128,128]{1,0:T(8,128)(2,1)S(1)}, bf16[128,128]{1,0:T(8,128)(2,1)}, u32[]{:S(2)}) copy-start(bf16[128,128]{1,0:T(8,128)(2,1)} %w.1) | copy-start | bytes 98308

commit v13 on v12

--- a/solution.py
+++ b/solution.py
@@ -12,7 +12,7 @@
 COLS, BLOCK, ROWS = 512, 512, 4
 KEYS = 4 * BLOCK
 SHARE = COLS // 16
-PAD = 40
+PAD = 48
 STEP = 2
 LOG2E = 1.4426950408889634
 LOW, HIGH = 1e-26, 1e30

time: 138 us -> 138 us (level)
  no operation moved by 1% of the time
where the time goes in v13:
time: 138 us
  Pallas kernels  46.3 us (34%)
  waiting for transfers between devices  32.7 us (24%)
  blocking collectives  26.6 us (19%)
  starting transfers between devices  26 us (19%)
  other arithmetic  2.54 us (2%)
  between operations  2.14 us (2%)
  local copies, waits for them, and re-layouts  1.81 us (1%)
    pallas_call x2, Pallas kernels, attend(): pl.pallas_call(functools.partial(attend_kernel, len(x_ks)), grid=(ROWS //...  40.9 us
    ppermute x14, waiting for transfers between devices, shift(): return lax.ppermute(x, axis, [(i, (i + step) % 4) for i in range(4)])  32.7 us
    all_to_all x1, blocking collectives, shards(): lax.all_to_all(message, ROW_AXES, split_axis=0, concat_axis=0, tiled=True)  26.6 us
    ppermute x14, starting transfers between devices, shift(): return lax.ppermute(x, axis, [(i, (i + step) % 4) for i in range(4)])  16.4 us
    ppermute x5, starting transfers between devices, swap(): return lax.ppermute(x, 'core', [(0, 1), (1, 0)])  9.66 us
    pallas_call x1, Pallas kernels, prepare(): pl.pallas_call(prepare_kernel, grid=(ROWS // 2,), in_specs=[whole(COLS, C...  2.79 us
  transfers between devices with their start and end apart: 19, of which 9 were waited for; matrix products, arithmetic and copies ran while one was open for 3% of the time, Pallas kernels for 15%

profile of v13, /device:TPU:1, one launch (start us, length us, event | category | flops | bytes accessed | tf_op | source)
XLA Modules:
  0.0 138.2 jit_solution(6575477730647387136)
XLA Ops:
  0.0 2.8 %prepare.1 = (bf16[4,512,128]{2,1,0:T(8,128)(2,1)}, bf16[4,256,512]{2,1,0:T(8,128)(2,1)}) custom-call(bf16[4,512,128]{2,1,0:T(8,128)(2,1)} %pair.1, f32[1,128]{1,0:T(1,128)} %bitcast.4, bf16[4,512,256]{2,1,0:T(8,128)(2,1)} %bias.1), custom_call_target="tpu_custom_call" | custom-call | tf_op jit(solution)/shard_map/prepare/pallas_call | solution.py:46
  2.8 1.4 %collective-permute-start.3 = (bf16[4,256,512]{2,1,0:T(8,128)(2,1)}, bf16[4,256,512]{2,1,0:T(8,128)(2,1)S(1)}, u32[]{:S(2)}, u32[]{:S(2)}) collective-permute-start(bf16[4,256,512]{2,1,0:T(8,128)(2,1)} %get-tuple-element.8.rest_6_.rest_5_), channel_id=1, source_target_pairs={{0,8},{8,0},{1,9},{9,1},{2,10},{10,2},{3,11},{11,3},{4,12},{12,4},... | collective-permute-start | bytes 3145736 | tf_op jit(solution)/shard_map/ppermute | solution.py:274
  4.2 2.6 %collective-permute-start.2 = (bf16[4,512,128]{2,1,0:T(8,128)(2,1)}, bf16[4,512,128]{2,1,0:T(8,128)(2,1)}, u32[]{:S(2)}, u32[]{:S(2)}) collective-permute-start(bf16[4,512,128]{2,1,0:T(8,128)(2,1)} %get-tuple-element.7.xq), channel_id=1, source_target_pairs={{0,17},{1,0},{16,1},{17,16},{2,19},{3,2},{18,3},{19,18},{4,21},{5,... | collective-permute-start | bytes 1572872 | tf_op jit(solution)/shard_map/ppermute | solution.py:270
  8.1 1.4 %collective-permute-start.9 = (bf16[4,256,512]{2,1,0:T(8,128)(2,1)}, bf16[4,256,512]{2,1,0:T(8,128)(2,1)S(1)}, u32[]{:S(2)}, u32[]{:S(2)}) collective-permute-start(bf16[4,256,512]{2,1,0:T(8,128)(2,1)} %get-tuple-element.8.rest_6_.rest_5_), channel_id=1, source_target_pairs={{0,96},{32,0},{64,32},{96,64},{1,97},{33,1},{65,33},{97,65},{2,98}... | collective-permute-start | bytes 3145736 | tf_op jit(solution)/shard_map/ppermute | solution.py:270
  10.7 7.6 %collective-permute-done.2 = bf16[4,512,128]{2,1,0:T(8,128)(2,1)} collective-permute-done((bf16[4,512,128]{2,1,0:T(8,128)(2,1)}, bf16[4,512,128]{2,1,0:T(8,128)(2,1)}, u32[]{:S(2)}, u32[]{:S(2)}) %collective-permute-start.2) | collective-permute-done | bytes 524320 | tf_op jit(solution)/shard_map/ppermute | solution.py:270
  18.4 3.1 %collective-permute-done = bf16[4,512,128]{2,1,0:T(8,128)(2,1)} collective-permute-done((bf16[4,512,128]{2,1,0:T(8,128)(2,1)}, bf16[4,512,128]{2,1,0:T(8,128)(2,1)}, u32[]{:S(2)}, u32[]{:S(2)}) %collective-permute-start) | collective-permute-done | bytes 524320 | tf_op jit(solution)/shard_map/ppermute | solution.py:270
  22.7 1.7 %collective-permute-start.5 = (bf16[4,512,128]{2,1,0:T(8,128)(2,1)S(1)}, bf16[4,512,128]{2,1,0:T(8,128)(2,1)S(1)}, u32[]{:S(2)}, u32[]{:S(2)}) collective-permute-start(bf16[4,512,128]{2,1,0:T(8,128)(2,1)S(1)} %select_add_fusion.rest_0_), channel_id=1, source_target_pairs={{0,2},{2,4},{4,6},{6,0},{1,3},{3,5},{5,7},{7,1},{8,10},{10,12},{12... | collective-permute-start | bytes 1572872 | tf_op jit(solution)/shard_map/ppermute | solution.py:270
  24.4 2.2 %collective-permute-start.4 = (bf16[4,512,128]{2,1,0:T(8,128)(2,1)S(1)}, bf16[4,512,128]{2,1,0:T(8,128)(2,1)S(1)}, u32[]{:S(2)}, u32[]{:S(2)}) collective-permute-start(bf16[4,512,128]{2,1,0:T(8,128)(2,1)S(1)} %select_add_fusion.rest_0_), channel_id=1, source_target_pairs={{0,6},{2,0},{4,2},{6,4},{1,7},{3,1},{5,3},{7,5},{8,14},{10,8},{12,... | collective-permute-start | bytes 1572872 | tf_op jit(solution)/shard_map/ppermute | solution.py:270
  26.6 6.1 %collective-permute-done.11.rest_10_.rest_9_ = bf16[4,256,512]{2,1,0:T(8,128)(2,1)S(1)} collective-permute-done((bf16[4,256,512]{2,1,0:T(8,128)(2,1)}, bf16[4,256,512]{2,1,0:T(8,128)(2,1)S(1)}, u32[]{:S(2)}, u32[]{:S(2)}) %collective-permute-start.11) | collective-permute-done | bytes 1048608 | tf_op jit(solution)/shard_map/ppermute | solution.py:270
  32.9 1.4 %collective-permute-start.12 = (bf16[4,256,512]{2,1,0:T(8,128)(2,1)S(1)}, bf16[4,256,512]{2,1,0:T(8,128)(2,1)S(1)}, u32[]{:S(2)}, u32[]{:S(2)}) collective-permute-start(bf16[4,256,512]{2,1,0:T(8,128)(2,1)S(1)} %collective-permute-done.11.rest_10_.rest_9_), channel_id=1, source_target_pairs={{0,8},{8,0},{1,9},{9,1},{2,10},{10,2},{3,11},{11,3},{4,12},{12,4},... | collective-permute-start | bytes 3145736 | tf_op jit(solution)/shard_map/ppermute | solution.py:274
  34.3 3.3 %collective-permute-done.5.rest_4_ = bf16[4,512,128]{2,1,0:T(8,128)(2,1)S(1)} collective-permute-done((bf16[4,512,128]{2,1,0:T(8,128)(2,1)S(1)}, bf16[4,512,128]{2,1,0:T(8,128)(2,1)S(1)}, u32[]{:S(2)}, u32[]{:S(2)}) %collective-permute-start.5) | collective-permute-done | bytes 524320 | tf_op jit(solution)/shard_map/ppermute | solution.py:270
  37.6 2.7 %collective-permute-start.15 = (bf16[2,256,512]{2,1,0:T(8,128)(2,1)S(1)}, bf16[2,256,512]{2,1,0:T(8,128)(2,1)S(1)}, u32[]{:S(2)}, u32[]{:S(2)}) collective-permute-start(bf16[2,256,512]{2,1,0:T(8,128)(2,1)S(1)} %slice.34), channel_id=1, source_target_pairs={{0,96},{32,0},{64,32},{96,64},{1,97},{33,1},{65,33},{97,65},{2,98}... | collective-permute-start | bytes 1572872 | tf_op jit(solution)/shard_map/ppermute | solution.py:270
  40.4 2.1 %collective-permute-start.10 = (bf16[4,256,512]{2,1,0:T(8,128)(2,1)S(1)}, bf16[4,256,512]{2,1,0:T(8,128)(2,1)S(1)}, u32[]{:S(2)}, u32[]{:S(2)}) collective-permute-start(bf16[4,256,512]{2,1,0:T(8,128)(2,1)S(1)} %collective-permute-done.9.rest_8_.rest_7_), channel_id=1, source_target_pairs={{0,8},{8,0},{1,9},{9,1},{2,10},{10,2},{3,11},{11,3},{4,12},{12,4},... | collective-permute-start | bytes 3145736 | tf_op jit(solution)/shard_map/ppermute | solution.py:274
  43.7 1.5 %collective-permute-start.18 = (bf16[4,256,128]{2,1,0:T(8,128)(2,1)S(1)}, bf16[4,256,128]{2,1,0:T(8,128)(2,1)S(1)}, u32[]{:S(2)}, u32[]{:S(2)}) collective-permute-start(bf16[4,256,128]{2,1,0:T(8,128)(2,1)S(1)} %slice_add_fusion), channel_id=1, source_target_pairs={{0,6},{2,0},{4,2},{6,4},{1,7},{3,1},{5,3},{7,5},{8,14},{10,8},{12,... | collective-permute-start | bytes 786440 | tf_op jit(solution)/shard_map/ppermute | solution.py:270
  46.4 2.0 %collective-permute-start.14 = (bf16[2,256,512]{2,1,0:T(8,128)(2,1)S(1)}, bf16[2,256,512]{2,1,0:T(8,128)(2,1)S(1)}, u32[]{:S(2)}, u32[]{:S(2)}) collective-permute-start(bf16[2,256,512]{2,1,0:T(8,128)(2,1)S(1)} %collective-permute-done.13.rest_12_.rest_11_), channel_id=1, source_target_pairs={{0,8},{8,0},{1,9},{9,1},{2,10},{10,2},{3,11},{11,3},{4,12},{12,4},... | collective-permute-start | bytes 1572872 | tf_op jit(solution)/shard_map/ppermute | solution.py:274
  48.4 1.4 collective-permute-done.15.rest_14_.rest_13_
  49.8 2.7 %collective-permute-start.16 = (bf16[2,256,512]{2,1,0:T(8,128)(2,1)S(1)}, bf16[2,256,512]{2,1,0:T(8,128)(2,1)S(1)}, u32[]{:S(2)}, u32[]{:S(2)}) collective-permute-start(bf16[2,256,512]{2,1,0:T(8,128)(2,1)S(1)} %collective-permute-done.15.rest_14_.rest_13_), channel_id=1, source_target_pairs={{0,8},{8,0},{1,9},{9,1},{2,10},{10,2},{3,11},{11,3},{4,12},{12,4},... | collective-permute-start | bytes 1572872 | tf_op jit(solution)/shard_map/ppermute | solution.py:274
  55.2 7.9 %collective-permute-done.17.rest_2_ = bf16[4,256,128]{2,1,0:T(8,128)(2,1)S(1)} collective-permute-done((bf16[4,256,128]{2,1,0:T(8,128)(2,1)S(1)}, bf16[4,256,128]{2,1,0:T(8,128)(2,1)S(1)}, u32[]{:S(2)}, u32[]{:S(2)}) %collective-permute-start.17) | collective-permute-done | bytes 262176 | tf_op jit(solution)/shard_map/ppermute | solution.py:270
  64.2 1.7 %collective-permute-start.6 = (bf16[4,512,128]{2,1,0:T(8,128)(2,1)S(1)}, bf16[4,512,128]{2,1,0:T(8,128)(2,1)S(1)}, u32[]{:S(2)}, u32[]{:S(2)}) collective-permute-start(bf16[4,512,128]{2,1,0:T(8,128)(2,1)S(1)} %add_add_fusion.rest_0_), channel_id=1, source_target_pairs={{0,6},{2,0},{4,2},{6,4},{1,7},{3,1},{5,3},{7,5},{8,14},{10,8},{12,... | collective-permute-start | bytes 1572872 | tf_op jit(solution)/shard_map/ppermute | solution.py:270
  65.9 20.6 %attend.2.rest_15_ = bf16[16,10,32,128]{3,2,1,0:T(8,128)(2,1)S(1)} custom-call(bf16[4,512,128]{2,1,0:T(8,128)(2,1)S(1)} %copy-done, bf16[4,512,128]{2,1,0:T(8,128)(2,1)S(1)} %select_add_fusion.rest_0_, bf16[4,512,128]{2,1,0:T(8,128)(2,1)S(1)} %collective-permute-done.4.rest_1_, bf16[4,256,128]{2,1,0:T(8,128)(2,1)S(1)} %collective-permute-done.17.rest_2_, ...), custom_call_target="tpu_custom_call" | custom-call | flops 8589934592 | bytes 16777216 | tf_op jit(solution)/shard_map/attend/pallas_call | solution.py:199
  86.4 1.8 %collective-permute-done.8.rest_3_ = bf16[4,512,128]{2,1,0:T(8,128)(2,1)S(1)} collective-permute-done((bf16[4,512,128]{2,1,0:T(8,128)(2,1)S(1)}, bf16[4,512,128]{2,1,0:T(8,128)(2,1)S(1)}, u32[]{:S(2)}, u32[]{:S(2)}) %collective-permute-start.8) | collective-permute-done | bytes 524320 | tf_op jit(solution)/shard_map/ppermute | solution.py:270
  88.6 20.3 %attend.3 = bf16[16,10,32,128]{3,2,1,0:T(8,128)(2,1)S(1)} custom-call(bf16[4,512,128]{2,1,0:T(8,128)(2,1)S(1)} %collective-permute-done.1.xq, bf16[4,512,128]{2,1,0:T(8,128)(2,1)S(1)} %add_add_fusion.rest_0_, bf16[4,512,128]{2,1,0:T(8,128)(2,1)S(1)} %collective-permute-done.6.rest_1_, ...), custom_call_target="tpu_custom_call", output_to_operand_aliasing={{}: (16, {})} | custom-call | flops 8589934592 | bytes 16777216 | tf_op jit(solution)/shard_map/attend/pallas_call | solution.py:199
  108.9 26.6 %all_to_all.5.message = bf16[16,10,32,128]{3,2,1,0:T(8,128)(2,1)S(1)} all-to-all(bf16[16,10,32,128]{3,2,1,0:T(8,128)(2,1)S(1)} %attend.3), channel_id=1, replica_groups=mesh['y'=4,'xh'=2,'core'=2,'z'=4,'xl'=2] {'y','xh','core'}, dimensions={0} | all-to-all | bytes 2621440 | tf_op jit(solution)/shard_map/all_to_all | solution.py:308
  135.5 2.6 %merge.1 = bf16[32,64,128]{2,1,0:T(8,128)(2,1)} custom-call(bf16[16,10,32,128]{3,2,1,0:T(8,128)(2,1)S(1)} %all_to_all.5.message, bf16[128,128]{1,0:T(8,128)(2,1)S(1)} %copy-done.1), custom_call_target="tpu_custom_call" | custom-call | tf_op jit(solution)/shard_map/merge/pallas_call | solution.py:249
  (36 shorter events, 8.4 us)
Async XLA Ops:
  2.8 6.7 %collective-permute-start.3 = (bf16[4,256,512]{2,1,0:T(8,128)(2,1)}, bf16[4,256,512]{2,1,0:T(8,128)(2,1)S(1)}, u32[]{:S(2)}, u32[]{:S(2)}) collective-permute-start(bf16[4,256,512]{2,1,0:T(8,128)(2,1)} %get-tuple-element.8.rest_6_.rest_5_), channel_id=1, source_target_pairs={{0,8},{8,0},{1,9},{9,1},{2,10},{10,2},{3,11},{11,3},{4,12},{12,4},... | collective-permute-start | bytes 3145736 | tf_op jit(solution)/shard_map/ppermute | solution.py:274
  4.2 14.2 %collective-permute-start.2 = (bf16[4,512,128]{2,1,0:T(8,128)(2,1)}, bf16[4,512,128]{2,1,0:T(8,128)(2,1)}, u32[]{:S(2)}, u32[]{:S(2)}) collective-permute-start(bf16[4,512,128]{2,1,0:T(8,128)(2,1)} %get-tuple-element.7.xq), channel_id=1, source_target_pairs={{0,17},{1,0},{16,1},{17,16},{2,19},{3,2},{18,3},{19,18},{4,21},{5,... | collective-permute-start | bytes 1572872 | tf_op jit(solution)/shard_map/ppermute | solution.py:270
  6.8 14.7 %collective-permute-start = (bf16[4,512,128]{2,1,0:T(8,128)(2,1)}, bf16[4,512,128]{2,1,0:T(8,128)(2,1)}, u32[]{:S(2)}, u32[]{:S(2)}) collective-permute-start(bf16[4,512,128]{2,1,0:T(8,128)(2,1)} %get-tuple-element.7.xq), channel_id=1, source_target_pairs={{0,1},{1,16},{16,17},{17,0},{2,3},{3,18},{18,19},{19,2},{4,5},{5,2... | collective-permute-start | bytes 1572872 | tf_op jit(solution)/shard_map/ppermute | solution.py:270
  6.8 26.0 %collective-permute-start.11 = (bf16[4,256,512]{2,1,0:T(8,128)(2,1)}, bf16[4,256,512]{2,1,0:T(8,128)(2,1)S(1)}, u32[]{:S(2)}, u32[]{:S(2)}) collective-permute-start(bf16[4,256,512]{2,1,0:T(8,128)(2,1)} %get-tuple-element.8.rest_6_.rest_5_), channel_id=1, source_target_pairs={{0,32},{32,64},{64,96},{96,0},{1,33},{33,65},{65,97},{97,1},{2,34}... | collective-permute-start | bytes 3145736 | tf_op jit(solution)/shard_map/ppermute | solution.py:270
  8.1 24.8 %collective-permute-start.9 = (bf16[4,256,512]{2,1,0:T(8,128)(2,1)}, bf16[4,256,512]{2,1,0:T(8,128)(2,1)S(1)}, u32[]{:S(2)}, u32[]{:S(2)}) collective-permute-start(bf16[4,256,512]{2,1,0:T(8,128)(2,1)} %get-tuple-element.8.rest_6_.rest_5_), channel_id=1, source_target_pairs={{0,96},{32,0},{64,32},{96,64},{1,97},{33,1},{65,33},{97,65},{2,98}... | collective-permute-start | bytes 3145736 | tf_op jit(solution)/shard_map/ppermute | solution.py:270
  22.7 14.9 %collective-permute-start.5 = (bf16[4,512,128]{2,1,0:T(8,128)(2,1)S(1)}, bf16[4,512,128]{2,1,0:T(8,128)(2,1)S(1)}, u32[]{:S(2)}, u32[]{:S(2)}) collective-permute-start(bf16[4,512,128]{2,1,0:T(8,128)(2,1)S(1)} %select_add_fusion.rest_0_), channel_id=1, source_target_pairs={{0,2},{2,4},{4,6},{6,0},{1,3},{3,5},{5,7},{7,1},{8,10},{10,12},{12... | collective-permute-start | bytes 1572872 | tf_op jit(solution)/shard_map/ppermute | solution.py:270
  24.4 15.9 %collective-permute-start.4 = (bf16[4,512,128]{2,1,0:T(8,128)(2,1)S(1)}, bf16[4,512,128]{2,1,0:T(8,128)(2,1)S(1)}, u32[]{:S(2)}, u32[]{:S(2)}) collective-permute-start(bf16[4,512,128]{2,1,0:T(8,128)(2,1)S(1)} %select_add_fusion.rest_0_), channel_id=1, source_target_pairs={{0,6},{2,0},{4,2},{6,4},{1,7},{3,1},{5,3},{7,5},{8,14},{10,8},{12,... | collective-permute-start | bytes 1572872 | tf_op jit(solution)/shard_map/ppermute | solution.py:270
  26.6 17.1 %collective-permute-start.1 = (bf16[4,512,128]{2,1,0:T(8,128)(2,1)}, bf16[4,512,128]{2,1,0:T(8,128)(2,1)S(1)}, u32[]{:S(2)}, u32[]{:S(2)}) collective-permute-start(bf16[4,512,128]{2,1,0:T(8,128)(2,1)} %collective-permute-done), channel_id=1, source_target_pairs={{0,1},{1,16},{16,17},{17,0},{2,3},{3,18},{18,19},{19,2},{4,5},{5,2... | collective-permute-start | bytes 1572872 | tf_op jit(solution)/shard_map/ppermute | solution.py:270
  32.8 13.6 %collective-permute-start.13 = (bf16[2,256,512]{2,1,0:T(8,128)(2,1)S(1)}, bf16[2,256,512]{2,1,0:T(8,128)(2,1)S(1)}, u32[]{:S(2)}, u32[]{:S(2)}) collective-permute-start(bf16[2,256,512]{2,1,0:T(8,128)(2,1)S(1)} %slice.33), channel_id=1, source_target_pairs={{0,32},{32,64},{64,96},{96,0},{1,33},{33,65},{65,97},{97,1},{2,34}... | collective-permute-start | bytes 1572872 | tf_op jit(solution)/shard_map/ppermute | solution.py:270
  32.9 31.3 %collective-permute-start.12 = (bf16[4,256,512]{2,1,0:T(8,128)(2,1)S(1)}, bf16[4,256,512]{2,1,0:T(8,128)(2,1)S(1)}, u32[]{:S(2)}, u32[]{:S(2)}) collective-permute-start(bf16[4,256,512]{2,1,0:T(8,128)(2,1)S(1)} %collective-permute-done.11.rest_10_.rest_9_), channel_id=1, source_target_pairs={{0,8},{8,0},{1,9},{9,1},{2,10},{10,2},{3,11},{11,3},{4,12},{12,4},... | collective-permute-start | bytes 3145736 | tf_op jit(solution)/shard_map/ppermute | solution.py:274
  37.6 12.1 %collective-permute-start.15 = (bf16[2,256,512]{2,1,0:T(8,128)(2,1)S(1)}, bf16[2,256,512]{2,1,0:T(8,128)(2,1)S(1)}, u32[]{:S(2)}, u32[]{:S(2)}) collective-permute-start(bf16[2,256,512]{2,1,0:T(8,128)(2,1)S(1)} %slice.34), channel_id=1, source_target_pairs={{0,96},{32,0},{64,32},{96,64},{1,97},{33,1},{65,33},{97,65},{2,98}... | collective-permute-start | bytes 1572872 | tf_op jit(solution)/shard_map/ppermute | solution.py:270
  40.4 25.5 %collective-permute-start.10 = (bf16[4,256,512]{2,1,0:T(8,128)(2,1)S(1)}, bf16[4,256,512]{2,1,0:T(8,128)(2,1)S(1)}, u32[]{:S(2)}, u32[]{:S(2)}) collective-permute-start(bf16[4,256,512]{2,1,0:T(8,128)(2,1)S(1)} %collective-permute-done.9.rest_8_.rest_7_), channel_id=1, source_target_pairs={{0,8},{8,0},{1,9},{9,1},{2,10},{10,2},{3,11},{11,3},{4,12},{12,4},... | collective-permute-start | bytes 3145736 | tf_op jit(solution)/shard_map/ppermute | solution.py:274
  43.7 10.2 %collective-permute-start.18 = (bf16[4,256,128]{2,1,0:T(8,128)(2,1)S(1)}, bf16[4,256,128]{2,1,0:T(8,128)(2,1)S(1)}, u32[]{:S(2)}, u32[]{:S(2)}) collective-permute-start(bf16[4,256,128]{2,1,0:T(8,128)(2,1)S(1)} %slice_add_fusion), channel_id=1, source_target_pairs={{0,6},{2,0},{4,2},{6,4},{1,7},{3,1},{5,3},{7,5},{8,14},{10,8},{12,... | collective-permute-start | bytes 786440 | tf_op jit(solution)/shard_map/ppermute | solution.py:270
  46.4 16.7 %collective-permute-start.14 = (bf16[2,256,512]{2,1,0:T(8,128)(2,1)S(1)}, bf16[2,256,512]{2,1,0:T(8,128)(2,1)S(1)}, u32[]{:S(2)}, u32[]{:S(2)}) collective-permute-start(bf16[2,256,512]{2,1,0:T(8,128)(2,1)S(1)} %collective-permute-done.13.rest_12_.rest_11_), channel_id=1, source_target_pairs={{0,8},{8,0},{1,9},{9,1},{2,10},{10,2},{3,11},{11,3},{4,12},{12,4},... | collective-permute-start | bytes 1572872 | tf_op jit(solution)/shard_map/ppermute | solution.py:274
  49.8 16.1 %collective-permute-start.16 = (bf16[2,256,512]{2,1,0:T(8,128)(2,1)S(1)}, bf16[2,256,512]{2,1,0:T(8,128)(2,1)S(1)}, u32[]{:S(2)}, u32[]{:S(2)}) collective-permute-start(bf16[2,256,512]{2,1,0:T(8,128)(2,1)S(1)} %collective-permute-done.15.rest_14_.rest_13_), channel_id=1, source_target_pairs={{0,8},{8,0},{1,9},{9,1},{2,10},{10,2},{3,11},{11,3},{4,12},{12,4},... | collective-permute-start | bytes 1572872 | tf_op jit(solution)/shard_map/ppermute | solution.py:274
  53.8 12.1 %copy-start = (bf16[4,512,128]{2,1,0:T(8,128)(2,1)S(1)}, bf16[4,512,128]{2,1,0:T(8,128)(2,1)}, u32[]{:S(2)}) copy-start(bf16[4,512,128]{2,1,0:T(8,128)(2,1)} %get-tuple-element.7.xq) | copy-start | bytes 1572868
  53.8 12.1 %copy-start.2 = (bf16[4,256,512]{2,1,0:T(8,128)(2,1)S(1)}, bf16[4,256,512]{2,1,0:T(8,128)(2,1)}, u32[]{:S(2)}) copy-start(bf16[4,256,512]{2,1,0:T(8,128)(2,1)} %get-tuple-element.8.rest_6_.rest_5_) | copy-start | bytes 3145732
  53.8 12.1 %copy-start.3 = (bf16[128,512]{1,0:T(8,128)(2,1)S(1)}, bf16[128,512]{1,0:T(8,128)(2,1)}, u32[]{:S(2)}) copy-start(bf16[128,512]{1,0:T(8,128)(2,1)} %rest_4_.1) | copy-start | bytes 393220
  53.9 9.2 %collective-permute-start.17 = (bf16[4,256,128]{2,1,0:T(8,128)(2,1)S(1)}, bf16[4,256,128]{2,1,0:T(8,128)(2,1)S(1)}, u32[]{:S(2)}, u32[]{:S(2)}) collective-permute-start(bf16[4,256,128]{2,1,0:T(8,128)(2,1)S(1)} %slice_add_fusion.1), channel_id=1, source_target_pairs={{0,2},{2,4},{4,6},{6,0},{1,3},{3,5},{5,7},{7,1},{8,10},{10,12},{12... | collective-permute-start | bytes 786440 | tf_op jit(solution)/shard_map/ppermute | solution.py:270
  63.1 25.1 %collective-permute-start.8 = (bf16[4,512,128]{2,1,0:T(8,128)(2,1)S(1)}, bf16[4,512,128]{2,1,0:T(8,128)(2,1)S(1)}, u32[]{:S(2)}, u32[]{:S(2)}) collective-permute-start(bf16[4,512,128]{2,1,0:T(8,128)(2,1)S(1)} %add_add_fusion.rest_0_), channel_id=1, source_target_pairs={{0,2},{2,4},{4,6},{6,0},{1,3},{3,5},{5,7},{7,1},{8,10},{10,12},{12... | collective-permute-start | bytes 1572872 | tf_op jit(solution)/shard_map/ppermute | solution.py:270
  63.1 25.1 %collective-permute-start.7 = (bf16[4,512,128]{2,1,0:T(8,128)(2,1)S(1)}, bf16[4,512,128]{2,1,0:T(8,128)(2,1)S(1)}, u32[]{:S(2)}, u32[]{:S(2)}) collective-permute-start(bf16[4,512,128]{2,1,0:T(8,128)(2,1)S(1)} %add_add_fusion.rest_0_), channel_id=1, source_target_pairs={{0,4},{2,6},{4,0},{6,2},{1,5},{3,7},{5,1},{7,3},{8,12},{10,14},{12... | collective-permute-start | bytes 1572872 | tf_op jit(solution)/shard_map/ppermute | solution.py:270
  64.2 24.4 %collective-permute-start.6 = (bf16[4,512,128]{2,1,0:T(8,128)(2,1)S(1)}, bf16[4,512,128]{2,1,0:T(8,128)(2,1)S(1)}, u32[]{:S(2)}, u32[]{:S(2)}) collective-permute-start(bf16[4,512,128]{2,1,0:T(8,128)(2,1)S(1)} %add_add_fusion.rest_0_), channel_id=1, source_target_pairs={{0,6},{2,0},{4,2},{6,4},{1,7},{3,1},{5,3},{7,5},{8,14},{10,8},{12,... | collective-permute-start | bytes 1572872 | tf_op jit(solution)/shard_map/ppermute | solution.py:270
  108.9 26.7 %copy-start.1 = (bf16[128,128]{1,0:T(8,128)(2,1)S(1)}, bf16[128,128]{1,0:T(8,128)(2,1)}, u32[]{:S(2)}) copy-start(bf16[128,128]{1,0:T(8,128)(2,1)} %w.1) | copy-start | bytes 98308

commit v14 on v13

--- a/solution.py
+++ b/solution.py
@@ -40,12 +40,12 @@
 
 def prepare(pair_block, norm_gain, head_bias):
     def whole(*shape):
-        return pl.BlockSpec((2,) + shape, lambda i: (i, 0, 0))
+        return pl.BlockSpec((ROWS,) + shape, lambda i: (i, 0, 0))
 
     keys = head_bias.shape[2]
     return pl.pallas_call(
         prepare_kernel,
-        grid=(ROWS // 2,),
+        grid=(1,),
         in_specs=[
             whole(COLS, CHANNELS),
             pl.BlockSpec((1, CHANNELS), lambda i: (0, 0)),

time: 138 us -> 139 us (level)
  no operation moved by 1% of the time
where the time goes in v14:
time: 139 us
  Pallas kernels  46.7 us (34%)
  waiting for transfers between devices  33.2 us (24%)
  blocking collectives  26.6 us (19%)
  starting transfers between devices  25.7 us (18%)
  other arithmetic  2.54 us (2%)
  between operations  2.14 us (2%)
  local copies, waits for them, and re-layouts  1.81 us (1%)
    pallas_call x2, Pallas kernels, attend(): pl.pallas_call(functools.partial(attend_kernel, len(x_ks)), grid=(ROWS //...  40.9 us
    ppermute x14, waiting for transfers between devices, shift(): return lax.ppermute(x, axis, [(i, (i + step) % 4) for i in range(4)])  33.2 us
    all_to_all x1, blocking collectives, shards(): lax.all_to_all(message, ROW_AXES, split_axis=0, concat_axis=0, tiled=True)  26.6 us
    ppermute x14, starting transfers between devices, shift(): return lax.ppermute(x, axis, [(i, (i + step) % 4) for i in range(4)])  16.4 us
    ppermute x5, starting transfers between devices, swap(): return lax.ppermute(x, 'core', [(0, 1), (1, 0)])  9.34 us
    pallas_call x1, Pallas kernels, prepare(): pl.pallas_call(prepare_kernel, grid=(1,), in_specs=[whole(COLS, CHANNELS)...  3.18 us
  transfers between devices with their start and end apart: 19, of which 9 were waited for; matrix products, arithmetic and copies ran while one was open for 3% of the time, Pallas kernels for 15%

profile of v14, /device:TPU:1, one launch (start us, length us, event | category | flops | bytes accessed | tf_op | source)
XLA Modules:
  0.0 138.7 jit_solution(5676304081319002729)
XLA Ops:
  0.0 3.2 %prepare.1 = (bf16[4,512,128]{2,1,0:T(8,128)(2,1)}, bf16[4,256,512]{2,1,0:T(8,128)(2,1)}) custom-call(bf16[4,512,128]{2,1,0:T(8,128)(2,1)} %pair.1, f32[1,128]{1,0:T(1,128)} %bitcast.4, bf16[4,512,256]{2,1,0:T(8,128)(2,1)} %bias.1), custom_call_target="tpu_custom_call" | custom-call | tf_op jit(solution)/shard_map/prepare/pallas_call | solution.py:46
  3.2 1.4 %collective-permute-start.3 = (bf16[4,256,512]{2,1,0:T(8,128)(2,1)}, bf16[4,256,512]{2,1,0:T(8,128)(2,1)S(1)}, u32[]{:S(2)}, u32[]{:S(2)}) collective-permute-start(bf16[4,256,512]{2,1,0:T(8,128)(2,1)} %get-tuple-element.8.rest_6_.rest_5_), channel_id=1, source_target_pairs={{0,8},{8,0},{1,9},{9,1},{2,10},{10,2},{3,11},{11,3},{4,12},{12,4},... | collective-permute-start | bytes 3145736 | tf_op jit(solution)/shard_map/ppermute | solution.py:274
  4.6 2.6 %collective-permute-start.2 = (bf16[4,512,128]{2,1,0:T(8,128)(2,1)}, bf16[4,512,128]{2,1,0:T(8,128)(2,1)}, u32[]{:S(2)}, u32[]{:S(2)}) collective-permute-start(bf16[4,512,128]{2,1,0:T(8,128)(2,1)} %get-tuple-element.7.xq), channel_id=1, source_target_pairs={{0,17},{1,0},{16,1},{17,16},{2,19},{3,2},{18,3},{19,18},{4,21},{5,... | collective-permute-start | bytes 1572872 | tf_op jit(solution)/shard_map/ppermute | solution.py:270
  8.5 1.4 %collective-permute-start.9 = (bf16[4,256,512]{2,1,0:T(8,128)(2,1)}, bf16[4,256,512]{2,1,0:T(8,128)(2,1)S(1)}, u32[]{:S(2)}, u32[]{:S(2)}) collective-permute-start(bf16[4,256,512]{2,1,0:T(8,128)(2,1)} %get-tuple-element.8.rest_6_.rest_5_), channel_id=1, source_target_pairs={{0,96},{32,0},{64,32},{96,64},{1,97},{33,1},{65,33},{97,65},{2,98}... | collective-permute-start | bytes 3145736 | tf_op jit(solution)/shard_map/ppermute | solution.py:270
  11.1 7.7 %collective-permute-done.2 = bf16[4,512,128]{2,1,0:T(8,128)(2,1)} collective-permute-done((bf16[4,512,128]{2,1,0:T(8,128)(2,1)}, bf16[4,512,128]{2,1,0:T(8,128)(2,1)}, u32[]{:S(2)}, u32[]{:S(2)}) %collective-permute-start.2) | collective-permute-done | bytes 524320 | tf_op jit(solution)/shard_map/ppermute | solution.py:270
  18.8 3.1 %collective-permute-done = bf16[4,512,128]{2,1,0:T(8,128)(2,1)} collective-permute-done((bf16[4,512,128]{2,1,0:T(8,128)(2,1)}, bf16[4,512,128]{2,1,0:T(8,128)(2,1)}, u32[]{:S(2)}, u32[]{:S(2)}) %collective-permute-start) | collective-permute-done | bytes 524320 | tf_op jit(solution)/shard_map/ppermute | solution.py:270
  23.2 1.7 %collective-permute-start.5 = (bf16[4,512,128]{2,1,0:T(8,128)(2,1)S(1)}, bf16[4,512,128]{2,1,0:T(8,128)(2,1)S(1)}, u32[]{:S(2)}, u32[]{:S(2)}) collective-permute-start(bf16[4,512,128]{2,1,0:T(8,128)(2,1)S(1)} %select_add_fusion.rest_0_), channel_id=1, source_target_pairs={{0,2},{2,4},{4,6},{6,0},{1,3},{3,5},{5,7},{7,1},{8,10},{10,12},{12... | collective-permute-start | bytes 1572872 | tf_op jit(solution)/shard_map/ppermute | solution.py:270
  24.9 2.2 %collective-permute-start.4 = (bf16[4,512,128]{2,1,0:T(8,128)(2,1)S(1)}, bf16[4,512,128]{2,1,0:T(8,128)(2,1)S(1)}, u32[]{:S(2)}, u32[]{:S(2)}) collective-permute-start(bf16[4,512,128]{2,1,0:T(8,128)(2,1)S(1)} %select_add_fusion.rest_0_), channel_id=1, source_target_pairs={{0,6},{2,0},{4,2},{6,4},{1,7},{3,1},{5,3},{7,5},{8,14},{10,8},{12,... | collective-permute-start | bytes 1572872 | tf_op jit(solution)/shard_map/ppermute | solution.py:270
  27.1 6.1 %collective-permute-done.11.rest_10_.rest_9_ = bf16[4,256,512]{2,1,0:T(8,128)(2,1)S(1)} collective-permute-done((bf16[4,256,512]{2,1,0:T(8,128)(2,1)}, bf16[4,256,512]{2,1,0:T(8,128)(2,1)S(1)}, u32[]{:S(2)}, u32[]{:S(2)}) %collective-permute-start.11) | collective-permute-done | bytes 1048608 | tf_op jit(solution)/shard_map/ppermute | solution.py:270
  33.3 1.3 collective-permute-start.12
  34.7 3.5 %collective-permute-done.5.rest_4_ = bf16[4,512,128]{2,1,0:T(8,128)(2,1)S(1)} collective-permute-done((bf16[4,512,128]{2,1,0:T(8,128)(2,1)S(1)}, bf16[4,512,128]{2,1,0:T(8,128)(2,1)S(1)}, u32[]{:S(2)}, u32[]{:S(2)}) %collective-permute-start.5) | collective-permute-done | bytes 524320 | tf_op jit(solution)/shard_map/ppermute | solution.py:270
  38.2 2.7 %collective-permute-start.15 = (bf16[2,256,512]{2,1,0:T(8,128)(2,1)S(1)}, bf16[2,256,512]{2,1,0:T(8,128)(2,1)S(1)}, u32[]{:S(2)}, u32[]{:S(2)}) collective-permute-start(bf16[2,256,512]{2,1,0:T(8,128)(2,1)S(1)} %slice.34), channel_id=1, source_target_pairs={{0,96},{32,0},{64,32},{96,64},{1,97},{33,1},{65,33},{97,65},{2,98}... | collective-permute-start | bytes 1572872 | tf_op jit(solution)/shard_map/ppermute | solution.py:270
  40.9 2.0 %collective-permute-start.10 = (bf16[4,256,512]{2,1,0:T(8,128)(2,1)S(1)}, bf16[4,256,512]{2,1,0:T(8,128)(2,1)S(1)}, u32[]{:S(2)}, u32[]{:S(2)}) collective-permute-start(bf16[4,256,512]{2,1,0:T(8,128)(2,1)S(1)} %collective-permute-done.9.rest_8_.rest_7_), channel_id=1, source_target_pairs={{0,8},{8,0},{1,9},{9,1},{2,10},{10,2},{3,11},{11,3},{4,12},{12,4},... | collective-permute-start | bytes 3145736 | tf_op jit(solution)/shard_map/ppermute | solution.py:274
  44.2 1.5 %collective-permute-start.18 = (bf16[4,256,128]{2,1,0:T(8,128)(2,1)S(1)}, bf16[4,256,128]{2,1,0:T(8,128)(2,1)S(1)}, u32[]{:S(2)}, u32[]{:S(2)}) collective-permute-start(bf16[4,256,128]{2,1,0:T(8,128)(2,1)S(1)} %slice_add_fusion), channel_id=1, source_target_pairs={{0,6},{2,0},{4,2},{6,4},{1,7},{3,1},{5,3},{7,5},{8,14},{10,8},{12,... | collective-permute-start | bytes 786440 | tf_op jit(solution)/shard_map/ppermute | solution.py:270
  46.9 2.0 %collective-permute-start.14 = (bf16[2,256,512]{2,1,0:T(8,128)(2,1)S(1)}, bf16[2,256,512]{2,1,0:T(8,128)(2,1)S(1)}, u32[]{:S(2)}, u32[]{:S(2)}) collective-permute-start(bf16[2,256,512]{2,1,0:T(8,128)(2,1)S(1)} %collective-permute-done.13.rest_12_.rest_11_), channel_id=1, source_target_pairs={{0,8},{8,0},{1,9},{9,1},{2,10},{10,2},{3,11},{11,3},{4,12},{12,4},... | collective-permute-start | bytes 1572872 | tf_op jit(solution)/shard_map/ppermute | solution.py:274
  48.8 1.6 %collective-permute-done.15.rest_14_.rest_13_ = bf16[2,256,512]{2,1,0:T(8,128)(2,1)S(1)} collective-permute-done((bf16[2,256,512]{2,1,0:T(8,128)(2,1)S(1)}, bf16[2,256,512]{2,1,0:T(8,128)(2,1)S(1)}, u32[]{:S(2)}, u32[]{:S(2)}) %collective-permute-start.15) | collective-permute-done | bytes 524320 | tf_op jit(solution)/shard_map/ppermute | solution.py:270
  50.4 2.6 %collective-permute-start.16 = (bf16[2,256,512]{2,1,0:T(8,128)(2,1)S(1)}, bf16[2,256,512]{2,1,0:T(8,128)(2,1)S(1)}, u32[]{:S(2)}, u32[]{:S(2)}) collective-permute-start(bf16[2,256,512]{2,1,0:T(8,128)(2,1)S(1)} %collective-permute-done.15.rest_14_.rest_13_), channel_id=1, source_target_pairs={{0,8},{8,0},{1,9},{9,1},{2,10},{10,2},{3,11},{11,3},{4,12},{12,4},... | collective-permute-start | bytes 1572872 | tf_op jit(solution)/shard_map/ppermute | solution.py:274
  55.8 7.9 %collective-permute-done.17.rest_2_ = bf16[4,256,128]{2,1,0:T(8,128)(2,1)S(1)} collective-permute-done((bf16[4,256,128]{2,1,0:T(8,128)(2,1)S(1)}, bf16[4,256,128]{2,1,0:T(8,128)(2,1)S(1)}, u32[]{:S(2)}, u32[]{:S(2)}) %collective-permute-start.17) | collective-permute-done | bytes 262176 | tf_op jit(solution)/shard_map/ppermute | solution.py:270
  64.8 1.6 %collective-permute-start.6 = (bf16[4,512,128]{2,1,0:T(8,128)(2,1)S(1)}, bf16[4,512,128]{2,1,0:T(8,128)(2,1)S(1)}, u32[]{:S(2)}, u32[]{:S(2)}) collective-permute-start(bf16[4,512,128]{2,1,0:T(8,128)(2,1)S(1)} %add_add_fusion.rest_0_), channel_id=1, source_target_pairs={{0,6},{2,0},{4,2},{6,4},{1,7},{3,1},{5,3},{7,5},{8,14},{10,8},{12,... | collective-permute-start | bytes 1572872 | tf_op jit(solution)/shard_map/ppermute | solution.py:270
  66.5 20.6 %attend.2.rest_15_ = bf16[16,10,32,128]{3,2,1,0:T(8,128)(2,1)S(1)} custom-call(bf16[4,512,128]{2,1,0:T(8,128)(2,1)S(1)} %copy-done, bf16[4,512,128]{2,1,0:T(8,128)(2,1)S(1)} %select_add_fusion.rest_0_, bf16[4,512,128]{2,1,0:T(8,128)(2,1)S(1)} %collective-permute-done.4.rest_1_, bf16[4,256,128]{2,1,0:T(8,128)(2,1)S(1)} %collective-permute-done.17.rest_2_, ...), custom_call_target="tpu_custom_call" | custom-call | flops 8589934592 | bytes 16777216 | tf_op jit(solution)/shard_map/attend/pallas_call | solution.py:199
  87.0 1.8 %collective-permute-done.8.rest_3_ = bf16[4,512,128]{2,1,0:T(8,128)(2,1)S(1)} collective-permute-done((bf16[4,512,128]{2,1,0:T(8,128)(2,1)S(1)}, bf16[4,512,128]{2,1,0:T(8,128)(2,1)S(1)}, u32[]{:S(2)}, u32[]{:S(2)}) %collective-permute-start.8) | collective-permute-done | bytes 524320 | tf_op jit(solution)/shard_map/ppermute | solution.py:270
  89.1 20.3 %attend.3 = bf16[16,10,32,128]{3,2,1,0:T(8,128)(2,1)S(1)} custom-call(bf16[4,512,128]{2,1,0:T(8,128)(2,1)S(1)} %collective-permute-done.1.xq, bf16[4,512,128]{2,1,0:T(8,128)(2,1)S(1)} %add_add_fusion.rest_0_, bf16[4,512,128]{2,1,0:T(8,128)(2,1)S(1)} %collective-permute-done.6.rest_1_, ...), custom_call_target="tpu_custom_call", output_to_operand_aliasing={{}: (16, {})} | custom-call | flops 8589934592 | bytes 16777216 | tf_op jit(solution)/shard_map/attend/pallas_call | solution.py:199
  109.5 26.6 %all_to_all.5.message = bf16[16,10,32,128]{3,2,1,0:T(8,128)(2,1)S(1)} all-to-all(bf16[16,10,32,128]{3,2,1,0:T(8,128)(2,1)S(1)} %attend.3), channel_id=1, replica_groups=mesh['y'=4,'xh'=2,'core'=2,'z'=4,'xl'=2] {'y','xh','core'}, dimensions={0} | all-to-all | bytes 2621440 | tf_op jit(solution)/shard_map/all_to_all | solution.py:308
  136.1 2.6 %merge.1 = bf16[32,64,128]{2,1,0:T(8,128)(2,1)} custom-call(bf16[16,10,32,128]{3,2,1,0:T(8,128)(2,1)S(1)} %all_to_all.5.message, bf16[128,128]{1,0:T(8,128)(2,1)S(1)} %copy-done.1), custom_call_target="tpu_custom_call" | custom-call | tf_op jit(solution)/shard_map/merge/pallas_call | solution.py:249
  (36 shorter events, 8.5 us)
Async XLA Ops:
  3.2 6.7 %collective-permute-start.3 = (bf16[4,256,512]{2,1,0:T(8,128)(2,1)}, bf16[4,256,512]{2,1,0:T(8,128)(2,1)S(1)}, u32[]{:S(2)}, u32[]{:S(2)}) collective-permute-start(bf16[4,256,512]{2,1,0:T(8,128)(2,1)} %get-tuple-element.8.rest_6_.rest_5_), channel_id=1, source_target_pairs={{0,8},{8,0},{1,9},{9,1},{2,10},{10,2},{3,11},{11,3},{4,12},{12,4},... | collective-permute-start | bytes 3145736 | tf_op jit(solution)/shard_map/ppermute | solution.py:274
  4.6 14.2 %collective-permute-start.2 = (bf16[4,512,128]{2,1,0:T(8,128)(2,1)}, bf16[4,512,128]{2,1,0:T(8,128)(2,1)}, u32[]{:S(2)}, u32[]{:S(2)}) collective-permute-start(bf16[4,512,128]{2,1,0:T(8,128)(2,1)} %get-tuple-element.7.xq), channel_id=1, source_target_pairs={{0,17},{1,0},{16,1},{17,16},{2,19},{3,2},{18,3},{19,18},{4,21},{5,... | collective-permute-start | bytes 1572872 | tf_op jit(solution)/shard_map/ppermute | solution.py:270
  7.2 14.8 %collective-permute-start = (bf16[4,512,128]{2,1,0:T(8,128)(2,1)}, bf16[4,512,128]{2,1,0:T(8,128)(2,1)}, u32[]{:S(2)}, u32[]{:S(2)}) collective-permute-start(bf16[4,512,128]{2,1,0:T(8,128)(2,1)} %get-tuple-element.7.xq), channel_id=1, source_target_pairs={{0,1},{1,16},{16,17},{17,0},{2,3},{3,18},{18,19},{19,2},{4,5},{5,2... | collective-permute-start | bytes 1572872 | tf_op jit(solution)/shard_map/ppermute | solution.py:270
  7.2 26.0 %collective-permute-start.11 = (bf16[4,256,512]{2,1,0:T(8,128)(2,1)}, bf16[4,256,512]{2,1,0:T(8,128)(2,1)S(1)}, u32[]{:S(2)}, u32[]{:S(2)}) collective-permute-start(bf16[4,256,512]{2,1,0:T(8,128)(2,1)} %get-tuple-element.8.rest_6_.rest_5_), channel_id=1, source_target_pairs={{0,32},{32,64},{64,96},{96,0},{1,33},{33,65},{65,97},{97,1},{2,34}... | collective-permute-start | bytes 3145736 | tf_op jit(solution)/shard_map/ppermute | solution.py:270
  8.5 24.8 %collective-permute-start.9 = (bf16[4,256,512]{2,1,0:T(8,128)(2,1)}, bf16[4,256,512]{2,1,0:T(8,128)(2,1)S(1)}, u32[]{:S(2)}, u32[]{:S(2)}) collective-permute-start(bf16[4,256,512]{2,1,0:T(8,128)(2,1)} %get-tuple-element.8.rest_6_.rest_5_), channel_id=1, source_target_pairs={{0,96},{32,0},{64,32},{96,64},{1,97},{33,1},{65,33},{97,65},{2,98}... | collective-permute-start | bytes 3145736 | tf_op jit(solution)/shard_map/ppermute | solution.py:270
  23.2 15.0 %collective-permute-start.5 = (bf16[4,512,128]{2,1,0:T(8,128)(2,1)S(1)}, bf16[4,512,128]{2,1,0:T(8,128)(2,1)S(1)}, u32[]{:S(2)}, u32[]{:S(2)}) collective-permute-start(bf16[4,512,128]{2,1,0:T(8,128)(2,1)S(1)} %select_add_fusion.rest_0_), channel_id=1, source_target_pairs={{0,2},{2,4},{4,6},{6,0},{1,3},{3,5},{5,7},{7,1},{8,10},{10,12},{12... | collective-permute-start | bytes 1572872 | tf_op jit(solution)/shard_map/ppermute | solution.py:270
  24.9 16.0 %collective-permute-start.4 = (bf16[4,512,128]{2,1,0:T(8,128)(2,1)S(1)}, bf16[4,512,128]{2,1,0:T(8,128)(2,1)S(1)}, u32[]{:S(2)}, u32[]{:S(2)}) collective-permute-start(bf16[4,512,128]{2,1,0:T(8,128)(2,1)S(1)} %select_add_fusion.rest_0_), channel_id=1, source_target_pairs={{0,6},{2,0},{4,2},{6,4},{1,7},{3,1},{5,3},{7,5},{8,14},{10,8},{12,... | collective-permute-start | bytes 1572872 | tf_op jit(solution)/shard_map/ppermute | solution.py:270
  27.1 17.1 %collective-permute-start.1 = (bf16[4,512,128]{2,1,0:T(8,128)(2,1)}, bf16[4,512,128]{2,1,0:T(8,128)(2,1)S(1)}, u32[]{:S(2)}, u32[]{:S(2)}) collective-permute-start(bf16[4,512,128]{2,1,0:T(8,128)(2,1)} %collective-permute-done), channel_id=1, source_target_pairs={{0,1},{1,16},{16,17},{17,0},{2,3},{3,18},{18,19},{19,2},{4,5},{5,2... | collective-permute-start | bytes 1572872 | tf_op jit(solution)/shard_map/ppermute | solution.py:270
  33.2 13.7 %collective-permute-start.13 = (bf16[2,256,512]{2,1,0:T(8,128)(2,1)S(1)}, bf16[2,256,512]{2,1,0:T(8,128)(2,1)S(1)}, u32[]{:S(2)}, u32[]{:S(2)}) collective-permute-start(bf16[2,256,512]{2,1,0:T(8,128)(2,1)S(1)} %slice.33), channel_id=1, source_target_pairs={{0,32},{32,64},{64,96},{96,0},{1,33},{33,65},{65,97},{97,1},{2,34}... | collective-permute-start | bytes 1572872 | tf_op jit(solution)/shard_map/ppermute | solution.py:270
  33.3 31.5 %collective-permute-start.12 = (bf16[4,256,512]{2,1,0:T(8,128)(2,1)S(1)}, bf16[4,256,512]{2,1,0:T(8,128)(2,1)S(1)}, u32[]{:S(2)}, u32[]{:S(2)}) collective-permute-start(bf16[4,256,512]{2,1,0:T(8,128)(2,1)S(1)} %collective-permute-done.11.rest_10_.rest_9_), channel_id=1, source_target_pairs={{0,8},{8,0},{1,9},{9,1},{2,10},{10,2},{3,11},{11,3},{4,12},{12,4},... | collective-permute-start | bytes 3145736 | tf_op jit(solution)/shard_map/ppermute | solution.py:274
  38.2 12.2 %collective-permute-start.15 = (bf16[2,256,512]{2,1,0:T(8,128)(2,1)S(1)}, bf16[2,256,512]{2,1,0:T(8,128)(2,1)S(1)}, u32[]{:S(2)}, u32[]{:S(2)}) collective-permute-start(bf16[2,256,512]{2,1,0:T(8,128)(2,1)S(1)} %slice.34), channel_id=1, source_target_pairs={{0,96},{32,0},{64,32},{96,64},{1,97},{33,1},{65,33},{97,65},{2,98}... | collective-permute-start | bytes 1572872 | tf_op jit(solution)/shard_map/ppermute | solution.py:270
  40.9 25.5 %collective-permute-start.10 = (bf16[4,256,512]{2,1,0:T(8,128)(2,1)S(1)}, bf16[4,256,512]{2,1,0:T(8,128)(2,1)S(1)}, u32[]{:S(2)}, u32[]{:S(2)}) collective-permute-start(bf16[4,256,512]{2,1,0:T(8,128)(2,1)S(1)} %collective-permute-done.9.rest_8_.rest_7_), channel_id=1, source_target_pairs={{0,8},{8,0},{1,9},{9,1},{2,10},{10,2},{3,11},{11,3},{4,12},{12,4},... | collective-permute-start | bytes 3145736 | tf_op jit(solution)/shard_map/ppermute | solution.py:274
  44.2 10.3 %collective-permute-start.18 = (bf16[4,256,128]{2,1,0:T(8,128)(2,1)S(1)}, bf16[4,256,128]{2,1,0:T(8,128)(2,1)S(1)}, u32[]{:S(2)}, u32[]{:S(2)}) collective-permute-start(bf16[4,256,128]{2,1,0:T(8,128)(2,1)S(1)} %slice_add_fusion), channel_id=1, source_target_pairs={{0,6},{2,0},{4,2},{6,4},{1,7},{3,1},{5,3},{7,5},{8,14},{10,8},{12,... | collective-permute-start | bytes 786440 | tf_op jit(solution)/shard_map/ppermute | solution.py:270
  46.9 16.8 %collective-permute-start.14 = (bf16[2,256,512]{2,1,0:T(8,128)(2,1)S(1)}, bf16[2,256,512]{2,1,0:T(8,128)(2,1)S(1)}, u32[]{:S(2)}, u32[]{:S(2)}) collective-permute-start(bf16[2,256,512]{2,1,0:T(8,128)(2,1)S(1)} %collective-permute-done.13.rest_12_.rest_11_), channel_id=1, source_target_pairs={{0,8},{8,0},{1,9},{9,1},{2,10},{10,2},{3,11},{11,3},{4,12},{12,4},... | collective-permute-start | bytes 1572872 | tf_op jit(solution)/shard_map/ppermute | solution.py:274
  50.4 16.0 %collective-permute-start.16 = (bf16[2,256,512]{2,1,0:T(8,128)(2,1)S(1)}, bf16[2,256,512]{2,1,0:T(8,128)(2,1)S(1)}, u32[]{:S(2)}, u32[]{:S(2)}) collective-permute-start(bf16[2,256,512]{2,1,0:T(8,128)(2,1)S(1)} %collective-permute-done.15.rest_14_.rest_13_), channel_id=1, source_target_pairs={{0,8},{8,0},{1,9},{9,1},{2,10},{10,2},{3,11},{11,3},{4,12},{12,4},... | collective-permute-start | bytes 1572872 | tf_op jit(solution)/shard_map/ppermute | solution.py:274
  54.4 12.1 %copy-start = (bf16[4,512,128]{2,1,0:T(8,128)(2,1)S(1)}, bf16[4,512,128]{2,1,0:T(8,128)(2,1)}, u32[]{:S(2)}) copy-start(bf16[4,512,128]{2,1,0:T(8,128)(2,1)} %get-tuple-element.7.xq) | copy-start | bytes 1572868
  54.4 12.1 %copy-start.2 = (bf16[4,256,512]{2,1,0:T(8,128)(2,1)S(1)}, bf16[4,256,512]{2,1,0:T(8,128)(2,1)}, u32[]{:S(2)}) copy-start(bf16[4,256,512]{2,1,0:T(8,128)(2,1)} %get-tuple-element.8.rest_6_.rest_5_) | copy-start | bytes 3145732
  54.4 12.1 %copy-start.3 = (bf16[128,512]{1,0:T(8,128)(2,1)S(1)}, bf16[128,512]{1,0:T(8,128)(2,1)}, u32[]{:S(2)}) copy-start(bf16[128,512]{1,0:T(8,128)(2,1)} %rest_4_.1) | copy-start | bytes 393220
  54.4 9.2 %collective-permute-start.17 = (bf16[4,256,128]{2,1,0:T(8,128)(2,1)S(1)}, bf16[4,256,128]{2,1,0:T(8,128)(2,1)S(1)}, u32[]{:S(2)}, u32[]{:S(2)}) collective-permute-start(bf16[4,256,128]{2,1,0:T(8,128)(2,1)S(1)} %slice_add_fusion.1), channel_id=1, source_target_pairs={{0,2},{2,4},{4,6},{6,0},{1,3},{3,5},{5,7},{7,1},{8,10},{10,12},{12... | collective-permute-start | bytes 786440 | tf_op jit(solution)/shard_map/ppermute | solution.py:270
  63.7 25.1 %collective-permute-start.8 = (bf16[4,512,128]{2,1,0:T(8,128)(2,1)S(1)}, bf16[4,512,128]{2,1,0:T(8,128)(2,1)S(1)}, u32[]{:S(2)}, u32[]{:S(2)}) collective-permute-start(bf16[4,512,128]{2,1,0:T(8,128)(2,1)S(1)} %add_add_fusion.rest_0_), channel_id=1, source_target_pairs={{0,2},{2,4},{4,6},{6,0},{1,3},{3,5},{5,7},{7,1},{8,10},{10,12},{12... | collective-permute-start | bytes 1572872 | tf_op jit(solution)/shard_map/ppermute | solution.py:270
  63.7 25.1 %collective-permute-start.7 = (bf16[4,512,128]{2,1,0:T(8,128)(2,1)S(1)}, bf16[4,512,128]{2,1,0:T(8,128)(2,1)S(1)}, u32[]{:S(2)}, u32[]{:S(2)}) collective-permute-start(bf16[4,512,128]{2,1,0:T(8,128)(2,1)S(1)} %add_add_fusion.rest_0_), channel_id=1, source_target_pairs={{0,4},{2,6},{4,0},{6,2},{1,5},{3,7},{5,1},{7,3},{8,12},{10,14},{12... | collective-permute-start | bytes 1572872 | tf_op jit(solution)/shard_map/ppermute | solution.py:270
  64.8 24.3 %collective-permute-start.6 = (bf16[4,512,128]{2,1,0:T(8,128)(2,1)S(1)}, bf16[4,512,128]{2,1,0:T(8,128)(2,1)S(1)}, u32[]{:S(2)}, u32[]{:S(2)}) collective-permute-start(bf16[4,512,128]{2,1,0:T(8,128)(2,1)S(1)} %add_add_fusion.rest_0_), channel_id=1, source_target_pairs={{0,6},{2,0},{4,2},{6,4},{1,7},{3,1},{5,3},{7,5},{8,14},{10,8},{12,... | collective-permute-start | bytes 1572872 | tf_op jit(solution)/shard_map/ppermute | solution.py:270
  109.4 26.7 %copy-start.1 = (bf16[128,128]{1,0:T(8,128)(2,1)S(1)}, bf16[128,128]{1,0:T(8,128)(2,1)}, u32[]{:S(2)}) copy-start(bf16[128,128]{1,0:T(8,128)(2,1)} %w.1) | copy-start | bytes 98308
